TPU v7x, 128 devices: a whole 4x4x4 slice. The times are simulated.
128 devices in a mesh: chan: 32 (over y, z, core), tm: 4 (over x).
Axes of the slice: x: 4, y: 4, z: 4, core: 2. Of those that a mesh axis runs over, the one named last changes fastest.
Arguments:
- records: bfloat16 [16, 1920, 4096], P('tm', 'chan'), may hold values from -6 to 6
- quality: int32 [16, 4096], P('tm', 'chan'), may hold values 0 or 1
- tile_list: int32 [96, 2], replicated, may hold values from 0 to 31, as said below
- tile_slot_owner: int32 [96], replicated, may hold values from 0 to 191, as said below
Outputs:
- correlations: float32 [192, 16, 128, 512], P('chan', 'tm')
Inputs may be any that keep to these rules, and one draw needn't show every extreme that they name: `tile_list`: row t holds source block t // 3 and a receiver block within 2 blocks of it along the looped fibre (mod 32); the receivers of one source block are distinct. `tile_slot_owner`: entry t is owner * 6 + slot; the tiles of source block b are owned by block b's device or device b + 1 (mod 32); no slot holds two tiles; some device owns exactly 6 tiles.
All inputs are finite; a program needn't handle non-finite values. No bound on the sum of `quality` on one device may be relied on, other than what follows from the above.
Results may differ from a plain program's by a relative error of at most 0.015.
Values may be sent and summed in bfloat16 or wider, within the bound.
No kernel may reach another device: no remote copies, remote signals or barrier semaphores. Data moves between devices by JAX's collectives and lax.ppermute only.
A program may use at most 192 MiB of HBM per device.

v0:
```python
import math

import jax
import jax.numpy as jnp
from jax import lax
from jax.sharding import PartitionSpec as P

L = 1920
F = 768
K0 = 8
HALF = 32
LAG_COUNT = 512
BLOCK_CHANNELS = 128
VIRTUAL_SOURCES = 16
REACH = 2
SEG_DEV = 4
TCAP = 6


def shifted(block, axis, distance):
    devices = range(lax.axis_size(axis))
    route = [((i - distance) % len(devices), i) for i in devices]
    return lax.ppermute(block, axis, route)


def forward_table():
    samples = jnp.arange(L, dtype=jnp.int32)[:, None]
    bins = K0 + jnp.arange(F, dtype=jnp.int32)[None, :]
    angles = jnp.mod(samples * bins, L).astype(jnp.float32) * (2.0 * math.pi / L)
    window = 0.5 - 0.5 * jnp.cos(
        jnp.arange(L, dtype=jnp.int32).astype(jnp.float32) * (2.0 * math.pi / L)
    )
    return jnp.concatenate([jnp.cos(angles), -jnp.sin(angles)], axis=1) * window[:, None]


def smoothing():
    indices = jnp.arange(F, dtype=jnp.int32)
    in_window = (jnp.abs(indices[:, None] - indices[None, :]) <= HALF).astype(jnp.float32)
    return in_window / jnp.sum(in_window, axis=0, keepdims=True)


def inverse_table(seg_total):
    bins = K0 + jnp.arange(F, dtype=jnp.int32)[:, None]
    lag_index = jnp.arange(LAG_COUNT, dtype=jnp.int32)[None, :] - LAG_COUNT // 2
    angles = jnp.mod(bins * lag_index, L).astype(jnp.float32) * (2.0 * math.pi / L)
    factor = 1.0 / math.sqrt(seg_total * F)
    return (jnp.concatenate([jnp.cos(angles), -jnp.sin(angles)], axis=0) * factor).astype(
        jnp.bfloat16
    )


def whiten(pieces):
    spectrum = jnp.einsum(
        "snc,nf->scf", pieces.astype(jnp.float32), forward_table(), precision=lax.Precision.HIGHEST
    )
    real_part = spectrum[..., :F]
    imag_part = spectrum[..., F:]
    magnitude = jnp.sqrt(real_part * real_part + imag_part * imag_part)
    level = jnp.einsum("scf,fg->scg", magnitude, smoothing(), precision=lax.Precision.HIGHEST)
    inverse_level = 1.0 / (level + 1e-06)
    return (spectrum * jnp.concatenate([inverse_level, inverse_level], axis=-1)).astype(
        jnp.bfloat16
    )


def cross_spectra(source_rows, receiver_rows):
    src_real = source_rows[:, :, None, :F].astype(jnp.float32)
    src_imag = source_rows[:, :, None, F:].astype(jnp.float32)
    rcv_real = receiver_rows[:, None, :, :F].astype(jnp.float32)
    rcv_imag = receiver_rows[:, None, :, F:].astype(jnp.float32)
    real_sum = jnp.sum(src_real * rcv_real + src_imag * rcv_imag, axis=0)
    imag_sum = jnp.sum(src_real * rcv_imag - src_imag * rcv_real, axis=0)
    return jnp.concatenate([real_sum, imag_sum], axis=-1).astype(jnp.bfloat16)


def correlate(nearby, source_at, receiver_at, inverse, source_count):
    stride = BLOCK_CHANNELS // VIRTUAL_SOURCES
    seg_rows = nearby.shape[0]
    groups = seg_rows // SEG_DEV
    source_rows = lax.dynamic_index_in_dim(nearby, source_at, 1, keepdims=False)[:, ::stride]
    receiver_rows = lax.dynamic_index_in_dim(nearby, receiver_at, 1, keepdims=False)
    source_rows = source_rows.reshape(groups, SEG_DEV, source_count, 2 * F)
    receiver_rows = receiver_rows.reshape(groups, SEG_DEV, BLOCK_CHANNELS, 2 * F)
    cross_part = jax.vmap(cross_spectra)(source_rows, receiver_rows)
    return jnp.einsum("gvck,kl->vcl", cross_part, inverse, preferred_element_type=jnp.float32)


def deliver(stacked, halo_width, own_index, chan_count):
    pieces = []
    for offset in range(-halo_width, halo_width + 1):
        if offset == 0:
            pieces.append(stacked)
        else:
            pieces.append(shifted(stacked, "chan", -offset))
    nearby = jnp.concatenate(pieces, axis=1)

    def locate(block):
        return (
            jnp.mod(block - own_index + chan_count // 2, chan_count) - chan_count // 2 + halo_width
        )

    return (nearby, locate)


def stack_over_time(partial_value):
    return lax.psum_scatter(
        partial_value.astype(jnp.bfloat16), "tm", scatter_dimension=1, tiled=True
    ).astype(jnp.float32)


def per_device(records, quality, tile_list, tile_slot_owner):
    chan_count = lax.axis_size("chan")
    segment_time_count = lax.axis_size("tm")
    own_index = lax.axis_index("chan")
    inverse = inverse_table(records.shape[0] * segment_time_count)
    white = whiten(lax.all_to_all(records, "chan", split_axis=2, concat_axis=1, tiled=True))
    white = white * quality.astype(jnp.bfloat16)[:, :, None]
    source_count = VIRTUAL_SOURCES
    stacked = white[:, None]
    tile_total = tile_slot_owner.shape[0]
    nearby, locate = deliver(stacked, REACH + 1, own_index, chan_count)

    def single_slot(slot_index):
        matches = tile_slot_owner == own_index * TCAP + slot_index
        is_used = jnp.any(matches)
        tile_index = jnp.sum(jnp.where(matches, jnp.arange(tile_total, dtype=jnp.int32), 0))
        source_block = tile_list[tile_index, 0]
        receiver_block = tile_list[tile_index, 1]
        return lax.cond(
            is_used,
            lambda: correlate(
                nearby, locate(source_block), locate(receiver_block), inverse, source_count
            ),
            lambda: jnp.zeros((source_count, BLOCK_CHANNELS, LAG_COUNT), jnp.float32),
        )

    partial_value = lax.map(single_slot, jnp.arange(TCAP, dtype=jnp.int32))
    return stack_over_time(partial_value)


def solution(mesh):
    placed = (P("tm", "chan", None), P("tm", "chan"), P(), P())
    return jax.shard_map(
        per_device,
        mesh=mesh,
        in_specs=placed,
        out_specs=P("chan", "tm", None, None),
        check_vma=False,
    )
```

profile of v0, /device:TPU:0, one launch (start us, length us, event | category | flops | bytes accessed | tf_op | source)
XLA Modules:
  0.0 633.1 jit_solution(18381512295850458456)
XLA Ops:
  6.5 7.2 %copy.26 = bf16[4,60,4096]{1,0,2:T(4,128)(2,1)} copy(bf16[4,60,4096]{2,0,1:T(4,128)(2,1)} %param.8) | data formatting | bytes 3932160 | tf_op args[0]
  13.8 14.9 %reshape.148 = bf16[32,2,15360]{2,1,0:T(2,128)(2,1)} reshape(bf16[4096,4,60]{2,1,0:T(4,128)(2,1)} %bitcast.64) | data formatting | bytes 3932160
  28.7 8.6 %all-to-all-start = ((bf16[32,2,15360]{2,1,0:T(2,128)(2,1)}), bf16[32,2,15360]{2,1,0:T(2,128)(2,1)S(1)}, u32[]{:S(2)}, u32[]{:S(2)}) async-start(bf16[32,2,15360]{2,1,0:T(2,128)(2,1)} %reshape.148), calls=%async_computation | async-start | bytes 3932160 | tf_op jit(solution)/shard_map/all_to_all | solution.py:116
  37.5 26.4 %fusion.23 = (f32[1920,768]{0,1:T(8,128)}, f32[1920,768]{0,1:T(8,128)}) fusion(s32[768]{0:T(1024)S(1)} %iota_add_fusion), kind=kLoop, calls=%fused_computation.37 | loop fusion | flops 14745600 | bytes 11799552 | tf_op jit(solution)/shard_map/cos | solution.py:33
  63.9 0.8 all-to-all-done
  64.7 15.2 %reshape.149 = bf16[4096,4,60]{2,1,0:T(4,128)(2,1)} reshape(bf16[32,2,15360]{2,1,0:T(2,128)(2,1)S(1)} %all-to-all-done) | data formatting | bytes 3932160
  79.9 6.3 %copy.27 = bf16[4,60,32,128]{3,0,1,2:T(4,128)(2,1)S(1)} copy(bf16[4,60,32,128]{1,0,3,2:T(4,128)(2,1)} %bitcast.63) | data formatting | bytes 3932160 | tf_op jit(solution)/shard_map/all_to_all | solution.py:116
  86.3 13.9 %fusion.25 = f32[4,128,1536]{1,2,0:T(8,128)S(1)} fusion(f32[1920,768]{0,1:T(8,128)} %get-tuple-element.266, f32[1920,768]{0,1:T(8,128)} %get-tuple-element.265, f32[1920]{0:T(1024)S(1)} %multiply_subtract_fusion, bf16[4,1920,128]{2,0,1:T(4,128)(2,1)S(1)} %bitcast.65), kind=kOutput, calls=%fused_computation.39 | convolution fusion | flops 18125291520 | bytes 16915968 | tf_op jit(solution)/shard_map/snc,nf->scf/dot_general | solution.py:53
  100.2 4.4 add_divide_fusion
  105.0 0.9 collective-permute-start
  105.8 1.5 collective-permute-start.1
  107.3 0.7 collective-permute-start.2
  108.0 4.4 collective-permute-start.3
  112.4 6.4 %fusion.43 = (f32[768,512]{1,0:T(8,128)S(1)}, f32[768,512]{1,0:T(8,128)S(1)}) fusion(s32[512]{0:T(512)S(1)} %iota_add_fusion.1, s32[768]{0:T(1024)S(1)} %iota_add_fusion), kind=kLoop, calls=%fused_computation.64 | loop fusion | flops 3932160 | bytes 3150848 | tf_op jit(solution)/shard_map/cos | solution.py:47
  119.5 1.6 fusion.29
  121.1 22.4 %collective-permute-done = bf16[4,1,128,1536]{2,3,0,1:T(8,128)(2,1)} collective-permute-done((bf16[4,1,128,1536]{2,3,0,1:T(8,128)(2,1)S(1)}, bf16[4,1,128,1536]{2,3,0,1:T(8,128)(2,1)}, u32[]{:S(2)}, u32[]{:S(2)}) %collective-permute-start) | collective-permute-done | bytes 1572896 | tf_op jit(solution)/shard_map/ppermute | solution.py:23
  143.5 19.6 %collective-permute-start.5 = (bf16[4,1,128,1536]{2,3,0,1:T(8,128)(2,1)S(1)}, bf16[4,1,128,1536]{2,3,0,1:T(8,128)(2,1)S(1)}, u32[]{:S(2)}, u32[]{:S(2)}) collective-permute-start(bf16[4,1,128,1536]{2,3,0,1:T(8,128)(2,1)S(1)} %fusion.37), channel_id=1, source_target_pairs={{12,0},{16,4},{20,8},{24,12},{28,16},{32,20},{36,24},{40,28},{44,3... | collective-permute-start | bytes 4718600 | tf_op jit(solution)/shard_map/ppermute | solution.py:23
  163.1 2.7 constant_dynamic-update-slice_fusion.7
  165.7 12.5 %collective-permute-done.1 = bf16[4,1,128,1536]{2,3,0,1:T(8,128)(2,1)} collective-permute-done((bf16[4,1,128,1536]{2,3,0,1:T(8,128)(2,1)S(1)}, bf16[4,1,128,1536]{2,3,0,1:T(8,128)(2,1)}, u32[]{:S(2)}, u32[]{:S(2)}) %collective-permute-start.1) | collective-permute-done | bytes 1572896 | tf_op jit(solution)/shard_map/ppermute | solution.py:23
  178.2 2.7 constant_dynamic-update-slice_fusion.6
  180.9 16.2 %collective-permute-done.2 = bf16[4,1,128,1536]{2,3,0,1:T(8,128)(2,1)S(1)} collective-permute-done((bf16[4,1,128,1536]{2,3,0,1:T(8,128)(2,1)S(1)}, bf16[4,1,128,1536]{2,3,0,1:T(8,128)(2,1)S(1)}, u32[]{:S(2)}, u32[]{:S(2)}) %collective-permute-start.2) | collective-permute-done | bytes 1572896 | tf_op jit(solution)/shard_map/ppermute | solution.py:23
  197.2 1.2 constant_dynamic-update-slice_fusion.5
  198.4 1.3 constant_dynamic-update-slice_fusion.4
  199.7 1.2 constant_dynamic-update-slice_fusion.3
  200.9 4.6 collective-permute-done.4
  205.5 1.3 constant_dynamic-update-slice_fusion.2
  206.8 20.6 %collective-permute-done.5 = bf16[4,1,128,1536]{2,3,0,1:T(8,128)(2,1)S(1)} collective-permute-done((bf16[4,1,128,1536]{2,3,0,1:T(8,128)(2,1)S(1)}, bf16[4,1,128,1536]{2,3,0,1:T(8,128)(2,1)S(1)}, u32[]{:S(2)}, u32[]{:S(2)}) %collective-permute-start.5) | collective-permute-done | bytes 1572896 | tf_op jit(solution)/shard_map/ppermute | solution.py:23
  227.4 1.2 constant_dynamic-update-slice_fusion.1
  228.7 14.6 %copy.31 = bf16[4,7,128,1536]{3,2,0,1:T(8,128)(2,1)} copy(bf16[4,7,128,1536]{2,3,0,1:T(8,128)(2,1)} %constant_dynamic-update-slice_fusion.1) | data formatting | bytes 22020096 | tf_op jit(solution)/shard_map/while | solution.py:137
  243.2 72.5 %while.11 = (s32[]{:T(128)}, bf16[6,16,128,512]{3,2,1,0:T(8,128)(2,1)}, s32[6]{0:T(128)S(1)}, s32[]{:T(128)}, s32[96]{0:T(128)S(1)}, /*index=5*/s32[96,2]{0,1:T(...) while((s32[]{:T(128)}, bf16[6,16,128,512]{3,2,1,0:T(8,128)(2,1)}, ...), condition=%wide.region_8.9_spmd, body=%wide.region_1.8_spmd.sunk | while | flops 3281879552 | bytes 42273216 | solution.py:137
  245.8 23.4 %conditional.2 = (bf16[1,16,128,512]{3,2,1,0:T(8,128)(2,1)S(1)}) conditional(s32[]{:T(128)} %convert_element_type.149, () %tuple.55, (pred[96]{0:T(512)(128)(4,1)S(1)}, s32[96]{0:T(128)S(1)}, s32[96,2]{0,1:T(2,128)S(1)}, s32[]{:T(128)}, bf16[4,7,128,1536]{3,2,0,1:T(8,128)(2,1)}, /*index=5*/bf16[1536,512]{1,0:T(8,128)(2,1)}) %tuple.56), branch_computations={%region_3.3_spmd, %region_4.7_spmd} | conditional | flops 3281879296 | bytes 38077356 | solution.py:129
  250.3 3.3 dynamic-slice_bitcast_fusion.1
  253.8 1.6 slice.29
  255.5 10.2 %add_reduce_fusion = (bf16[16,128,768]{2,1,0:T(8,128)(2,1)S(1)}, bf16[16,128,768]{2,1,0:T(8,128)(2,1)S(1)}) fusion(f32[4,128,768]{2,1,0:T(8,128)S(1)} %get-tuple-element.258, f32[4,16,768]{2,1,0:T(8,128)S(1)} %get-tuple-element.260, f32[4,128,768]{2,1,0:T(8,128)S(1)} %get-tuple-element.257, f32[4,16,768]{2,1,0:T(8,128)S(1)} %get-tuple-element.259), kind=kLoop, calls=%fused_computation.1 | loop fusion | flops 47185920 | bytes 9830400 | tf_op jit(solution)/shard_map/while/body/eval_jaxpr/cond/branch_1_fun/vmap()/reduce_sum | solution.py:71
  265.6 3.6 fusion.4
  269.2 1.6 constant_dynamic-update-slice_fusion.9
  273.4 23.5 %conditional.2 = (bf16[1,16,128,512]{3,2,1,0:T(8,128)(2,1)S(1)}) conditional(s32[]{:T(128)} %convert_element_type.149, () %tuple.55, (pred[96]{0:T(512)(128)(4,1)S(1)}, s32[96]{0:T(128)S(1)}, s32[96,2]{0,1:T(2,128)S(1)}, s32[]{:T(128)}, bf16[4,7,128,1536]{3,2,0,1:T(8,128)(2,1)}, /*index=5*/bf16[1536,512]{1,0:T(8,128)(2,1)}) %tuple.56), branch_computations={%region_3.3_spmd, %region_4.7_spmd} | conditional | flops 3281879296 | bytes 38077356 | solution.py:129
  277.9 3.3 dynamic-slice_bitcast_fusion.1
  281.4 1.6 slice.29
  283.0 10.2 %add_reduce_fusion = (bf16[16,128,768]{2,1,0:T(8,128)(2,1)S(1)}, bf16[16,128,768]{2,1,0:T(8,128)(2,1)S(1)}) fusion(f32[4,128,768]{2,1,0:T(8,128)S(1)} %get-tuple-element.258, f32[4,16,768]{2,1,0:T(8,128)S(1)} %get-tuple-element.260, f32[4,128,768]{2,1,0:T(8,128)S(1)} %get-tuple-element.257, f32[4,16,768]{2,1,0:T(8,128)S(1)} %get-tuple-element.259), kind=kLoop, calls=%fused_computation.1 | loop fusion | flops 47185920 | bytes 9830400 | tf_op jit(solution)/shard_map/while/body/eval_jaxpr/cond/branch_1_fun/vmap()/reduce_sum | solution.py:71
  293.2 3.6 fusion.4
  296.8 1.5 constant_dynamic-update-slice_fusion.9
  301.1 1.5 constant_dynamic-update-slice_fusion.9
  305.4 1.6 constant_dynamic-update-slice_fusion.9
  309.8 1.6 constant_dynamic-update-slice_fusion.9
  314.1 1.6 constant_dynamic-update-slice_fusion.9
  317.6 303.2 %all-reduce.3.cloned.1.call-done = bf16[6,16,128,512]{3,2,1,0:T(8,128)(2,1)} async-done(((bf16[6,16,128,512]{3,2,1,0:T(8,128)(2,1)}), bf16[6,16,128,512]{3,2,1,0:T(8,128)(2,1)}) %all-reduce.3.cloned.1.call-update) | async-done | bytes 12582928
  620.8 5.5 dynamic-slice_convert_fusion
  (59 shorter events, 15.0 us)
Async XLA Ops:
  28.7 8.6 %copy-start.3 = (s32[4,128]{1,0:T(4,128)S(1)}, s32[4,128]{1,0:T(4,128)}, u32[]{:S(2)}) copy-start(s32[4,128]{1,0:T(4,128)} %param.9) | copy-start | bytes 6148
  28.7 36.0 %all-to-all-start = ((bf16[32,2,15360]{2,1,0:T(2,128)(2,1)}), bf16[32,2,15360]{2,1,0:T(2,128)(2,1)S(1)}, u32[]{:S(2)}, u32[]{:S(2)}) async-start(bf16[32,2,15360]{2,1,0:T(2,128)(2,1)} %reshape.148), calls=%async_computation | async-start | bytes 3932160 | tf_op jit(solution)/shard_map/all_to_all | solution.py:116
  37.2 583.5 %all-reduce.3.cloned.1.call-start = ((), (), s32[]{:S(2)}) async-start(), calls=%async_computation.1 | async-start | bytes 25165824
  105.0 38.5 %collective-permute-start = (bf16[4,1,128,1536]{2,3,0,1:T(8,128)(2,1)S(1)}, bf16[4,1,128,1536]{2,3,0,1:T(8,128)(2,1)}, u32[]{:S(2)}, u32[]{:S(2)}) collective-permute-start(bf16[4,1,128,1536]{2,3,0,1:T(8,128)(2,1)S(1)} %fusion.37), channel_id=1, source_target_pairs={{116,0},{120,4},{124,8},{0,12},{4,16},{8,20},{12,24},{16,28},{20,3... | collective-permute-start | bytes 4718600 | tf_op jit(solution)/shard_map/ppermute | solution.py:23
  105.8 72.4 %collective-permute-start.1 = (bf16[4,1,128,1536]{2,3,0,1:T(8,128)(2,1)S(1)}, bf16[4,1,128,1536]{2,3,0,1:T(8,128)(2,1)}, u32[]{:S(2)}, u32[]{:S(2)}) collective-permute-start(bf16[4,1,128,1536]{2,3,0,1:T(8,128)(2,1)S(1)} %fusion.37), channel_id=1, source_target_pairs={{120,0},{124,4},{0,8},{4,12},{8,16},{12,20},{16,24},{20,28},{24,32... | collective-permute-start | bytes 4718600 | tf_op jit(solution)/shard_map/ppermute | solution.py:23
  107.3 89.8 %collective-permute-start.2 = (bf16[4,1,128,1536]{2,3,0,1:T(8,128)(2,1)S(1)}, bf16[4,1,128,1536]{2,3,0,1:T(8,128)(2,1)S(1)}, u32[]{:S(2)}, u32[]{:S(2)}) collective-permute-start(bf16[4,1,128,1536]{2,3,0,1:T(8,128)(2,1)S(1)} %fusion.37), channel_id=1, source_target_pairs={{124,0},{0,4},{4,8},{8,12},{12,16},{16,20},{20,24},{24,28},{28,32}... | collective-permute-start | bytes 4718600 | tf_op jit(solution)/shard_map/ppermute | solution.py:23
  108.0 91.7 %collective-permute-start.3 = (bf16[4,1,128,1536]{2,3,0,1:T(8,128)(2,1)S(1)}, bf16[4,1,128,1536]{2,3,0,1:T(8,128)(2,1)S(1)}, u32[]{:S(2)}, u32[]{:S(2)}) collective-permute-start(bf16[4,1,128,1536]{2,3,0,1:T(8,128)(2,1)S(1)} %fusion.37), channel_id=1, source_target_pairs={{4,0},{8,4},{12,8},{16,12},{20,16},{24,20},{28,24},{32,28},{36,32}... | collective-permute-start | bytes 4718600 | tf_op jit(solution)/shard_map/ppermute | solution.py:23
  118.9 86.6 %collective-permute-start.4 = (bf16[4,1,128,1536]{2,3,0,1:T(8,128)(2,1)S(1)}, bf16[4,1,128,1536]{2,3,0,1:T(8,128)(2,1)S(1)}, u32[]{:S(2)}, u32[]{:S(2)}) collective-permute-start(bf16[4,1,128,1536]{2,3,0,1:T(8,128)(2,1)S(1)} %fusion.37), channel_id=1, source_target_pairs={{8,0},{12,4},{16,8},{20,12},{24,16},{28,20},{32,24},{36,28},{40,32... | collective-permute-start | bytes 4718600 | tf_op jit(solution)/shard_map/ppermute | solution.py:23
  143.5 83.9 %collective-permute-start.5 = (bf16[4,1,128,1536]{2,3,0,1:T(8,128)(2,1)S(1)}, bf16[4,1,128,1536]{2,3,0,1:T(8,128)(2,1)S(1)}, u32[]{:S(2)}, u32[]{:S(2)}) collective-permute-start(bf16[4,1,128,1536]{2,3,0,1:T(8,128)(2,1)S(1)} %fusion.37), channel_id=1, source_target_pairs={{12,0},{16,4},{20,8},{24,12},{28,16},{32,20},{36,24},{40,28},{44,3... | collective-permute-start | bytes 4718600 | tf_op jit(solution)/shard_map/ppermute | solution.py:23
  228.6 14.6 %copy-start.1 = (s32[96,2]{0,1:T(2,128)S(1)}, s32[96,2]{0,1:T(2,128)}, u32[]{:S(2)}) copy-start(s32[96,2]{0,1:T(2,128)} %param.10) | copy-start | bytes 2308
  228.6 14.6 %copy-start.2 = (s32[96]{0:T(128)S(1)}, s32[96]{0:T(128)}, u32[]{:S(2)}) copy-start(s32[96]{0:T(128)} %param.11) | copy-start | bytes 1156
  255.4 10.2 %copy-start = (bf16[1536,512]{1,0:T(8,128)(2,1)S(1)}, bf16[1536,512]{1,0:T(8,128)(2,1)}, u32[]{:S(2)}) copy-start(bf16[1536,512]{1,0:T(8,128)(2,1)} %get-tuple-element.175) | copy-start | bytes 4718596 | tf_op jit(solution)/shard_map/while/body/eval_jaxpr/cond
  283.0 10.2 %copy-start = (bf16[1536,512]{1,0:T(8,128)(2,1)S(1)}, bf16[1536,512]{1,0:T(8,128)(2,1)}, u32[]{:S(2)}) copy-start(bf16[1536,512]{1,0:T(8,128)(2,1)} %get-tuple-element.175) | copy-start | bytes 4718596 | tf_op jit(solution)/shard_map/while/body/eval_jaxpr/cond
  315.7 0.7 copy-start.4
Sparse Core Ops, SparseCore 0:
  315.8 304.8 all-reduce.2
where the time goes:
time: 635 us; the launch traced here: 633 us
  waiting for transfers between devices  380 us (60%)
  local copies, waits for them, and re-layouts  95.8 us (15%)
  other arithmetic  66.7 us (11%)
  starting transfers between devices  36.2 us (6%)
  matrix products  25.6 us (4%)
  loops' own time  14.3 us (2%)
  between operations  14.1 us (2%)
    unnamed x2, waiting for transfers between devices  303 us
    ppermute x6, waiting for transfers between devices, shifted(): return lax.ppermute(block, axis, route)  76.3 us
    unnamed x18, local copies, waits for them, and re-layouts  49 us
    ppermute x6, starting transfers between devices, shifted(): return lax.ppermute(block, axis, route)  27.6 us
    cos x1, other arithmetic, forward_table(): jnp.cos(angles)  26.4 us
    reduce_sum x2, other arithmetic, cross_spectra(): real_sum = jnp.sum(src_real * rcv_real + src_imag * rcv_imag, axis=0)  20.3 us
    while x1, local copies, waits for them, and re-layouts, per_device(): partial_value = lax.map(single_slot, jnp.arange(TCAP, dtype=jnp.int32))  14.6 us
    dot_general x1, matrix products, whiten(): jnp.einsum('snc,nf->scf', pieces.astype(jnp.float32), forward_table(), pr...  13.9 us
  transfers between devices with their start and end apart: 8, of which 7 were waited for; matrix products, arithmetic and copies ran while one was open for 7% of the time, Pallas kernels for 0%

commit v1 on v0

v1 whole, which is shorter than its diff:
```python
import math

import jax
import jax.numpy as jnp
import ml_dtypes
import numpy as np
from jax import lax
from jax.experimental import pallas as pl
from jax.experimental.pallas import tpu as pltpu
from jax.sharding import PartitionSpec as P

L = 1920
F = 768
K0 = 8
HALF = 32
LAG_COUNT = 512
BLOCK = 128
SOURCES = 16
TPS = 3
REACH = 2
SEG_DEV = 4
SEGS = 16
NB = 32
TCAP = 6
TM = 4
SLAB = L // NB
ROWS = 64
PART = BLOCK // TM
SRC_PART = SOURCES // TM
MIB = 1 << 20

BF16 = jnp.bfloat16
F32 = jnp.float32


def forward_table():
    n = np.arange(L)[:, None]
    q = K0 + np.arange(F)[None, :]
    angles = (n * q % L) * (2.0 * np.pi / L)
    window = 0.5 - 0.5 * np.cos(np.arange(L) * (2.0 * np.pi / L))
    table = np.concatenate([np.cos(angles), -np.sin(angles)], axis=1) * window[:, None]
    padded = np.zeros((NB, ROWS, 2 * F))
    padded[:, :SLAB] = table.reshape(NB, SLAB, 2 * F)
    return padded.reshape(NB * ROWS, 2 * F).astype(ml_dtypes.bfloat16)


def smoothing():
    k = np.arange(F)
    inside = (np.abs(k[:, None] - k[None, :]) <= HALF).astype(np.float64)
    inverse_count = 1.0 / inside.sum(axis=0, keepdims=True)
    return inside.astype(ml_dtypes.bfloat16), inverse_count.astype(np.float32)


def inverse_table():
    q = K0 + np.arange(F)[:, None]
    lag = np.arange(LAG_COUNT)[None, :] - LAG_COUNT // 2
    angles = (q * lag % L) * (2.0 * np.pi / L)
    table = np.concatenate([np.cos(angles), -np.sin(angles)], axis=0) / math.sqrt(SEGS * F)
    return table.astype(ml_dtypes.bfloat16)


def interleave():
    order = np.zeros((SEG_DEV * BLOCK, SEG_DEV * BLOCK))
    for s in range(SEG_DEV):
        for j in range(TM):
            for c in range(PART):
                order[s * BLOCK + j * PART + c, j * BLOCK + s * PART + c] = 1.0
    return order.astype(ml_dtypes.bfloat16)


PACK_BLOCKS = 8


def pack_kernel(own, records, quality, order, spread, out):
    step = pl.program_id(0)
    marks = jnp.concatenate([quality[s : s + 1, :] for s in range(SEG_DEV)], axis=1)
    marks = jnp.broadcast_to(marks.astype(F32), (16, SEG_DEV * BLOCK)).astype(BF16)
    marks = jnp.dot(marks, order[...], preferred_element_type=F32)[:1]
    row = lax.broadcasted_iota(jnp.int32, (ROWS, SEG_DEV * BLOCK), 0)
    for k in range(PACK_BLOCKS):
        lanes = slice(k * BLOCK, (k + 1) * BLOCK)
        x = jnp.concatenate([records[s, :, lanes] for s in range(SEG_DEV)], axis=1)
        y = jnp.dot(x, order[...], preferred_element_type=F32).astype(BF16)
        y = jnp.dot(spread[...], y, preferred_element_type=F32)
        mine = step * PACK_BLOCKS + k == own[0]
        y = jnp.where((row == SLAB) & mine, marks, y).astype(BF16)
        for j in range(TM):
            out[k * TM + j] = y[:, j * BLOCK : (j + 1) * BLOCK]


def pack(own, records, quality):
    spread = np.eye(ROWS, SLAB).astype(ml_dtypes.bfloat16)
    return pl.pallas_call(
        pack_kernel,
        out_shape=jax.ShapeDtypeStruct((NB * TM, ROWS, BLOCK), BF16),
        grid_spec=pltpu.PrefetchScalarGridSpec(
            num_scalar_prefetch=1,
            grid=(NB // PACK_BLOCKS,),
            in_specs=[
                pl.BlockSpec((SEG_DEV, SLAB, PACK_BLOCKS * BLOCK), lambda g, own: (0, 0, g)),
                pl.BlockSpec((SEG_DEV, BLOCK), lambda g, own: (0, 0)),
                pl.BlockSpec((SEG_DEV * BLOCK, SEG_DEV * BLOCK), lambda g, own: (0, 0)),
                pl.BlockSpec((ROWS, SLAB), lambda g, own: (0, 0)),
            ],
            out_specs=pl.BlockSpec((PACK_BLOCKS * TM, ROWS, BLOCK), lambda g, own: (g, 0, 0)),
        ),
        compiler_params=pltpu.CompilerParams(vmem_limit_bytes=32 * MIB),
        name="pack",
    )(own, records, quality, interleave(), spread)


def whiten_kernel(own, slabs, table, inside, inverse_count, white, sources):
    marks = slabs[pl.ds(own[0], 1), 0, pl.ds(48, 16), :][0, SLAB - 48 : SLAB - 47, :]
    x = slabs[:, 0].reshape(NB * ROWS, BLOCK) * marks
    spectrum = lax.dot_general(x, table[...], (((0,), (0,)), ((), ())), preferred_element_type=F32)
    re = spectrum[:, :F]
    im = spectrum[:, F:]
    magnitude = jnp.sqrt(re * re + im * im).astype(BF16)
    level = jnp.dot(magnitude, inside[...], preferred_element_type=F32) * inverse_count[...]
    inverse_level = 1.0 / (level + 1e-6)
    for half, part in ((0, re), (1, im)):
        lanes = slice(half * F, (half + 1) * F)
        value = part * inverse_level
        white[0, :, lanes] = value.astype(BF16)
        picked = value.reshape(SEG_DEV * SRC_PART, BLOCK // SOURCES, F)[:, 0, :]
        sources[0, :, lanes] = picked.astype(BF16)


def whiten(own, slabs):
    inside, inverse_count = smoothing()
    rows = SEG_DEV * PART
    return pl.pallas_call(
        whiten_kernel,
        out_shape=(
            jax.ShapeDtypeStruct((TM, rows, 2 * F), BF16),
            jax.ShapeDtypeStruct((TM, SEG_DEV * SRC_PART, 2 * F), BF16),
        ),
        grid_spec=pltpu.PrefetchScalarGridSpec(
            num_scalar_prefetch=1,
            grid=(TM,),
            in_specs=[
                pl.BlockSpec((NB, 1, ROWS, BLOCK), lambda i, own: (0, i, 0, 0)),
                pl.BlockSpec((NB * ROWS, 2 * F), lambda i, own: (0, 0)),
                pl.BlockSpec((F, F), lambda i, own: (0, 0)),
                pl.BlockSpec((1, F), lambda i, own: (0, 0)),
            ],
            out_specs=(
                pl.BlockSpec((1, rows, 2 * F), lambda i, own: (i, 0, 0)),
                pl.BlockSpec((1, SEG_DEV * SRC_PART, 2 * F), lambda i, own: (i, 0, 0)),
            ),
        ),
        compiler_params=pltpu.CompilerParams(vmem_limit_bytes=48 * MIB),
        name="whiten",
    )(own, slabs.reshape(NB, TM, ROWS, BLOCK), forward_table(), inside, inverse_count)


LANES = 128


def tile_kernel(
    pick, s0, s1, s2, s3, inverse, r0, r1, r2, r3, r4, r5, o0, o1, o2, o3, held, src, rcv, cross, sem
):
    for index, ref in enumerate((r0, r1, r2, r3, r4, r5)):

        @pl.when(pick[0] == index)
        def _():
            pltpu.make_async_copy(ref, held, sem).start()

    for rel, ref in enumerate((s0, s1, s2, s3)):
        src[rel] = ref[...].astype(F32)
    pltpu.make_async_copy(r0, held, sem).wait()
    rcv[...] = held[...].astype(F32)
    steps = F // LANES

    def body(step, carry):
        rel = step // steps
        at = pl.multiple_of(lax.rem(step, steps) * LANES, LANES)
        re = [jnp.zeros((PART, LANES), F32)] * SRC_PART
        im = [jnp.zeros((PART, LANES), F32)] * SRC_PART
        for s in range(SEGS):
            br = rcv[s * PART : (s + 1) * PART, pl.ds(at, LANES)]
            bi = rcv[s * PART : (s + 1) * PART, pl.ds(F + at, LANES)]
            for v in range(SRC_PART):
                row = s * SRC_PART + v
                ar = src[rel, row : row + 1, pl.ds(at, LANES)]
                ai = src[rel, row : row + 1, pl.ds(F + at, LANES)]
                re[v] = re[v] + (ar * br + ai * bi)
                im[v] = im[v] + (ar * bi - ai * br)
        for v in range(SRC_PART):
            rows = slice(v * PART, (v + 1) * PART)
            cross[rel, rows, pl.ds(at, LANES)] = re[v].astype(BF16)
            cross[rel, rows, pl.ds(F + at, LANES)] = im[v].astype(BF16)
        return carry

    lax.fori_loop(0, TM * steps, body, 0)
    for rel, ref in enumerate((o0, o1, o2, o3)):
        ref[...] = jnp.dot(cross[rel], inverse[...], preferred_element_type=F32).astype(BF16)


def tile(pick, sources, inverse, receivers):
    whole = lambda: pl.BlockSpec(memory_space=pltpu.VMEM)
    rows = SRC_PART * PART
    return pl.pallas_call(
        tile_kernel,
        out_shape=[jax.ShapeDtypeStruct((rows, LAG_COUNT), BF16)] * TM,
        in_specs=[pl.BlockSpec(memory_space=pltpu.SMEM)]
        + [whole() for _ in range(TM + 1)]
        + [pl.BlockSpec(memory_space=pl.ANY)] * 6,
        out_specs=[whole() for _ in range(TM)],
        scratch_shapes=[
            pltpu.VMEM((SEGS * PART, 2 * F), BF16),
            pltpu.VMEM((TM, SEGS * SRC_PART, 2 * F), F32),
            pltpu.VMEM((SEGS * PART, 2 * F), F32),
            pltpu.VMEM((TM, rows, 2 * F), BF16),
            pltpu.SemaphoreType.DMA,
        ],
        compiler_params=pltpu.CompilerParams(vmem_limit_bytes=48 * MIB),
        cost_estimate=pl.CostEstimate(
            flops=2 * SOURCES * PART * 2 * F * LAG_COUNT, bytes_accessed=8 * MIB, transcendentals=0
        ),
        name="tile",
    )(pick, *sources, inverse, *receivers)


def gather_kernel(place, own, *refs):
    pieces, out = refs[:-1], refs[-1]
    slot = pl.program_id(0)
    for candidate in range(2 * TPS + 1):

        @pl.when(place[slot] == candidate)
        def _():
            if candidate == 2 * TPS:
                out[...] = jnp.zeros_like(out)
                return
            for rel in range(TM):
                value = pieces[candidate * TM + rel][...].astype(F32)
                at = pl.multiple_of(lax.rem(own[0] + TM - rel, TM) * PART, PART)
                out[0, :, pl.ds(at, PART), :] = value.reshape(SRC_PART, PART, LAG_COUNT)


def gather(place, own, pieces):
    rows = SRC_PART * PART
    return pl.pallas_call(
        gather_kernel,
        out_shape=jax.ShapeDtypeStruct((TCAP, SRC_PART, BLOCK, LAG_COUNT), F32),
        grid_spec=pltpu.PrefetchScalarGridSpec(
            num_scalar_prefetch=2,
            grid=(TCAP,),
            in_specs=[pl.BlockSpec((rows, LAG_COUNT), lambda s, *_: (0, 0)) for _ in pieces],
            out_specs=pl.BlockSpec((1, SRC_PART, BLOCK, LAG_COUNT), lambda s, *_: (s, 0, 0, 0)),
        ),
        compiler_params=pltpu.CompilerParams(vmem_limit_bytes=48 * MIB),
        name="gather",
    )(place, own, *pieces)


def shifted(value, axis, distance):
    count = lax.axis_size(axis)
    return lax.ppermute(value, axis, [(i, (i + distance) % count) for i in range(count)])


def per_device(records, quality, tile_list, tile_slot_owner):
    chan = lax.axis_index("chan").astype(jnp.int32)
    time = lax.axis_index("tm").astype(jnp.int32)
    own = chan.reshape(1)

    slabs = pack(own, records, quality)
    slabs = lax.all_to_all(slabs, ("chan", "tm"), split_axis=0, concat_axis=0, tiled=True)
    white, sources = whiten(own, slabs)
    white = white.reshape(SEGS * PART, 2 * F)
    sources = sources.reshape(SEGS * SRC_PART, 2 * F)
    sources = [sources] + [shifted(sources, "tm", -rel) for rel in range(1, TM)]

    below = shifted(white, "chan", 2)
    above = shifted(white, "chan", -2)
    mate = lax.ppermute(white, "chan", [(i, i ^ 1) for i in range(NB)])
    even_below = lax.ppermute(below, "chan", [(i, i - 1) for i in range(1, NB, 2)])
    odd_above = lax.ppermute(above, "chan", [(i, i + 1) for i in range(0, NB, 2)])
    receivers = [white, below, above, mate, even_below, odd_above]
    odd = lax.rem(chan, 2)

    first = chan * TPS
    mine = lax.dynamic_slice(tile_list, (first, 0), (TPS, 2))[:, 1]
    offset = jnp.mod(mine - chan + REACH, NB)
    choice = jnp.where(
        odd == 1, jnp.array([1, 3, 0, 5, 2], jnp.int32), jnp.array([1, 4, 0, 3, 2], jnp.int32)
    )
    choice = jnp.sum(
        jnp.where(offset[:, None] == jnp.arange(2 * REACH + 1)[None, :], choice[None, :], 0), axis=1
    ).astype(jnp.int32)

    home = lax.dynamic_slice(tile_slot_owner, (first,), (TPS,))
    moved = lax.dynamic_slice(tile_slot_owner, (jnp.mod(chan - 1, NB) * TPS,), (TPS,))
    named = jnp.concatenate([home, moved])
    slots = chan * TCAP + jnp.arange(TCAP, dtype=jnp.int32)
    place = 2 * TPS + jnp.sum(
        jnp.where(
            slots[:, None] == named[None, :],
            jnp.arange(2 * TPS, dtype=jnp.int32)[None, :] - 2 * TPS,
            0,
        ),
        axis=1,
    )

    inverse = inverse_table()
    stay, move = [], []
    for t in range(TPS):
        parts = tile(choice[t : t + 1], sources, inverse, receivers)
        parts = [parts[0]] + [shifted(parts[rel], "tm", rel) for rel in range(1, TM)]
        stay += parts
        move += [shifted(part, "chan", 1) for part in parts]
    return gather(place.astype(jnp.int32), time.reshape(1), stay + move)


def solution(mesh):
    placed = (P("tm", "chan", None), P("tm", "chan"), P(), P())
    return jax.shard_map(
        per_device,
        mesh=mesh,
        in_specs=placed,
        out_specs=P("chan", "tm", None, None),
        check_vma=False,
    )
```

time: 635 us -> 207 us (0.33)
  waiting for transfers between devices: 380 us -> 66.1 us
  local copies, waits for them, and re-layouts: 95.8 us -> 6.94 us
  other arithmetic: 66.7 us -> 0.47 us
  Pallas kernels: 0 us -> 59.2 us
  blocking collectives: 0 us -> 41.1 us
  matrix products: 25.6 us -> 0 us
  loops' own time: 14.3 us -> 0 us
  between operations: 14.1 us -> 0.23 us
    unnamed x2 -> x0, waiting for transfers between devices: 303 us -> none
    pallas_call x0 -> x6, Pallas kernels: none -> 59.2 us  [the longest x3 37.1 us: tile(): pl.pallas_call(tile_kernel, out_shape=[jax.ShapeDtypeStruct((rows, LAG_CO...]
    unnamed x18 -> x33, local copies, waits for them, and re-layouts: 49 us -> 6.13 us
    all_to_all x0 -> x1, blocking collectives: none -> 41.1 us  [per_device(): lax.all_to_all(slabs, ('chan', 'tm'), split_axis=0, concat_axis=0, tiled=...]
    cos x2 -> x0, other arithmetic: 32.8 us -> none  [the longest x1 26.4 us: forward_table(): jnp.cos(angles)]
    dot_general x4 -> x0, matrix products: 25.6 us -> none  [the longest x1 13.9 us: whiten(): jnp.einsum('snc,nf->scf', pieces.astype(jnp.float32), forward_table(), pr...]
    reduce_sum x5 -> x2, other arithmetic: 21.8 us -> 0.37 us  [the longest x1 0.18 us: per_device(): jnp.sum(jnp.where(slots[:, None] == named[None, :], jnp.arange(2 * TPS, d...]
    while x1 -> x0, local copies, waits for them, and re-layouts: 14.6 us -> none  [per_device(): partial_value = lax.map(single_slot, jnp.arange(TCAP, dtype=jnp.int32))]
  transfers between devices with their start and end apart: 8 -> 29, of which waited for: 7 -> 17; matrix products, arithmetic and copies ran while one was open for 7% -> 1% of each run, Pallas kernels for 0% -> 12%
where the time goes in v1:
time: 207 us; the launch traced here: 206 us
  waiting for transfers between devices  66.1 us (32%)
  Pallas kernels  59.2 us (29%)
  blocking collectives  41.1 us (20%)
  starting transfers between devices  32.2 us (16%)
  local copies, waits for them, and re-layouts  6.94 us (3%)
    ppermute x26, waiting for transfers between devices, shifted(): lax.ppermute(value, axis, [(i, (i + distance) % count) for i in range(cou...  66.1 us
    all_to_all x1, blocking collectives, per_device(): lax.all_to_all(slabs, ('chan', 'tm'), split_axis=0, concat_axis=0, tiled=...  41.1 us
    pallas_call x3, Pallas kernels, tile(): pl.pallas_call(tile_kernel, out_shape=[jax.ShapeDtypeStruct((rows, LAG_CO...  37.1 us
    ppermute x26, starting transfers between devices, shifted(): lax.ppermute(value, axis, [(i, (i + distance) % count) for i in range(cou...  25.5 us
    pallas_call x1, Pallas kernels, whiten(): pl.pallas_call(whiten_kernel, out_shape=(jax.ShapeDtypeStruct((TM, rows,...  8.54 us
    pallas_call x1, Pallas kernels, pack(): pl.pallas_call(pack_kernel, out_shape=jax.ShapeDtypeStruct((NB * TM, ROWS...  8.19 us
    unnamed x33, local copies, waits for them, and re-layouts  6.13 us
    ppermute x1, starting transfers between devices, per_device(): lax.ppermute(above, 'chan', [(i, i + 1) for i in range(0, NB, 2)])  5.41 us
  transfers between devices with their start and end apart: 29, of which 17 were waited for; matrix products, arithmetic and copies ran while one was open for 1% of the time, Pallas kernels for 12%

profile of v1, /device:TPU:0, one launch (start us, length us, event | category | flops | bytes accessed | tf_op | source)
XLA Modules:
  0.0 206.3 jit_solution(9396188994745073291)
XLA Ops:
  0.0 2.7 %copy.14.records = bf16[4,60,4096]{2,1,0:T(8,128)(2,1)S(1)} copy(bf16[4,60,4096]{2,0,1:T(4,128)(2,1)} %param.12) | data formatting | bytes 3932160 | tf_op args[0]
  2.7 8.2 %pack.1 = bf16[128,64,128]{2,1,0:T(8,128)(2,1)S(1)} custom-call(s32[1]{0:T(128)} %bitcast.2.own, bf16[4,60,4096]{2,1,0:T(8,128)(2,1)S(1)} %copy.14.records, s32[4,128]{1,0:T(4,128)S(1)} %copy-done.12, bf16[512,512]{1,0:T(8,128)(2,1)S(1)} %copy-done.7, bf16[64,60]{1,0:T(8,128)(2,1)S(1)} %copy-done.10), custom_call_target="tpu_custom_call" | custom-call | tf_op jit(solution)/shard_map/pack/pallas_call | solution.py:93
  11.0 41.1 %all_to_all.5 = bf16[128,64,128]{2,1,0:T(8,128)(2,1)S(1)} all-to-all(bf16[128,64,128]{2,1,0:T(8,128)(2,1)S(1)} %pack.1), channel_id=1, replica_groups=mesh['chan'=32,'tm'=4] {'chan','tm'}, dimensions={0} | all-to-all | bytes 4194304 | tf_op jit(solution)/shard_map/all_to_all | solution.py:268
  52.1 8.5 %whiten.1 = (bf16[4,128,1536]{2,1,0:T(8,128)(2,1)S(1)}, bf16[4,16,1536]{2,1,0:T(8,128)(2,1)S(1)}) custom-call(s32[1]{0:T(128)} %bitcast.2.own, bf16[32,4,64,128]{3,2,1,0:T(8,128)(2,1)S(1)} %bitcast.13, bf16[2048,1536]{1,0:T(8,128)(2,1)} %constant.68.clone.table, bf16[768,768]{1,0:T(8,128)(2,1)S(1)} %copy-done.6, f32[1,768]{1,0:T(1,128)S(1)} %copy-done.11), custom_call_target="tpu_custom_call" | custom-call | tf_op jit(solution)/shard_map/whiten/pallas_call | solution.py:132
  60.7 0.9 collective-permute-start.3
  61.5 4.5 %collective-permute-start.4 = (bf16[512,1536]{1,0:T(8,128)(2,1)S(1)}, bf16[512,1536]{1,0:T(8,128)(2,1)}, u32[]{:S(2)}, u32[]{:S(2)}) collective-permute-start(bf16[512,1536]{1,0:T(8,128)(2,1)S(1)} %bitcast.8), channel_id=1, source_target_pairs={{0,120},{4,124},{8,0},{12,4},{16,8},{20,12},{24,16},{28,20},{32,24... | collective-permute-start | bytes 4718600 | tf_op jit(solution)/shard_map/ppermute | solution.py:259
  66.1 34.6 %collective-permute-done.3.r1 = bf16[512,1536]{1,0:T(8,128)(2,1)} collective-permute-done((bf16[512,1536]{1,0:T(8,128)(2,1)S(1)}, bf16[512,1536]{1,0:T(8,128)(2,1)}, u32[]{:S(2)}, u32[]{:S(2)}) %collective-permute-start.3) | collective-permute-done | bytes 1572896 | tf_op jit(solution)/shard_map/ppermute | solution.py:259
  100.7 1.3 collective-permute-start.6
  102.0 5.4 %collective-permute-start.7 = (bf16[512,1536]{1,0:T(8,128)(2,1)}, bf16[512,1536]{1,0:T(8,128)(2,1)}, u32[]{:S(2)}, u32[]{:S(2)}) collective-permute-start(bf16[512,1536]{1,0:T(8,128)(2,1)} %collective-permute-done.4.r2), channel_id=1, source_target_pairs={{0,4},{8,12},{16,20},{24,28},{32,36},{40,44},{48,52},{56,60},{64,6... | collective-permute-start | bytes 4718600 | tf_op jit(solution)/shard_map/ppermute | solution.py:278
  107.5 0.7 collective-permute-start
  108.3 2.1 %collective-permute-start.1 = (bf16[64,1536]{1,0:T(8,128)(2,1)S(1)}, bf16[64,1536]{1,0:T(8,128)(2,1)S(1)}, u32[]{:S(2)}, u32[]{:S(2)}) collective-permute-start(bf16[64,1536]{1,0:T(8,128)(2,1)S(1)} %bitcast.15), channel_id=1, source_target_pairs={{0,2},{1,3},{2,0},{3,1},{4,6},{5,7},{6,4},{7,5},{8,10},{9,11},{10,... | collective-permute-start | bytes 589832 | tf_op jit(solution)/shard_map/ppermute | solution.py:259
  110.3 4.3 %collective-permute-done.s1 = bf16[64,1536]{1,0:T(8,128)(2,1)S(1)} collective-permute-done((bf16[64,1536]{1,0:T(8,128)(2,1)S(1)}, bf16[64,1536]{1,0:T(8,128)(2,1)S(1)}, u32[]{:S(2)}, u32[]{:S(2)}) %collective-permute-start) | collective-permute-done | bytes 196640 | tf_op jit(solution)/shard_map/ppermute | solution.py:259
  114.7 3.4 %collective-permute-start.2 = (bf16[64,1536]{1,0:T(8,128)(2,1)S(1)}, bf16[64,1536]{1,0:T(8,128)(2,1)S(1)}, u32[]{:S(2)}, u32[]{:S(2)}) collective-permute-start(bf16[64,1536]{1,0:T(8,128)(2,1)S(1)} %bitcast.16), channel_id=1, source_target_pairs={{0,1},{1,2},{2,3},{3,0},{4,5},{5,6},{6,7},{7,4},{8,9},{9,10},{10,1... | collective-permute-start | bytes 589832 | tf_op jit(solution)/shard_map/ppermute | solution.py:259
  118.0 0.2 select_reduce_fusion.1
  118.2 0.7 fusion.2
  118.9 2.7 %collective-permute-done.2.s3 = bf16[64,1536]{1,0:T(8,128)(2,1)S(1)} collective-permute-done((bf16[64,1536]{1,0:T(8,128)(2,1)S(1)}, bf16[64,1536]{1,0:T(8,128)(2,1)S(1)}, u32[]{:S(2)}, u32[]{:S(2)}) %collective-permute-start.2) | collective-permute-done | bytes 196640 | tf_op jit(solution)/shard_map/ppermute | solution.py:259
  121.6 11.5 %tile.3 = (bf16[128,512]{1,0:T(8,128)(2,1)}, bf16[128,512]{1,0:T(8,128)(2,1)S(1)}, bf16[128,512]{1,0:T(8,128)(2,1)}, bf16[128,512]{1,0:T(8,128)(2,1)}) custom-call(s32[1]{0:T(128)} %get-tuple-element.35.pick, bf16[64,1536]{1,0:T(8,128)(2,1)S(1)} %bitcast.17, bf16[64,1536]{1,0:T(8,128)(2,1)S(1)} %collective-permute-done.s1, ...), custom_call_target="tpu_custom_call" | custom-call | flops 805306368 | bytes 8388608 | tf_op jit(solution)/shard_map/tile/pallas_call | solution.py:203
  133.1 2.2 %collective-permute-start.8 = (bf16[128,512]{1,0:T(8,128)(2,1)S(1)}, bf16[128,512]{1,0:T(8,128)(2,1)}, u32[]{:S(2)}, u32[]{:S(2)}) collective-permute-start(bf16[128,512]{1,0:T(8,128)(2,1)S(1)} %get-tuple-element.22), channel_id=1, source_target_pairs={{0,1},{1,2},{2,3},{3,0},{4,5},{5,6},{6,7},{7,4},{8,9},{9,10},{10,1... | collective-permute-start | bytes 393224 | tf_op jit(solution)/shard_map/ppermute | solution.py:259
  135.3 0.7 collective-permute-start.9
  136.0 2.1 %collective-permute-start.10 = (bf16[128,512]{1,0:T(8,128)(2,1)}, bf16[128,512]{1,0:T(8,128)(2,1)}, u32[]{:S(2)}, u32[]{:S(2)}) collective-permute-start(bf16[128,512]{1,0:T(8,128)(2,1)} %get-tuple-element.24), channel_id=1, source_target_pairs={{0,3},{1,0},{2,1},{3,2},{4,7},{5,4},{6,5},{7,6},{8,11},{9,8},{10,9... | collective-permute-start | bytes 393224 | tf_op jit(solution)/shard_map/ppermute | solution.py:259
  138.1 12.7 %tile.4 = (bf16[128,512]{1,0:T(8,128)(2,1)}, bf16[128,512]{1,0:T(8,128)(2,1)}, bf16[128,512]{1,0:T(8,128)(2,1)}, bf16[128,512]{1,0:T(8,128)(2,1)}) custom-call(s32[1]{0:T(128)} %get-tuple-element.34.pick, bf16[64,1536]{1,0:T(8,128)(2,1)S(1)} %bitcast.18, bf16[64,1536]{1,0:T(8,128)(2,1)S(1)} %collective-permute-done.s1, ...), custom_call_target="tpu_custom_call" | custom-call | flops 805306368 | bytes 8388608 | tf_op jit(solution)/shard_map/tile/pallas_call | solution.py:203
  150.9 2.8 %collective-permute-start.12 = (bf16[128,512]{1,0:T(8,128)(2,1)}, bf16[128,512]{1,0:T(8,128)(2,1)}, u32[]{:S(2)}, u32[]{:S(2)}) collective-permute-start(bf16[128,512]{1,0:T(8,128)(2,1)} %get-tuple-element.27), channel_id=1, source_target_pairs={{0,2},{1,3},{2,0},{3,1},{4,6},{5,7},{6,4},{7,5},{8,10},{9,11},{10,... | collective-permute-start | bytes 393224 | tf_op jit(solution)/shard_map/ppermute | solution.py:259
  153.7 1.1 collective-permute-start.13
  154.8 0.9 copy-done.3
  155.7 0.9 copy-done.5
  156.6 12.8 %tile.5 = (bf16[128,512]{1,0:T(8,128)(2,1)S(1)}, bf16[128,512]{1,0:T(8,128)(2,1)}, bf16[128,512]{1,0:T(8,128)(2,1)}, bf16[128,512]{1,0:T(8,128)(2,1)}) custom-call(s32[1]{0:T(128)} %get-tuple-element.33.pick, bf16[64,1536]{1,0:T(8,128)(2,1)S(1)} %bitcast.19, bf16[64,1536]{1,0:T(8,128)(2,1)S(1)} %collective-permute-done.s1, bf16[64,1536]{1,0:T(8,128)(2,1)S(1)} %copy-done.3, ...), custom_call_target="tpu_custom_call" | custom-call | flops 805306368 | bytes 8388608 | tf_op jit(solution)/shard_map/tile/pallas_call | solution.py:203
  169.5 0.6 copy-done.8
  170.1 0.9 collective-permute-start.14
  171.1 1.4 collective-permute-start.15
  172.5 2.5 %collective-permute-start.16 = (bf16[128,512]{1,0:T(8,128)(2,1)}, bf16[128,512]{1,0:T(8,128)(2,1)S(1)}, u32[]{:S(2)}, u32[]{:S(2)}) collective-permute-start(bf16[128,512]{1,0:T(8,128)(2,1)} %get-tuple-element.32), channel_id=1, source_target_pairs={{0,3},{1,0},{2,1},{3,2},{4,7},{5,4},{6,5},{7,6},{8,11},{9,8},{10,9... | collective-permute-start | bytes 393224 | tf_op jit(solution)/shard_map/ppermute | solution.py:259
  175.2 0.1 fusion.3
  175.3 2.6 %collective-permute-done.14.refs_9_ = bf16[128,512]{1,0:T(8,128)(2,1)S(1)} collective-permute-done((bf16[128,512]{1,0:T(8,128)(2,1)}, bf16[128,512]{1,0:T(8,128)(2,1)S(1)}, u32[]{:S(2)}, u32[]{:S(2)}) %collective-permute-start.14) | collective-permute-done | bytes 131104 | tf_op jit(solution)/shard_map/ppermute | solution.py:259
  177.9 0.8 collective-permute-done.16.refs_11_
  178.8 4.2 %collective-permute-done.17.refs_12_ = bf16[128,512]{1,0:T(8,128)(2,1)S(1)} collective-permute-done((bf16[128,512]{1,0:T(8,128)(2,1)}, bf16[128,512]{1,0:T(8,128)(2,1)S(1)}, u32[]{:S(2)}, u32[]{:S(2)}) %collective-permute-start.17) | collective-permute-done | bytes 131104 | tf_op jit(solution)/shard_map/ppermute | solution.py:259
  183.0 1.4 collective-permute-done.21.refs_16_
  184.4 0.2 select_reduce_fusion
  184.6 1.3 collective-permute-done.25.refs_20_
  185.8 1.4 collective-permute-done.18.refs_13_
  187.3 1.4 collective-permute-done.19.refs_14_
  188.7 2.3 %collective-permute-done.20.refs_15_ = bf16[128,512]{1,0:T(8,128)(2,1)S(1)} collective-permute-done((bf16[128,512]{1,0:T(8,128)(2,1)}, bf16[128,512]{1,0:T(8,128)(2,1)S(1)}, u32[]{:S(2)}, u32[]{:S(2)}) %collective-permute-start.20) | collective-permute-done | bytes 131104 | tf_op jit(solution)/shard_map/ppermute | solution.py:259
  190.9 1.4 collective-permute-done.22.refs_17_
  192.3 1.4 collective-permute-done.23.refs_18_
  193.8 1.4 collective-permute-done.24.refs_19_
  195.2 1.4 collective-permute-done.26.refs_21_
  196.6 2.0 collective-permute-done.27.refs_22_
  198.6 1.4 collective-permute-done.28.refs_23_
  200.0 0.9 copy-done.9
  200.9 5.4 %gather.1 = f32[6,4,128,512]{3,2,1,0:T(8,128)} custom-call(s32[6]{0:T(128)S(1)} %broadcast_add_fusion.place, s32[1]{0:T(128)} %bitcast.own, bf16[128,512]{1,0:T(8,128)(2,1)} %get-tuple-element.21.refs_0_, bf16[128,512]{1,0:T(8,128)(2,1)} %collective-permute-done.8.refs_1_, bf16[128,512]{1,0:T(8,128)(2,1)} %collective-permute-done.9.refs_2_, ...), custom_call_target="tpu_custom_call" | custom-call | tf_op jit(solution)/shard_map/gather/pallas_call | solution.py:243
  (60 shorter events, 0.4 us)
Async XLA Ops:
  0.0 107.4 %copy-start = (s32[96,2]{0,1:T(2,128)S(1)}, s32[96,2]{0,1:T(2,128)}, u32[]{:S(2)}) copy-start(s32[96,2]{0,1:T(2,128)} %param.14) | copy-start | bytes 2308
  0.0 2.7 %copy-start.7 = (bf16[512,512]{1,0:T(8,128)(2,1)S(1)}, bf16[512,512]{1,0:T(8,128)(2,1)}, u32[]{:S(2)}) copy-start(bf16[512,512]{1,0:T(8,128)(2,1)} %constant.66.clone.order) | copy-start | bytes 1572868
  0.0 2.7 %copy-start.10 = (bf16[64,60]{1,0:T(8,128)(2,1)S(1)}, bf16[64,60]{1,0:T(8,128)(2,1)}, u32[]{:S(2)}) copy-start(bf16[64,60]{1,0:T(8,128)(2,1)} %constant.67.clone.spread) | copy-start | bytes 23044
  0.0 2.7 %copy-start.12 = (s32[4,128]{1,0:T(4,128)S(1)}, s32[4,128]{1,0:T(4,128)}, u32[]{:S(2)}) copy-start(s32[4,128]{1,0:T(4,128)} %quality.1) | copy-start | bytes 6148
  10.9 41.1 %copy-start.6 = (bf16[768,768]{1,0:T(8,128)(2,1)S(1)}, bf16[768,768]{1,0:T(8,128)(2,1)}, u32[]{:S(2)}) copy-start(bf16[768,768]{1,0:T(8,128)(2,1)} %constant.69.clone.inside) | copy-start | bytes 3538948
  10.9 41.1 %copy-start.11 = (f32[1,768]{1,0:T(1,128)S(1)}, f32[1,768]{1,0:T(1,128)}, u32[]{:S(2)}) copy-start(f32[1,768]{1,0:T(1,128)} %constant.70.clone.inverse_count) | copy-start | bytes 9220
  52.1 56.2 %copy-start.14 = (s32[5]{0:T(128)S(1)}, s32[5]{0:T(128)}, u32[]{:S(2)}) copy-start(s32[5]{0:T(128)} %constant.71.clone) | copy-start | bytes 64
  52.1 56.2 %copy-start.15 = (s32[5]{0:T(128)S(1)}, s32[5]{0:T(128)}, u32[]{:S(2)}) copy-start(s32[5]{0:T(128)} %constant.72.clone) | copy-start | bytes 64
  52.1 69.5 %copy-start.1 = (bf16[1536,512]{1,0:T(8,128)(2,1)S(1)}, bf16[1536,512]{1,0:T(8,128)(2,1)}, u32[]{:S(2)}) copy-start(bf16[1536,512]{1,0:T(8,128)(2,1)} %constant.73.clone.inverse) | copy-start | bytes 4718596
  60.7 40.1 %collective-permute-start.3 = (bf16[512,1536]{1,0:T(8,128)(2,1)S(1)}, bf16[512,1536]{1,0:T(8,128)(2,1)}, u32[]{:S(2)}, u32[]{:S(2)}) collective-permute-start(bf16[512,1536]{1,0:T(8,128)(2,1)S(1)} %bitcast.7), channel_id=1, source_target_pairs={{0,8},{4,12},{8,16},{12,20},{16,24},{20,28},{24,32},{28,36},{32,40... | collective-permute-start | bytes 4718600 | tf_op jit(solution)/shard_map/ppermute | solution.py:259
  61.5 40.5 %collective-permute-start.4 = (bf16[512,1536]{1,0:T(8,128)(2,1)S(1)}, bf16[512,1536]{1,0:T(8,128)(2,1)}, u32[]{:S(2)}, u32[]{:S(2)}) collective-permute-start(bf16[512,1536]{1,0:T(8,128)(2,1)S(1)} %bitcast.8), channel_id=1, source_target_pairs={{0,120},{4,124},{8,0},{12,4},{16,8},{20,12},{24,16},{28,20},{32,24... | collective-permute-start | bytes 4718600 | tf_op jit(solution)/shard_map/ppermute | solution.py:259
  66.1 55.5 %collective-permute-start.5 = (bf16[512,1536]{1,0:T(8,128)(2,1)S(1)}, bf16[512,1536]{1,0:T(8,128)(2,1)}, u32[]{:S(2)}, u32[]{:S(2)}) collective-permute-start(bf16[512,1536]{1,0:T(8,128)(2,1)S(1)} %bitcast.9), channel_id=1, source_target_pairs={{0,4},{4,0},{8,12},{12,8},{16,20},{20,16},{24,28},{28,24},{32,36},... | collective-permute-start | bytes 4718600 | tf_op jit(solution)/shard_map/ppermute | solution.py:276
  100.7 20.8 %collective-permute-start.6 = (bf16[512,1536]{1,0:T(8,128)(2,1)}, bf16[512,1536]{1,0:T(8,128)(2,1)}, u32[]{:S(2)}, u32[]{:S(2)}) collective-permute-start(bf16[512,1536]{1,0:T(8,128)(2,1)} %collective-permute-done.3.r1), channel_id=1, source_target_pairs={{4,0},{12,8},{20,16},{28,24},{36,32},{44,40},{52,48},{60,56},{68,6... | collective-permute-start | bytes 4718600 | tf_op jit(solution)/shard_map/ppermute | solution.py:277
  102.0 19.5 %collective-permute-start.7 = (bf16[512,1536]{1,0:T(8,128)(2,1)}, bf16[512,1536]{1,0:T(8,128)(2,1)}, u32[]{:S(2)}, u32[]{:S(2)}) collective-permute-start(bf16[512,1536]{1,0:T(8,128)(2,1)} %collective-permute-done.4.r2), channel_id=1, source_target_pairs={{0,4},{8,12},{16,20},{24,28},{32,36},{40,44},{48,52},{56,60},{64,6... | collective-permute-start | bytes 4718600 | tf_op jit(solution)/shard_map/ppermute | solution.py:278
  107.5 7.1 %collective-permute-start = (bf16[64,1536]{1,0:T(8,128)(2,1)S(1)}, bf16[64,1536]{1,0:T(8,128)(2,1)S(1)}, u32[]{:S(2)}, u32[]{:S(2)}) collective-permute-start(bf16[64,1536]{1,0:T(8,128)(2,1)S(1)} %bitcast.14), channel_id=1, source_target_pairs={{0,3},{1,0},{2,1},{3,2},{4,7},{5,4},{6,5},{7,6},{8,11},{9,8},{10,9... | collective-permute-start | bytes 589832 | tf_op jit(solution)/shard_map/ppermute | solution.py:259
  108.3 10.6 %collective-permute-start.1 = (bf16[64,1536]{1,0:T(8,128)(2,1)S(1)}, bf16[64,1536]{1,0:T(8,128)(2,1)S(1)}, u32[]{:S(2)}, u32[]{:S(2)}) collective-permute-start(bf16[64,1536]{1,0:T(8,128)(2,1)S(1)} %bitcast.15), channel_id=1, source_target_pairs={{0,2},{1,3},{2,0},{3,1},{4,6},{5,7},{6,4},{7,5},{8,10},{9,11},{10,... | collective-permute-start | bytes 589832 | tf_op jit(solution)/shard_map/ppermute | solution.py:259
  114.7 6.9 %collective-permute-start.2 = (bf16[64,1536]{1,0:T(8,128)(2,1)S(1)}, bf16[64,1536]{1,0:T(8,128)(2,1)S(1)}, u32[]{:S(2)}, u32[]{:S(2)}) collective-permute-start(bf16[64,1536]{1,0:T(8,128)(2,1)S(1)} %bitcast.16), channel_id=1, source_target_pairs={{0,1},{1,2},{2,3},{3,0},{4,5},{5,6},{6,7},{7,4},{8,9},{9,10},{10,1... | collective-permute-start | bytes 589832 | tf_op jit(solution)/shard_map/ppermute | solution.py:259
  118.9 19.2 %copy-start.2 = (bf16[64,1536]{1,0:T(8,128)(2,1)}, bf16[64,1536]{1,0:T(8,128)(2,1)S(1)}, u32[]{:S(2)}) copy-start(bf16[64,1536]{1,0:T(8,128)(2,1)S(1)} %collective-permute-done.1.s2) | copy-start | bytes 589828
  121.5 16.6 %copy-start.4 = (bf16[64,1536]{1,0:T(8,128)(2,1)}, bf16[64,1536]{1,0:T(8,128)(2,1)S(1)}, u32[]{:S(2)}) copy-start(bf16[64,1536]{1,0:T(8,128)(2,1)S(1)} %collective-permute-done.2.s3) | copy-start | bytes 589828
  133.1 20.6 %collective-permute-start.8 = (bf16[128,512]{1,0:T(8,128)(2,1)S(1)}, bf16[128,512]{1,0:T(8,128)(2,1)}, u32[]{:S(2)}, u32[]{:S(2)}) collective-permute-start(bf16[128,512]{1,0:T(8,128)(2,1)S(1)} %get-tuple-element.22), channel_id=1, source_target_pairs={{0,1},{1,2},{2,3},{3,0},{4,5},{5,6},{6,7},{7,4},{8,9},{9,10},{10,1... | collective-permute-start | bytes 393224 | tf_op jit(solution)/shard_map/ppermute | solution.py:259
  135.3 34.8 %collective-permute-start.9 = (bf16[128,512]{1,0:T(8,128)(2,1)}, bf16[128,512]{1,0:T(8,128)(2,1)}, u32[]{:S(2)}, u32[]{:S(2)}) collective-permute-start(bf16[128,512]{1,0:T(8,128)(2,1)} %get-tuple-element.23), channel_id=1, source_target_pairs={{0,2},{1,3},{2,0},{3,1},{4,6},{5,7},{6,4},{7,5},{8,10},{9,11},{10,... | collective-permute-start | bytes 393224 | tf_op jit(solution)/shard_map/ppermute | solution.py:259
  136.0 35.1 %collective-permute-start.10 = (bf16[128,512]{1,0:T(8,128)(2,1)}, bf16[128,512]{1,0:T(8,128)(2,1)}, u32[]{:S(2)}, u32[]{:S(2)}) collective-permute-start(bf16[128,512]{1,0:T(8,128)(2,1)} %get-tuple-element.24), channel_id=1, source_target_pairs={{0,3},{1,0},{2,1},{3,2},{4,7},{5,4},{6,5},{7,6},{8,11},{9,8},{10,9... | collective-permute-start | bytes 393224 | tf_op jit(solution)/shard_map/ppermute | solution.py:259
  150.8 21.7 %collective-permute-start.11 = (bf16[128,512]{1,0:T(8,128)(2,1)}, bf16[128,512]{1,0:T(8,128)(2,1)}, u32[]{:S(2)}, u32[]{:S(2)}) collective-permute-start(bf16[128,512]{1,0:T(8,128)(2,1)} %get-tuple-element.26), channel_id=1, source_target_pairs={{0,1},{1,2},{2,3},{3,0},{4,5},{5,6},{6,7},{7,4},{8,9},{9,10},{10,1... | collective-permute-start | bytes 393224 | tf_op jit(solution)/shard_map/ppermute | solution.py:259
  150.9 24.1 %collective-permute-start.12 = (bf16[128,512]{1,0:T(8,128)(2,1)}, bf16[128,512]{1,0:T(8,128)(2,1)}, u32[]{:S(2)}, u32[]{:S(2)}) collective-permute-start(bf16[128,512]{1,0:T(8,128)(2,1)} %get-tuple-element.27), channel_id=1, source_target_pairs={{0,2},{1,3},{2,0},{3,1},{4,6},{5,7},{6,4},{7,5},{8,10},{9,11},{10,... | collective-permute-start | bytes 393224 | tf_op jit(solution)/shard_map/ppermute | solution.py:259
  153.7 21.4 %collective-permute-start.13 = (bf16[128,512]{1,0:T(8,128)(2,1)}, bf16[128,512]{1,0:T(8,128)(2,1)}, u32[]{:S(2)}, u32[]{:S(2)}) collective-permute-start(bf16[128,512]{1,0:T(8,128)(2,1)} %get-tuple-element.28), channel_id=1, source_target_pairs={{0,3},{1,0},{2,1},{3,2},{4,7},{5,4},{6,5},{7,6},{8,11},{9,8},{10,9... | collective-permute-start | bytes 393224 | tf_op jit(solution)/shard_map/ppermute | solution.py:259
  154.8 0.9 copy-start.3
  155.7 0.9 copy-start.5
  156.6 18.5 %copy-start.13 = (s32[96]{0:T(128)S(1)}, s32[96]{0:T(128)}, u32[]{:S(2)}) copy-start(s32[96]{0:T(128)} %param.15) | copy-start | bytes 1156
  169.5 0.6 copy-start.8
  170.1 7.8 %collective-permute-start.14 = (bf16[128,512]{1,0:T(8,128)(2,1)}, bf16[128,512]{1,0:T(8,128)(2,1)S(1)}, u32[]{:S(2)}, u32[]{:S(2)}) collective-permute-start(bf16[128,512]{1,0:T(8,128)(2,1)} %get-tuple-element.30), channel_id=1, source_target_pairs={{0,1},{1,2},{2,3},{3,0},{4,5},{5,6},{6,7},{7,4},{8,9},{9,10},{10,1... | collective-permute-start | bytes 393224 | tf_op jit(solution)/shard_map/ppermute | solution.py:259
  171.1 6.8 %collective-permute-start.15 = (bf16[128,512]{1,0:T(8,128)(2,1)}, bf16[128,512]{1,0:T(8,128)(2,1)S(1)}, u32[]{:S(2)}, u32[]{:S(2)}) collective-permute-start(bf16[128,512]{1,0:T(8,128)(2,1)} %get-tuple-element.31), channel_id=1, source_target_pairs={{0,2},{1,3},{2,0},{3,1},{4,6},{5,7},{6,4},{7,5},{8,10},{9,11},{10,... | collective-permute-start | bytes 393224 | tf_op jit(solution)/shard_map/ppermute | solution.py:259
  172.5 6.3 %collective-permute-start.16 = (bf16[128,512]{1,0:T(8,128)(2,1)}, bf16[128,512]{1,0:T(8,128)(2,1)S(1)}, u32[]{:S(2)}, u32[]{:S(2)}) collective-permute-start(bf16[128,512]{1,0:T(8,128)(2,1)} %get-tuple-element.32), channel_id=1, source_target_pairs={{0,3},{1,0},{2,1},{3,2},{4,7},{5,4},{6,5},{7,6},{8,11},{9,8},{10,9... | collective-permute-start | bytes 393224 | tf_op jit(solution)/shard_map/ppermute | solution.py:259
  175.1 7.9 %collective-permute-start.17 = (bf16[128,512]{1,0:T(8,128)(2,1)}, bf16[128,512]{1,0:T(8,128)(2,1)S(1)}, u32[]{:S(2)}, u32[]{:S(2)}) collective-permute-start(bf16[128,512]{1,0:T(8,128)(2,1)} %get-tuple-element.21.refs_0_), channel_id=1, source_target_pairs={{0,4},{4,8},{8,12},{12,16},{16,20},{20,24},{24,28},{28,32},{32,36}... | collective-permute-start | bytes 393224 | tf_op jit(solution)/shard_map/ppermute | solution.py:259
  175.1 9.3 %collective-permute-start.21 = (bf16[128,512]{1,0:T(8,128)(2,1)}, bf16[128,512]{1,0:T(8,128)(2,1)S(1)}, u32[]{:S(2)}, u32[]{:S(2)}) collective-permute-start(bf16[128,512]{1,0:T(8,128)(2,1)} %get-tuple-element.25.refs_4_), channel_id=1, source_target_pairs={{0,4},{4,8},{8,12},{12,16},{16,20},{20,24},{24,28},{28,32},{32,36}... | collective-permute-start | bytes 393224 | tf_op jit(solution)/shard_map/ppermute | solution.py:259
  177.9 7.9 %collective-permute-start.25 = (bf16[128,512]{1,0:T(8,128)(2,1)}, bf16[128,512]{1,0:T(8,128)(2,1)S(1)}, u32[]{:S(2)}, u32[]{:S(2)}) collective-permute-start(bf16[128,512]{1,0:T(8,128)(2,1)} %copy-done.8), channel_id=1, source_target_pairs={{0,4},{4,8},{8,12},{12,16},{16,20},{20,24},{24,28},{28,32},{32,36}... | collective-permute-start | bytes 393224 | tf_op jit(solution)/shard_map/ppermute | solution.py:259
  177.9 9.3 %collective-permute-start.18 = (bf16[128,512]{1,0:T(8,128)(2,1)}, bf16[128,512]{1,0:T(8,128)(2,1)S(1)}, u32[]{:S(2)}, u32[]{:S(2)}) collective-permute-start(bf16[128,512]{1,0:T(8,128)(2,1)} %collective-permute-done.8.refs_1_), channel_id=1, source_target_pairs={{0,4},{4,8},{8,12},{12,16},{16,20},{20,24},{24,28},{28,32},{32,36}... | collective-permute-start | bytes 393224 | tf_op jit(solution)/shard_map/ppermute | solution.py:259
  178.8 9.9 %collective-permute-start.19 = (bf16[128,512]{1,0:T(8,128)(2,1)}, bf16[128,512]{1,0:T(8,128)(2,1)S(1)}, u32[]{:S(2)}, u32[]{:S(2)}) collective-permute-start(bf16[128,512]{1,0:T(8,128)(2,1)} %collective-permute-done.9.refs_2_), channel_id=1, source_target_pairs={{0,4},{4,8},{8,12},{12,16},{16,20},{20,24},{24,28},{28,32},{32,36}... | collective-permute-start | bytes 393224 | tf_op jit(solution)/shard_map/ppermute | solution.py:259
  183.0 7.9 %collective-permute-start.20 = (bf16[128,512]{1,0:T(8,128)(2,1)}, bf16[128,512]{1,0:T(8,128)(2,1)S(1)}, u32[]{:S(2)}, u32[]{:S(2)}) collective-permute-start(bf16[128,512]{1,0:T(8,128)(2,1)} %collective-permute-done.10.refs_3_), channel_id=1, source_target_pairs={{0,4},{4,8},{8,12},{12,16},{16,20},{20,24},{24,28},{28,32},{32,36}... | collective-permute-start | bytes 393224 | tf_op jit(solution)/shard_map/ppermute | solution.py:259
  184.4 7.9 %collective-permute-start.22 = (bf16[128,512]{1,0:T(8,128)(2,1)}, bf16[128,512]{1,0:T(8,128)(2,1)S(1)}, u32[]{:S(2)}, u32[]{:S(2)}) collective-permute-start(bf16[128,512]{1,0:T(8,128)(2,1)} %collective-permute-done.11.refs_5_), channel_id=1, source_target_pairs={{0,4},{4,8},{8,12},{12,16},{16,20},{20,24},{24,28},{28,32},{32,36}... | collective-permute-start | bytes 393224 | tf_op jit(solution)/shard_map/ppermute | solution.py:259
  185.8 7.9 %collective-permute-start.23 = (bf16[128,512]{1,0:T(8,128)(2,1)}, bf16[128,512]{1,0:T(8,128)(2,1)S(1)}, u32[]{:S(2)}, u32[]{:S(2)}) collective-permute-start(bf16[128,512]{1,0:T(8,128)(2,1)} %collective-permute-done.12.refs_6_), channel_id=1, source_target_pairs={{0,4},{4,8},{8,12},{12,16},{16,20},{20,24},{24,28},{28,32},{32,36}... | collective-permute-start | bytes 393224 | tf_op jit(solution)/shard_map/ppermute | solution.py:259
  187.3 7.9 %collective-permute-start.24 = (bf16[128,512]{1,0:T(8,128)(2,1)}, bf16[128,512]{1,0:T(8,128)(2,1)S(1)}, u32[]{:S(2)}, u32[]{:S(2)}) collective-permute-start(bf16[128,512]{1,0:T(8,128)(2,1)} %collective-permute-done.13.refs_7_), channel_id=1, source_target_pairs={{0,4},{4,8},{8,12},{12,16},{16,20},{20,24},{24,28},{28,32},{32,36}... | collective-permute-start | bytes 393224 | tf_op jit(solution)/shard_map/ppermute | solution.py:259
  188.7 7.9 %collective-permute-start.26 = (bf16[128,512]{1,0:T(8,128)(2,1)S(1)}, bf16[128,512]{1,0:T(8,128)(2,1)S(1)}, u32[]{:S(2)}, u32[]{:S(2)}) collective-permute-start(bf16[128,512]{1,0:T(8,128)(2,1)S(1)} %collective-permute-done.14.refs_9_), channel_id=1, source_target_pairs={{0,4},{4,8},{8,12},{12,16},{16,20},{20,24},{24,28},{28,32},{32,36}... | collective-permute-start | bytes 393224 | tf_op jit(solution)/shard_map/ppermute | solution.py:259
  190.9 7.7 %collective-permute-start.27 = (bf16[128,512]{1,0:T(8,128)(2,1)S(1)}, bf16[128,512]{1,0:T(8,128)(2,1)S(1)}, u32[]{:S(2)}, u32[]{:S(2)}) collective-permute-start(bf16[128,512]{1,0:T(8,128)(2,1)S(1)} %collective-permute-done.15.refs_10_), channel_id=1, source_target_pairs={{0,4},{4,8},{8,12},{12,16},{16,20},{20,24},{24,28},{28,32},{32,36}... | collective-permute-start | bytes 393224 | tf_op jit(solution)/shard_map/ppermute | solution.py:259
  192.3 7.7 %collective-permute-start.28 = (bf16[128,512]{1,0:T(8,128)(2,1)S(1)}, bf16[128,512]{1,0:T(8,128)(2,1)S(1)}, u32[]{:S(2)}, u32[]{:S(2)}) collective-permute-start(bf16[128,512]{1,0:T(8,128)(2,1)S(1)} %collective-permute-done.16.refs_11_), channel_id=1, source_target_pairs={{0,4},{4,8},{8,12},{12,16},{16,20},{20,24},{24,28},{28,32},{32,36}... | collective-permute-start | bytes 393224 | tf_op jit(solution)/shard_map/ppermute | solution.py:259
  200.0 0.9 copy-start.9

commit v2 on v1

v2 whole, which is shorter than its diff:
```python
import math

import jax
import jax.numpy as jnp
import ml_dtypes
import numpy as np
from jax import lax
from jax.experimental import pallas as pl
from jax.experimental.pallas import tpu as pltpu
from jax.sharding import PartitionSpec as P

L = 1920
F = 768
K0 = 8
HALF = 32
LAG_COUNT = 512
BLOCK = 128
SOURCES = 16
TPS = 3
REACH = 2
SEG_DEV = 4
SEGS = 16
NB = 32
TCAP = 6
TM = 4
SLAB = L // NB
ROWS = 64
PART = BLOCK // TM
SRC_PART = SOURCES // TM
MIB = 1 << 20
LANES = 128
GROUP = 8
STEP = 128

BF16 = jnp.bfloat16
F32 = jnp.float32


def forward_table():
    n = np.arange(L)[None, :]
    q = K0 + np.arange(F)[:, None]
    angles = (n * q % L) * (2.0 * np.pi / L)
    window = 0.5 - 0.5 * np.cos(np.arange(L) * (2.0 * np.pi / L))
    table = np.concatenate([np.cos(angles), -np.sin(angles)], axis=0) * window[None, :]
    padded = np.zeros((2 * F, NB, ROWS))
    padded[:, :, :SLAB] = table.reshape(2 * F, NB, SLAB)
    return padded.reshape(2 * F, NB * ROWS).astype(ml_dtypes.bfloat16)


def smoothing():
    k = np.arange(F)
    inside = (np.abs(k[:, None] - k[None, :]) <= HALF).astype(np.float64)
    inverse_count = 1.0 / inside.sum(axis=1, keepdims=True)
    return inside.astype(ml_dtypes.bfloat16), inverse_count.astype(np.float32)


def inverse_table():
    q = K0 + np.arange(F)[None, :]
    lag = np.arange(LAG_COUNT)[:, None] - LAG_COUNT // 2
    angles = (q * lag % L) * (2.0 * np.pi / L)
    table = np.concatenate([np.cos(angles), -np.sin(angles)], axis=1) / math.sqrt(SEGS * F)
    return table.astype(ml_dtypes.bfloat16)


def source_lanes():
    pick = np.zeros((TM, 2, BLOCK, LANES))
    for i in range(TM):
        for half in range(2):
            for s in range(SEG_DEV):
                for v in range(SRC_PART):
                    lane = half * SRC_PART * SEGS + v * SEGS + i * SEG_DEV + s
                    pick[i, half, s * PART + v * (BLOCK // SOURCES), lane] = 1.0
    return pick.astype(ml_dtypes.bfloat16)


def spread_lanes():
    spread = np.zeros((SRC_PART, LANES, 2 * LANES))
    for v in range(SRC_PART):
        for half in range(2):
            for s in range(SEGS):
                lane = half * LANES + s * GROUP
                spread[v, half * SRC_PART * SEGS + v * SEGS + s, lane : lane + GROUP] = 1.0
    return spread.astype(ml_dtypes.bfloat16)


def tile_lanes():
    order = np.zeros((TPS * LANES, SEG_DEV * LANES))
    for t in range(TPS):
        for s in range(SEG_DEV):
            for c in range(PART):
                order[t * LANES + s * PART + c, s * LANES + t * PART + c] = 1.0
    return order.astype(ml_dtypes.bfloat16)


def interleave():
    order = np.zeros((SEG_DEV * BLOCK, SEG_DEV * BLOCK))
    for s in range(SEG_DEV):
        for j in range(TM):
            for c in range(PART):
                order[s * BLOCK + j * PART + c, j * BLOCK + s * PART + c] = 1.0
    return order.astype(ml_dtypes.bfloat16)


PACK_BLOCKS = 8


def pack_kernel(own, records, quality, order, out):
    step = pl.program_id(0)
    marks = jnp.concatenate([quality[s : s + 1, :] for s in range(SEG_DEV)], axis=1)
    marks = jnp.broadcast_to(marks.astype(F32), (16, SEG_DEV * BLOCK)).astype(BF16)
    marks = jnp.dot(marks, order[...], preferred_element_type=F32)[:1]
    row = lax.broadcasted_iota(jnp.int32, (ROWS, SEG_DEV * BLOCK), 0)
    x = jnp.concatenate(
        [
            jnp.concatenate(
                [records[s, :, k * BLOCK : (k + 1) * BLOCK] for s in range(SEG_DEV)], axis=1
            )
            for k in range(PACK_BLOCKS)
        ],
        axis=0,
    )
    y = jnp.dot(x, order[...], preferred_element_type=F32)
    for k in range(PACK_BLOCKS):
        mine = step * PACK_BLOCKS + k == own[0]
        extra = jnp.where((row == SLAB) & mine, marks, 0.0)
        block = jnp.where(row < SLAB, y[k * ROWS : (k + 1) * ROWS], extra).astype(BF16)
        for j in range(TM):
            out[k * TM + j] = block[:, j * BLOCK : (j + 1) * BLOCK]


def pack(own, records, quality):
    return pl.pallas_call(
        pack_kernel,
        out_shape=jax.ShapeDtypeStruct((NB * TM, ROWS, BLOCK), BF16),
        grid_spec=pltpu.PrefetchScalarGridSpec(
            num_scalar_prefetch=1,
            grid=(NB // PACK_BLOCKS,),
            in_specs=[
                pl.BlockSpec((SEG_DEV, ROWS, PACK_BLOCKS * BLOCK), lambda g, own: (0, 0, g)),
                pl.BlockSpec((SEG_DEV, BLOCK), lambda g, own: (0, 0)),
                pl.BlockSpec(memory_space=pltpu.VMEM),
            ],
            out_specs=pl.BlockSpec((PACK_BLOCKS * TM, ROWS, BLOCK), lambda g, own: (g, 0, 0)),
        ),
        compiler_params=pltpu.CompilerParams(vmem_limit_bytes=24 * MIB),
        name="pack",
    )(own, records, quality, interleave())


PAIR = 2


def whiten_kernel(own, slabs, table, inside, inverse_count, pick, white, sources, total):
    step = pl.program_id(0)
    lanes = []
    for i in range(PAIR):
        marks = slabs[pl.ds(own[0], 1), i, pl.ds(48, 16), :][0, SLAB - 48 : SLAB - 47, :]
        lanes.append(slabs[:, i].reshape(NB * ROWS, BLOCK) * marks)
    x = jnp.concatenate(lanes, axis=1)
    spectrum = jnp.dot(table[...], x, preferred_element_type=F32)
    re = spectrum[:F]
    im = spectrum[F:]
    magnitude = jnp.sqrt(re * re + im * im).astype(BF16)
    level = jnp.dot(inside[...], magnitude, preferred_element_type=F32) * inverse_count[...]
    inverse_level = 1.0 / (level + 1e-6)

    @pl.when(step == 0)
    def _():
        total[...] = jnp.zeros_like(total)

    for half, part in ((0, re), (1, im)):
        value = (part * inverse_level).astype(BF16)
        for i in range(PAIR):
            mine = value[:, i * BLOCK : (i + 1) * BLOCK]
            white[i, half] = mine
            total[...] += jnp.dot(mine, pick[step * PAIR + i, half], preferred_element_type=F32)
    sources[...] = total[...].astype(BF16)


def whiten(own, slabs):
    inside, inverse_count = smoothing()
    return pl.pallas_call(
        whiten_kernel,
        out_shape=(
            jax.ShapeDtypeStruct((TM, 2, F, BLOCK), BF16),
            jax.ShapeDtypeStruct((F, LANES), BF16),
        ),
        grid_spec=pltpu.PrefetchScalarGridSpec(
            num_scalar_prefetch=1,
            grid=(TM // PAIR,),
            in_specs=[pl.BlockSpec((NB, PAIR, ROWS, BLOCK), lambda i, own: (0, i, 0, 0))]
            + [pl.BlockSpec(memory_space=pltpu.VMEM)] * 4,
            out_specs=(
                pl.BlockSpec((PAIR, 2, F, BLOCK), lambda i, own: (i, 0, 0, 0)),
                pl.BlockSpec((F, LANES), lambda i, own: (0, 0)),
            ),
            scratch_shapes=[pltpu.VMEM((F, LANES), F32)],
        ),
        compiler_params=pltpu.CompilerParams(vmem_limit_bytes=28 * MIB),
        name="whiten",
    )(own, slabs.reshape(NB, TM, ROWS, BLOCK), forward_table(), inside, inverse_count, source_lanes())


def diagonal_kernel(s0, s1, s2, s3, spread, out):
    rows = STEP
    groups = rows // GROUP
    row = lax.broadcasted_iota(jnp.int32, (rows, 2 * LANES), 0)
    lane = lax.broadcasted_iota(jnp.int32, (rows, 2 * LANES), 1)
    keep = jnp.bitwise_and(row, GROUP - 1) == jnp.bitwise_and(lane, GROUP - 1)
    for rel, ref in enumerate((s0, s1, s2, s3)):
        for pair in range(SRC_PART // 2):
            same, turned = [], []
            for v in (2 * pair, 2 * pair + 1):
                wide = jnp.dot(ref[...], spread[v], preferred_element_type=F32)
                wide = jnp.where(keep, wide, 0.0)
                swap = jnp.concatenate([-wide[:, LANES:], wide[:, :LANES]], axis=1)
                same.append(wide.reshape(groups, GROUP, 2 * LANES))
                turned.append(swap.reshape(groups, GROUP, 2 * LANES))
            at = (rel * SRC_PART + 2 * pair) * GROUP
            out[:, at : at + 2 * GROUP, :] = jnp.concatenate(same, axis=1).astype(BF16)
            at += SOURCES * GROUP
            out[:, at : at + 2 * GROUP, :] = jnp.concatenate(turned, axis=1).astype(BF16)


def diagonal(sources):
    groups = STEP // GROUP
    wide = 2 * SOURCES * GROUP
    return pl.pallas_call(
        diagonal_kernel,
        out_shape=jax.ShapeDtypeStruct((F // GROUP, wide, 2 * LANES), BF16),
        grid=(F // STEP,),
        in_specs=[pl.BlockSpec((STEP, LANES), lambda g: (g, 0))] * TM
        + [pl.BlockSpec(memory_space=pltpu.VMEM)],
        out_specs=pl.BlockSpec((groups, wide, 2 * LANES), lambda g: (g, 0, 0)),
        compiler_params=pltpu.CompilerParams(vmem_limit_bytes=24 * MIB),
        cost_estimate=pl.CostEstimate(flops=1, bytes_accessed=1, transcendentals=0),
        name="diagonal",
    )(*sources, spread_lanes())


def cross_kernel(pick, diag, order, *refs):
    receivers, (out, held, wide, sem) = refs[:6], refs[6:]
    step = pl.program_id(0)
    steps = F // STEP

    def copy(ref, t, k):
        rows = pl.ds(k * STEP, STEP)
        return pltpu.make_async_copy(
            ref.at[:, :, rows, :], held.at[k, t], sem.at[k, t]
        )

    @pl.when(step == 0)
    def _():
        for k in range(steps):
            for t in range(TPS):
                for index, ref in enumerate(receivers):

                    @pl.when(pick[t] == index)
                    def _():
                        copy(ref, t, k).start()

    for t in range(TPS):
        copy(receivers[0], t, step).wait()
    x = jnp.concatenate(
        [held[step, t].reshape(TM * 2 * STEP, LANES) for t in range(TPS)], axis=1
    )
    y = jnp.dot(x, order[...], preferred_element_type=F32)
    for i in range(TM):
        for half in range(2):
            at = (i * 2 + half) * STEP
            for s in range(SEG_DEV):
                wide[half * SEGS + i * SEG_DEV + s] = y[
                    at : at + STEP, s * LANES : (s + 1) * LANES
                ]

    def group(pair, carry):
        outs = []
        for g in range(2):
            at = pl.multiple_of((pair * 2 + g) * GROUP, GROUP)
            b = wide[:, pl.ds(at, GROUP), :].reshape(2 * SEGS * GROUP, LANES).astype(BF16)
            outs.append(jnp.dot(diag[pair * 2 + g], b, preferred_element_type=F32))
        both = jnp.concatenate(
            [o.reshape(2 * SOURCES, GROUP, LANES) for o in outs], axis=1
        ).astype(BF16)
        rows = pl.ds(pl.multiple_of(pair * 2 * GROUP, 2 * GROUP), 2 * GROUP)
        out[:, 0, rows, :] = both[:SOURCES]
        out[:, 1, rows, :] = both[SOURCES:]
        return carry

    lax.fori_loop(0, STEP // (2 * GROUP), group, 0, unroll=2)


def cross(pick, diag, receivers):
    groups = STEP // GROUP
    wide = 2 * SOURCES * GROUP
    return pl.pallas_call(
        cross_kernel,
        out_shape=jax.ShapeDtypeStruct((SOURCES, 2, F, LANES), BF16),
        grid_spec=pltpu.PrefetchScalarGridSpec(
            num_scalar_prefetch=1,
            grid=(F // STEP,),
            in_specs=[
                pl.BlockSpec((groups, wide, 2 * LANES), lambda g, *_: (g, 0, 0)),
                pl.BlockSpec(memory_space=pltpu.VMEM),
            ]
            + [pl.BlockSpec(memory_space=pl.ANY)] * 6,
            out_specs=pl.BlockSpec((SOURCES, 2, STEP, LANES), lambda g, *_: (0, 0, g, 0)),
            scratch_shapes=[
                pltpu.VMEM((F // STEP, TPS, TM, 2, STEP, LANES), BF16),
                pltpu.VMEM((2 * SEGS, STEP, LANES), F32),
                pltpu.SemaphoreType.DMA((F // STEP, TPS)),
            ],
        ),
        compiler_params=pltpu.CompilerParams(vmem_limit_bytes=32 * MIB),
        cost_estimate=pl.CostEstimate(flops=1, bytes_accessed=1, transcendentals=0),
        name="cross",
    )(pick, diag, tile_lanes(), *receivers)


def stack_kernel(spectra, inverse, out):
    for pair in range(SRC_PART // 2):
        x = jnp.concatenate(
            [spectra[2 * pair + v].reshape(2 * F, LANES) for v in range(2)], axis=1
        )
        y = jnp.dot(inverse[...], x, preferred_element_type=F32)
        for v in range(2):
            value = y[:, v * LANES : (v + 1) * LANES].T.astype(BF16)
            for t in range(TPS):
                at = (t * SRC_PART + 2 * pair + v) * PART
                out[at : at + PART, :] = value[t * PART : (t + 1) * PART, :]


def stack(spectra, rel, inverse):
    rows = TPS * SRC_PART * PART
    return pl.pallas_call(
        stack_kernel,
        out_shape=jax.ShapeDtypeStruct((rows, LAG_COUNT), BF16),
        grid=(1,),
        in_specs=[
            pl.BlockSpec((SRC_PART, 2, F, LANES), lambda g: (rel, 0, 0, 0)),
            pl.BlockSpec(memory_space=pltpu.VMEM),
        ],
        out_specs=pl.BlockSpec((rows, LAG_COUNT), lambda g: (0, 0)),
        compiler_params=pltpu.CompilerParams(vmem_limit_bytes=24 * MIB),
        cost_estimate=pl.CostEstimate(flops=1, bytes_accessed=1, transcendentals=0),
        name="stack",
    )(spectra, inverse)


def gather_kernel(place, own, *refs):
    pieces, out = refs[:-1], refs[-1]
    slot = pl.program_id(0)
    rows = SRC_PART * PART
    for candidate in range(2 * TPS + 1):

        @pl.when(place[slot] == candidate)
        def _():
            if candidate == 2 * TPS:
                out[...] = jnp.zeros_like(out)
                return
            moved, t = divmod(candidate, TPS)
            for rel in range(TM):
                value = pieces[moved * TM + rel][t * rows : (t + 1) * rows, :].astype(F32)
                at = pl.multiple_of(lax.rem(own[0] + TM - rel, TM) * PART, PART)
                out[0, :, pl.ds(at, PART), :] = value.reshape(SRC_PART, PART, LAG_COUNT)


def gather(place, own, pieces):
    return pl.pallas_call(
        gather_kernel,
        out_shape=jax.ShapeDtypeStruct((TCAP, SRC_PART, BLOCK, LAG_COUNT), F32),
        grid_spec=pltpu.PrefetchScalarGridSpec(
            num_scalar_prefetch=2,
            grid=(TCAP,),
            in_specs=[pl.BlockSpec(memory_space=pltpu.VMEM) for _ in pieces],
            out_specs=pl.BlockSpec((1, SRC_PART, BLOCK, LAG_COUNT), lambda s, *_: (s, 0, 0, 0)),
        ),
        compiler_params=pltpu.CompilerParams(vmem_limit_bytes=24 * MIB),
        name="gather",
    )(place, own, *pieces)


def shifted(value, axis, distance):
    count = lax.axis_size(axis)
    return lax.ppermute(value, axis, [(i, (i + distance) % count) for i in range(count)])


def on_chip(below, above):
    return [
        lax.ppermute(below, "chan", [(i, i - 1) for i in range(1, NB, 2)]),
        lax.ppermute(above, "chan", [(i, i + 1) for i in range(0, NB, 2)]),
    ]


def per_device(records, quality, tile_list, tile_slot_owner):
    chan = lax.axis_index("chan").astype(jnp.int32)
    time = lax.axis_index("tm").astype(jnp.int32)
    own = chan.reshape(1)

    slabs = pack(own, records, quality)
    slabs = lax.all_to_all(slabs, ("chan", "tm"), split_axis=0, concat_axis=0, tiled=True)
    white, sources = whiten(own, slabs)
    sources = [sources] + [shifted(sources, "tm", -rel) for rel in range(1, TM)]
    diag = diagonal(sources)
    below = shifted(white, "chan", 2)
    above = shifted(white, "chan", -2)
    mate = lax.ppermute(white, "chan", [(i, i ^ 1) for i in range(NB)])
    below, above, diag = lax.optimization_barrier((below, above, diag))
    receivers = [white, below, above, mate] + on_chip(below, above)
    odd = lax.rem(chan, 2)

    first = chan * TPS
    mine = lax.dynamic_slice(tile_list, (first, 0), (TPS, 2))[:, 1]
    offset = jnp.mod(mine - chan + REACH, NB)
    choice = jnp.where(
        odd == 1, jnp.array([1, 3, 0, 5, 2], jnp.int32), jnp.array([1, 4, 0, 3, 2], jnp.int32)
    )
    choice = jnp.sum(
        jnp.where(offset[:, None] == jnp.arange(2 * REACH + 1)[None, :], choice[None, :], 0), axis=1
    ).astype(jnp.int32)

    home = lax.dynamic_slice(tile_slot_owner, (first,), (TPS,))
    moved = lax.dynamic_slice(tile_slot_owner, (jnp.mod(chan - 1, NB) * TPS,), (TPS,))
    named = jnp.concatenate([home, moved])
    slots = chan * TCAP + jnp.arange(TCAP, dtype=jnp.int32)
    place = 2 * TPS + jnp.sum(
        jnp.where(
            slots[:, None] == named[None, :],
            jnp.arange(2 * TPS, dtype=jnp.int32)[None, :] - 2 * TPS,
            0,
        ),
        axis=1,
    )

    inverse = inverse_table()
    spectra = cross(choice, diag, receivers)
    stay, move = [None] * TM, [None] * TM
    for rel in (2, 0, 1, 3):
        part = stack(spectra, rel, inverse)
        stay[rel] = shifted(part, "tm", rel) if rel else part
        move[rel] = shifted(stay[rel], "chan", 1)
    return gather(place.astype(jnp.int32), time.reshape(1), stay + move)


def solution(mesh):
    placed = (P("tm", "chan", None), P("tm", "chan"), P(), P())
    return jax.shard_map(
        per_device,
        mesh=mesh,
        in_specs=placed,
        out_specs=P("chan", "tm", None, None),
        check_vma=False,
    )
```

time: 207 us -> 166 us (0.80)
  Pallas kernels: 59.2 us -> 38 us
  starting transfers between devices: 32.2 us -> 16.5 us
  waiting for transfers between devices: 66.1 us -> 58.3 us
  local copies, waits for them, and re-layouts: 6.94 us -> 11 us
    ppermute x26 -> x12, starting transfers between devices: 25.5 us -> 9.88 us  [shifted(): lax.ppermute(value, axis, [(i, (i + distance) % count) for i in range(cou...]
    pallas_call x4 -> x7, Pallas kernels: 45.6 us -> 31.7 us  [the longest x1 15.1 us: cross(): pl.pallas_call(cross_kernel, out_shape=jax.ShapeDtypeStruct((SOURCES, 2,...]
    ppermute x26 -> x12, waiting for transfers between devices: 66.1 us -> 56.4 us  [shifted(): lax.ppermute(value, axis, [(i, (i + distance) % count) for i in range(cou...]
    pallas_call x1, Pallas kernels: 8.19 us -> 2.22 us  [pack(): pl.pallas_call(pack_kernel, out_shape=jax.ShapeDtypeStruct((NB * TM, ROWS...]
    unnamed x33 -> x35, local copies, waits for them, and re-layouts: 6.13 us -> 10.8 us
  transfers between devices with their start and end apart: 29 -> 15, of which waited for: 17 -> 10; matrix products, arithmetic and copies ran while one was open for 1% -> 0% of each run, Pallas kernels for 12% -> 4%
where the time goes in v2:
time: 166 us
  waiting for transfers between devices  58.3 us (35%)
  blocking collectives  41.1 us (25%)
  Pallas kernels  38 us (23%)
  starting transfers between devices  16.5 us (10%)
  local copies, waits for them, and re-layouts  11 us (7%)
    ppermute x12, waiting for transfers between devices, shifted(): lax.ppermute(value, axis, [(i, (i + distance) % count) for i in range(cou...  56.4 us
    all_to_all x1, blocking collectives, per_device(): lax.all_to_all(slabs, ('chan', 'tm'), split_axis=0, concat_axis=0, tiled=...  41.1 us
    pallas_call x1, Pallas kernels, cross(): pl.pallas_call(cross_kernel, out_shape=jax.ShapeDtypeStruct((SOURCES, 2,...  15.1 us
    unnamed x35, local copies, waits for them, and re-layouts  10.8 us
    ppermute x12, starting transfers between devices, shifted(): lax.ppermute(value, axis, [(i, (i + distance) % count) for i in range(cou...  9.88 us
    pallas_call x1, Pallas kernels, whiten(): pl.pallas_call(whiten_kernel, out_shape=(jax.ShapeDtypeStruct((TM, 2, F,...  7.37 us
    pallas_call x4, Pallas kernels, stack(): pl.pallas_call(stack_kernel, out_shape=jax.ShapeDtypeStruct((rows, LAG_CO...  6.59 us
    ppermute x1, starting transfers between devices, on_chip(): lax.ppermute(above, 'chan', [(i, i + 1) for i in range(0, NB, 2)])  5.35 us
  transfers between devices with their start and end apart: 15, of which 10 were waited for; matrix products, arithmetic and copies ran while one was open for 0% of the time, Pallas kernels for 4%

profile of v2, /device:TPU:0, one launch (start us, length us, event | category | flops | bytes accessed | tf_op | source)
XLA Modules:
  0.0 165.6 jit_solution(2126218055383680483)
XLA Ops:
  0.0 2.8 %copy.16.records = bf16[4,60,4096]{2,1,0:T(8,128)(2,1)S(1)} copy(bf16[4,60,4096]{2,0,1:T(4,128)(2,1)} %param.14) | data formatting | bytes 3932160 | tf_op args[0]
  2.8 0.0 copy-start.11
  2.8 0.7 copy-done.11
  3.5 2.2 %pack.1 = bf16[128,64,128]{2,1,0:T(8,128)(2,1)S(1)} custom-call(s32[1]{0:T(128)} %bitcast.2.own, bf16[4,60,4096]{2,1,0:T(8,128)(2,1)S(1)} %copy.16.records, s32[4,128]{1,0:T(4,128)S(1)} %copy-done.11, bf16[512,512]{1,0:T(8,128)(2,1)S(1)} %copy-done.6), custom_call_target="tpu_custom_call" | custom-call | tf_op jit(solution)/shard_map/pack/pallas_call | solution.py:132
  5.7 0.0 copy-start.5
  5.7 0.0 copy-start.8
  5.7 0.0 copy-start.9
  5.8 41.1 %all_to_all.5 = bf16[128,64,128]{2,1,0:T(8,128)(2,1)S(1)} all-to-all(bf16[128,64,128]{2,1,0:T(8,128)(2,1)S(1)} %pack.1), channel_id=1, replica_groups=mesh['chan'=32,'tm'=4] {'chan','tm'}, dimensions={0} | all-to-all | bytes 4194304 | tf_op jit(solution)/shard_map/all_to_all | solution.py:401
  46.9 0.0 copy-start.10
  46.9 7.4 %whiten.1 = (bf16[4,2,768,128]{3,2,1,0:T(8,128)(2,1)S(1)}, bf16[768,128]{1,0:T(8,128)(2,1)S(1)}) custom-call(s32[1]{0:T(128)} %bitcast.2.own, bf16[32,4,64,128]{3,2,1,0:T(8,128)(2,1)S(1)} %bitcast.5, bf16[1536,2048]{1,0:T(8,128)(2,1)S(1)} %bitcast.7, bf16[768,768]{1,0:T(8,128)(2,1)S(1)} %copy-done.5, f32[768,1]{1,0:T(8,128)S(1)} %copy-done.8, ...), custom_call_target="tpu_custom_call" | custom-call | tf_op jit(solution)/shard_map/whiten/pallas_call | solution.py:182
  54.3 1.1 collective-permute-start.1
  55.4 1.0 collective-permute-start
  56.4 0.6 collective-permute-start.4
  57.0 2.5 %collective-permute-start.3 = (bf16[768,128]{1,0:T(8,128)(2,1)S(1)}, bf16[768,128]{1,0:T(8,128)(2,1)S(1)}, u32[]{:S(2)}, u32[]{:S(2)}) collective-permute-start(bf16[768,128]{1,0:T(8,128)(2,1)S(1)} %get-tuple-element.11.s0), channel_id=1, source_target_pairs={{0,2},{1,3},{2,0},{3,1},{4,6},{5,7},{6,4},{7,5},{8,10},{9,11},{10,... | collective-permute-start | bytes 589832 | tf_op jit(solution)/shard_map/ppermute | solution.py:385
  59.5 0.6 collective-permute-start.2
  60.0 8.3 %collective-permute-done.4.s3 = bf16[768,128]{1,0:T(8,128)(2,1)S(1)} collective-permute-done((bf16[768,128]{1,0:T(8,128)(2,1)S(1)}, bf16[768,128]{1,0:T(8,128)(2,1)S(1)}, u32[]{:S(2)}, u32[]{:S(2)}) %collective-permute-start.4) | collective-permute-done | bytes 196640 | tf_op jit(solution)/shard_map/ppermute | solution.py:385
  68.3 0.0 collective-permute-start.5
  68.3 0.0 collective-permute-done.3.s2
  68.4 0.6 collective-permute-done.2.s1
  69.0 2.6 %diagonal.1.diag = bf16[96,256,256]{2,1,0:T(8,128)(2,1)S(1)} custom-call(bf16[768,128]{1,0:T(8,128)(2,1)S(1)} %get-tuple-element.11.s0, bf16[768,128]{1,0:T(8,128)(2,1)S(1)} %collective-permute-done.2.s1, bf16[768,128]{1,0:T(8,128)(2,1)S(1)} %collective-permute-done.3.s2, bf16[768,128]{1,0:T(8,128)(2,1)S(1)} %collective-permute-done.4.s3, ...), custom_call_target="tpu_custom_call" | custom-call | flops 1 | bytes 1 | tf_op jit(solution)/shard_map/diagonal/pallas_call | solution.py:228
  71.6 4.5 %copy-done.3 = bf16[96,256,256]{2,1,0:T(8,128)(2,1)} copy-done((bf16[96,256,256]{2,1,0:T(8,128)(2,1)}, bf16[96,256,256]{2,1,0:T(8,128)(2,1)S(1)}, u32[]{:S(2)}) %copy-start.3) | copy-done | bytes 12582936
  76.1 15.0 %collective-permute-done.1.refs_2_ = bf16[4,2,768,128]{3,2,1,0:T(8,128)(2,1)} collective-permute-done((bf16[4,2,768,128]{3,2,1,0:T(8,128)(2,1)S(1)}, bf16[4,2,768,128]{3,2,1,0:T(8,128)(2,1)}, u32[]{:S(2)}, u32[]{:S(2)}) %collective-permute-start.1) | collective-permute-done | bytes 1572896 | tf_op jit(solution)/shard_map/ppermute | solution.py:385
  91.0 3.8 %collective-permute-done.refs_1_ = bf16[4,2,768,128]{3,2,1,0:T(8,128)(2,1)} collective-permute-done((bf16[4,2,768,128]{3,2,1,0:T(8,128)(2,1)S(1)}, bf16[4,2,768,128]{3,2,1,0:T(8,128)(2,1)}, u32[]{:S(2)}, u32[]{:S(2)}) %collective-permute-start) | collective-permute-done | bytes 1572896 | tf_op jit(solution)/shard_map/ppermute | solution.py:385
  94.8 1.3 collective-permute-start.6
  96.1 5.3 %collective-permute-start.7 = (bf16[4,2,768,128]{3,2,1,0:T(8,128)(2,1)}, bf16[4,2,768,128]{3,2,1,0:T(8,128)(2,1)}, u32[]{:S(2)}, u32[]{:S(2)}) collective-permute-start(bf16[4,2,768,128]{3,2,1,0:T(8,128)(2,1)} %collective-permute-done.1.refs_2_), channel_id=1, source_target_pairs={{0,4},{8,12},{16,20},{24,28},{32,36},{40,44},{48,52},{56,60},{64,6... | collective-permute-start | bytes 4718600 | tf_op jit(solution)/shard_map/ppermute | solution.py:391
  101.5 0.1 constant_dynamic-slice_fusion
  101.6 0.2 select_reduce_fusion.1.pick
  101.8 1.9 %collective-permute-done.7.refs_5_ = bf16[4,2,768,128]{3,2,1,0:T(8,128)(2,1)} collective-permute-done((bf16[4,2,768,128]{3,2,1,0:T(8,128)(2,1)}, bf16[4,2,768,128]{3,2,1,0:T(8,128)(2,1)}, u32[]{:S(2)}, u32[]{:S(2)}) %collective-permute-start.7) | collective-permute-done | bytes 1572896 | tf_op jit(solution)/shard_map/ppermute | solution.py:391
  103.7 15.1 %cross.1.spectra = bf16[16,2,768,128]{3,2,1,0:T(8,128)(2,1)S(1)} custom-call(s32[3]{0:T(128)S(1)} %select_reduce_fusion.1.pick, bf16[96,256,256]{2,1,0:T(8,128)(2,1)} %copy-done.3, bf16[384,512]{1,0:T(8,128)(2,1)S(1)} %copy-done.7, bf16[4,2,768,128]{3,2,1,0:T(8,128)(2,1)S(1)} %get-tuple-element.10.refs_0_, ...), custom_call_target="tpu_custom_call" | custom-call | flops 1 | bytes 1 | tf_op jit(solution)/shard_map/cross/pallas_call | solution.py:296
  118.8 0.0 copy-start.1
  118.9 2.4 %stack.5 = bf16[384,512]{1,0:T(8,128)(2,1)} custom-call(bf16[16,2,768,128]{3,2,1,0:T(8,128)(2,1)S(1)} %cross.1.spectra, bf16[512,1536]{1,0:T(8,128)(2,1)S(1)} %copy-done.4), custom_call_target="tpu_custom_call" | custom-call | flops 1 | bytes 1 | tf_op jit(solution)/shard_map/stack/pallas_call | solution.py:335
  121.2 0.6 collective-permute-start.8
  121.8 1.9 %stack.6 = bf16[384,512]{1,0:T(8,128)(2,1)} custom-call(bf16[16,2,768,128]{3,2,1,0:T(8,128)(2,1)S(1)} %cross.1.spectra, bf16[512,1536]{1,0:T(8,128)(2,1)S(1)} %copy-done.4), custom_call_target="tpu_custom_call" | custom-call | flops 1 | bytes 1 | tf_op jit(solution)/shard_map/stack/pallas_call | solution.py:335
  123.7 1.9 %collective-permute-start.9 = (bf16[384,512]{1,0:T(8,128)(2,1)}, bf16[384,512]{1,0:T(8,128)(2,1)S(1)}, u32[]{:S(2)}, u32[]{:S(2)}) collective-permute-start(bf16[384,512]{1,0:T(8,128)(2,1)} %stack.6), channel_id=1, source_target_pairs={{0,2},{1,3},{2,0},{3,1},{4,6},{5,7},{6,4},{7,5},{8,10},{9,11},{10,... | collective-permute-start | bytes 1179656 | tf_op jit(solution)/shard_map/ppermute | solution.py:385
  125.6 1.1 stack.7
  126.8 1.6 collective-permute-start.10
  128.4 0.1 fusion.2
  128.5 0.1 pad_add_fusion
  128.5 2.8 %copy-done.2 = bf16[16,2,768,128]{3,2,1,0:T(8,128)(2,1)S(1)} copy-done((bf16[16,2,768,128]{3,2,1,0:T(8,128)(2,1)S(1)}, bf16[16,2,768,128]{3,2,1,0:T(8,128)(2,1)}, u32[]{:S(2)}) %copy-start.2) | copy-done | bytes 6291480
  131.3 1.2 stack.4.refs_0_
  132.5 0.1 collective-permute-start.11
  132.6 10.0 %collective-permute-done.8.refs_1_ = bf16[384,512]{1,0:T(8,128)(2,1)S(1)} collective-permute-done((bf16[384,512]{1,0:T(8,128)(2,1)}, bf16[384,512]{1,0:T(8,128)(2,1)S(1)}, u32[]{:S(2)}, u32[]{:S(2)}) %collective-permute-start.8) | collective-permute-done | bytes 393248 | tf_op jit(solution)/shard_map/ppermute | solution.py:385
  142.6 2.5 %collective-permute-done.10.refs_3_ = bf16[384,512]{1,0:T(8,128)(2,1)S(1)} collective-permute-done((bf16[384,512]{1,0:T(8,128)(2,1)S(1)}, bf16[384,512]{1,0:T(8,128)(2,1)S(1)}, u32[]{:S(2)}, u32[]{:S(2)}) %collective-permute-start.10) | collective-permute-done | bytes 393248 | tf_op jit(solution)/shard_map/ppermute | solution.py:385
  145.1 0.2 select_reduce_fusion
  145.3 7.8 %collective-permute-done.12.refs_5_ = bf16[384,512]{1,0:T(8,128)(2,1)S(1)} collective-permute-done((bf16[384,512]{1,0:T(8,128)(2,1)S(1)}, bf16[384,512]{1,0:T(8,128)(2,1)S(1)}, u32[]{:S(2)}, u32[]{:S(2)}) %collective-permute-start.12) | collective-permute-done | bytes 393248 | tf_op jit(solution)/shard_map/ppermute | solution.py:385
  153.1 4.2 %collective-permute-done.13.refs_6_ = bf16[384,512]{1,0:T(8,128)(2,1)S(1)} collective-permute-done((bf16[384,512]{1,0:T(8,128)(2,1)S(1)}, bf16[384,512]{1,0:T(8,128)(2,1)S(1)}, u32[]{:S(2)}, u32[]{:S(2)}) %collective-permute-start.13) | collective-permute-done | bytes 393248 | tf_op jit(solution)/shard_map/ppermute | solution.py:385
  157.3 4.2 %collective-permute-done.14.refs_7_ = bf16[384,512]{1,0:T(8,128)(2,1)S(1)} collective-permute-done((bf16[384,512]{1,0:T(8,128)(2,1)S(1)}, bf16[384,512]{1,0:T(8,128)(2,1)S(1)}, u32[]{:S(2)}, u32[]{:S(2)}) %collective-permute-start.14) | collective-permute-done | bytes 393248 | tf_op jit(solution)/shard_map/ppermute | solution.py:385
  161.5 4.1 %gather.1 = f32[6,4,128,512]{3,2,1,0:T(8,128)} custom-call(s32[6]{0:T(128)S(1)} %broadcast_add_fusion.place, s32[1]{0:T(128)} %bitcast.own, bf16[384,512]{1,0:T(8,128)(2,1)S(1)} %stack.4.refs_0_, bf16[384,512]{1,0:T(8,128)(2,1)S(1)} %collective-permute-done.8.refs_1_, bf16[384,512]{1,0:T(8,128)(2,1)S(1)} %collective-permute-done.9.refs_2_, ...), custom_call_target="tpu_custom_call" | custom-call | tf_op jit(solution)/shard_map/gather/pallas_call | solution.py:369
  (37 shorter events, 0.1 us)
Async XLA Ops:
  0.0 101.5 %copy-start = (s32[96,2]{0,1:T(2,128)S(1)}, s32[96,2]{0,1:T(2,128)}, u32[]{:S(2)}) copy-start(s32[96,2]{0,1:T(2,128)} %param.16) | copy-start | bytes 2308
  0.0 2.8 %copy-start.6 = (bf16[512,512]{1,0:T(8,128)(2,1)S(1)}, bf16[512,512]{1,0:T(8,128)(2,1)}, u32[]{:S(2)}) copy-start(bf16[512,512]{1,0:T(8,128)(2,1)} %constant.70.clone.order) | copy-start | bytes 1572868
  0.0 46.9 %slice-start = ((s8[6291456]{0:T(1024)(128)(4,1)}), s8[4194304]{0:T(1024)(128)(4,1)S(1)}, s32[]{:S(2)}) async-start(s8[6291456]{0:T(1024)(128)(4,1)} %bitcast.6), calls=%async_computation.1 | async-start | bytes 8388608
  2.8 0.7 copy-start.11
  3.5 43.4 %slice-start.1 = ((s8[6291456]{0:T(1024)(128)(4,1)}), s8[2097152]{0:T(1024)(128)(4,1)S(1)}, s32[]{:S(2)}) async-start(s8[6291456]{0:T(1024)(128)(4,1)} %bitcast.6), calls=%async_computation.2 | async-start | bytes 4194304
  5.7 41.2 %copy-start.5 = (bf16[768,768]{1,0:T(8,128)(2,1)S(1)}, bf16[768,768]{1,0:T(8,128)(2,1)}, u32[]{:S(2)}) copy-start(bf16[768,768]{1,0:T(8,128)(2,1)} %constant.72.clone.inside) | copy-start | bytes 3538948
  5.7 41.2 %copy-start.8 = (f32[768,1]{1,0:T(8,128)S(1)}, f32[768,1]{1,0:T(8,128)}, u32[]{:S(2)}) copy-start(f32[768,1]{1,0:T(8,128)} %constant.73.clone.inverse_count) | copy-start | bytes 9220
  5.7 41.1 %copy-start.9 = (bf16[4,2,128,128]{3,2,1,0:T(8,128)(2,1)S(1)}, bf16[4,2,128,128]{3,2,1,0:T(8,128)(2,1)}, u32[]{:S(2)}) copy-start(bf16[4,2,128,128]{3,2,1,0:T(8,128)(2,1)} %constant.74.clone.pick) | copy-start | bytes 786436
  46.9 22.1 %copy-start.10 = (bf16[4,128,256]{2,1,0:T(8,128)(2,1)S(1)}, bf16[4,128,256]{2,1,0:T(8,128)(2,1)}, u32[]{:S(2)}) copy-start(bf16[4,128,256]{2,1,0:T(8,128)(2,1)} %constant.75.clone.spread) | copy-start | bytes 786436
  54.3 36.7 %collective-permute-start.1 = (bf16[4,2,768,128]{3,2,1,0:T(8,128)(2,1)S(1)}, bf16[4,2,768,128]{3,2,1,0:T(8,128)(2,1)}, u32[]{:S(2)}, u32[]{:S(2)}) collective-permute-start(bf16[4,2,768,128]{3,2,1,0:T(8,128)(2,1)S(1)} %get-tuple-element.10.refs_0_), channel_id=1, source_target_pairs={{0,120},{4,124},{8,0},{12,4},{16,8},{20,12},{24,16},{28,20},{32,24... | collective-permute-start | bytes 4718600 | tf_op jit(solution)/shard_map/ppermute | solution.py:385
  55.4 39.5 %collective-permute-start = (bf16[4,2,768,128]{3,2,1,0:T(8,128)(2,1)S(1)}, bf16[4,2,768,128]{3,2,1,0:T(8,128)(2,1)}, u32[]{:S(2)}, u32[]{:S(2)}) collective-permute-start(bf16[4,2,768,128]{3,2,1,0:T(8,128)(2,1)S(1)} %get-tuple-element.10.refs_0_), channel_id=1, source_target_pairs={{0,8},{4,12},{8,16},{12,20},{16,24},{20,28},{24,32},{28,36},{32,40... | collective-permute-start | bytes 4718600 | tf_op jit(solution)/shard_map/ppermute | solution.py:385
  56.4 45.2 %copy-start.13 = (s32[5]{0:T(128)S(1)}, s32[5]{0:T(128)}, u32[]{:S(2)}) copy-start(s32[5]{0:T(128)} %constant.77.clone) | copy-start | bytes 64
  56.4 45.2 %copy-start.14 = (s32[5]{0:T(128)S(1)}, s32[5]{0:T(128)}, u32[]{:S(2)}) copy-start(s32[5]{0:T(128)} %constant.76.clone) | copy-start | bytes 64
  56.4 47.3 %copy-start.7 = (bf16[384,512]{1,0:T(8,128)(2,1)S(1)}, bf16[384,512]{1,0:T(8,128)(2,1)}, u32[]{:S(2)}) copy-start(bf16[384,512]{1,0:T(8,128)(2,1)} %constant.78.clone.order) | copy-start | bytes 1179652
  56.4 11.9 %collective-permute-start.4 = (bf16[768,128]{1,0:T(8,128)(2,1)S(1)}, bf16[768,128]{1,0:T(8,128)(2,1)S(1)}, u32[]{:S(2)}, u32[]{:S(2)}) collective-permute-start(bf16[768,128]{1,0:T(8,128)(2,1)S(1)} %get-tuple-element.11.s0), channel_id=1, source_target_pairs={{0,1},{1,2},{2,3},{3,0},{4,5},{5,6},{6,7},{7,4},{8,9},{9,10},{10,1... | collective-permute-start | bytes 589832 | tf_op jit(solution)/shard_map/ppermute | solution.py:385
  57.0 11.4 %collective-permute-start.3 = (bf16[768,128]{1,0:T(8,128)(2,1)S(1)}, bf16[768,128]{1,0:T(8,128)(2,1)S(1)}, u32[]{:S(2)}, u32[]{:S(2)}) collective-permute-start(bf16[768,128]{1,0:T(8,128)(2,1)S(1)} %get-tuple-element.11.s0), channel_id=1, source_target_pairs={{0,2},{1,3},{2,0},{3,1},{4,6},{5,7},{6,4},{7,5},{8,10},{9,11},{10,... | collective-permute-start | bytes 589832 | tf_op jit(solution)/shard_map/ppermute | solution.py:385
  59.5 9.5 %collective-permute-start.2 = (bf16[768,128]{1,0:T(8,128)(2,1)S(1)}, bf16[768,128]{1,0:T(8,128)(2,1)S(1)}, u32[]{:S(2)}, u32[]{:S(2)}) collective-permute-start(bf16[768,128]{1,0:T(8,128)(2,1)S(1)} %get-tuple-element.11.s0), channel_id=1, source_target_pairs={{0,3},{1,0},{2,1},{3,2},{4,7},{5,4},{6,5},{7,6},{8,11},{9,8},{10,9... | collective-permute-start | bytes 589832 | tf_op jit(solution)/shard_map/ppermute | solution.py:385
  68.3 33.4 %collective-permute-start.5 = (bf16[4,2,768,128]{3,2,1,0:T(8,128)(2,1)S(1)}, bf16[4,2,768,128]{3,2,1,0:T(8,128)(2,1)}, u32[]{:S(2)}, u32[]{:S(2)}) collective-permute-start(bf16[4,2,768,128]{3,2,1,0:T(8,128)(2,1)S(1)} %get-tuple-element.10.refs_0_), channel_id=1, source_target_pairs={{0,4},{4,0},{8,12},{12,8},{16,20},{20,16},{24,28},{28,24},{32,36},... | collective-permute-start | bytes 4718600 | tf_op jit(solution)/shard_map/ppermute | solution.py:407
  71.6 4.5 %copy-start.3 = (bf16[96,256,256]{2,1,0:T(8,128)(2,1)}, bf16[96,256,256]{2,1,0:T(8,128)(2,1)S(1)}, u32[]{:S(2)}) copy-start(bf16[96,256,256]{2,1,0:T(8,128)(2,1)S(1)} %diagonal.1.diag) | copy-start | bytes 37748740
  94.8 7.0 %collective-permute-start.6 = (bf16[4,2,768,128]{3,2,1,0:T(8,128)(2,1)}, bf16[4,2,768,128]{3,2,1,0:T(8,128)(2,1)}, u32[]{:S(2)}, u32[]{:S(2)}) collective-permute-start(bf16[4,2,768,128]{3,2,1,0:T(8,128)(2,1)} %collective-permute-done.refs_1_), channel_id=1, source_target_pairs={{4,0},{12,8},{20,16},{28,24},{36,32},{44,40},{52,48},{60,56},{68,6... | collective-permute-start | bytes 4718600 | tf_op jit(solution)/shard_map/ppermute | solution.py:390
  96.1 7.6 %collective-permute-start.7 = (bf16[4,2,768,128]{3,2,1,0:T(8,128)(2,1)}, bf16[4,2,768,128]{3,2,1,0:T(8,128)(2,1)}, u32[]{:S(2)}, u32[]{:S(2)}) collective-permute-start(bf16[4,2,768,128]{3,2,1,0:T(8,128)(2,1)} %collective-permute-done.1.refs_2_), channel_id=1, source_target_pairs={{0,4},{8,12},{16,20},{24,28},{32,36},{40,44},{48,52},{56,60},{64,6... | collective-permute-start | bytes 4718600 | tf_op jit(solution)/shard_map/ppermute | solution.py:391
  101.8 17.1 %copy-start.4 = (bf16[512,1536]{1,0:T(8,128)(2,1)S(1)}, bf16[512,1536]{1,0:T(8,128)(2,1)}, u32[]{:S(2)}) copy-start(bf16[512,1536]{1,0:T(8,128)(2,1)} %constant.79.clone.inverse) | copy-start | bytes 4718596
  118.8 6.8 %copy-start.1 = (bf16[16,2,768,128]{3,2,1,0:T(8,128)(2,1)}, bf16[16,2,768,128]{3,2,1,0:T(8,128)(2,1)S(1)}, u32[]{:S(2)}) copy-start(bf16[16,2,768,128]{3,2,1,0:T(8,128)(2,1)S(1)} %cross.1.spectra) | copy-start | bytes 18874372
  121.2 21.3 %collective-permute-start.8 = (bf16[384,512]{1,0:T(8,128)(2,1)}, bf16[384,512]{1,0:T(8,128)(2,1)S(1)}, u32[]{:S(2)}, u32[]{:S(2)}) collective-permute-start(bf16[384,512]{1,0:T(8,128)(2,1)} %stack.5), channel_id=1, source_target_pairs={{0,1},{1,2},{2,3},{3,0},{4,5},{5,6},{6,7},{7,4},{8,9},{9,10},{10,1... | collective-permute-start | bytes 1179656 | tf_op jit(solution)/shard_map/ppermute | solution.py:385
  123.7 4.7 %copy-start.12 = (s32[96]{0:T(128)S(1)}, s32[96]{0:T(128)}, u32[]{:S(2)}) copy-start(s32[96]{0:T(128)} %param.17) | copy-start | bytes 1156
  123.7 18.8 %collective-permute-start.9 = (bf16[384,512]{1,0:T(8,128)(2,1)}, bf16[384,512]{1,0:T(8,128)(2,1)S(1)}, u32[]{:S(2)}, u32[]{:S(2)}) collective-permute-start(bf16[384,512]{1,0:T(8,128)(2,1)} %stack.6), channel_id=1, source_target_pairs={{0,2},{1,3},{2,0},{3,1},{4,6},{5,7},{6,4},{7,5},{8,10},{9,11},{10,... | collective-permute-start | bytes 1179656 | tf_op jit(solution)/shard_map/ppermute | solution.py:385
  126.8 18.3 %collective-permute-start.10 = (bf16[384,512]{1,0:T(8,128)(2,1)S(1)}, bf16[384,512]{1,0:T(8,128)(2,1)S(1)}, u32[]{:S(2)}, u32[]{:S(2)}) collective-permute-start(bf16[384,512]{1,0:T(8,128)(2,1)S(1)} %stack.7), channel_id=1, source_target_pairs={{0,3},{1,0},{2,1},{3,2},{4,7},{5,4},{6,5},{7,6},{8,11},{9,8},{10,9... | collective-permute-start | bytes 1179656 | tf_op jit(solution)/shard_map/ppermute | solution.py:385
  128.5 2.8 %copy-start.2 = (bf16[16,2,768,128]{3,2,1,0:T(8,128)(2,1)S(1)}, bf16[16,2,768,128]{3,2,1,0:T(8,128)(2,1)}, u32[]{:S(2)}) copy-start(bf16[16,2,768,128]{3,2,1,0:T(8,128)(2,1)} %copy-done.1) | copy-start | bytes 18874372
  132.5 12.8 %collective-permute-start.11 = (bf16[384,512]{1,0:T(8,128)(2,1)S(1)}, bf16[384,512]{1,0:T(8,128)(2,1)S(1)}, u32[]{:S(2)}, u32[]{:S(2)}) collective-permute-start(bf16[384,512]{1,0:T(8,128)(2,1)S(1)} %stack.4.refs_0_), channel_id=1, source_target_pairs={{0,4},{4,8},{8,12},{12,16},{16,20},{20,24},{24,28},{28,32},{32,36}... | collective-permute-start | bytes 1179656 | tf_op jit(solution)/shard_map/ppermute | solution.py:385
  142.6 10.5 %collective-permute-start.12 = (bf16[384,512]{1,0:T(8,128)(2,1)S(1)}, bf16[384,512]{1,0:T(8,128)(2,1)S(1)}, u32[]{:S(2)}, u32[]{:S(2)}) collective-permute-start(bf16[384,512]{1,0:T(8,128)(2,1)S(1)} %collective-permute-done.8.refs_1_), channel_id=1, source_target_pairs={{0,4},{4,8},{8,12},{12,16},{16,20},{20,24},{24,28},{28,32},{32,36}... | collective-permute-start | bytes 1179656 | tf_op jit(solution)/shard_map/ppermute | solution.py:385
  142.6 14.7 %collective-permute-start.13 = (bf16[384,512]{1,0:T(8,128)(2,1)S(1)}, bf16[384,512]{1,0:T(8,128)(2,1)S(1)}, u32[]{:S(2)}, u32[]{:S(2)}) collective-permute-start(bf16[384,512]{1,0:T(8,128)(2,1)S(1)} %collective-permute-done.9.refs_2_), channel_id=1, source_target_pairs={{0,4},{4,8},{8,12},{12,16},{16,20},{20,24},{24,28},{28,32},{32,36}... | collective-permute-start | bytes 1179656 | tf_op jit(solution)/shard_map/ppermute | solution.py:385
  145.1 16.4 %collective-permute-start.14 = (bf16[384,512]{1,0:T(8,128)(2,1)S(1)}, bf16[384,512]{1,0:T(8,128)(2,1)S(1)}, u32[]{:S(2)}, u32[]{:S(2)}) collective-permute-start(bf16[384,512]{1,0:T(8,128)(2,1)S(1)} %collective-permute-done.10.refs_3_), channel_id=1, source_target_pairs={{0,4},{4,8},{8,12},{12,16},{16,20},{20,24},{24,28},{28,32},{32,36}... | collective-permute-start | bytes 1179656 | tf_op jit(solution)/shard_map/ppermute | solution.py:385

commit v3 on v2

v3 whole, which is shorter than its diff:
```python
import functools
import math

import jax
import jax.numpy as jnp
import ml_dtypes
import numpy as np
from jax import lax
from jax.experimental import pallas as pl
from jax.experimental.pallas import tpu as pltpu
from jax.sharding import PartitionSpec as P

L = 1920
F = 768
K0 = 8
HALF = 32
LAG_COUNT = 512
BLOCK = 128
SOURCES = 16
TPS = 3
REACH = 2
SEG_DEV = 4
SEGS = 16
NB = 32
TCAP = 6
TM = 4
SLAB = L // NB
ROWS = 64
PART = BLOCK // TM
SRC_PART = SOURCES // TM
MIB = 1 << 20
LANES = 128
GROUP = 8
STEP = 128
HALF_PART = PART // 2

BF16 = jnp.bfloat16
F32 = jnp.float32


def forward_table():
    n = np.arange(L)[None, :]
    q = K0 + np.arange(F)[:, None]
    angles = (n * q % L) * (2.0 * np.pi / L)
    window = 0.5 - 0.5 * np.cos(np.arange(L) * (2.0 * np.pi / L))
    table = np.concatenate([np.cos(angles), -np.sin(angles)], axis=0) * window[None, :]
    padded = np.zeros((2 * F, NB, ROWS))
    padded[:, :, :SLAB] = table.reshape(2 * F, NB, SLAB)
    return padded.reshape(2 * F, NB * ROWS).astype(ml_dtypes.bfloat16)


def smoothing():
    k = np.arange(F)
    inside = (np.abs(k[:, None] - k[None, :]) <= HALF).astype(np.float64)
    inverse_count = 1.0 / inside.sum(axis=1, keepdims=True)
    return inside.astype(ml_dtypes.bfloat16), inverse_count.astype(np.float32)


def inverse_table():
    q = K0 + np.arange(F)[None, :]
    lag = np.arange(LAG_COUNT)[:, None] - LAG_COUNT // 2
    angles = (q * lag % L) * (2.0 * np.pi / L)
    table = np.concatenate([np.cos(angles), -np.sin(angles)], axis=1) / math.sqrt(SEGS * F)
    return table.astype(ml_dtypes.bfloat16)


PAIR = 2
PARTS = TM // PAIR


def source_lanes():
    pick = np.zeros((TM, 2, BLOCK, LANES))
    for i in range(TM):
        for half in range(2):
            for s in range(SEG_DEV):
                for v in range(SRC_PART):
                    part, at = divmod(v * (BLOCK // SOURCES), HALF_PART)
                    lane = half * SRC_PART * SEGS + v * SEGS + i * SEG_DEV + s
                    pick[i, half, (part * SEG_DEV + s) * HALF_PART + at, lane] = 1.0
    return pick.astype(ml_dtypes.bfloat16)


def spread_lanes():
    spread = np.zeros((SRC_PART, LANES, 2 * LANES))
    for v in range(SRC_PART):
        for half in range(2):
            for s in range(SEGS):
                lane = half * LANES + s * GROUP
                spread[v, half * SRC_PART * SEGS + v * SEGS + s, lane : lane + GROUP] = 1.0
    return spread.astype(ml_dtypes.bfloat16)


def tile_lanes():
    count = PAIR * SEG_DEV
    order = np.zeros((TPS * LANES, count * LANES))
    for t in range(TPS):
        for s in range(count):
            for c in range(HALF_PART):
                for twin in range(2):
                    lane = s * LANES + twin * (LANES // 2) + t * HALF_PART + c
                    order[t * LANES + s * HALF_PART + c, lane] = 1.0
    return order.astype(ml_dtypes.bfloat16)


def interleave():
    order = np.zeros((SEG_DEV * BLOCK, SEG_DEV * BLOCK))
    for s in range(SEG_DEV):
        for j in range(TM):
            for c in range(PART):
                part, at = divmod(c, HALF_PART)
                lane = j * BLOCK + (part * SEG_DEV + s) * HALF_PART + at
                order[s * BLOCK + j * PART + c, lane] = 1.0
    return order.astype(ml_dtypes.bfloat16)


PACK_BLOCKS = 8


def pack_kernel(own, records, quality, order, out):
    step = pl.program_id(0)
    marks = jnp.concatenate([quality[s : s + 1, :] for s in range(SEG_DEV)], axis=1)
    marks = jnp.broadcast_to(marks.astype(F32), (16, SEG_DEV * BLOCK)).astype(BF16)
    marks = jnp.dot(marks, order[...], preferred_element_type=F32)[:1]
    row = lax.broadcasted_iota(jnp.int32, (ROWS, SEG_DEV * BLOCK), 0)
    x = jnp.concatenate(
        [
            jnp.concatenate(
                [records[s, :, k * BLOCK : (k + 1) * BLOCK] for s in range(SEG_DEV)], axis=1
            )
            for k in range(PACK_BLOCKS)
        ],
        axis=0,
    )
    y = jnp.dot(x, order[...], preferred_element_type=F32)
    for k in range(PACK_BLOCKS):
        mine = step * PACK_BLOCKS + k == own[0]
        extra = jnp.where((row == SLAB) & mine, marks, 0.0)
        block = jnp.where(row < SLAB, y[k * ROWS : (k + 1) * ROWS], extra).astype(BF16)
        for j in range(TM):
            out[k * TM + j] = block[:, j * BLOCK : (j + 1) * BLOCK]


def pack(own, records, quality):
    return pl.pallas_call(
        pack_kernel,
        out_shape=jax.ShapeDtypeStruct((NB * TM, ROWS, BLOCK), BF16),
        grid_spec=pltpu.PrefetchScalarGridSpec(
            num_scalar_prefetch=1,
            grid=(NB // PACK_BLOCKS,),
            in_specs=[
                pl.BlockSpec((SEG_DEV, ROWS, PACK_BLOCKS * BLOCK), lambda g, own: (0, 0, g)),
                pl.BlockSpec((SEG_DEV, BLOCK), lambda g, own: (0, 0)),
                pl.BlockSpec(memory_space=pltpu.VMEM),
            ],
            out_specs=pl.BlockSpec((PACK_BLOCKS * TM, ROWS, BLOCK), lambda g, own: (g, 0, 0)),
        ),
        compiler_params=pltpu.CompilerParams(vmem_limit_bytes=20 * MIB),
        name="pack",
    )(own, records, quality, interleave())


def whiten_kernel(own, slabs, table, inside, inverse_count, pick, low, high, sources, total):
    step = pl.program_id(0)
    lanes = []
    for i in range(PAIR):
        marks = slabs[pl.ds(own[0], 1), i, pl.ds(48, 16), :][0, SLAB - 48 : SLAB - 47, :]
        lanes.append(slabs[:, i].reshape(NB * ROWS, BLOCK) * marks)
    x = jnp.concatenate(lanes, axis=1)
    spectrum = jnp.dot(table[...], x, preferred_element_type=F32)
    re = spectrum[:F]
    im = spectrum[F:]
    magnitude = jnp.sqrt(re * re + im * im).astype(BF16)
    level = jnp.dot(inside[...], magnitude, preferred_element_type=F32) * inverse_count[...]
    inverse_level = 1.0 / (level + 1e-6)

    @pl.when(step == 0)
    def _():
        total[...] = jnp.zeros_like(total)

    first = lax.broadcasted_iota(jnp.int32, (F, LANES), 1) < LANES // 2
    for half, part in ((0, re), (1, im)):
        value = part * inverse_level
        pair = [value[:, i * BLOCK : (i + 1) * BLOCK] for i in range(PAIR)]
        turned = [pltpu.roll(one, LANES // 2, 1) for one in pair]
        low[0, half] = jnp.where(first, pair[0], turned[1]).astype(BF16)
        high[0, half] = jnp.where(first, turned[0], pair[1]).astype(BF16)
        for i in range(PAIR):
            total[...] += jnp.dot(
                pair[i].astype(BF16), pick[step * PAIR + i, half], preferred_element_type=F32
            )
    sources[...] = total[...].astype(BF16)


def whiten(own, slabs):
    inside, inverse_count = smoothing()
    shape = jax.ShapeDtypeStruct((TM // PAIR, 2, F, LANES), BF16)
    spec = pl.BlockSpec((1, 2, F, LANES), lambda i, own: (i, 0, 0, 0))
    return pl.pallas_call(
        whiten_kernel,
        out_shape=(shape, shape, jax.ShapeDtypeStruct((F, LANES), BF16)),
        grid_spec=pltpu.PrefetchScalarGridSpec(
            num_scalar_prefetch=1,
            grid=(TM // PAIR,),
            in_specs=[pl.BlockSpec((NB, PAIR, ROWS, BLOCK), lambda i, own: (0, i, 0, 0))]
            + [pl.BlockSpec(memory_space=pltpu.VMEM)] * 4,
            out_specs=(spec, spec, pl.BlockSpec((F, LANES), lambda i, own: (0, 0))),
            scratch_shapes=[pltpu.VMEM((F, LANES), F32)],
        ),
        compiler_params=pltpu.CompilerParams(vmem_limit_bytes=20 * MIB),
        name="whiten",
    )(own, slabs.reshape(NB, TM, ROWS, BLOCK), forward_table(), inside, inverse_count, source_lanes())


def choose_kernel(chan, below, above, out, sem):
    odd = lax.rem(chan[0], 2)

    @pl.when(odd == 1)
    def _():
        pltpu.make_async_copy(below, out, sem).start()

    @pl.when(odd == 0)
    def _():
        pltpu.make_async_copy(above, out, sem).start()

    pltpu.make_async_copy(below, out, sem).wait()


def choose(chan, below, above):
    return pl.pallas_call(
        choose_kernel,
        out_shape=jax.ShapeDtypeStruct(below.shape, below.dtype),
        in_specs=[pl.BlockSpec(memory_space=pltpu.SMEM)]
        + [pl.BlockSpec(memory_space=pl.ANY)] * 2,
        out_specs=pl.BlockSpec(memory_space=pl.ANY),
        scratch_shapes=[pltpu.SemaphoreType.DMA],
        compiler_params=pltpu.CompilerParams(vmem_limit_bytes=MIB),
        cost_estimate=pl.CostEstimate(flops=1, bytes_accessed=1, transcendentals=0),
        name="choose",
    )(chan, below, above)


def diagonal_kernel(s0, s1, s2, s3, spread, out):
    rows = STEP
    groups = rows // GROUP
    place = pl.ds(pl.program_id(0) * groups, groups)
    row = lax.broadcasted_iota(jnp.int32, (rows, 2 * LANES), 0)
    lane = lax.broadcasted_iota(jnp.int32, (rows, 2 * LANES), 1)
    keep = jnp.bitwise_and(row, GROUP - 1) == jnp.bitwise_and(lane, GROUP - 1)
    for rel, ref in enumerate((s0, s1, s2, s3)):
        for pair in range(SRC_PART // 2):
            same, turned = [], []
            for v in (2 * pair, 2 * pair + 1):
                wide = jnp.dot(ref[...], spread[v], preferred_element_type=F32)
                wide = jnp.where(keep, wide, 0.0)
                swap = jnp.concatenate([-wide[:, LANES:], wide[:, :LANES]], axis=1)
                same.append(wide.reshape(groups, GROUP, 2 * LANES))
                turned.append(swap.reshape(groups, GROUP, 2 * LANES))
            at = (rel * SRC_PART + 2 * pair) * GROUP
            out[place, at : at + 2 * GROUP, :] = jnp.concatenate(same, axis=1).astype(BF16)
            at += SOURCES * GROUP
            out[place, at : at + 2 * GROUP, :] = jnp.concatenate(turned, axis=1).astype(BF16)


def diagonal(sources):
    wide = 2 * SOURCES * GROUP
    return pl.pallas_call(
        diagonal_kernel,
        out_shape=jax.ShapeDtypeStruct((F // GROUP, wide, 2 * LANES), BF16),
        grid=(F // STEP,),
        in_specs=[pl.BlockSpec((STEP, LANES), lambda g: (g, 0))] * TM
        + [pl.BlockSpec(memory_space=pltpu.VMEM)],
        out_specs=pl.BlockSpec(memory_space=pltpu.VMEM),
        compiler_params=pltpu.CompilerParams(vmem_limit_bytes=20 * MIB),
        cost_estimate=pl.CostEstimate(flops=1, bytes_accessed=1, transcendentals=0),
        name="diagonal",
    )(*sources, spread_lanes())


RECEIVERS = 2 * REACH + 1


def chosen(chan, tiles, t):
    offset = lax.rem(tiles[1, chan * TPS + t] - chan + REACH + NB, NB)
    mate = jnp.where(lax.rem(chan, 2) == 1, 1, 3)
    near = jnp.where(offset == REACH, 0, jnp.where(offset == mate, 3, 4))
    return jnp.where(offset == 0, 1, jnp.where(offset == 2 * REACH, 2, near))


def cross_kernel(chan, tiles, diag, order, *refs):
    receivers, (out, held, wide, sem) = refs[:RECEIVERS], refs[RECEIVERS:]
    step = pl.program_id(0)
    steps = F // STEP

    def copy(ref, t, k):
        rows = pl.ds(k * STEP, STEP)
        return pltpu.make_async_copy(ref.at[:, :, rows, :], held.at[k, t], sem.at[k, t])

    @pl.when(step == 0)
    def _():
        picks = [chosen(chan[0], tiles, t) for t in range(TPS)]
        for k in range(steps):
            for t in range(TPS):
                for index, ref in enumerate(receivers):

                    @pl.when(picks[t] == index)
                    def _():
                        copy(ref, t, k).start()

    for t in range(TPS):
        copy(receivers[0], t, step).wait()
    x = jnp.concatenate(
        [held[step, t].reshape(TM // PAIR * 2 * STEP, LANES) for t in range(TPS)], axis=1
    )
    y = jnp.dot(x, order[...], preferred_element_type=F32)
    count = PAIR * SEG_DEV
    for i in range(TM // PAIR):
        for half in range(2):
            at = (i * 2 + half) * STEP
            for s in range(count):
                wide[half * SEGS + i * count + s] = y[at : at + STEP, s * LANES : (s + 1) * LANES]
    first = lax.broadcasted_iota(jnp.int32, (1, GROUP, LANES), 2) < LANES // 2

    def group(pair, carry):
        outs = []
        for g in range(2):
            at = pl.multiple_of((pair * 2 + g) * GROUP, GROUP)
            b = wide[:, pl.ds(at, GROUP), :].reshape(2 * SEGS * GROUP, LANES).astype(BF16)
            o = jnp.dot(diag[step * (STEP // GROUP) + pair * 2 + g], b, preferred_element_type=F32)
            o = o.reshape(SOURCES, 2, GROUP, LANES)
            outs.append(jnp.where(first, o[:, 0], o[:, 1]))
        both = jnp.concatenate(outs, axis=1).astype(BF16)
        rows = pl.ds(pl.multiple_of(step * STEP + pair * 2 * GROUP, 2 * GROUP), 2 * GROUP)
        out[:, 0, rows, :] = both[: SOURCES // 2]
        out[:, 1, rows, :] = both[SOURCES // 2 :]
        return carry

    lax.fori_loop(0, STEP // (2 * GROUP), group, 0, unroll=UNROLL)


UNROLL = 8


def cross(chan, tiles, diag, receivers):
    return pl.pallas_call(
        cross_kernel,
        out_shape=jax.ShapeDtypeStruct((SOURCES // 2, 2, F, LANES), BF16),
        grid_spec=pltpu.PrefetchScalarGridSpec(
            num_scalar_prefetch=2,
            grid=(F // STEP,),
            in_specs=[pl.BlockSpec(memory_space=pltpu.VMEM)] * 2
            + [pl.BlockSpec(memory_space=pl.ANY)] * RECEIVERS,
            out_specs=pl.BlockSpec(memory_space=pltpu.VMEM),
            scratch_shapes=[
                pltpu.VMEM((F // STEP, TPS, TM // PAIR, 2, STEP, LANES), BF16),
                pltpu.VMEM((2 * SEGS, STEP, LANES), F32),
                pltpu.SemaphoreType.DMA((F // STEP, TPS)),
            ],
        ),
        compiler_params=pltpu.CompilerParams(vmem_limit_bytes=20 * MIB),
        cost_estimate=pl.CostEstimate(flops=1, bytes_accessed=1, transcendentals=0),
        name="cross",
    )(chan, tiles, diag, tile_lanes(), *receivers)


def stack_kernel(rel, spectra, inverse, out):
    first = rel * SRC_PART // 2
    x = jnp.concatenate(
        [spectra[first + pair].reshape(2 * F, LANES) for pair in range(SRC_PART // 2)], axis=1
    )
    y = jnp.dot(inverse[...], x, preferred_element_type=F32)
    for pair in range(SRC_PART // 2):
        value = y[:, pair * LANES : (pair + 1) * LANES].T.astype(BF16)
        for v in range(2):
            for t in range(TPS):
                at = (t * SRC_PART + 2 * pair + v) * HALF_PART
                row = v * (LANES // 2) + t * HALF_PART
                out[at : at + HALF_PART, :] = value[row : row + HALF_PART, :]


def stack(spectra, rel, inverse):
    rows = TPS * SRC_PART * HALF_PART
    return pl.pallas_call(
        functools.partial(stack_kernel, rel),
        out_shape=jax.ShapeDtypeStruct((rows, LAG_COUNT), BF16),
        in_specs=[pl.BlockSpec(memory_space=pltpu.VMEM)] * 2,
        out_specs=pl.BlockSpec(memory_space=pltpu.VMEM),
        compiler_params=pltpu.CompilerParams(vmem_limit_bytes=10 * MIB),
        cost_estimate=pl.CostEstimate(flops=1, bytes_accessed=1, transcendentals=0),
        name="stack",
    )(spectra, inverse)


def arrange(time, pieces, t):
    rows = SRC_PART * HALF_PART
    for index, ref in enumerate(pieces):
        half, rel = divmod(index, TM)
        value = ref[t * rows : (t + 1) * rows, :].astype(F32)
        at = lax.rem(time + TM - rel, TM) * PART + half * HALF_PART
        yield pl.multiple_of(at, HALF_PART), value.reshape(SRC_PART, HALF_PART, LAG_COUNT)


def home_kernel(owners, chan, time, *refs):
    pieces, out = refs[:-1], refs[-1]
    slot = pl.program_id(0)
    out[...] = jnp.zeros_like(out)
    for t in range(TPS):

        @pl.when(owners[chan[0] * TPS + t] == chan[0] * TCAP + slot)
        def _():
            for at, value in arrange(time[0], pieces, t):
                out[0, :, pl.ds(at, HALF_PART), :] = value


def home(owners, chan, time, pieces):
    return pl.pallas_call(
        home_kernel,
        out_shape=jax.ShapeDtypeStruct((TCAP, SRC_PART, BLOCK, LAG_COUNT), F32),
        grid_spec=pltpu.PrefetchScalarGridSpec(
            num_scalar_prefetch=3,
            grid=(TCAP,),
            in_specs=[pl.BlockSpec(memory_space=pltpu.VMEM) for _ in pieces],
            out_specs=pl.BlockSpec((1, SRC_PART, BLOCK, LAG_COUNT), lambda s, *_: (s, 0, 0, 0)),
        ),
        compiler_params=pltpu.CompilerParams(vmem_limit_bytes=10 * MIB),
        cost_estimate=pl.CostEstimate(flops=1, bytes_accessed=1, transcendentals=0),
        name="home",
    )(owners, chan, time, *pieces)


def moved_kernel(owners, chan, time, *refs):
    pieces, (_, out, held, sem) = refs[:-4], refs[-4:]
    source = lax.rem(chan[0] + NB - 1, NB)
    copies = []
    for t in range(TPS):
        slot = owners[source * TPS + t] - chan[0] * TCAP
        mine = (slot >= 0) & (slot < TCAP)
        copy = pltpu.make_async_copy(held.at[t], out.at[jnp.clip(slot, 0, TCAP - 1)], sem.at[t])
        copies.append((mine, copy))

        @pl.when(mine)
        def _():
            for at, value in arrange(time[0], pieces, t):
                held[t, :, pl.ds(at, HALF_PART), :] = value
            copy.start()

    for mine, copy in copies:

        @pl.when(mine)
        def _():
            copy.wait()


def moved(owners, chan, time, pieces, result):
    return pl.pallas_call(
        moved_kernel,
        out_shape=jax.ShapeDtypeStruct(result.shape, result.dtype),
        in_specs=[pl.BlockSpec(memory_space=pltpu.SMEM)] * 3
        + [pl.BlockSpec(memory_space=pltpu.VMEM) for _ in pieces]
        + [pl.BlockSpec(memory_space=pl.ANY)],
        out_specs=pl.BlockSpec(memory_space=pl.ANY),
        scratch_shapes=[
            pltpu.VMEM((TPS, SRC_PART, BLOCK, LAG_COUNT), F32),
            pltpu.SemaphoreType.DMA((TPS,)),
        ],
        input_output_aliases={3 + len(pieces): 0},
        compiler_params=pltpu.CompilerParams(vmem_limit_bytes=12 * MIB),
        cost_estimate=pl.CostEstimate(flops=1, bytes_accessed=1, transcendentals=0),
        name="moved",
    )(owners, chan, time, *pieces, result)


def shifted(value, axis, distance):
    count = lax.axis_size(axis)
    return lax.ppermute(value, axis, [(i, (i + distance) % count) for i in range(count)])


def per_device(records, quality, tile_list, tile_slot_owner):
    chan = lax.axis_index("chan").astype(jnp.int32).reshape(1)
    time = lax.axis_index("tm").astype(jnp.int32).reshape(1)
    tiles = tile_list.T
    swap = [(i, i ^ 1) for i in range(NB)]

    slabs = pack(chan, records, quality)
    slabs = lax.all_to_all(slabs, ("chan", "tm"), split_axis=0, concat_axis=0, tiled=True)
    low, high, sources = whiten(chan, slabs)
    sources = [sources] + [shifted(sources, "tm", -rel) for rel in range(1, TM)]
    diag = diagonal(sources)

    def halo(white):
        mate = lax.ppermute(white, "chan", swap)
        return [white, shifted(white, "chan", 2), shifted(white, "chan", -2), mate]

    def complete(blocks):
        other = choose(chan, blocks[1], blocks[2])
        return blocks + [lax.ppermute(other, "chan", swap)]

    inverse = inverse_table()
    order = (2, 0, 1, 3)
    low = halo(low)
    high, low[3] = lax.optimization_barrier((high, low[3]))
    high = halo(high)
    low, diag = lax.optimization_barrier((low, diag))
    spectra = cross(chan, tiles, diag, complete(low))
    parts = [stack(spectra, rel, inverse) for rel in range(TM)]
    stay_low = [shifted(part, "tm", rel) if rel else part for rel, part in enumerate(parts)]
    high, stay_low = lax.optimization_barrier((high, stay_low))
    high = complete(high)
    move_low = [shifted(part, "chan", 1) for part in stay_low]
    spectra = cross(chan, tiles, diag, high)
    stay_high, move_high = [None] * TM, [None] * TM
    for rel in order:
        part = stack(spectra, rel, inverse)
        if rel == 0:
            part, move_low = lax.optimization_barrier((part, move_low))
        stay_high[rel] = shifted(part, "tm", rel) if rel else part
        move_high[rel] = shifted(stay_high[rel], "chan", 1)
    result = home(tile_slot_owner, chan, time, stay_low + stay_high)
    return moved(tile_slot_owner, chan, time, move_low + move_high, result)


def solution(mesh):
    placed = (P("tm", "chan", None), P("tm", "chan"), P(), P())
    return jax.shard_map(
        per_device,
        mesh=mesh,
        in_specs=placed,
        out_specs=P("chan", "tm", None, None),
        check_vma=False,
    )
```

time: 166 us -> 151 us (0.910)
  waiting for transfers between devices: 58.3 us -> 36.4 us
  starting transfers between devices: 16.5 us -> 24.8 us
  local copies, waits for them, and re-layouts: 11 us -> 2.85 us
  Pallas kernels: 38 us -> 44.6 us
    ppermute x12 -> x21, waiting for transfers between devices: 56.4 us -> 34.7 us  [shifted(): lax.ppermute(value, axis, [(i, (i + distance) % count) for i in range(cou...]
    ppermute x12 -> x21, starting transfers between devices: 9.88 us -> 24.3 us  [shifted(): lax.ppermute(value, axis, [(i, (i + distance) % count) for i in range(cou...]
    unnamed x35 -> x25, local copies, waits for them, and re-layouts: 10.8 us -> 2.85 us
    pallas_call x7 -> x15, Pallas kernels: 33.2 us -> 39.8 us  [the longest x2 20.6 us: cross(): pl.pallas_call(cross_kernel, out_shape=jax.ShapeDtypeStruct((SOURCES // 2...]
    ppermute x3 -> x4, starting transfers between devices: 6.63 us -> 0.52 us  [the longest x2 0.35 us: halo(): mate = lax.ppermute(white, 'chan', swap)]
  transfers between devices with their start and end apart: 15 -> 25, of which waited for: 10 -> 12; matrix products, arithmetic and copies ran while one was open for 0% -> 0% of each run, Pallas kernels for 4% -> 22%
where the time goes in v3:
time: 151 us; the launch traced here: 150 us
  Pallas kernels  44.6 us (30%)
  blocking collectives  41.1 us (27%)
  waiting for transfers between devices  36.4 us (24%)
  starting transfers between devices  24.8 us (16%)
  local copies, waits for them, and re-layouts  2.85 us (2%)
    all_to_all x1, blocking collectives, per_device(): lax.all_to_all(slabs, ('chan', 'tm'), split_axis=0, concat_axis=0, tiled=...  41.1 us
    ppermute x21, waiting for transfers between devices, shifted(): lax.ppermute(value, axis, [(i, (i + distance) % count) for i in range(cou...  34.7 us
    ppermute x21, starting transfers between devices, shifted(): lax.ppermute(value, axis, [(i, (i + distance) % count) for i in range(cou...  24.3 us
    pallas_call x2, Pallas kernels, cross(): pl.pallas_call(cross_kernel, out_shape=jax.ShapeDtypeStruct((SOURCES // 2...  20.6 us
    pallas_call x1, Pallas kernels, whiten(): pl.pallas_call(whiten_kernel, out_shape=(shape, shape, jax.ShapeDtypeStru...  7.38 us
    pallas_call x8, Pallas kernels, stack(): pl.pallas_call(functools.partial(stack_kernel, rel), out_shape=jax.ShapeD...  5.41 us
    pallas_call x1, Pallas kernels, home(): pl.pallas_call(home_kernel, out_shape=jax.ShapeDtypeStruct((TCAP, SRC_PAR...  4.26 us
  transfers between devices with their start and end apart: 25, of which 12 were waited for; matrix products, arithmetic and copies ran while one was open for 0% of the time, Pallas kernels for 22%

profile of v3, /device:TPU:0, one launch (start us, length us, event | category | flops | bytes accessed | tf_op | source)
XLA Modules:
  0.0 150.3 jit_solution(8804612196285452443)
XLA Ops:
  0.0 2.8 %copy.15.records = bf16[4,60,4096]{2,1,0:T(8,128)(2,1)S(1)} copy(bf16[4,60,4096]{2,0,1:T(4,128)(2,1)} %param.13) | data formatting | bytes 3932160 | tf_op args[0]
  2.8 2.2 %pack.1 = bf16[128,64,128]{2,1,0:T(8,128)(2,1)S(1)} custom-call(s32[1]{0:T(128)} %bitcast.own.chan, bf16[4,60,4096]{2,1,0:T(8,128)(2,1)S(1)} %copy.15.records, s32[4,128]{1,0:T(4,128)S(1)} %copy-done.8, bf16[512,512]{1,0:T(8,128)(2,1)S(1)} %copy-done.3), custom_call_target="tpu_custom_call" | custom-call | tf_op jit(solution)/shard_map/pack/pallas_call | solution.py:144
  5.1 41.1 %all_to_all.5 = bf16[128,64,128]{2,1,0:T(8,128)(2,1)S(1)} all-to-all(bf16[128,64,128]{2,1,0:T(8,128)(2,1)S(1)} %pack.1), channel_id=1, replica_groups=mesh['chan'=32,'tm'=4] {'chan','tm'}, dimensions={0} | all-to-all | bytes 4194304 | tf_op jit(solution)/shard_map/all_to_all | solution.py:484
  46.3 7.4 %whiten.1 = (bf16[2,2,768,128]{3,2,1,0:T(8,128)(2,1)S(1)}, bf16[2,2,768,128]{3,2,1,0:T(8,128)(2,1)S(1)}, bf16[768,128]{1,0:T(8,128)(2,1)S(1)}) custom-call(s32[1]{0:T(128)} %bitcast.own.chan, bf16[32,4,64,128]{3,2,1,0:T(8,128)(2,1)S(1)} %bitcast.4, bf16[1536,2048]{1,0:T(8,128)(2,1)S(1)} %bitcast.6, bf16[768,768]{1,0:T(8,128)(2,1)S(1)} %copy-done.2, ...), custom_call_target="tpu_custom_call" | custom-call | tf_op jit(solution)/shard_map/whiten/pallas_call | solution.py:198
  53.7 0.3 collective-permute-start.2
  54.0 0.6 collective-permute-start
  54.7 4.7 %collective-permute-start.1 = (bf16[2,2,768,128]{3,2,1,0:T(8,128)(2,1)S(1)}, bf16[2,2,768,128]{3,2,1,0:T(8,128)(2,1)S(1)}, u32[]{:S(2)}, u32[]{:S(2)}) collective-permute-start(bf16[2,2,768,128]{3,2,1,0:T(8,128)(2,1)S(1)} %get-tuple-element.34.refs_0_), channel_id=1, source_target_pairs={{0,120},{4,124},{8,0},{12,4},{16,8},{20,12},{24,16},{28,20},{32,24... | collective-permute-start | bytes 2359304 | tf_op jit(solution)/shard_map/ppermute | solution.py:474
  59.4 1.4 collective-permute-start.3
  60.8 1.2 collective-permute-start.4
  62.0 5.2 %collective-permute-done.3.s1 = bf16[768,128]{1,0:T(8,128)(2,1)S(1)} collective-permute-done((bf16[768,128]{1,0:T(8,128)(2,1)S(1)}, bf16[768,128]{1,0:T(8,128)(2,1)S(1)}, u32[]{:S(2)}, u32[]{:S(2)}) %collective-permute-start.3) | collective-permute-done | bytes 196640 | tf_op jit(solution)/shard_map/ppermute | solution.py:474
  67.2 1.5 %collective-permute-done.4.s2 = bf16[768,128]{1,0:T(8,128)(2,1)S(1)} collective-permute-done((bf16[768,128]{1,0:T(8,128)(2,1)S(1)}, bf16[768,128]{1,0:T(8,128)(2,1)S(1)}, u32[]{:S(2)}, u32[]{:S(2)}) %collective-permute-start.4) | collective-permute-done | bytes 196640 | tf_op jit(solution)/shard_map/ppermute | solution.py:474
  68.7 7.8 %collective-permute-done.5.s3 = bf16[768,128]{1,0:T(8,128)(2,1)S(1)} collective-permute-done((bf16[768,128]{1,0:T(8,128)(2,1)S(1)}, bf16[768,128]{1,0:T(8,128)(2,1)S(1)}, u32[]{:S(2)}, u32[]{:S(2)}) %collective-permute-start.5) | collective-permute-done | bytes 196640 | tf_op jit(solution)/shard_map/ppermute | solution.py:474
  76.5 2.6 %diagonal.1.diag = bf16[96,256,256]{2,1,0:T(8,128)(2,1)S(1)} custom-call(bf16[768,128]{1,0:T(8,128)(2,1)S(1)} %get-tuple-element.31.s0, bf16[768,128]{1,0:T(8,128)(2,1)S(1)} %collective-permute-done.3.s1, bf16[768,128]{1,0:T(8,128)(2,1)S(1)} %collective-permute-done.4.s2, bf16[768,128]{1,0:T(8,128)(2,1)S(1)} %collective-permute-done.5.s3, ...), custom_call_target="tpu_custom_call" | custom-call | flops 1 | bytes 1 | tf_op jit(solution)/shard_map/diagonal/pallas_call | solution.py:266
  79.2 0.1 choose.2
  79.3 0.1 collective-permute-start.9
  79.3 0.1 collective-permute-start.6
  79.4 5.3 %collective-permute-start.7 = (bf16[2,2,768,128]{3,2,1,0:T(8,128)(2,1)S(1)}, bf16[2,2,768,128]{3,2,1,0:T(8,128)(2,1)S(1)}, u32[]{:S(2)}, u32[]{:S(2)}) collective-permute-start(bf16[2,2,768,128]{3,2,1,0:T(8,128)(2,1)S(1)} %get-tuple-element.38.refs_0_), channel_id=1, source_target_pairs={{0,120},{4,124},{8,0},{12,4},{16,8},{20,12},{24,16},{28,20},{32,24... | collective-permute-start | bytes 2359304 | tf_op jit(solution)/shard_map/ppermute | solution.py:474
  84.8 10.3 %cross.2.spectra = bf16[8,2,768,128]{3,2,1,0:T(8,128)(2,1)S(1)} custom-call(s32[1]{0:T(128)} %bitcast.own.chan, s32[2,96]{1,0:T(2,128)S(1)} %bitcast.7, bf16[96,256,256]{2,1,0:T(8,128)(2,1)S(1)} %diagonal.1.diag, bf16[384,1024]{1,0:T(8,128)(2,1)S(1)} %copy-done.1, bf16[2,2,768,128]{3,2,1,0:T(8,128)(2,1)S(1)} %get-tuple-element.34.refs_0_, ...), custom_call_target="tpu_custom_call" | custom-call | flops 1 | bytes 1 | tf_op jit(solution)/shard_map/cross/pallas_call | solution.py:344
  95.1 0.7 stack.9
  95.8 0.7 stack.10
  96.5 0.3 collective-permute-start.10
  96.8 3.5 %collective-permute-start.11 = (bf16[192,512]{1,0:T(8,128)(2,1)S(1)}, bf16[192,512]{1,0:T(8,128)(2,1)S(1)}, u32[]{:S(2)}, u32[]{:S(2)}) collective-permute-start(bf16[192,512]{1,0:T(8,128)(2,1)S(1)} %stack.10), channel_id=1, source_target_pairs={{0,2},{1,3},{2,0},{3,1},{4,6},{5,7},{6,4},{7,5},{8,10},{9,11},{10,... | collective-permute-start | bytes 589832 | tf_op jit(solution)/shard_map/ppermute | solution.py:474
  100.2 0.7 stack.11
  100.9 1.7 %collective-permute-done.6.below.refs_1_ = bf16[2,2,768,128]{3,2,1,0:T(8,128)(2,1)S(1)} collective-permute-done((bf16[2,2,768,128]{3,2,1,0:T(8,128)(2,1)S(1)}, bf16[2,2,768,128]{3,2,1,0:T(8,128)(2,1)S(1)}, u32[]{:S(2)}, u32[]{:S(2)}) %collective-permute-start.6) | collective-permute-done | bytes 786464 | tf_op jit(solution)/shard_map/ppermute | solution.py:474
  102.6 2.0 %collective-permute-start.12 = (bf16[192,512]{1,0:T(8,128)(2,1)S(1)}, bf16[192,512]{1,0:T(8,128)(2,1)S(1)}, u32[]{:S(2)}, u32[]{:S(2)}) collective-permute-start(bf16[192,512]{1,0:T(8,128)(2,1)S(1)} %stack.11), channel_id=1, source_target_pairs={{0,3},{1,0},{2,1},{3,2},{4,7},{5,4},{6,5},{7,6},{8,11},{9,8},{10,9... | collective-permute-start | bytes 589832 | tf_op jit(solution)/shard_map/ppermute | solution.py:474
  104.7 0.7 stack.8.refs_0_
  105.4 4.4 %collective-permute-done.11.refs_2_ = bf16[192,512]{1,0:T(8,128)(2,1)S(1)} collective-permute-done((bf16[192,512]{1,0:T(8,128)(2,1)S(1)}, bf16[192,512]{1,0:T(8,128)(2,1)S(1)}, u32[]{:S(2)}, u32[]{:S(2)}) %collective-permute-start.11) | collective-permute-done | bytes 196640 | tf_op jit(solution)/shard_map/ppermute | solution.py:474
  109.7 0.3 collective-permute-done.12.refs_3_
  110.0 0.1 choose.3
  110.1 0.1 collective-permute-start.13
  110.2 0.5 collective-permute-start.14
  110.7 0.1 collective-permute-start.17
  110.8 1.7 %collective-permute-done.13.refs_4_ = bf16[2,2,768,128]{3,2,1,0:T(8,128)(2,1)S(1)} collective-permute-done((bf16[2,2,768,128]{3,2,1,0:T(8,128)(2,1)S(1)}, bf16[2,2,768,128]{3,2,1,0:T(8,128)(2,1)S(1)}, u32[]{:S(2)}, u32[]{:S(2)}) %collective-permute-start.13) | collective-permute-done | bytes 786464 | tf_op jit(solution)/shard_map/ppermute | solution.py:495
  112.5 10.3 %cross.3.spectra = bf16[8,2,768,128]{3,2,1,0:T(8,128)(2,1)S(1)} custom-call(s32[1]{0:T(128)} %bitcast.own.chan, s32[2,96]{1,0:T(2,128)S(1)} %bitcast.8, bf16[96,256,256]{2,1,0:T(8,128)(2,1)S(1)} %diagonal.1.diag, bf16[384,1024]{1,0:T(8,128)(2,1)S(1)} %copy-done.1, bf16[2,2,768,128]{3,2,1,0:T(8,128)(2,1)S(1)} %get-tuple-element.38.refs_0_, ...), custom_call_target="tpu_custom_call" | custom-call | flops 1 | bytes 1 | tf_op jit(solution)/shard_map/cross/pallas_call | solution.py:344
  122.8 0.7 stack.13
  123.5 0.7 stack.14
  124.2 0.5 collective-permute-start.19
  124.6 0.7 stack.15
  125.3 4.0 %collective-permute-start.21 = (bf16[192,512]{1,0:T(8,128)(2,1)S(1)}, bf16[192,512]{1,0:T(8,128)(2,1)S(1)}, u32[]{:S(2)}, u32[]{:S(2)}) collective-permute-start(bf16[192,512]{1,0:T(8,128)(2,1)S(1)} %stack.14), channel_id=1, source_target_pairs={{0,2},{1,3},{2,0},{3,1},{4,6},{5,7},{6,4},{7,5},{8,10},{9,11},{10,... | collective-permute-start | bytes 589832 | tf_op jit(solution)/shard_map/ppermute | solution.py:474
  129.3 0.7 stack.12.refs_4_
  130.0 0.1 collective-permute-start.18
  130.1 2.3 %collective-permute-done.19.refs_5_ = bf16[192,512]{1,0:T(8,128)(2,1)S(1)} collective-permute-done((bf16[192,512]{1,0:T(8,128)(2,1)S(1)}, bf16[192,512]{1,0:T(8,128)(2,1)S(1)}, u32[]{:S(2)}, u32[]{:S(2)}) %collective-permute-start.19) | collective-permute-done | bytes 196640 | tf_op jit(solution)/shard_map/ppermute | solution.py:474
  132.4 5.3 %collective-permute-done.21.refs_6_ = bf16[192,512]{1,0:T(8,128)(2,1)S(1)} collective-permute-done((bf16[192,512]{1,0:T(8,128)(2,1)S(1)}, bf16[192,512]{1,0:T(8,128)(2,1)S(1)}, u32[]{:S(2)}, u32[]{:S(2)}) %collective-permute-start.21) | collective-permute-done | bytes 196640 | tf_op jit(solution)/shard_map/ppermute | solution.py:474
  137.7 0.3 collective-permute-done.23.refs_7_
  138.0 4.3 %home.1.refs_8_ = f32[6,4,128,512]{3,2,1,0:T(8,128)} custom-call(s32[96]{0:T(128)S(1)} %copy-done.9, s32[1]{0:T(128)} %bitcast.own.chan, s32[1]{0:T(128)} %bitcast.1.time, bf16[192,512]{1,0:T(8,128)(2,1)S(1)} %stack.8.refs_0_, bf16[192,512]{1,0:T(8,128)(2,1)S(1)} %collective-permute-done.10.refs_1_, bf16[192,512]{1,0:T(8,128)(2,1)S(1)} %collective-permute-done.11.refs_2_, ...), custom_call_target="tpu_custom_call" | custom-call | flops 1 | bytes 1 | tf_op jit(solution)/shard_map/home/pallas_call | solution.py:415
  142.3 3.8 %collective-permute-done.22.refs_6_ = bf16[192,512]{1,0:T(8,128)(2,1)S(1)} collective-permute-done((bf16[192,512]{1,0:T(8,128)(2,1)S(1)}, bf16[192,512]{1,0:T(8,128)(2,1)S(1)}, u32[]{:S(2)}, u32[]{:S(2)}) %collective-permute-start.22) | collective-permute-done | bytes 196640 | tf_op jit(solution)/shard_map/ppermute | solution.py:474
  146.1 2.1 %collective-permute-done.24.refs_7_ = bf16[192,512]{1,0:T(8,128)(2,1)S(1)} collective-permute-done((bf16[192,512]{1,0:T(8,128)(2,1)S(1)}, bf16[192,512]{1,0:T(8,128)(2,1)S(1)}, u32[]{:S(2)}, u32[]{:S(2)}) %collective-permute-start.24) | collective-permute-done | bytes 196640 | tf_op jit(solution)/shard_map/ppermute | solution.py:474
  148.2 2.0 %moved.1 = f32[6,4,128,512]{3,2,1,0:T(8,128)} custom-call(s32[96]{0:T(128)S(1)} %copy-done.9, s32[1]{0:T(128)} %bitcast.own.chan, s32[1]{0:T(128)} %bitcast.1.time, bf16[192,512]{1,0:T(8,128)(2,1)S(1)} %collective-permute-done.14.refs_0_, bf16[192,512]{1,0:T(8,128)(2,1)S(1)} %collective-permute-done.15.refs_1_, ...), custom_call_target="tpu_custom_call", output_to_operand_aliasing={{}: (11, {})} | custom-call | flops 1 | bytes 1 | tf_op jit(solution)/shard_map/moved/pallas_call | solution.py:454
  (46 shorter events, 0.1 us)
Async XLA Ops:
  0.0 2.8 %copy-start.3 = (bf16[512,512]{1,0:T(8,128)(2,1)S(1)}, bf16[512,512]{1,0:T(8,128)(2,1)}, u32[]{:S(2)}) copy-start(bf16[512,512]{1,0:T(8,128)(2,1)} %constant.25.clone.order) | copy-start | bytes 1572868
  0.0 2.8 %copy-start.8 = (s32[4,128]{1,0:T(4,128)S(1)}, s32[4,128]{1,0:T(4,128)}, u32[]{:S(2)}) copy-start(s32[4,128]{1,0:T(4,128)} %quality.1) | copy-start | bytes 6148
  0.0 46.2 %slice-start = ((s8[6291456]{0:T(1024)(128)(4,1)}), s8[4194304]{0:T(1024)(128)(4,1)S(1)}, s32[]{:S(2)}) async-start(s8[6291456]{0:T(1024)(128)(4,1)} %bitcast.5), calls=%async_computation.1 | async-start | bytes 8388608
  2.8 43.4 %slice-start.1 = ((s8[6291456]{0:T(1024)(128)(4,1)}), s8[2097152]{0:T(1024)(128)(4,1)S(1)}, s32[]{:S(2)}) async-start(s8[6291456]{0:T(1024)(128)(4,1)} %bitcast.5), calls=%async_computation.2 | async-start | bytes 4194304
  5.1 41.2 %copy-start.2 = (bf16[768,768]{1,0:T(8,128)(2,1)S(1)}, bf16[768,768]{1,0:T(8,128)(2,1)}, u32[]{:S(2)}) copy-start(bf16[768,768]{1,0:T(8,128)(2,1)} %constant.27.clone.inside) | copy-start | bytes 3538948
  5.1 41.1 %copy-start.4 = (f32[768,1]{1,0:T(8,128)S(1)}, f32[768,1]{1,0:T(8,128)}, u32[]{:S(2)}) copy-start(f32[768,1]{1,0:T(8,128)} %constant.28.clone.inverse_count) | copy-start | bytes 9220
  5.1 41.1 %copy-start.5 = (bf16[4,2,128,128]{3,2,1,0:T(8,128)(2,1)S(1)}, bf16[4,2,128,128]{3,2,1,0:T(8,128)(2,1)}, u32[]{:S(2)}) copy-start(bf16[4,2,128,128]{3,2,1,0:T(8,128)(2,1)} %constant.29.clone.pick) | copy-start | bytes 786436
  46.3 30.3 %copy-start.6 = (bf16[4,128,256]{2,1,0:T(8,128)(2,1)S(1)}, bf16[4,128,256]{2,1,0:T(8,128)(2,1)}, u32[]{:S(2)}) copy-start(bf16[4,128,256]{2,1,0:T(8,128)(2,1)} %constant.30.clone.spread) | copy-start | bytes 786436
  53.7 25.5 %collective-permute-start.2 = (bf16[2,2,768,128]{3,2,1,0:T(8,128)(2,1)S(1)}, bf16[2,2,768,128]{3,2,1,0:T(8,128)(2,1)S(1)}, u32[]{:S(2)}, u32[]{:S(2)}) collective-permute-start(bf16[2,2,768,128]{3,2,1,0:T(8,128)(2,1)S(1)} %get-tuple-element.34.refs_0_), channel_id=1, source_target_pairs={{0,4},{4,0},{8,12},{12,8},{16,20},{20,16},{24,28},{28,24},{32,36},... | collective-permute-start | bytes 2359304 | tf_op jit(solution)/shard_map/ppermute | solution.py:490
  54.0 25.1 %collective-permute-start = (bf16[2,2,768,128]{3,2,1,0:T(8,128)(2,1)S(1)}, bf16[2,2,768,128]{3,2,1,0:T(8,128)(2,1)S(1)}, u32[]{:S(2)}, u32[]{:S(2)}) collective-permute-start(bf16[2,2,768,128]{3,2,1,0:T(8,128)(2,1)S(1)} %get-tuple-element.34.refs_0_), channel_id=1, source_target_pairs={{0,8},{4,12},{8,16},{12,20},{16,24},{20,28},{24,32},{28,36},{32,40... | collective-permute-start | bytes 2359304 | tf_op jit(solution)/shard_map/ppermute | solution.py:474
  54.7 24.5 %collective-permute-start.1 = (bf16[2,2,768,128]{3,2,1,0:T(8,128)(2,1)S(1)}, bf16[2,2,768,128]{3,2,1,0:T(8,128)(2,1)S(1)}, u32[]{:S(2)}, u32[]{:S(2)}) collective-permute-start(bf16[2,2,768,128]{3,2,1,0:T(8,128)(2,1)S(1)} %get-tuple-element.34.refs_0_), channel_id=1, source_target_pairs={{0,120},{4,124},{8,0},{12,4},{16,8},{20,12},{24,16},{28,20},{32,24... | collective-permute-start | bytes 2359304 | tf_op jit(solution)/shard_map/ppermute | solution.py:474
  59.4 25.4 %copy-start.1 = (bf16[384,1024]{1,0:T(8,128)(2,1)S(1)}, bf16[384,1024]{1,0:T(8,128)(2,1)}, u32[]{:S(2)}) copy-start(bf16[384,1024]{1,0:T(8,128)(2,1)} %constant.31.clone.order) | copy-start | bytes 2359300
  59.4 25.4 %copy-start.7 = (s32[96,2]{0,1:T(2,128)S(1)}, s32[96,2]{0,1:T(2,128)}, u32[]{:S(2)}) copy-start(s32[96,2]{0,1:T(2,128)} %param.15) | copy-start | bytes 2308
  59.4 7.8 %collective-permute-start.3 = (bf16[768,128]{1,0:T(8,128)(2,1)S(1)}, bf16[768,128]{1,0:T(8,128)(2,1)S(1)}, u32[]{:S(2)}, u32[]{:S(2)}) collective-permute-start(bf16[768,128]{1,0:T(8,128)(2,1)S(1)} %get-tuple-element.31.s0), channel_id=1, source_target_pairs={{0,3},{1,0},{2,1},{3,2},{4,7},{5,4},{6,5},{7,6},{8,11},{9,8},{10,9... | collective-permute-start | bytes 589832 | tf_op jit(solution)/shard_map/ppermute | solution.py:474
  60.8 7.9 %collective-permute-start.4 = (bf16[768,128]{1,0:T(8,128)(2,1)S(1)}, bf16[768,128]{1,0:T(8,128)(2,1)S(1)}, u32[]{:S(2)}, u32[]{:S(2)}) collective-permute-start(bf16[768,128]{1,0:T(8,128)(2,1)S(1)} %get-tuple-element.31.s0), channel_id=1, source_target_pairs={{0,2},{1,3},{2,0},{3,1},{4,6},{5,7},{6,4},{7,5},{8,10},{9,11},{10,... | collective-permute-start | bytes 589832 | tf_op jit(solution)/shard_map/ppermute | solution.py:474
  67.2 9.4 %collective-permute-start.5 = (bf16[768,128]{1,0:T(8,128)(2,1)S(1)}, bf16[768,128]{1,0:T(8,128)(2,1)S(1)}, u32[]{:S(2)}, u32[]{:S(2)}) collective-permute-start(bf16[768,128]{1,0:T(8,128)(2,1)S(1)} %get-tuple-element.31.s0), channel_id=1, source_target_pairs={{0,1},{1,2},{2,3},{3,0},{4,5},{5,6},{6,7},{7,4},{8,9},{9,10},{10,1... | collective-permute-start | bytes 589832 | tf_op jit(solution)/shard_map/ppermute | solution.py:474
  79.3 5.5 %collective-permute-start.9 = (bf16[2,2,768,128]{3,2,1,0:T(8,128)(2,1)S(1)}, bf16[2,2,768,128]{3,2,1,0:T(8,128)(2,1)S(1)}, u32[]{:S(2)}, u32[]{:S(2)}) collective-permute-start(bf16[2,2,768,128]{3,2,1,0:T(8,128)(2,1)S(1)} %choose.2), channel_id=1, source_target_pairs={{0,4},{4,0},{8,12},{12,8},{16,20},{20,16},{24,28},{28,24},{32,36},... | collective-permute-start | bytes 2359304 | tf_op jit(solution)/shard_map/ppermute | solution.py:495
  79.3 23.3 %collective-permute-start.6 = (bf16[2,2,768,128]{3,2,1,0:T(8,128)(2,1)S(1)}, bf16[2,2,768,128]{3,2,1,0:T(8,128)(2,1)S(1)}, u32[]{:S(2)}, u32[]{:S(2)}) collective-permute-start(bf16[2,2,768,128]{3,2,1,0:T(8,128)(2,1)S(1)} %get-tuple-element.38.refs_0_), channel_id=1, source_target_pairs={{0,8},{4,12},{8,16},{12,20},{16,24},{20,28},{24,32},{28,36},{32,40... | collective-permute-start | bytes 2359304 | tf_op jit(solution)/shard_map/ppermute | solution.py:474
  79.4 25.9 %collective-permute-start.7 = (bf16[2,2,768,128]{3,2,1,0:T(8,128)(2,1)S(1)}, bf16[2,2,768,128]{3,2,1,0:T(8,128)(2,1)S(1)}, u32[]{:S(2)}, u32[]{:S(2)}) collective-permute-start(bf16[2,2,768,128]{3,2,1,0:T(8,128)(2,1)S(1)} %get-tuple-element.38.refs_0_), channel_id=1, source_target_pairs={{0,120},{4,124},{8,0},{12,4},{16,8},{20,12},{24,16},{28,20},{32,24... | collective-permute-start | bytes 2359304 | tf_op jit(solution)/shard_map/ppermute | solution.py:474
  84.8 20.6 %collective-permute-start.8 = (bf16[2,2,768,128]{3,2,1,0:T(8,128)(2,1)S(1)}, bf16[2,2,768,128]{3,2,1,0:T(8,128)(2,1)S(1)}, u32[]{:S(2)}, u32[]{:S(2)}) collective-permute-start(bf16[2,2,768,128]{3,2,1,0:T(8,128)(2,1)S(1)} %get-tuple-element.38.refs_0_), channel_id=1, source_target_pairs={{0,4},{4,0},{8,12},{12,8},{16,20},{20,16},{24,28},{28,24},{32,36},... | collective-permute-start | bytes 2359304 | tf_op jit(solution)/shard_map/ppermute | solution.py:490
  84.8 10.3 %copy-start = (bf16[512,1536]{1,0:T(8,128)(2,1)S(1)}, bf16[512,1536]{1,0:T(8,128)(2,1)}, u32[]{:S(2)}) copy-start(bf16[512,1536]{1,0:T(8,128)(2,1)} %constant.32.clone.inverse) | copy-start | bytes 4718596
  96.5 8.9 %collective-permute-start.10 = (bf16[192,512]{1,0:T(8,128)(2,1)S(1)}, bf16[192,512]{1,0:T(8,128)(2,1)S(1)}, u32[]{:S(2)}, u32[]{:S(2)}) collective-permute-start(bf16[192,512]{1,0:T(8,128)(2,1)S(1)} %stack.9), channel_id=1, source_target_pairs={{0,1},{1,2},{2,3},{3,0},{4,5},{5,6},{6,7},{7,4},{8,9},{9,10},{10,1... | collective-permute-start | bytes 589832 | tf_op jit(solution)/shard_map/ppermute | solution.py:474
  96.8 13.0 %collective-permute-start.11 = (bf16[192,512]{1,0:T(8,128)(2,1)S(1)}, bf16[192,512]{1,0:T(8,128)(2,1)S(1)}, u32[]{:S(2)}, u32[]{:S(2)}) collective-permute-start(bf16[192,512]{1,0:T(8,128)(2,1)S(1)} %stack.10), channel_id=1, source_target_pairs={{0,2},{1,3},{2,0},{3,1},{4,6},{5,7},{6,4},{7,5},{8,10},{9,11},{10,... | collective-permute-start | bytes 589832 | tf_op jit(solution)/shard_map/ppermute | solution.py:474
  102.6 7.4 %collective-permute-start.12 = (bf16[192,512]{1,0:T(8,128)(2,1)S(1)}, bf16[192,512]{1,0:T(8,128)(2,1)S(1)}, u32[]{:S(2)}, u32[]{:S(2)}) collective-permute-start(bf16[192,512]{1,0:T(8,128)(2,1)S(1)} %stack.11), channel_id=1, source_target_pairs={{0,3},{1,0},{2,1},{3,2},{4,7},{5,4},{6,5},{7,6},{8,11},{9,8},{10,9... | collective-permute-start | bytes 589832 | tf_op jit(solution)/shard_map/ppermute | solution.py:474
  110.1 2.4 %collective-permute-start.13 = (bf16[2,2,768,128]{3,2,1,0:T(8,128)(2,1)S(1)}, bf16[2,2,768,128]{3,2,1,0:T(8,128)(2,1)S(1)}, u32[]{:S(2)}, u32[]{:S(2)}) collective-permute-start(bf16[2,2,768,128]{3,2,1,0:T(8,128)(2,1)S(1)} %choose.3), channel_id=1, source_target_pairs={{0,4},{4,0},{8,12},{12,8},{16,20},{20,16},{24,28},{28,24},{32,36},... | collective-permute-start | bytes 2359304 | tf_op jit(solution)/shard_map/ppermute | solution.py:495
  110.2 15.1 %collective-permute-start.14 = (bf16[192,512]{1,0:T(8,128)(2,1)S(1)}, bf16[192,512]{1,0:T(8,128)(2,1)S(1)}, u32[]{:S(2)}, u32[]{:S(2)}) collective-permute-start(bf16[192,512]{1,0:T(8,128)(2,1)S(1)} %stack.8.refs_0_), channel_id=1, source_target_pairs={{0,4},{4,8},{8,12},{12,16},{16,20},{20,24},{24,28},{28,32},{32,36}... | collective-permute-start | bytes 589832 | tf_op jit(solution)/shard_map/ppermute | solution.py:474
  110.7 18.6 %collective-permute-start.15 = (bf16[192,512]{1,0:T(8,128)(2,1)S(1)}, bf16[192,512]{1,0:T(8,128)(2,1)S(1)}, u32[]{:S(2)}, u32[]{:S(2)}) collective-permute-start(bf16[192,512]{1,0:T(8,128)(2,1)S(1)} %collective-permute-done.10.refs_1_), channel_id=1, source_target_pairs={{0,4},{4,8},{8,12},{12,16},{16,20},{20,24},{24,28},{28,32},{32,36}... | collective-permute-start | bytes 589832 | tf_op jit(solution)/shard_map/ppermute | solution.py:474
  110.7 19.3 %collective-permute-start.16 = (bf16[192,512]{1,0:T(8,128)(2,1)S(1)}, bf16[192,512]{1,0:T(8,128)(2,1)S(1)}, u32[]{:S(2)}, u32[]{:S(2)}) collective-permute-start(bf16[192,512]{1,0:T(8,128)(2,1)S(1)} %collective-permute-done.11.refs_2_), channel_id=1, source_target_pairs={{0,4},{4,8},{8,12},{12,16},{16,20},{20,24},{24,28},{28,32},{32,36}... | collective-permute-start | bytes 589832 | tf_op jit(solution)/shard_map/ppermute | solution.py:474
  110.7 19.3 %collective-permute-start.17 = (bf16[192,512]{1,0:T(8,128)(2,1)S(1)}, bf16[192,512]{1,0:T(8,128)(2,1)S(1)}, u32[]{:S(2)}, u32[]{:S(2)}) collective-permute-start(bf16[192,512]{1,0:T(8,128)(2,1)S(1)} %collective-permute-done.12.refs_3_), channel_id=1, source_target_pairs={{0,4},{4,8},{8,12},{12,16},{16,20},{20,24},{24,28},{28,32},{32,36}... | collective-permute-start | bytes 589832 | tf_op jit(solution)/shard_map/ppermute | solution.py:474
  124.2 8.2 %collective-permute-start.19 = (bf16[192,512]{1,0:T(8,128)(2,1)S(1)}, bf16[192,512]{1,0:T(8,128)(2,1)S(1)}, u32[]{:S(2)}, u32[]{:S(2)}) collective-permute-start(bf16[192,512]{1,0:T(8,128)(2,1)S(1)} %stack.13), channel_id=1, source_target_pairs={{0,1},{1,2},{2,3},{3,0},{4,5},{5,6},{6,7},{7,4},{8,9},{9,10},{10,1... | collective-permute-start | bytes 589832 | tf_op jit(solution)/shard_map/ppermute | solution.py:474
  125.3 12.7 %copy-start.9 = (s32[96]{0:T(128)S(1)}, s32[96]{0:T(128)}, u32[]{:S(2)}) copy-start(s32[96]{0:T(128)} %owners.3) | copy-start | bytes 1156
  125.3 12.3 %collective-permute-start.21 = (bf16[192,512]{1,0:T(8,128)(2,1)S(1)}, bf16[192,512]{1,0:T(8,128)(2,1)S(1)}, u32[]{:S(2)}, u32[]{:S(2)}) collective-permute-start(bf16[192,512]{1,0:T(8,128)(2,1)S(1)} %stack.14), channel_id=1, source_target_pairs={{0,2},{1,3},{2,0},{3,1},{4,6},{5,7},{6,4},{7,5},{8,10},{9,11},{10,... | collective-permute-start | bytes 589832 | tf_op jit(solution)/shard_map/ppermute | solution.py:474
  129.3 8.7 %collective-permute-start.23 = (bf16[192,512]{1,0:T(8,128)(2,1)S(1)}, bf16[192,512]{1,0:T(8,128)(2,1)S(1)}, u32[]{:S(2)}, u32[]{:S(2)}) collective-permute-start(bf16[192,512]{1,0:T(8,128)(2,1)S(1)} %stack.15), channel_id=1, source_target_pairs={{0,3},{1,0},{2,1},{3,2},{4,7},{5,4},{6,5},{7,6},{8,11},{9,8},{10,9... | collective-permute-start | bytes 589832 | tf_op jit(solution)/shard_map/ppermute | solution.py:474
  130.0 12.2 %collective-permute-start.18 = (bf16[192,512]{1,0:T(8,128)(2,1)S(1)}, bf16[192,512]{1,0:T(8,128)(2,1)S(1)}, u32[]{:S(2)}, u32[]{:S(2)}) collective-permute-start(bf16[192,512]{1,0:T(8,128)(2,1)S(1)} %stack.12.refs_4_), channel_id=1, source_target_pairs={{0,4},{4,8},{8,12},{12,16},{16,20},{20,24},{24,28},{28,32},{32,36}... | collective-permute-start | bytes 589832 | tf_op jit(solution)/shard_map/ppermute | solution.py:474
  132.4 9.9 %collective-permute-start.20 = (bf16[192,512]{1,0:T(8,128)(2,1)S(1)}, bf16[192,512]{1,0:T(8,128)(2,1)S(1)}, u32[]{:S(2)}, u32[]{:S(2)}) collective-permute-start(bf16[192,512]{1,0:T(8,128)(2,1)S(1)} %collective-permute-done.19.refs_5_), channel_id=1, source_target_pairs={{0,4},{4,8},{8,12},{12,16},{16,20},{20,24},{24,28},{28,32},{32,36}... | collective-permute-start | bytes 589832 | tf_op jit(solution)/shard_map/ppermute | solution.py:474
  137.7 8.4 %collective-permute-start.22 = (bf16[192,512]{1,0:T(8,128)(2,1)S(1)}, bf16[192,512]{1,0:T(8,128)(2,1)S(1)}, u32[]{:S(2)}, u32[]{:S(2)}) collective-permute-start(bf16[192,512]{1,0:T(8,128)(2,1)S(1)} %collective-permute-done.21.refs_6_), channel_id=1, source_target_pairs={{0,4},{4,8},{8,12},{12,16},{16,20},{20,24},{24,28},{28,32},{32,36}... | collective-permute-start | bytes 589832 | tf_op jit(solution)/shard_map/ppermute | solution.py:474
  138.0 10.2 %collective-permute-start.24 = (bf16[192,512]{1,0:T(8,128)(2,1)S(1)}, bf16[192,512]{1,0:T(8,128)(2,1)S(1)}, u32[]{:S(2)}, u32[]{:S(2)}) collective-permute-start(bf16[192,512]{1,0:T(8,128)(2,1)S(1)} %collective-permute-done.23.refs_7_), channel_id=1, source_target_pairs={{0,4},{4,8},{8,12},{12,16},{16,20},{20,24},{24,28},{28,32},{32,36}... | collective-permute-start | bytes 589832 | tf_op jit(solution)/shard_map/ppermute | solution.py:474

commit v4 on v3

--- a/solution.py
+++ b/solution.py
@@ -92,71 +92,89 @@
 
 def tile_lanes():
     count = PAIR * SEG_DEV
-    order = np.zeros((TPS * LANES, count * LANES))
+    order = np.zeros((TPS * LANES, count * LANES // 2))
     for t in range(TPS):
         for s in range(count):
             for c in range(HALF_PART):
-                for twin in range(2):
-                    lane = s * LANES + twin * (LANES // 2) + t * HALF_PART + c
-                    order[t * LANES + s * HALF_PART + c, lane] = 1.0
+                lane = s * (LANES // 2) + t * HALF_PART + c
+                order[t * LANES + s * HALF_PART + c, lane] = 1.0
     return order.astype(ml_dtypes.bfloat16)
 
 
-def interleave():
-    order = np.zeros((SEG_DEV * BLOCK, SEG_DEV * BLOCK))
-    for s in range(SEG_DEV):
-        for j in range(TM):
-            for c in range(PART):
-                part, at = divmod(c, HALF_PART)
-                lane = j * BLOCK + (part * SEG_DEV + s) * HALF_PART + at
-                order[s * BLOCK + j * PART + c, lane] = 1.0
-    return order.astype(ml_dtypes.bfloat16)
-
-
 PACK_BLOCKS = 8
-
-
-def pack_kernel(own, records, quality, order, out):
-    step = pl.program_id(0)
-    marks = jnp.concatenate([quality[s : s + 1, :] for s in range(SEG_DEV)], axis=1)
-    marks = jnp.broadcast_to(marks.astype(F32), (16, SEG_DEV * BLOCK)).astype(BF16)
-    marks = jnp.dot(marks, order[...], preferred_element_type=F32)[:1]
+PACK_STEPS = NB // PACK_BLOCKS
+
+
+def pack_kernel(own, records, quality, out, held, marks, order, rows, sem, mark_sem):
+    lanes = PACK_BLOCKS * BLOCK
+
+    def copy(step):
+        part = records.at[:, :, pl.ds(step * lanes, lanes)]
+        return pltpu.make_async_copy(part, held.at[step], sem.at[step])
+
+    pltpu.make_async_copy(quality, marks, mark_sem).start()
+    for step in range(PACK_STEPS):
+        copy(step).start()
+    row = lax.broadcasted_iota(jnp.int32, order.shape, 0)
+    lane = lax.broadcasted_iota(jnp.int32, order.shape, 1)
+    s, j = row // BLOCK, row // PART % TM
+    part, at = row // HALF_PART % 2, row % HALF_PART
+    target = j * BLOCK + (part * SEG_DEV + s) * HALF_PART + at
+    order[...] = jnp.where(lane == target, 1.0, 0.0).astype(BF16)
+    row = lax.broadcasted_iota(jnp.int32, rows.shape, 0)
+    lane = lax.broadcasted_iota(jnp.int32, rows.shape, 1)
+    s, n = row // ROWS, row % ROWS
+    keep = (lane == n * SEG_DEV + s) & (n < SLAB)
+    rows[...] = jnp.where(keep, 1.0, 0.0).astype(BF16)
+    pltpu.make_async_copy(quality, marks, mark_sem).wait()
+    mark = jnp.concatenate([marks[s : s + 1, :] for s in range(SEG_DEV)], axis=1)
+    mark = jnp.broadcast_to(mark.astype(F32), (16, SEG_DEV * BLOCK)).astype(BF16)
+    mark = jnp.dot(mark, order[...], preferred_element_type=F32)[:1]
     row = lax.broadcasted_iota(jnp.int32, (ROWS, SEG_DEV * BLOCK), 0)
-    x = jnp.concatenate(
-        [
-            jnp.concatenate(
-                [records[s, :, k * BLOCK : (k + 1) * BLOCK] for s in range(SEG_DEV)], axis=1
-            )
-            for k in range(PACK_BLOCKS)
-        ],
-        axis=0,
-    )
-    y = jnp.dot(x, order[...], preferred_element_type=F32)
-    for k in range(PACK_BLOCKS):
-        mine = step * PACK_BLOCKS + k == own[0]
-        extra = jnp.where((row == SLAB) & mine, marks, 0.0)
-        block = jnp.where(row < SLAB, y[k * ROWS : (k + 1) * ROWS], extra).astype(BF16)
-        for j in range(TM):
-            out[k * TM + j] = block[:, j * BLOCK : (j + 1) * BLOCK]
+    for step in range(PACK_STEPS):
+        copy(step).wait()
+        flat = held[step].reshape(SLAB * SEG_DEV, lanes)
+        flat = jnp.dot(rows[...], flat, preferred_element_type=F32).astype(BF16)
+        x = jnp.concatenate(
+            [
+                jnp.concatenate(
+                    [
+                        flat[s * ROWS : (s + 1) * ROWS, k * BLOCK : (k + 1) * BLOCK]
+                        for s in range(SEG_DEV)
+                    ],
+                    axis=1,
+                )
+                for k in range(PACK_BLOCKS)
+            ],
+            axis=0,
+        )
+        y = jnp.dot(x, order[...], preferred_element_type=F32)
+        for k in range(PACK_BLOCKS):
+            index = step * PACK_BLOCKS + k
+            extra = jnp.where((row == SLAB) & (own[0] == index), mark, 0.0)
+            block = (y[k * ROWS : (k + 1) * ROWS] + extra).astype(BF16)
+            for j in range(TM):
+                out[index * TM + j] = block[:, j * BLOCK : (j + 1) * BLOCK]
 
 
 def pack(own, records, quality):
     return pl.pallas_call(
         pack_kernel,
         out_shape=jax.ShapeDtypeStruct((NB * TM, ROWS, BLOCK), BF16),
-        grid_spec=pltpu.PrefetchScalarGridSpec(
-            num_scalar_prefetch=1,
-            grid=(NB // PACK_BLOCKS,),
-            in_specs=[
-                pl.BlockSpec((SEG_DEV, ROWS, PACK_BLOCKS * BLOCK), lambda g, own: (0, 0, g)),
-                pl.BlockSpec((SEG_DEV, BLOCK), lambda g, own: (0, 0)),
-                pl.BlockSpec(memory_space=pltpu.VMEM),
-            ],
-            out_specs=pl.BlockSpec((PACK_BLOCKS * TM, ROWS, BLOCK), lambda g, own: (g, 0, 0)),
-        ),
+        in_specs=[pl.BlockSpec(memory_space=pltpu.SMEM)]
+        + [pl.BlockSpec(memory_space=pltpu.HBM)] * 2,
+        out_specs=pl.BlockSpec(memory_space=pltpu.VMEM),
+        scratch_shapes=[
+            pltpu.VMEM((PACK_STEPS, SLAB, SEG_DEV, PACK_BLOCKS * BLOCK), BF16),
+            pltpu.VMEM((SEG_DEV, BLOCK), jnp.int32),
+            pltpu.VMEM((SEG_DEV * BLOCK, SEG_DEV * BLOCK), BF16),
+            pltpu.VMEM((SEG_DEV * ROWS, SLAB * SEG_DEV), BF16),
+            pltpu.SemaphoreType.DMA((PACK_STEPS,)),
+            pltpu.SemaphoreType.DMA,
+        ],
         compiler_params=pltpu.CompilerParams(vmem_limit_bytes=20 * MIB),
         name="pack",
-    )(own, records, quality, interleave())
+    )(own, records.transpose(1, 0, 2), quality)
 
 
 def whiten_kernel(own, slabs, table, inside, inverse_count, pick, low, high, sources, total):
@@ -211,28 +229,32 @@
     )(own, slabs.reshape(NB, TM, ROWS, BLOCK), forward_table(), inside, inverse_count, source_lanes())
 
 
-def choose_kernel(chan, below, above, out, sem):
+def choose_kernel(chan, below, above, *refs):
+    outs, sem = refs[:-1], refs[-1]
     odd = lax.rem(chan[0], 2)
-
-    @pl.when(odd == 1)
-    def _():
-        pltpu.make_async_copy(below, out, sem).start()
-
-    @pl.when(odd == 0)
-    def _():
-        pltpu.make_async_copy(above, out, sem).start()
-
-    pltpu.make_async_copy(below, out, sem).wait()
-
-
-def choose(chan, below, above):
+    count = below.shape[0] // len(outs)
+    for index, out in enumerate(outs):
+        for parity, ref in ((1, below), (0, above)):
+
+            @pl.when(odd == parity)
+            def _():
+                part = ref.at[pl.ds(index * count, count)]
+                pltpu.make_async_copy(part, out, sem.at[index]).start()
+
+    for index, out in enumerate(outs):
+        part = below.at[pl.ds(index * count, count)]
+        pltpu.make_async_copy(part, out, sem.at[index]).wait()
+
+
+def choose(chan, below, above, parts):
+    shape = (below.shape[0] // parts, *below.shape[1:])
     return pl.pallas_call(
         choose_kernel,
-        out_shape=jax.ShapeDtypeStruct(below.shape, below.dtype),
+        out_shape=[jax.ShapeDtypeStruct(shape, below.dtype)] * parts,
         in_specs=[pl.BlockSpec(memory_space=pltpu.SMEM)]
         + [pl.BlockSpec(memory_space=pl.ANY)] * 2,
-        out_specs=pl.BlockSpec(memory_space=pl.ANY),
-        scratch_shapes=[pltpu.SemaphoreType.DMA],
+        out_specs=[pl.BlockSpec(memory_space=pl.ANY)] * parts,
+        scratch_shapes=[pltpu.SemaphoreType.DMA((parts,))],
         compiler_params=pltpu.CompilerParams(vmem_limit_bytes=MIB),
         cost_estimate=pl.CostEstimate(flops=1, bytes_accessed=1, transcendentals=0),
         name="choose",
@@ -287,37 +309,50 @@
 
 
 def cross_kernel(chan, tiles, diag, order, *refs):
-    receivers, (out, held, wide, sem) = refs[:RECEIVERS], refs[RECEIVERS:]
+    receivers, (out, held, wide, sem) = refs[:-4], refs[-4:]
     step = pl.program_id(0)
     steps = F // STEP
 
-    def copy(ref, t, k):
+    def copy(index, t, k):
         rows = pl.ds(k * STEP, STEP)
-        return pltpu.make_async_copy(ref.at[:, :, rows, :], held.at[k, t], sem.at[k, t])
+        refs = receivers[index:] if index == RECEIVERS - 1 else receivers[index : index + 1]
+        count = held.shape[2] // len(refs)
+        return [
+            pltpu.make_async_copy(
+                ref.at[:, :, rows, :], held.at[k, t, pl.ds(part * count, count)], sem.at[k, t]
+            )
+            for part, ref in enumerate(refs)
+        ]
 
     @pl.when(step == 0)
     def _():
         picks = [chosen(chan[0], tiles, t) for t in range(TPS)]
         for k in range(steps):
             for t in range(TPS):
-                for index, ref in enumerate(receivers):
+                for index in range(RECEIVERS):
 
                     @pl.when(picks[t] == index)
                     def _():
-                        copy(ref, t, k).start()
+                        for one in copy(index, t, k):
+                            one.start()
 
     for t in range(TPS):
-        copy(receivers[0], t, step).wait()
+        copy(0, t, step)[0].wait()
     x = jnp.concatenate(
         [held[step, t].reshape(TM // PAIR * 2 * STEP, LANES) for t in range(TPS)], axis=1
     )
     y = jnp.dot(x, order[...], preferred_element_type=F32)
     count = PAIR * SEG_DEV
+    left = lax.broadcasted_iota(jnp.int32, (STEP, LANES), 1) < LANES // 2
     for i in range(TM // PAIR):
         for half in range(2):
             at = (i * 2 + half) * STEP
-            for s in range(count):
-                wide[half * SEGS + i * count + s] = y[at : at + STEP, s * LANES : (s + 1) * LANES]
+            for s in range(0, count, 2):
+                one = y[at : at + STEP, s * LANES // 2 : s * LANES // 2 + LANES]
+                turned = pltpu.roll(one, LANES // 2, 1)
+                index = half * SEGS + i * count + s
+                wide[index] = jnp.where(left, one, turned)
+                wide[index + 1] = jnp.where(left, turned, one)
     first = lax.broadcasted_iota(jnp.int32, (1, GROUP, LANES), 2) < LANES // 2
 
     def group(pair, carry):
@@ -348,7 +383,7 @@
             num_scalar_prefetch=2,
             grid=(F // STEP,),
             in_specs=[pl.BlockSpec(memory_space=pltpu.VMEM)] * 2
-            + [pl.BlockSpec(memory_space=pl.ANY)] * RECEIVERS,
+            + [pl.BlockSpec(memory_space=pl.ANY)] * len(receivers),
             out_specs=pl.BlockSpec(memory_space=pltpu.VMEM),
             scratch_shapes=[
                 pltpu.VMEM((F // STEP, TPS, TM // PAIR, 2, STEP, LANES), BF16),
@@ -390,11 +425,42 @@
     )(spectra, inverse)
 
 
+def merge_kernel(*refs):
+    pieces, out, sem = refs[:TM], refs[TM], refs[TM + 1]
+    rows = pieces[0].shape[0]
+    copies = [
+        pltpu.make_async_copy(ref, out.at[pl.ds(rel * rows, rows), :], sem.at[rel])
+        for rel, ref in enumerate(pieces)
+    ]
+    for copy in copies:
+        copy.start()
+    for copy in copies:
+        copy.wait()
+
+
+def merge(pieces):
+    rows, width = pieces[0].shape
+    return pl.pallas_call(
+        merge_kernel,
+        out_shape=jax.ShapeDtypeStruct((TM * rows, width), pieces[0].dtype),
+        in_specs=[pl.BlockSpec(memory_space=pl.ANY)] * TM,
+        out_specs=pl.BlockSpec(memory_space=pl.ANY),
+        scratch_shapes=[pltpu.SemaphoreType.DMA((TM,))],
+        compiler_params=pltpu.CompilerParams(vmem_limit_bytes=MIB),
+        cost_estimate=pl.CostEstimate(flops=1, bytes_accessed=1, transcendentals=0),
+        name="merge",
+    )(*pieces)
+
+
 def arrange(time, pieces, t):
     rows = SRC_PART * HALF_PART
-    for index, ref in enumerate(pieces):
+    parts = []
+    for ref in pieces:
+        count = ref.shape[0] // (TPS * rows)
+        parts += [(ref, part * TPS * rows) for part in range(count)]
+    for index, (ref, first) in enumerate(parts):
         half, rel = divmod(index, TM)
-        value = ref[t * rows : (t + 1) * rows, :].astype(F32)
+        value = ref[first + t * rows : first + (t + 1) * rows, :].astype(F32)
         at = lax.rem(time + TM - rel, TM) * PART + half * HALF_PART
         yield pl.multiple_of(at, HALF_PART), value.reshape(SRC_PART, HALF_PART, LAG_COUNT)
 
@@ -484,38 +550,39 @@
     slabs = lax.all_to_all(slabs, ("chan", "tm"), split_axis=0, concat_axis=0, tiled=True)
     low, high, sources = whiten(chan, slabs)
     sources = [sources] + [shifted(sources, "tm", -rel) for rel in range(1, TM)]
-    diag = diagonal(sources)
 
     def halo(white):
         mate = lax.ppermute(white, "chan", swap)
         return [white, shifted(white, "chan", 2), shifted(white, "chan", -2), mate]
 
-    def complete(blocks):
-        other = choose(chan, blocks[1], blocks[2])
-        return blocks + [lax.ppermute(other, "chan", swap)]
+    def complete(blocks, parts):
+        others = choose(chan, blocks[1], blocks[2], parts)
+        return blocks + [lax.ppermute(other, "chan", swap) for other in others]
 
     inverse = inverse_table()
     order = (2, 0, 1, 3)
     low = halo(low)
     high, low[3] = lax.optimization_barrier((high, low[3]))
     high = halo(high)
-    low, diag = lax.optimization_barrier((low, diag))
-    spectra = cross(chan, tiles, diag, complete(low))
+    low, sources = lax.optimization_barrier((low, sources))
+    diag = diagonal(sources)
+    spectra = cross(chan, tiles, diag, complete(low, 2))
     parts = [stack(spectra, rel, inverse) for rel in range(TM)]
     stay_low = [shifted(part, "tm", rel) if rel else part for rel, part in enumerate(parts)]
-    high, stay_low = lax.optimization_barrier((high, stay_low))
-    high = complete(high)
-    move_low = [shifted(part, "chan", 1) for part in stay_low]
+    high, _ = lax.optimization_barrier((high, parts))
+    high = complete(high, 1)
     spectra = cross(chan, tiles, diag, high)
+    spectra, stay_low = lax.optimization_barrier((spectra, stay_low))
+    move_low = shifted(merge(stay_low), "chan", 1)
     stay_high, move_high = [None] * TM, [None] * TM
     for rel in order:
         part = stack(spectra, rel, inverse)
-        if rel == 0:
-            part, move_low = lax.optimization_barrier((part, move_low))
         stay_high[rel] = shifted(part, "tm", rel) if rel else part
+        if rel == 3:
+            stay_high[rel], move_low = lax.optimization_barrier((stay_high[rel], move_low))
         move_high[rel] = shifted(stay_high[rel], "chan", 1)
     result = home(tile_slot_owner, chan, time, stay_low + stay_high)
-    return moved(tile_slot_owner, chan, time, move_low + move_high, result)
+    return moved(tile_slot_owner, chan, time, [move_low] + move_high, result)
 
 
 def solution(mesh):

time: 151 us -> 134 us (0.89); the launches traced: 150 us -> 135 us
  waiting for transfers between devices: 36.4 us -> 26.3 us
  starting transfers between devices: 24.8 us -> 20.1 us
    ppermute x21 -> x18, waiting for transfers between devices: 34.7 us -> 26.2 us  [shifted(): lax.ppermute(value, axis, [(i, (i + distance) % count) for i in range(cou...]
    ppermute x21 -> x18, starting transfers between devices: 24.3 us -> 19.1 us  [shifted(): lax.ppermute(value, axis, [(i, (i + distance) % count) for i in range(cou...]
    pallas_call x2, Pallas kernels: 20.6 us -> 18.5 us  [cross(): pl.pallas_call(cross_kernel, out_shape=jax.ShapeDtypeStruct((SOURCES // 2...]
    ppermute x2 -> x3, waiting for transfers between devices: 1.69 us -> 0.01 us  [complete(): return blocks + [lax.ppermute(other, 'chan', swap) for other in others]]
  transfers between devices with their start and end apart: 25 -> 23, of which waited for: 12 -> 12; matrix products, arithmetic and copies ran while one was open for 0% -> 0% of each run, Pallas kernels for 22% -> 23%
where the time goes in v4:
time: 134 us; the launch traced here: 135 us
  Pallas kernels  44.9 us (34%)
  blocking collectives  41.1 us (31%)
  waiting for transfers between devices  26.3 us (20%)
  starting transfers between devices  20.1 us (15%)
  local copies, waits for them, and re-layouts  2.27 us (2%)
    all_to_all x1, blocking collectives, per_device(): lax.all_to_all(slabs, ('chan', 'tm'), split_axis=0, concat_axis=0, tiled=...  41.1 us
    ppermute x18, waiting for transfers between devices, shifted(): lax.ppermute(value, axis, [(i, (i + distance) % count) for i in range(cou...  26.2 us
    ppermute x18, starting transfers between devices, shifted(): lax.ppermute(value, axis, [(i, (i + distance) % count) for i in range(cou...  19.1 us
    pallas_call x2, Pallas kernels, cross(): pl.pallas_call(cross_kernel, out_shape=jax.ShapeDtypeStruct((SOURCES // 2...  18.5 us
    pallas_call x1, Pallas kernels, whiten(): pl.pallas_call(whiten_kernel, out_shape=(shape, shape, jax.ShapeDtypeStru...  7.36 us
    pallas_call x8, Pallas kernels, stack(): pl.pallas_call(functools.partial(stack_kernel, rel), out_shape=jax.ShapeD...  5.41 us
    pallas_call x1, Pallas kernels, home(): pl.pallas_call(home_kernel, out_shape=jax.ShapeDtypeStruct((TCAP, SRC_PAR...  4.26 us
    pallas_call x1, Pallas kernels, pack(): pl.pallas_call(pack_kernel, out_shape=jax.ShapeDtypeStruct((NB * TM, ROWS...  2.98 us
  transfers between devices with their start and end apart: 23, of which 12 were waited for; matrix products, arithmetic and copies ran while one was open for 0% of the time, Pallas kernels for 23%

profile of v4, /device:TPU:0, one launch (start us, length us, event | category | flops | bytes accessed | tf_op | source)
XLA Modules:
  0.0 135.1 jit_solution(7716512535475101946)
XLA Ops:
  0.0 1.5 %copy-done.2 = bf16[4,60,4096]{2,0,1:T(4,128)(2,1)S(1)} copy-done((bf16[4,60,4096]{2,0,1:T(4,128)(2,1)S(1)}, bf16[4,60,4096]{2,0,1:T(4,128)(2,1)}, u32[]{:S(2)}) %copy-start.2) | copy-done | bytes 1966104
  1.5 0.7 copy-done.9
  2.2 3.0 %pack.1 = bf16[128,64,128]{2,1,0:T(8,128)(2,1)S(1)} custom-call(s32[1]{0:T(128)} %bitcast.own.chan, bf16[60,4,4096]{2,1,0:T(4,128)(2,1)S(1)} %bitcast.6, s32[4,128]{1,0:T(4,128)S(1)} %copy-done.9), custom_call_target="tpu_custom_call" | custom-call | tf_op jit(solution)/shard_map/pack/pallas_call | solution.py:161
  5.2 41.1 %all_to_all.5 = bf16[128,64,128]{2,1,0:T(8,128)(2,1)S(1)} all-to-all(bf16[128,64,128]{2,1,0:T(8,128)(2,1)S(1)} %pack.1), channel_id=1, replica_groups=mesh['chan'=32,'tm'=4] {'chan','tm'}, dimensions={0} | all-to-all | bytes 4194304 | tf_op jit(solution)/shard_map/all_to_all | solution.py:550
  46.4 7.4 %whiten.1 = (bf16[2,2,768,128]{3,2,1,0:T(8,128)(2,1)S(1)}, bf16[2,2,768,128]{3,2,1,0:T(8,128)(2,1)S(1)}, bf16[768,128]{1,0:T(8,128)(2,1)S(1)}) custom-call(s32[1]{0:T(128)} %bitcast.own.chan, bf16[32,4,64,128]{3,2,1,0:T(8,128)(2,1)S(1)} %bitcast.5, bf16[1536,2048]{1,0:T(8,128)(2,1)S(1)} %copy-done.1, bf16[768,768]{1,0:T(8,128)(2,1)S(1)} %copy-done.4, ...), custom_call_target="tpu_custom_call" | custom-call | tf_op jit(solution)/shard_map/whiten/pallas_call | solution.py:216
  53.7 0.4 collective-permute-start.2
  54.1 0.6 collective-permute-start
  54.7 4.7 %collective-permute-start.1 = (bf16[2,2,768,128]{3,2,1,0:T(8,128)(2,1)S(1)}, bf16[2,2,768,128]{3,2,1,0:T(8,128)(2,1)S(1)}, u32[]{:S(2)}, u32[]{:S(2)}) collective-permute-start(bf16[2,2,768,128]{3,2,1,0:T(8,128)(2,1)S(1)} %get-tuple-element.40.refs_0_), channel_id=1, source_target_pairs={{0,120},{4,124},{8,0},{12,4},{16,8},{20,12},{24,16},{28,20},{32,24... | collective-permute-start | bytes 2359304 | tf_op jit(solution)/shard_map/ppermute | solution.py:540
  59.4 1.4 %collective-permute-start.3 = (bf16[768,128]{1,0:T(8,128)(2,1)S(1)}, bf16[768,128]{1,0:T(8,128)(2,1)S(1)}, u32[]{:S(2)}, u32[]{:S(2)}) collective-permute-start(bf16[768,128]{1,0:T(8,128)(2,1)S(1)} %get-tuple-element.35.s0), channel_id=1, source_target_pairs={{0,3},{1,0},{2,1},{3,2},{4,7},{5,4},{6,5},{7,6},{8,11},{9,8},{10,9... | collective-permute-start | bytes 589832 | tf_op jit(solution)/shard_map/ppermute | solution.py:540
  60.8 1.2 collective-permute-start.4
  62.1 5.2 %collective-permute-done.3.s1 = bf16[768,128]{1,0:T(8,128)(2,1)S(1)} collective-permute-done((bf16[768,128]{1,0:T(8,128)(2,1)S(1)}, bf16[768,128]{1,0:T(8,128)(2,1)S(1)}, u32[]{:S(2)}, u32[]{:S(2)}) %collective-permute-start.3) | collective-permute-done | bytes 196640 | tf_op jit(solution)/shard_map/ppermute | solution.py:540
  67.2 3.0 %collective-permute-done.4.s2 = bf16[768,128]{1,0:T(8,128)(2,1)S(1)} collective-permute-done((bf16[768,128]{1,0:T(8,128)(2,1)S(1)}, bf16[768,128]{1,0:T(8,128)(2,1)S(1)}, u32[]{:S(2)}, u32[]{:S(2)}) %collective-permute-start.4) | collective-permute-done | bytes 196640 | tf_op jit(solution)/shard_map/ppermute | solution.py:540
  70.2 2.4 %collective-permute-start.7 = (bf16[2,2,768,128]{3,2,1,0:T(8,128)(2,1)S(1)}, bf16[2,2,768,128]{3,2,1,0:T(8,128)(2,1)S(1)}, u32[]{:S(2)}, u32[]{:S(2)}) collective-permute-start(bf16[2,2,768,128]{3,2,1,0:T(8,128)(2,1)S(1)} %get-tuple-element.46.refs_0_), channel_id=1, source_target_pairs={{0,120},{4,124},{8,0},{12,4},{16,8},{20,12},{24,16},{28,20},{32,24... | collective-permute-start | bytes 2359304 | tf_op jit(solution)/shard_map/ppermute | solution.py:540
  72.6 0.4 collective-permute-done.5.s3
  73.0 4.8 %collective-permute-done.below.refs_1_ = bf16[2,2,768,128]{3,2,1,0:T(8,128)(2,1)S(1)} collective-permute-done((bf16[2,2,768,128]{3,2,1,0:T(8,128)(2,1)S(1)}, bf16[2,2,768,128]{3,2,1,0:T(8,128)(2,1)S(1)}, u32[]{:S(2)}, u32[]{:S(2)}) %collective-permute-start) | collective-permute-done | bytes 786464 | tf_op jit(solution)/shard_map/ppermute | solution.py:540
  77.8 0.4 choose.2
  78.2 0.1 collective-permute-start.10
  78.3 0.5 collective-permute-start.9
  78.8 2.6 %diagonal.1.diag = bf16[96,256,256]{2,1,0:T(8,128)(2,1)S(1)} custom-call(bf16[768,128]{1,0:T(8,128)(2,1)S(1)} %get-tuple-element.35.s0, bf16[768,128]{1,0:T(8,128)(2,1)S(1)} %collective-permute-done.3.s1, bf16[768,128]{1,0:T(8,128)(2,1)S(1)} %collective-permute-done.4.s2, bf16[768,128]{1,0:T(8,128)(2,1)S(1)} %collective-permute-done.5.s3, ...), custom_call_target="tpu_custom_call" | custom-call | flops 1 | bytes 1 | tf_op jit(solution)/shard_map/diagonal/pallas_call | solution.py:288
  81.4 9.4 %cross.2.spectra = bf16[8,2,768,128]{3,2,1,0:T(8,128)(2,1)S(1)} custom-call(s32[1]{0:T(128)} %bitcast.own.chan, s32[2,96]{1,0:T(2,128)S(1)} %bitcast.7, bf16[96,256,256]{2,1,0:T(8,128)(2,1)S(1)} %diagonal.1.diag, bf16[384,512]{1,0:T(8,128)(2,1)S(1)} %copy-done.3, bf16[2,2,768,128]{3,2,1,0:T(8,128)(2,1)S(1)} %get-tuple-element.40.refs_0_, ...), custom_call_target="tpu_custom_call" | custom-call | flops 1 | bytes 1 | tf_op jit(solution)/shard_map/cross/pallas_call | solution.py:379
  90.8 0.7 stack.8.refs_0_
  91.5 0.7 stack.9
  92.2 0.7 stack.10
  92.9 0.7 stack.11
  93.6 0.4 collective-permute-done.6.below.refs_1_
  94.0 0.1 collective-permute-start.11
  94.1 0.7 collective-permute-start.12
  94.8 2.5 %collective-permute-start.13 = (bf16[192,512]{1,0:T(8,128)(2,1)S(1)}, bf16[192,512]{1,0:T(8,128)(2,1)S(1)}, u32[]{:S(2)}, u32[]{:S(2)}) collective-permute-start(bf16[192,512]{1,0:T(8,128)(2,1)S(1)} %stack.10), channel_id=1, source_target_pairs={{0,2},{1,3},{2,0},{3,1},{4,6},{5,7},{6,4},{7,5},{8,10},{9,11},{10,... | collective-permute-start | bytes 589832 | tf_op jit(solution)/shard_map/ppermute | solution.py:540
  97.3 0.5 collective-permute-start.14
  97.8 9.1 %cross.3.spectra = bf16[8,2,768,128]{3,2,1,0:T(8,128)(2,1)S(1)} custom-call(s32[1]{0:T(128)} %bitcast.own.chan, s32[2,96]{1,0:T(2,128)S(1)} %bitcast.8, bf16[96,256,256]{2,1,0:T(8,128)(2,1)S(1)} %diagonal.1.diag, bf16[384,512]{1,0:T(8,128)(2,1)S(1)} %copy-done.3, bf16[2,2,768,128]{3,2,1,0:T(8,128)(2,1)S(1)} %get-tuple-element.46.refs_0_, ...), custom_call_target="tpu_custom_call" | custom-call | flops 1 | bytes 1 | tf_op jit(solution)/shard_map/cross/pallas_call | solution.py:379
  106.9 0.5 collective-permute-done.14.refs_3_
  107.5 1.0 merge.1
  108.5 0.1 collective-permute-start.16
  108.6 0.7 stack.14
  109.3 1.0 collective-permute-start.18
  110.3 0.7 stack.15
  111.0 3.0 %collective-permute-start.20 = (bf16[192,512]{1,0:T(8,128)(2,1)S(1)}, bf16[192,512]{1,0:T(8,128)(2,1)S(1)}, u32[]{:S(2)}, u32[]{:S(2)}) collective-permute-start(bf16[192,512]{1,0:T(8,128)(2,1)S(1)} %stack.15), channel_id=1, source_target_pairs={{0,2},{1,3},{2,0},{3,1},{4,6},{5,7},{6,4},{7,5},{8,10},{9,11},{10,... | collective-permute-start | bytes 589832 | tf_op jit(solution)/shard_map/ppermute | solution.py:540
  114.0 0.7 stack.12
  114.7 0.8 collective-permute-start.15
  115.5 0.7 stack.13.refs_4_
  116.3 0.4 collective-permute-done.18.refs_5_
  116.7 5.4 %collective-permute-done.20.refs_6_ = bf16[192,512]{1,0:T(8,128)(2,1)S(1)} collective-permute-done((bf16[192,512]{1,0:T(8,128)(2,1)S(1)}, bf16[192,512]{1,0:T(8,128)(2,1)S(1)}, u32[]{:S(2)}, u32[]{:S(2)}) %collective-permute-start.20) | collective-permute-done | bytes 196640 | tf_op jit(solution)/shard_map/ppermute | solution.py:540
  122.1 0.2 collective-permute-done.15.refs_7_
  122.3 1.1 collective-permute-done.16.refs_0_
  123.3 4.3 %home.1.refs_5_ = f32[6,4,128,512]{3,2,1,0:T(8,128)} custom-call(s32[96]{0:T(128)S(1)} %copy-done.10, s32[1]{0:T(128)} %bitcast.own.chan, s32[1]{0:T(128)} %bitcast.1.time, bf16[192,512]{1,0:T(8,128)(2,1)S(1)} %stack.8.refs_0_, bf16[192,512]{1,0:T(8,128)(2,1)S(1)} %collective-permute-done.12.refs_1_, bf16[192,512]{1,0:T(8,128)(2,1)S(1)} %collective-permute-done.13.refs_2_, ...), custom_call_target="tpu_custom_call" | custom-call | flops 1 | bytes 1 | tf_op jit(solution)/shard_map/home/pallas_call | solution.py:481
  127.6 2.9 %collective-permute-done.21.refs_3_ = bf16[192,512]{1,0:T(8,128)(2,1)S(1)} collective-permute-done((bf16[192,512]{1,0:T(8,128)(2,1)S(1)}, bf16[192,512]{1,0:T(8,128)(2,1)S(1)}, u32[]{:S(2)}, u32[]{:S(2)}) %collective-permute-start.21) | collective-permute-done | bytes 196640 | tf_op jit(solution)/shard_map/ppermute | solution.py:540
  130.5 2.1 %collective-permute-done.22.refs_4_ = bf16[192,512]{1,0:T(8,128)(2,1)S(1)} collective-permute-done((bf16[192,512]{1,0:T(8,128)(2,1)S(1)}, bf16[192,512]{1,0:T(8,128)(2,1)S(1)}, u32[]{:S(2)}, u32[]{:S(2)}) %collective-permute-start.22) | collective-permute-done | bytes 196640 | tf_op jit(solution)/shard_map/ppermute | solution.py:540
  132.6 2.3 %moved.1 = f32[6,4,128,512]{3,2,1,0:T(8,128)} custom-call(s32[96]{0:T(128)S(1)} %copy-done.10, s32[1]{0:T(128)} %bitcast.own.chan, s32[1]{0:T(128)} %bitcast.1.time, bf16[768,512]{1,0:T(8,128)(2,1)S(1)} %collective-permute-done.16.refs_0_, bf16[192,512]{1,0:T(8,128)(2,1)S(1)} %collective-permute-done.17.refs_1_, ...), custom_call_target="tpu_custom_call", output_to_operand_aliasing={{}: (8, {})} | custom-call | flops 1 | bytes 1 | tf_op jit(solution)/shard_map/moved/pallas_call | solution.py:520
  (39 shorter events, 0.2 us)
Async XLA Ops:
  0.0 1.5 %copy-start.2 = (bf16[4,60,4096]{2,0,1:T(4,128)(2,1)S(1)}, bf16[4,60,4096]{2,0,1:T(4,128)(2,1)}, u32[]{:S(2)}) copy-start(bf16[4,60,4096]{2,0,1:T(4,128)(2,1)} %param.12) | copy-start | bytes 5898244
  1.5 0.7 copy-start.9
  2.2 44.1 %copy-start.1 = (bf16[1536,2048]{1,0:T(8,128)(2,1)S(1)}, bf16[1536,2048]{1,0:T(8,128)(2,1)}, u32[]{:S(2)}) copy-start(bf16[1536,2048]{1,0:T(8,128)(2,1)} %constant.23.clone.table) | copy-start | bytes 18874372
  2.2 44.1 %copy-start.4 = (bf16[768,768]{1,0:T(8,128)(2,1)S(1)}, bf16[768,768]{1,0:T(8,128)(2,1)}, u32[]{:S(2)}) copy-start(bf16[768,768]{1,0:T(8,128)(2,1)} %constant.24.clone.inside) | copy-start | bytes 3538948
  2.2 44.1 %copy-start.5 = (f32[768,1]{1,0:T(8,128)S(1)}, f32[768,1]{1,0:T(8,128)}, u32[]{:S(2)}) copy-start(f32[768,1]{1,0:T(8,128)} %constant.25.clone.inverse_count) | copy-start | bytes 9220
  2.2 44.1 %copy-start.6 = (bf16[4,2,128,128]{3,2,1,0:T(8,128)(2,1)S(1)}, bf16[4,2,128,128]{3,2,1,0:T(8,128)(2,1)}, u32[]{:S(2)}) copy-start(bf16[4,2,128,128]{3,2,1,0:T(8,128)(2,1)} %constant.26.clone.pick) | copy-start | bytes 786436
  46.4 32.4 %copy-start.7 = (bf16[4,128,256]{2,1,0:T(8,128)(2,1)S(1)}, bf16[4,128,256]{2,1,0:T(8,128)(2,1)}, u32[]{:S(2)}) copy-start(bf16[4,128,256]{2,1,0:T(8,128)(2,1)} %constant.27.clone.spread) | copy-start | bytes 786436
  53.7 8.4 %collective-permute-start.2 = (bf16[2,2,768,128]{3,2,1,0:T(8,128)(2,1)S(1)}, bf16[2,2,768,128]{3,2,1,0:T(8,128)(2,1)S(1)}, u32[]{:S(2)}, u32[]{:S(2)}) collective-permute-start(bf16[2,2,768,128]{3,2,1,0:T(8,128)(2,1)S(1)} %get-tuple-element.40.refs_0_), channel_id=1, source_target_pairs={{0,4},{4,0},{8,12},{12,8},{16,20},{20,16},{24,28},{28,24},{32,36},... | collective-permute-start | bytes 2359304 | tf_op jit(solution)/shard_map/ppermute | solution.py:555
  54.1 23.7 %collective-permute-start = (bf16[2,2,768,128]{3,2,1,0:T(8,128)(2,1)S(1)}, bf16[2,2,768,128]{3,2,1,0:T(8,128)(2,1)S(1)}, u32[]{:S(2)}, u32[]{:S(2)}) collective-permute-start(bf16[2,2,768,128]{3,2,1,0:T(8,128)(2,1)S(1)} %get-tuple-element.40.refs_0_), channel_id=1, source_target_pairs={{0,8},{4,12},{8,16},{12,20},{16,24},{20,28},{24,32},{28,36},{32,40... | collective-permute-start | bytes 2359304 | tf_op jit(solution)/shard_map/ppermute | solution.py:540
  54.7 23.1 %collective-permute-start.1 = (bf16[2,2,768,128]{3,2,1,0:T(8,128)(2,1)S(1)}, bf16[2,2,768,128]{3,2,1,0:T(8,128)(2,1)S(1)}, u32[]{:S(2)}, u32[]{:S(2)}) collective-permute-start(bf16[2,2,768,128]{3,2,1,0:T(8,128)(2,1)S(1)} %get-tuple-element.40.refs_0_), channel_id=1, source_target_pairs={{0,120},{4,124},{8,0},{12,4},{16,8},{20,12},{24,16},{28,20},{32,24... | collective-permute-start | bytes 2359304 | tf_op jit(solution)/shard_map/ppermute | solution.py:540
  59.4 7.8 %collective-permute-start.3 = (bf16[768,128]{1,0:T(8,128)(2,1)S(1)}, bf16[768,128]{1,0:T(8,128)(2,1)S(1)}, u32[]{:S(2)}, u32[]{:S(2)}) collective-permute-start(bf16[768,128]{1,0:T(8,128)(2,1)S(1)} %get-tuple-element.35.s0), channel_id=1, source_target_pairs={{0,3},{1,0},{2,1},{3,2},{4,7},{5,4},{6,5},{7,6},{8,11},{9,8},{10,9... | collective-permute-start | bytes 589832 | tf_op jit(solution)/shard_map/ppermute | solution.py:540
  60.8 9.4 %collective-permute-start.4 = (bf16[768,128]{1,0:T(8,128)(2,1)S(1)}, bf16[768,128]{1,0:T(8,128)(2,1)S(1)}, u32[]{:S(2)}, u32[]{:S(2)}) collective-permute-start(bf16[768,128]{1,0:T(8,128)(2,1)S(1)} %get-tuple-element.35.s0), channel_id=1, source_target_pairs={{0,2},{1,3},{2,0},{3,1},{4,6},{5,7},{6,4},{7,5},{8,10},{9,11},{10,... | collective-permute-start | bytes 589832 | tf_op jit(solution)/shard_map/ppermute | solution.py:540
  62.1 10.9 %collective-permute-start.5 = (bf16[768,128]{1,0:T(8,128)(2,1)S(1)}, bf16[768,128]{1,0:T(8,128)(2,1)S(1)}, u32[]{:S(2)}, u32[]{:S(2)}) collective-permute-start(bf16[768,128]{1,0:T(8,128)(2,1)S(1)} %get-tuple-element.35.s0), channel_id=1, source_target_pairs={{0,1},{1,2},{2,3},{3,0},{4,5},{5,6},{6,7},{7,4},{8,9},{9,10},{10,1... | collective-permute-start | bytes 589832 | tf_op jit(solution)/shard_map/ppermute | solution.py:540
  67.2 26.7 %collective-permute-start.6 = (bf16[2,2,768,128]{3,2,1,0:T(8,128)(2,1)S(1)}, bf16[2,2,768,128]{3,2,1,0:T(8,128)(2,1)S(1)}, u32[]{:S(2)}, u32[]{:S(2)}) collective-permute-start(bf16[2,2,768,128]{3,2,1,0:T(8,128)(2,1)S(1)} %get-tuple-element.46.refs_0_), channel_id=1, source_target_pairs={{0,8},{4,12},{8,16},{12,20},{16,24},{20,28},{24,32},{28,36},{32,40... | collective-permute-start | bytes 2359304 | tf_op jit(solution)/shard_map/ppermute | solution.py:540
  70.2 23.7 %collective-permute-start.7 = (bf16[2,2,768,128]{3,2,1,0:T(8,128)(2,1)S(1)}, bf16[2,2,768,128]{3,2,1,0:T(8,128)(2,1)S(1)}, u32[]{:S(2)}, u32[]{:S(2)}) collective-permute-start(bf16[2,2,768,128]{3,2,1,0:T(8,128)(2,1)S(1)} %get-tuple-element.46.refs_0_), channel_id=1, source_target_pairs={{0,120},{4,124},{8,0},{12,4},{16,8},{20,12},{24,16},{28,20},{32,24... | collective-permute-start | bytes 2359304 | tf_op jit(solution)/shard_map/ppermute | solution.py:540
  73.0 21.0 %collective-permute-start.8 = (bf16[2,2,768,128]{3,2,1,0:T(8,128)(2,1)S(1)}, bf16[2,2,768,128]{3,2,1,0:T(8,128)(2,1)S(1)}, u32[]{:S(2)}, u32[]{:S(2)}) collective-permute-start(bf16[2,2,768,128]{3,2,1,0:T(8,128)(2,1)S(1)} %get-tuple-element.46.refs_0_), channel_id=1, source_target_pairs={{0,4},{4,0},{8,12},{12,8},{16,20},{20,16},{24,28},{28,24},{32,36},... | collective-permute-start | bytes 2359304 | tf_op jit(solution)/shard_map/ppermute | solution.py:555
  78.2 3.2 %collective-permute-start.10 = (bf16[1,2,768,128]{3,2,1,0:T(8,128)(2,1)S(1)}, bf16[1,2,768,128]{3,2,1,0:T(8,128)(2,1)S(1)}, u32[]{:S(2)}, u32[]{:S(2)}) collective-permute-start(bf16[1,2,768,128]{3,2,1,0:T(8,128)(2,1)S(1)} %get-tuple-element.45), channel_id=1, source_target_pairs={{0,4},{4,0},{8,12},{12,8},{16,20},{20,16},{24,28},{28,24},{32,36},... | collective-permute-start | bytes 1179656 | tf_op jit(solution)/shard_map/ppermute | solution.py:560
  78.3 3.1 %copy-start.3 = (bf16[384,512]{1,0:T(8,128)(2,1)S(1)}, bf16[384,512]{1,0:T(8,128)(2,1)}, u32[]{:S(2)}) copy-start(bf16[384,512]{1,0:T(8,128)(2,1)} %constant.28.clone.order) | copy-start | bytes 1179652
  78.3 3.1 %copy-start.8 = (s32[96,2]{0,1:T(2,128)S(1)}, s32[96,2]{0,1:T(2,128)}, u32[]{:S(2)}) copy-start(s32[96,2]{0,1:T(2,128)} %param.14) | copy-start | bytes 2308
  78.3 3.1 %collective-permute-start.9 = (bf16[1,2,768,128]{3,2,1,0:T(8,128)(2,1)S(1)}, bf16[1,2,768,128]{3,2,1,0:T(8,128)(2,1)S(1)}, u32[]{:S(2)}, u32[]{:S(2)}) collective-permute-start(bf16[1,2,768,128]{3,2,1,0:T(8,128)(2,1)S(1)} %get-tuple-element.44), channel_id=1, source_target_pairs={{0,4},{4,0},{8,12},{12,8},{16,20},{20,16},{24,28},{28,24},{32,36},... | collective-permute-start | bytes 1179656 | tf_op jit(solution)/shard_map/ppermute | solution.py:560
  81.4 9.4 %copy-start = (bf16[512,1536]{1,0:T(8,128)(2,1)S(1)}, bf16[512,1536]{1,0:T(8,128)(2,1)}, u32[]{:S(2)}) copy-start(bf16[512,1536]{1,0:T(8,128)(2,1)} %constant.29.clone.inverse) | copy-start | bytes 4718596
  94.0 3.8 %collective-permute-start.11 = (bf16[2,2,768,128]{3,2,1,0:T(8,128)(2,1)S(1)}, bf16[2,2,768,128]{3,2,1,0:T(8,128)(2,1)S(1)}, u32[]{:S(2)}, u32[]{:S(2)}) collective-permute-start(bf16[2,2,768,128]{3,2,1,0:T(8,128)(2,1)S(1)} %choose.3), channel_id=1, source_target_pairs={{0,4},{4,0},{8,12},{12,8},{16,20},{20,16},{24,28},{28,24},{32,36},... | collective-permute-start | bytes 2359304 | tf_op jit(solution)/shard_map/ppermute | solution.py:560
  94.1 12.8 %collective-permute-start.12 = (bf16[192,512]{1,0:T(8,128)(2,1)S(1)}, bf16[192,512]{1,0:T(8,128)(2,1)S(1)}, u32[]{:S(2)}, u32[]{:S(2)}) collective-permute-start(bf16[192,512]{1,0:T(8,128)(2,1)S(1)} %stack.9), channel_id=1, source_target_pairs={{0,1},{1,2},{2,3},{3,0},{4,5},{5,6},{6,7},{7,4},{8,9},{9,10},{10,1... | collective-permute-start | bytes 589832 | tf_op jit(solution)/shard_map/ppermute | solution.py:540
  94.8 12.2 %collective-permute-start.13 = (bf16[192,512]{1,0:T(8,128)(2,1)S(1)}, bf16[192,512]{1,0:T(8,128)(2,1)S(1)}, u32[]{:S(2)}, u32[]{:S(2)}) collective-permute-start(bf16[192,512]{1,0:T(8,128)(2,1)S(1)} %stack.10), channel_id=1, source_target_pairs={{0,2},{1,3},{2,0},{3,1},{4,6},{5,7},{6,4},{7,5},{8,10},{9,11},{10,... | collective-permute-start | bytes 589832 | tf_op jit(solution)/shard_map/ppermute | solution.py:540
  97.3 10.2 %collective-permute-start.14 = (bf16[192,512]{1,0:T(8,128)(2,1)S(1)}, bf16[192,512]{1,0:T(8,128)(2,1)S(1)}, u32[]{:S(2)}, u32[]{:S(2)}) collective-permute-start(bf16[192,512]{1,0:T(8,128)(2,1)S(1)} %stack.11), channel_id=1, source_target_pairs={{0,3},{1,0},{2,1},{3,2},{4,7},{5,4},{6,5},{7,6},{8,11},{9,8},{10,9... | collective-permute-start | bytes 589832 | tf_op jit(solution)/shard_map/ppermute | solution.py:540
  108.5 14.8 %collective-permute-start.16 = (bf16[768,512]{1,0:T(8,128)(2,1)S(1)}, bf16[768,512]{1,0:T(8,128)(2,1)S(1)}, u32[]{:S(2)}, u32[]{:S(2)}) collective-permute-start(bf16[768,512]{1,0:T(8,128)(2,1)S(1)} %merge.1), channel_id=1, source_target_pairs={{0,4},{4,8},{8,12},{12,16},{16,20},{20,24},{24,28},{28,32},{32,36}... | collective-permute-start | bytes 2359304 | tf_op jit(solution)/shard_map/ppermute | solution.py:540
  109.3 7.4 %collective-permute-start.18 = (bf16[192,512]{1,0:T(8,128)(2,1)S(1)}, bf16[192,512]{1,0:T(8,128)(2,1)S(1)}, u32[]{:S(2)}, u32[]{:S(2)}) collective-permute-start(bf16[192,512]{1,0:T(8,128)(2,1)S(1)} %stack.14), channel_id=1, source_target_pairs={{0,1},{1,2},{2,3},{3,0},{4,5},{5,6},{6,7},{7,4},{8,9},{9,10},{10,1... | collective-permute-start | bytes 589832 | tf_op jit(solution)/shard_map/ppermute | solution.py:540
  111.0 11.1 %collective-permute-start.20 = (bf16[192,512]{1,0:T(8,128)(2,1)S(1)}, bf16[192,512]{1,0:T(8,128)(2,1)S(1)}, u32[]{:S(2)}, u32[]{:S(2)}) collective-permute-start(bf16[192,512]{1,0:T(8,128)(2,1)S(1)} %stack.15), channel_id=1, source_target_pairs={{0,2},{1,3},{2,0},{3,1},{4,6},{5,7},{6,4},{7,5},{8,10},{9,11},{10,... | collective-permute-start | bytes 589832 | tf_op jit(solution)/shard_map/ppermute | solution.py:540
  114.7 8.6 %copy-start.10 = (s32[96]{0:T(128)S(1)}, s32[96]{0:T(128)}, u32[]{:S(2)}) copy-start(s32[96]{0:T(128)} %owners.3) | copy-start | bytes 1156
  114.7 7.5 %collective-permute-start.15 = (bf16[192,512]{1,0:T(8,128)(2,1)S(1)}, bf16[192,512]{1,0:T(8,128)(2,1)S(1)}, u32[]{:S(2)}, u32[]{:S(2)}) collective-permute-start(bf16[192,512]{1,0:T(8,128)(2,1)S(1)} %stack.12), channel_id=1, source_target_pairs={{0,3},{1,0},{2,1},{3,2},{4,7},{5,4},{6,5},{7,6},{8,11},{9,8},{10,9... | collective-permute-start | bytes 589832 | tf_op jit(solution)/shard_map/ppermute | solution.py:540
  116.2 11.4 %collective-permute-start.17 = (bf16[192,512]{1,0:T(8,128)(2,1)S(1)}, bf16[192,512]{1,0:T(8,128)(2,1)S(1)}, u32[]{:S(2)}, u32[]{:S(2)}) collective-permute-start(bf16[192,512]{1,0:T(8,128)(2,1)S(1)} %stack.13.refs_4_), channel_id=1, source_target_pairs={{0,4},{4,8},{8,12},{12,16},{16,20},{20,24},{24,28},{28,32},{32,36}... | collective-permute-start | bytes 589832 | tf_op jit(solution)/shard_map/ppermute | solution.py:540
  116.7 10.9 %collective-permute-start.19 = (bf16[192,512]{1,0:T(8,128)(2,1)S(1)}, bf16[192,512]{1,0:T(8,128)(2,1)S(1)}, u32[]{:S(2)}, u32[]{:S(2)}) collective-permute-start(bf16[192,512]{1,0:T(8,128)(2,1)S(1)} %collective-permute-done.18.refs_5_), channel_id=1, source_target_pairs={{0,4},{4,8},{8,12},{12,16},{16,20},{20,24},{24,28},{28,32},{32,36}... | collective-permute-start | bytes 589832 | tf_op jit(solution)/shard_map/ppermute | solution.py:540
  122.1 8.4 %collective-permute-start.21 = (bf16[192,512]{1,0:T(8,128)(2,1)S(1)}, bf16[192,512]{1,0:T(8,128)(2,1)S(1)}, u32[]{:S(2)}, u32[]{:S(2)}) collective-permute-start(bf16[192,512]{1,0:T(8,128)(2,1)S(1)} %collective-permute-done.20.refs_6_), channel_id=1, source_target_pairs={{0,4},{4,8},{8,12},{12,16},{16,20},{20,24},{24,28},{28,32},{32,36}... | collective-permute-start | bytes 589832 | tf_op jit(solution)/shard_map/ppermute | solution.py:540
  123.3 9.3 %collective-permute-start.22 = (bf16[192,512]{1,0:T(8,128)(2,1)S(1)}, bf16[192,512]{1,0:T(8,128)(2,1)S(1)}, u32[]{:S(2)}, u32[]{:S(2)}) collective-permute-start(bf16[192,512]{1,0:T(8,128)(2,1)S(1)} %collective-permute-done.15.refs_7_), channel_id=1, source_target_pairs={{0,4},{4,8},{8,12},{12,16},{16,20},{20,24},{24,28},{28,32},{32,36}... | collective-permute-start | bytes 589832 | tf_op jit(solution)/shard_map/ppermute | solution.py:540

commit v5 on v4

--- a/solution.py
+++ b/solution.py
@@ -177,54 +177,47 @@
     )(own, records.transpose(1, 0, 2), quality)
 
 
-def whiten_kernel(own, slabs, table, inside, inverse_count, pick, low, high, sources, total):
-    step = pl.program_id(0)
-    lanes = []
-    for i in range(PAIR):
-        marks = slabs[pl.ds(own[0], 1), i, pl.ds(48, 16), :][0, SLAB - 48 : SLAB - 47, :]
-        lanes.append(slabs[:, i].reshape(NB * ROWS, BLOCK) * marks)
-    x = jnp.concatenate(lanes, axis=1)
-    spectrum = jnp.dot(table[...], x, preferred_element_type=F32)
-    re = spectrum[:F]
-    im = spectrum[F:]
-    magnitude = jnp.sqrt(re * re + im * im).astype(BF16)
-    level = jnp.dot(inside[...], magnitude, preferred_element_type=F32) * inverse_count[...]
-    inverse_level = 1.0 / (level + 1e-6)
-
-    @pl.when(step == 0)
-    def _():
-        total[...] = jnp.zeros_like(total)
-
+def whiten_kernel(own, slabs, table, inside, inverse_count, pick, low, high, sources):
     first = lax.broadcasted_iota(jnp.int32, (F, LANES), 1) < LANES // 2
-    for half, part in ((0, re), (1, im)):
-        value = part * inverse_level
-        pair = [value[:, i * BLOCK : (i + 1) * BLOCK] for i in range(PAIR)]
-        turned = [pltpu.roll(one, LANES // 2, 1) for one in pair]
-        low[0, half] = jnp.where(first, pair[0], turned[1]).astype(BF16)
-        high[0, half] = jnp.where(first, turned[0], pair[1]).astype(BF16)
+    total = jnp.zeros((F, LANES), F32)
+    spectra = []
+    for step in range(PARTS):
+        lanes = []
         for i in range(PAIR):
-            total[...] += jnp.dot(
-                pair[i].astype(BF16), pick[step * PAIR + i, half], preferred_element_type=F32
-            )
-    sources[...] = total[...].astype(BF16)
+            at = step * PAIR + i
+            marks = slabs[pl.ds(own[0], 1), at, pl.ds(48, 16), :][0, SLAB - 48 : SLAB - 47, :]
+            lanes.append(slabs[:, at].reshape(NB * ROWS, BLOCK) * marks)
+        x = jnp.concatenate(lanes, axis=1)
+        spectra.append(jnp.dot(table[...], x, preferred_element_type=F32))
+    for step, spectrum in enumerate(spectra):
+        re = spectrum[:F]
+        im = spectrum[F:]
+        magnitude = jnp.sqrt(re * re + im * im).astype(BF16)
+        level = jnp.dot(inside[...], magnitude, preferred_element_type=F32) * inverse_count[...]
+        inverse_level = 1.0 / (level + 1e-6)
+        for half, part in ((0, re), (1, im)):
+            value = part * inverse_level
+            pair = [value[:, i * BLOCK : (i + 1) * BLOCK] for i in range(PAIR)]
+            turned = [pltpu.roll(one, LANES // 2, 1) for one in pair]
+            low[step, half] = jnp.where(first, pair[0], turned[1]).astype(BF16)
+            high[step, half] = jnp.where(first, turned[0], pair[1]).astype(BF16)
+            for i in range(PAIR):
+                total += jnp.dot(
+                    pair[i].astype(BF16), pick[step * PAIR + i, half], preferred_element_type=F32
+                )
+    sources[...] = total.astype(BF16)
 
 
 def whiten(own, slabs):
     inside, inverse_count = smoothing()
-    shape = jax.ShapeDtypeStruct((TM // PAIR, 2, F, LANES), BF16)
-    spec = pl.BlockSpec((1, 2, F, LANES), lambda i, own: (i, 0, 0, 0))
+    shape = jax.ShapeDtypeStruct((PARTS, 2, F, LANES), BF16)
     return pl.pallas_call(
         whiten_kernel,
         out_shape=(shape, shape, jax.ShapeDtypeStruct((F, LANES), BF16)),
-        grid_spec=pltpu.PrefetchScalarGridSpec(
-            num_scalar_prefetch=1,
-            grid=(TM // PAIR,),
-            in_specs=[pl.BlockSpec((NB, PAIR, ROWS, BLOCK), lambda i, own: (0, i, 0, 0))]
-            + [pl.BlockSpec(memory_space=pltpu.VMEM)] * 4,
-            out_specs=(spec, spec, pl.BlockSpec((F, LANES), lambda i, own: (0, 0))),
-            scratch_shapes=[pltpu.VMEM((F, LANES), F32)],
-        ),
-        compiler_params=pltpu.CompilerParams(vmem_limit_bytes=20 * MIB),
+        in_specs=[pl.BlockSpec(memory_space=pltpu.SMEM)]
+        + [pl.BlockSpec(memory_space=pltpu.VMEM)] * 5,
+        out_specs=[pl.BlockSpec(memory_space=pltpu.VMEM)] * 3,
+        compiler_params=pltpu.CompilerParams(vmem_limit_bytes=24 * MIB),
         name="whiten",
     )(own, slabs.reshape(NB, TM, ROWS, BLOCK), forward_table(), inside, inverse_count, source_lanes())
 
@@ -262,35 +255,25 @@
 
 
 def diagonal_kernel(s0, s1, s2, s3, spread, out):
-    rows = STEP
-    groups = rows // GROUP
-    place = pl.ds(pl.program_id(0) * groups, groups)
-    row = lax.broadcasted_iota(jnp.int32, (rows, 2 * LANES), 0)
-    lane = lax.broadcasted_iota(jnp.int32, (rows, 2 * LANES), 1)
+    row = lax.broadcasted_iota(jnp.int32, (F, 2 * LANES), 0)
+    lane = lax.broadcasted_iota(jnp.int32, (F, 2 * LANES), 1)
     keep = jnp.bitwise_and(row, GROUP - 1) == jnp.bitwise_and(lane, GROUP - 1)
     for rel, ref in enumerate((s0, s1, s2, s3)):
         for pair in range(SRC_PART // 2):
-            same, turned = [], []
+            wides = []
             for v in (2 * pair, 2 * pair + 1):
                 wide = jnp.dot(ref[...], spread[v], preferred_element_type=F32)
                 wide = jnp.where(keep, wide, 0.0)
-                swap = jnp.concatenate([-wide[:, LANES:], wide[:, :LANES]], axis=1)
-                same.append(wide.reshape(groups, GROUP, 2 * LANES))
-                turned.append(swap.reshape(groups, GROUP, 2 * LANES))
+                wides.append(wide.reshape(F // GROUP, GROUP, 2 * LANES))
             at = (rel * SRC_PART + 2 * pair) * GROUP
-            out[place, at : at + 2 * GROUP, :] = jnp.concatenate(same, axis=1).astype(BF16)
-            at += SOURCES * GROUP
-            out[place, at : at + 2 * GROUP, :] = jnp.concatenate(turned, axis=1).astype(BF16)
+            out[:, at : at + 2 * GROUP, :] = jnp.concatenate(wides, axis=1).astype(BF16)
 
 
 def diagonal(sources):
-    wide = 2 * SOURCES * GROUP
     return pl.pallas_call(
         diagonal_kernel,
-        out_shape=jax.ShapeDtypeStruct((F // GROUP, wide, 2 * LANES), BF16),
-        grid=(F // STEP,),
-        in_specs=[pl.BlockSpec((STEP, LANES), lambda g: (g, 0))] * TM
-        + [pl.BlockSpec(memory_space=pltpu.VMEM)],
+        out_shape=jax.ShapeDtypeStruct((F // GROUP, SOURCES * GROUP, 2 * LANES), BF16),
+        in_specs=[pl.BlockSpec(memory_space=pltpu.VMEM)] * (TM + 1),
         out_specs=pl.BlockSpec(memory_space=pltpu.VMEM),
         compiler_params=pltpu.CompilerParams(vmem_limit_bytes=20 * MIB),
         cost_estimate=pl.CostEstimate(flops=1, bytes_accessed=1, transcendentals=0),
@@ -345,28 +328,35 @@
     count = PAIR * SEG_DEV
     left = lax.broadcasted_iota(jnp.int32, (STEP, LANES), 1) < LANES // 2
     for i in range(TM // PAIR):
-        for half in range(2):
-            at = (i * 2 + half) * STEP
-            for s in range(0, count, 2):
-                one = y[at : at + STEP, s * LANES // 2 : s * LANES // 2 + LANES]
-                turned = pltpu.roll(one, LANES // 2, 1)
-                index = half * SEGS + i * count + s
-                wide[index] = jnp.where(left, one, turned)
-                wide[index + 1] = jnp.where(left, turned, one)
+        at = i * 2 * STEP
+        for s in range(0, count, 2):
+            lanes = slice(s * LANES // 2, s * LANES // 2 + LANES)
+            re = y[at : at + STEP, lanes]
+            im = y[at + STEP : at + 2 * STEP, lanes]
+            re_turned = pltpu.roll(re, LANES // 2, 1)
+            im_turned = pltpu.roll(im, LANES // 2, 1)
+            index = i * count + s
+            wide[index] = jnp.where(left, re, im_turned)
+            wide[index + 1] = jnp.where(left, re_turned, im)
+            wide[SEGS + index] = jnp.where(left, im, -re_turned)
+            wide[SEGS + index + 1] = jnp.where(left, im_turned, -re)
     first = lax.broadcasted_iota(jnp.int32, (1, GROUP, LANES), 2) < LANES // 2
 
     def group(pair, carry):
-        outs = []
+        parts = [], []
         for g in range(2):
             at = pl.multiple_of((pair * 2 + g) * GROUP, GROUP)
             b = wide[:, pl.ds(at, GROUP), :].reshape(2 * SEGS * GROUP, LANES).astype(BF16)
-            o = jnp.dot(diag[step * (STEP // GROUP) + pair * 2 + g], b, preferred_element_type=F32)
-            o = o.reshape(SOURCES, 2, GROUP, LANES)
-            outs.append(jnp.where(first, o[:, 0], o[:, 1]))
-        both = jnp.concatenate(outs, axis=1).astype(BF16)
+            o = jnp.dot(
+                diag[step * (STEP // GROUP) + pair * 2 + g], b, preferred_element_type=F32
+            )
+            turned = pltpu.roll(o, LANES // 2, 1).reshape(SOURCES // 2, 2, GROUP, LANES)
+            o = o.reshape(SOURCES // 2, 2, GROUP, LANES)
+            parts[0].append(jnp.where(first, o[:, 0], turned[:, 1]))
+            parts[1].append(jnp.where(first, turned[:, 0], o[:, 1]))
         rows = pl.ds(pl.multiple_of(step * STEP + pair * 2 * GROUP, 2 * GROUP), 2 * GROUP)
-        out[:, 0, rows, :] = both[: SOURCES // 2]
-        out[:, 1, rows, :] = both[SOURCES // 2 :]
+        for half in range(2):
+            out[:, half, rows, :] = jnp.concatenate(parts[half], axis=1).astype(BF16)
         return carry
 
     lax.fori_loop(0, STEP // (2 * GROUP), group, 0, unroll=UNROLL)
@@ -397,29 +387,30 @@
     )(chan, tiles, diag, tile_lanes(), *receivers)
 
 
-def stack_kernel(rel, spectra, inverse, out):
-    first = rel * SRC_PART // 2
-    x = jnp.concatenate(
-        [spectra[first + pair].reshape(2 * F, LANES) for pair in range(SRC_PART // 2)], axis=1
-    )
-    y = jnp.dot(inverse[...], x, preferred_element_type=F32)
-    for pair in range(SRC_PART // 2):
-        value = y[:, pair * LANES : (pair + 1) * LANES].T.astype(BF16)
-        for v in range(2):
-            for t in range(TPS):
-                at = (t * SRC_PART + 2 * pair + v) * HALF_PART
-                row = v * (LANES // 2) + t * HALF_PART
-                out[at : at + HALF_PART, :] = value[row : row + HALF_PART, :]
-
-
-def stack(spectra, rel, inverse):
+def stack_kernel(rels, spectra, inverse, *outs):
+    for rel, out in zip(rels, outs):
+        first = rel * SRC_PART // 2
+        x = jnp.concatenate(
+            [spectra[first + pair].reshape(2 * F, LANES) for pair in range(SRC_PART // 2)], axis=1
+        )
+        y = jnp.dot(inverse[...], x, preferred_element_type=F32)
+        for pair in range(SRC_PART // 2):
+            value = y[:, pair * LANES : (pair + 1) * LANES].T.astype(BF16)
+            for v in range(2):
+                for t in range(TPS):
+                    at = (t * SRC_PART + 2 * pair + v) * HALF_PART
+                    row = v * (LANES // 2) + t * HALF_PART
+                    out[at : at + HALF_PART, :] = value[row : row + HALF_PART, :]
+
+
+def stack(spectra, rels, inverse):
     rows = TPS * SRC_PART * HALF_PART
     return pl.pallas_call(
-        functools.partial(stack_kernel, rel),
-        out_shape=jax.ShapeDtypeStruct((rows, LAG_COUNT), BF16),
+        functools.partial(stack_kernel, rels),
+        out_shape=[jax.ShapeDtypeStruct((rows, LAG_COUNT), BF16)] * len(rels),
         in_specs=[pl.BlockSpec(memory_space=pltpu.VMEM)] * 2,
-        out_specs=pl.BlockSpec(memory_space=pltpu.VMEM),
-        compiler_params=pltpu.CompilerParams(vmem_limit_bytes=10 * MIB),
+        out_specs=[pl.BlockSpec(memory_space=pltpu.VMEM)] * len(rels),
+        compiler_params=pltpu.CompilerParams(vmem_limit_bytes=12 * MIB),
         cost_estimate=pl.CostEstimate(flops=1, bytes_accessed=1, transcendentals=0),
         name="stack",
     )(spectra, inverse)
@@ -567,7 +558,7 @@
     low, sources = lax.optimization_barrier((low, sources))
     diag = diagonal(sources)
     spectra = cross(chan, tiles, diag, complete(low, 2))
-    parts = [stack(spectra, rel, inverse) for rel in range(TM)]
+    parts = stack(spectra, tuple(range(TM)), inverse)
     stay_low = [shifted(part, "tm", rel) if rel else part for rel, part in enumerate(parts)]
     high, _ = lax.optimization_barrier((high, parts))
     high = complete(high, 1)
@@ -576,9 +567,9 @@
     move_low = shifted(merge(stay_low), "chan", 1)
     stay_high, move_high = [None] * TM, [None] * TM
     for rel in order:
-        part = stack(spectra, rel, inverse)
+        (part,) = stack(spectra, (rel,), inverse)
         stay_high[rel] = shifted(part, "tm", rel) if rel else part
-        if rel == 3:
+        if rel == 2:
             stay_high[rel], move_low = lax.optimization_barrier((stay_high[rel], move_low))
         move_high[rel] = shifted(stay_high[rel], "chan", 1)
     result = home(tile_slot_owner, chan, time, stay_low + stay_high)

time: 134 us -> 132 us (0.985); the launches traced: 135 us -> 131 us
  Pallas kernels: 44.9 us -> 38.3 us
  waiting for transfers between devices: 26.3 us -> 29.9 us
    ppermute x18, waiting for transfers between devices: 26.2 us -> 29.9 us  [shifted(): lax.ppermute(value, axis, [(i, (i + distance) % count) for i in range(cou...]
    pallas_call x2, Pallas kernels: 18.5 us -> 16.2 us  [cross(): pl.pallas_call(cross_kernel, out_shape=jax.ShapeDtypeStruct((SOURCES // 2...]
    pallas_call x1, Pallas kernels: 2.31 us -> 0.61 us  [moved(): pl.pallas_call(moved_kernel, out_shape=jax.ShapeDtypeStruct(result.shape,...]
    pallas_call x8 -> x5, Pallas kernels: 5.41 us -> 4.72 us  [stack(): pl.pallas_call(functools.partial(stack_kernel, rels), out_shape=[jax.Shap...]
  transfers between devices with their start and end apart: 23 -> 23, of which waited for: 12 -> 13; matrix products, arithmetic and copies ran while one was open for 0% -> 0% of each run, Pallas kernels for 23% -> 21%
where the time goes in v5:
time: 132 us; the launch traced here: 131 us
  blocking collectives  41.1 us (31%)
  Pallas kernels  38.3 us (29%)
  waiting for transfers between devices  29.9 us (23%)
  starting transfers between devices  19.4 us (15%)
  local copies, waits for them, and re-layouts  2.27 us (2%)
    all_to_all x1, blocking collectives, per_device(): lax.all_to_all(slabs, ('chan', 'tm'), split_axis=0, concat_axis=0, tiled=...  41.1 us
    ppermute x18, waiting for transfers between devices, shifted(): lax.ppermute(value, axis, [(i, (i + distance) % count) for i in range(cou...  29.9 us
    ppermute x18, starting transfers between devices, shifted(): lax.ppermute(value, axis, [(i, (i + distance) % count) for i in range(cou...  18.4 us
    pallas_call x2, Pallas kernels, cross(): pl.pallas_call(cross_kernel, out_shape=jax.ShapeDtypeStruct((SOURCES // 2...  16.2 us
    pallas_call x1, Pallas kernels, whiten(): pl.pallas_call(whiten_kernel, out_shape=(shape, shape, jax.ShapeDtypeStru...  6.2 us
    pallas_call x5, Pallas kernels, stack(): pl.pallas_call(functools.partial(stack_kernel, rels), out_shape=[jax.Shap...  4.72 us
    pallas_call x1, Pallas kernels, home(): pl.pallas_call(home_kernel, out_shape=jax.ShapeDtypeStruct((TCAP, SRC_PAR...  4.26 us
    pallas_call x1, Pallas kernels, pack(): pl.pallas_call(pack_kernel, out_shape=jax.ShapeDtypeStruct((NB * TM, ROWS...  2.98 us
  transfers between devices with their start and end apart: 23, of which 13 were waited for; matrix products, arithmetic and copies ran while one was open for 0% of the time, Pallas kernels for 21%

profile of v5, /device:TPU:0, one launch (start us, length us, event | category | flops | bytes accessed | tf_op | source)
XLA Modules:
  0.0 131.4 jit_solution(18022395742341215585)
XLA Ops:
  0.0 1.5 %copy-done.2 = bf16[4,60,4096]{2,0,1:T(4,128)(2,1)S(1)} copy-done((bf16[4,60,4096]{2,0,1:T(4,128)(2,1)S(1)}, bf16[4,60,4096]{2,0,1:T(4,128)(2,1)}, u32[]{:S(2)}) %copy-start.2) | copy-done | bytes 1966104
  1.5 0.7 copy-done.9
  2.2 3.0 %pack.1 = bf16[128,64,128]{2,1,0:T(8,128)(2,1)S(1)} custom-call(s32[1]{0:T(128)} %bitcast.own.chan, bf16[60,4,4096]{2,1,0:T(4,128)(2,1)S(1)} %bitcast.6, s32[4,128]{1,0:T(4,128)S(1)} %copy-done.9), custom_call_target="tpu_custom_call" | custom-call | tf_op jit(solution)/shard_map/pack/pallas_call | solution.py:161
  5.2 41.1 %all_to_all.5 = bf16[128,64,128]{2,1,0:T(8,128)(2,1)S(1)} all-to-all(bf16[128,64,128]{2,1,0:T(8,128)(2,1)S(1)} %pack.1), channel_id=1, replica_groups=mesh['chan'=32,'tm'=4] {'chan','tm'}, dimensions={0} | all-to-all | bytes 4194304 | tf_op jit(solution)/shard_map/all_to_all | solution.py:541
  46.4 6.2 %whiten.1 = (bf16[2,2,768,128]{3,2,1,0:T(8,128)(2,1)S(1)}, bf16[2,2,768,128]{3,2,1,0:T(8,128)(2,1)S(1)}, bf16[768,128]{1,0:T(8,128)(2,1)S(1)}) custom-call(s32[1]{0:T(128)} %bitcast.own.chan, bf16[32,4,64,128]{3,2,1,0:T(8,128)(2,1)S(1)} %bitcast.5, bf16[1536,2048]{1,0:T(8,128)(2,1)S(1)} %copy-done.1, bf16[768,768]{1,0:T(8,128)(2,1)S(1)} %copy-done.4, ...), custom_call_target="tpu_custom_call" | custom-call | tf_op jit(solution)/shard_map/whiten/pallas_call | solution.py:214
  52.6 0.4 collective-permute-start.2
  52.9 0.6 collective-permute-start
  53.6 4.7 %collective-permute-start.1 = (bf16[2,2,768,128]{3,2,1,0:T(8,128)(2,1)S(1)}, bf16[2,2,768,128]{3,2,1,0:T(8,128)(2,1)S(1)}, u32[]{:S(2)}, u32[]{:S(2)}) collective-permute-start(bf16[2,2,768,128]{3,2,1,0:T(8,128)(2,1)S(1)} %get-tuple-element.44.refs_0_), channel_id=1, source_target_pairs={{0,120},{4,124},{8,0},{12,4},{16,8},{20,12},{24,16},{28,20},{32,24... | collective-permute-start | bytes 2359304 | tf_op jit(solution)/shard_map/ppermute | solution.py:531
  58.3 1.4 %collective-permute-start.3 = (bf16[768,128]{1,0:T(8,128)(2,1)S(1)}, bf16[768,128]{1,0:T(8,128)(2,1)S(1)}, u32[]{:S(2)}, u32[]{:S(2)}) collective-permute-start(bf16[768,128]{1,0:T(8,128)(2,1)S(1)} %get-tuple-element.39.s0), channel_id=1, source_target_pairs={{0,3},{1,0},{2,1},{3,2},{4,7},{5,4},{6,5},{7,6},{8,11},{9,8},{10,9... | collective-permute-start | bytes 589832 | tf_op jit(solution)/shard_map/ppermute | solution.py:531
  59.7 1.2 collective-permute-start.4
  60.9 5.2 %collective-permute-done.3.s1 = bf16[768,128]{1,0:T(8,128)(2,1)S(1)} collective-permute-done((bf16[768,128]{1,0:T(8,128)(2,1)S(1)}, bf16[768,128]{1,0:T(8,128)(2,1)S(1)}, u32[]{:S(2)}, u32[]{:S(2)}) %collective-permute-start.3) | collective-permute-done | bytes 196640 | tf_op jit(solution)/shard_map/ppermute | solution.py:531
  66.1 3.0 %collective-permute-done.4.s2 = bf16[768,128]{1,0:T(8,128)(2,1)S(1)} collective-permute-done((bf16[768,128]{1,0:T(8,128)(2,1)S(1)}, bf16[768,128]{1,0:T(8,128)(2,1)S(1)}, u32[]{:S(2)}, u32[]{:S(2)}) %collective-permute-start.4) | collective-permute-done | bytes 196640 | tf_op jit(solution)/shard_map/ppermute | solution.py:531
  69.1 2.4 %collective-permute-start.7 = (bf16[2,2,768,128]{3,2,1,0:T(8,128)(2,1)S(1)}, bf16[2,2,768,128]{3,2,1,0:T(8,128)(2,1)S(1)}, u32[]{:S(2)}, u32[]{:S(2)}) collective-permute-start(bf16[2,2,768,128]{3,2,1,0:T(8,128)(2,1)S(1)} %get-tuple-element.54.refs_0_), channel_id=1, source_target_pairs={{0,120},{4,124},{8,0},{12,4},{16,8},{20,12},{24,16},{28,20},{32,24... | collective-permute-start | bytes 2359304 | tf_op jit(solution)/shard_map/ppermute | solution.py:531
  71.4 0.4 collective-permute-done.5.s3
  71.8 4.8 %collective-permute-done.below.refs_1_ = bf16[2,2,768,128]{3,2,1,0:T(8,128)(2,1)S(1)} collective-permute-done((bf16[2,2,768,128]{3,2,1,0:T(8,128)(2,1)S(1)}, bf16[2,2,768,128]{3,2,1,0:T(8,128)(2,1)S(1)}, u32[]{:S(2)}, u32[]{:S(2)}) %collective-permute-start) | collective-permute-done | bytes 786464 | tf_op jit(solution)/shard_map/ppermute | solution.py:531
  76.6 0.4 choose.2
  77.0 0.1 collective-permute-start.10
  77.1 0.5 collective-permute-start.9
  77.6 1.8 %diagonal.1.diag = bf16[96,128,256]{2,1,0:T(8,128)(2,1)S(1)} custom-call(bf16[768,128]{1,0:T(8,128)(2,1)S(1)} %get-tuple-element.39.s0, bf16[768,128]{1,0:T(8,128)(2,1)S(1)} %collective-permute-done.3.s1, bf16[768,128]{1,0:T(8,128)(2,1)S(1)} %collective-permute-done.4.s2, bf16[768,128]{1,0:T(8,128)(2,1)S(1)} %collective-permute-done.5.s3, ...), custom_call_target="tpu_custom_call" | custom-call | flops 1 | bytes 1 | tf_op jit(solution)/shard_map/diagonal/pallas_call | solution.py:273
  79.5 8.1 %cross.2.spectra = bf16[8,2,768,128]{3,2,1,0:T(8,128)(2,1)S(1)} custom-call(s32[1]{0:T(128)} %bitcast.own.chan, s32[2,96]{1,0:T(2,128)S(1)} %bitcast.7, bf16[96,128,256]{2,1,0:T(8,128)(2,1)S(1)} %diagonal.1.diag, bf16[384,512]{1,0:T(8,128)(2,1)S(1)} %copy-done.3, bf16[2,2,768,128]{3,2,1,0:T(8,128)(2,1)S(1)} %get-tuple-element.44.refs_0_, ...), custom_call_target="tpu_custom_call" | custom-call | flops 1 | bytes 1 | tf_op jit(solution)/shard_map/cross/pallas_call | solution.py:369
  87.6 2.0 %stack.5 = (bf16[192,512]{1,0:T(8,128)(2,1)S(1)}, bf16[192,512]{1,0:T(8,128)(2,1)S(1)}, bf16[192,512]{1,0:T(8,128)(2,1)S(1)}, bf16[192,512]{1,0:T(8,128)(2,1)S(1)}) custom-call(bf16[8,2,768,128]{3,2,1,0:T(8,128)(2,1)S(1)} %cross.2.spectra, bf16[512,1536]{1,0:T(8,128)(2,1)S(1)} %copy-done), custom_call_target="tpu_custom_call" | custom-call | flops 1 | bytes 1 | tf_op jit(solution)/shard_map/stack/pallas_call | solution.py:408
  89.6 3.1 %collective-permute-done.6.below.refs_1_ = bf16[2,2,768,128]{3,2,1,0:T(8,128)(2,1)S(1)} collective-permute-done((bf16[2,2,768,128]{3,2,1,0:T(8,128)(2,1)S(1)}, bf16[2,2,768,128]{3,2,1,0:T(8,128)(2,1)S(1)}, u32[]{:S(2)}, u32[]{:S(2)}) %collective-permute-start.6) | collective-permute-done | bytes 786464 | tf_op jit(solution)/shard_map/ppermute | solution.py:531
  92.8 0.1 choose.3
  92.9 0.1 collective-permute-start.11
  93.0 0.6 collective-permute-start.12
  93.6 2.5 %collective-permute-start.13 = (bf16[192,512]{1,0:T(8,128)(2,1)S(1)}, bf16[192,512]{1,0:T(8,128)(2,1)S(1)}, u32[]{:S(2)}, u32[]{:S(2)}) collective-permute-start(bf16[192,512]{1,0:T(8,128)(2,1)S(1)} %get-tuple-element.52), channel_id=1, source_target_pairs={{0,2},{1,3},{2,0},{3,1},{4,6},{5,7},{6,4},{7,5},{8,10},{9,11},{10,... | collective-permute-start | bytes 589832 | tf_op jit(solution)/shard_map/ppermute | solution.py:531
  96.1 0.5 collective-permute-start.14
  96.7 8.1 %cross.3.spectra = bf16[8,2,768,128]{3,2,1,0:T(8,128)(2,1)S(1)} custom-call(s32[1]{0:T(128)} %bitcast.own.chan, s32[2,96]{1,0:T(2,128)S(1)} %bitcast.8, bf16[96,128,256]{2,1,0:T(8,128)(2,1)S(1)} %diagonal.1.diag, bf16[384,512]{1,0:T(8,128)(2,1)S(1)} %copy-done.3, bf16[2,2,768,128]{3,2,1,0:T(8,128)(2,1)S(1)} %get-tuple-element.54.refs_0_, ...), custom_call_target="tpu_custom_call" | custom-call | flops 1 | bytes 1 | tf_op jit(solution)/shard_map/cross/pallas_call | solution.py:369
  104.8 0.9 collective-permute-done.12.refs_1_
  105.7 0.6 collective-permute-done.14.refs_3_
  106.3 1.0 merge.1
  107.4 0.1 collective-permute-start.16
  107.4 0.7 stack.8
  108.1 0.4 collective-permute-start.18
  108.5 0.7 stack.9
  109.2 3.0 %collective-permute-start.21 = (bf16[192,512]{1,0:T(8,128)(2,1)S(1)}, bf16[192,512]{1,0:T(8,128)(2,1)S(1)}, u32[]{:S(2)}, u32[]{:S(2)}) collective-permute-start(bf16[192,512]{1,0:T(8,128)(2,1)S(1)} %stack.9), channel_id=1, source_target_pairs={{0,3},{1,0},{2,1},{3,2},{4,7},{5,4},{6,5},{7,6},{8,11},{9,8},{10,9... | collective-permute-start | bytes 589832 | tf_op jit(solution)/shard_map/ppermute | solution.py:531
  112.2 0.7 stack.6
  112.9 0.8 collective-permute-start.15
  113.6 0.7 stack.7.refs_4_
  114.3 0.1 collective-permute-start.17
  114.4 1.1 collective-permute-done.18.refs_5_
  115.5 4.3 %collective-permute-done.21.refs_7_ = bf16[192,512]{1,0:T(8,128)(2,1)S(1)} collective-permute-done((bf16[192,512]{1,0:T(8,128)(2,1)S(1)}, bf16[192,512]{1,0:T(8,128)(2,1)S(1)}, u32[]{:S(2)}, u32[]{:S(2)}) %collective-permute-start.21) | collective-permute-done | bytes 196640 | tf_op jit(solution)/shard_map/ppermute | solution.py:531
  119.8 1.1 collective-permute-done.15.refs_6_
  120.9 1.2 collective-permute-done.16.refs_0_
  122.2 4.3 %home.1.refs_5_ = f32[6,4,128,512]{3,2,1,0:T(8,128)} custom-call(s32[96]{0:T(128)S(1)} %copy-done.10, s32[1]{0:T(128)} %bitcast.own.chan, s32[1]{0:T(128)} %bitcast.1.time, bf16[192,512]{1,0:T(8,128)(2,1)S(1)} %get-tuple-element.59.refs_0_, bf16[192,512]{1,0:T(8,128)(2,1)S(1)} %collective-permute-done.12.refs_1_, ...), custom_call_target="tpu_custom_call" | custom-call | flops 1 | bytes 1 | tf_op jit(solution)/shard_map/home/pallas_call | solution.py:472
  126.4 2.0 %collective-permute-done.22.refs_4_ = bf16[192,512]{1,0:T(8,128)(2,1)S(1)} collective-permute-done((bf16[192,512]{1,0:T(8,128)(2,1)S(1)}, bf16[192,512]{1,0:T(8,128)(2,1)S(1)}, u32[]{:S(2)}, u32[]{:S(2)}) %collective-permute-start.22) | collective-permute-done | bytes 196640 | tf_op jit(solution)/shard_map/ppermute | solution.py:531
  128.5 2.1 %collective-permute-done.20.refs_3_ = bf16[192,512]{1,0:T(8,128)(2,1)S(1)} collective-permute-done((bf16[192,512]{1,0:T(8,128)(2,1)S(1)}, bf16[192,512]{1,0:T(8,128)(2,1)S(1)}, u32[]{:S(2)}, u32[]{:S(2)}) %collective-permute-start.20) | collective-permute-done | bytes 196640 | tf_op jit(solution)/shard_map/ppermute | solution.py:531
  130.6 0.6 moved.1
  (36 shorter events, 0.1 us)
Async XLA Ops:
  0.0 1.5 %copy-start.2 = (bf16[4,60,4096]{2,0,1:T(4,128)(2,1)S(1)}, bf16[4,60,4096]{2,0,1:T(4,128)(2,1)}, u32[]{:S(2)}) copy-start(bf16[4,60,4096]{2,0,1:T(4,128)(2,1)} %param.12) | copy-start | bytes 5898244
  1.5 0.7 copy-start.9
  2.2 44.1 %copy-start.1 = (bf16[1536,2048]{1,0:T(8,128)(2,1)S(1)}, bf16[1536,2048]{1,0:T(8,128)(2,1)}, u32[]{:S(2)}) copy-start(bf16[1536,2048]{1,0:T(8,128)(2,1)} %constant.23.clone.table) | copy-start | bytes 18874372
  2.2 44.1 %copy-start.4 = (bf16[768,768]{1,0:T(8,128)(2,1)S(1)}, bf16[768,768]{1,0:T(8,128)(2,1)}, u32[]{:S(2)}) copy-start(bf16[768,768]{1,0:T(8,128)(2,1)} %constant.24.clone.inside) | copy-start | bytes 3538948
  2.2 44.1 %copy-start.5 = (f32[768,1]{1,0:T(8,128)S(1)}, f32[768,1]{1,0:T(8,128)}, u32[]{:S(2)}) copy-start(f32[768,1]{1,0:T(8,128)} %constant.25.clone.inverse_count) | copy-start | bytes 9220
  2.2 44.1 %copy-start.7 = (bf16[4,2,128,128]{3,2,1,0:T(8,128)(2,1)S(1)}, bf16[4,2,128,128]{3,2,1,0:T(8,128)(2,1)}, u32[]{:S(2)}) copy-start(bf16[4,2,128,128]{3,2,1,0:T(8,128)(2,1)} %constant.26.clone.pick) | copy-start | bytes 786436
  46.4 31.3 %copy-start.6 = (bf16[4,128,256]{2,1,0:T(8,128)(2,1)S(1)}, bf16[4,128,256]{2,1,0:T(8,128)(2,1)}, u32[]{:S(2)}) copy-start(bf16[4,128,256]{2,1,0:T(8,128)(2,1)} %constant.27.clone.spread) | copy-start | bytes 786436
  52.6 8.4 %collective-permute-start.2 = (bf16[2,2,768,128]{3,2,1,0:T(8,128)(2,1)S(1)}, bf16[2,2,768,128]{3,2,1,0:T(8,128)(2,1)S(1)}, u32[]{:S(2)}, u32[]{:S(2)}) collective-permute-start(bf16[2,2,768,128]{3,2,1,0:T(8,128)(2,1)S(1)} %get-tuple-element.44.refs_0_), channel_id=1, source_target_pairs={{0,4},{4,0},{8,12},{12,8},{16,20},{20,16},{24,28},{28,24},{32,36},... | collective-permute-start | bytes 2359304 | tf_op jit(solution)/shard_map/ppermute | solution.py:546
  52.9 23.7 %collective-permute-start = (bf16[2,2,768,128]{3,2,1,0:T(8,128)(2,1)S(1)}, bf16[2,2,768,128]{3,2,1,0:T(8,128)(2,1)S(1)}, u32[]{:S(2)}, u32[]{:S(2)}) collective-permute-start(bf16[2,2,768,128]{3,2,1,0:T(8,128)(2,1)S(1)} %get-tuple-element.44.refs_0_), channel_id=1, source_target_pairs={{0,8},{4,12},{8,16},{12,20},{16,24},{20,28},{24,32},{28,36},{32,40... | collective-permute-start | bytes 2359304 | tf_op jit(solution)/shard_map/ppermute | solution.py:531
  53.6 23.1 %collective-permute-start.1 = (bf16[2,2,768,128]{3,2,1,0:T(8,128)(2,1)S(1)}, bf16[2,2,768,128]{3,2,1,0:T(8,128)(2,1)S(1)}, u32[]{:S(2)}, u32[]{:S(2)}) collective-permute-start(bf16[2,2,768,128]{3,2,1,0:T(8,128)(2,1)S(1)} %get-tuple-element.44.refs_0_), channel_id=1, source_target_pairs={{0,120},{4,124},{8,0},{12,4},{16,8},{20,12},{24,16},{28,20},{32,24... | collective-permute-start | bytes 2359304 | tf_op jit(solution)/shard_map/ppermute | solution.py:531
  58.3 7.8 %collective-permute-start.3 = (bf16[768,128]{1,0:T(8,128)(2,1)S(1)}, bf16[768,128]{1,0:T(8,128)(2,1)S(1)}, u32[]{:S(2)}, u32[]{:S(2)}) collective-permute-start(bf16[768,128]{1,0:T(8,128)(2,1)S(1)} %get-tuple-element.39.s0), channel_id=1, source_target_pairs={{0,3},{1,0},{2,1},{3,2},{4,7},{5,4},{6,5},{7,6},{8,11},{9,8},{10,9... | collective-permute-start | bytes 589832 | tf_op jit(solution)/shard_map/ppermute | solution.py:531
  59.7 9.4 %collective-permute-start.4 = (bf16[768,128]{1,0:T(8,128)(2,1)S(1)}, bf16[768,128]{1,0:T(8,128)(2,1)S(1)}, u32[]{:S(2)}, u32[]{:S(2)}) collective-permute-start(bf16[768,128]{1,0:T(8,128)(2,1)S(1)} %get-tuple-element.39.s0), channel_id=1, source_target_pairs={{0,2},{1,3},{2,0},{3,1},{4,6},{5,7},{6,4},{7,5},{8,10},{9,11},{10,... | collective-permute-start | bytes 589832 | tf_op jit(solution)/shard_map/ppermute | solution.py:531
  60.9 10.9 %collective-permute-start.5 = (bf16[768,128]{1,0:T(8,128)(2,1)S(1)}, bf16[768,128]{1,0:T(8,128)(2,1)S(1)}, u32[]{:S(2)}, u32[]{:S(2)}) collective-permute-start(bf16[768,128]{1,0:T(8,128)(2,1)S(1)} %get-tuple-element.39.s0), channel_id=1, source_target_pairs={{0,1},{1,2},{2,3},{3,0},{4,5},{5,6},{6,7},{7,4},{8,9},{9,10},{10,1... | collective-permute-start | bytes 589832 | tf_op jit(solution)/shard_map/ppermute | solution.py:531
  66.1 26.7 %collective-permute-start.6 = (bf16[2,2,768,128]{3,2,1,0:T(8,128)(2,1)S(1)}, bf16[2,2,768,128]{3,2,1,0:T(8,128)(2,1)S(1)}, u32[]{:S(2)}, u32[]{:S(2)}) collective-permute-start(bf16[2,2,768,128]{3,2,1,0:T(8,128)(2,1)S(1)} %get-tuple-element.54.refs_0_), channel_id=1, source_target_pairs={{0,8},{4,12},{8,16},{12,20},{16,24},{20,28},{24,32},{28,36},{32,40... | collective-permute-start | bytes 2359304 | tf_op jit(solution)/shard_map/ppermute | solution.py:531
  69.1 23.7 %collective-permute-start.7 = (bf16[2,2,768,128]{3,2,1,0:T(8,128)(2,1)S(1)}, bf16[2,2,768,128]{3,2,1,0:T(8,128)(2,1)S(1)}, u32[]{:S(2)}, u32[]{:S(2)}) collective-permute-start(bf16[2,2,768,128]{3,2,1,0:T(8,128)(2,1)S(1)} %get-tuple-element.54.refs_0_), channel_id=1, source_target_pairs={{0,120},{4,124},{8,0},{12,4},{16,8},{20,12},{24,16},{28,20},{32,24... | collective-permute-start | bytes 2359304 | tf_op jit(solution)/shard_map/ppermute | solution.py:531
  71.8 21.0 %collective-permute-start.8 = (bf16[2,2,768,128]{3,2,1,0:T(8,128)(2,1)S(1)}, bf16[2,2,768,128]{3,2,1,0:T(8,128)(2,1)S(1)}, u32[]{:S(2)}, u32[]{:S(2)}) collective-permute-start(bf16[2,2,768,128]{3,2,1,0:T(8,128)(2,1)S(1)} %get-tuple-element.54.refs_0_), channel_id=1, source_target_pairs={{0,4},{4,0},{8,12},{12,8},{16,20},{20,16},{24,28},{28,24},{32,36},... | collective-permute-start | bytes 2359304 | tf_op jit(solution)/shard_map/ppermute | solution.py:546
  77.0 2.4 %collective-permute-start.10 = (bf16[1,2,768,128]{3,2,1,0:T(8,128)(2,1)S(1)}, bf16[1,2,768,128]{3,2,1,0:T(8,128)(2,1)S(1)}, u32[]{:S(2)}, u32[]{:S(2)}) collective-permute-start(bf16[1,2,768,128]{3,2,1,0:T(8,128)(2,1)S(1)} %get-tuple-element.49), channel_id=1, source_target_pairs={{0,4},{4,0},{8,12},{12,8},{16,20},{20,16},{24,28},{28,24},{32,36},... | collective-permute-start | bytes 1179656 | tf_op jit(solution)/shard_map/ppermute | solution.py:551
  77.1 2.3 %copy-start.3 = (bf16[384,512]{1,0:T(8,128)(2,1)S(1)}, bf16[384,512]{1,0:T(8,128)(2,1)}, u32[]{:S(2)}) copy-start(bf16[384,512]{1,0:T(8,128)(2,1)} %constant.28.clone.order) | copy-start | bytes 1179652
  77.1 2.3 %copy-start.8 = (s32[96,2]{0,1:T(2,128)S(1)}, s32[96,2]{0,1:T(2,128)}, u32[]{:S(2)}) copy-start(s32[96,2]{0,1:T(2,128)} %param.14) | copy-start | bytes 2308
  77.1 2.3 %collective-permute-start.9 = (bf16[1,2,768,128]{3,2,1,0:T(8,128)(2,1)S(1)}, bf16[1,2,768,128]{3,2,1,0:T(8,128)(2,1)S(1)}, u32[]{:S(2)}, u32[]{:S(2)}) collective-permute-start(bf16[1,2,768,128]{3,2,1,0:T(8,128)(2,1)S(1)} %get-tuple-element.48), channel_id=1, source_target_pairs={{0,4},{4,0},{8,12},{12,8},{16,20},{20,16},{24,28},{28,24},{32,36},... | collective-permute-start | bytes 1179656 | tf_op jit(solution)/shard_map/ppermute | solution.py:551
  79.5 8.2 %copy-start = (bf16[512,1536]{1,0:T(8,128)(2,1)S(1)}, bf16[512,1536]{1,0:T(8,128)(2,1)}, u32[]{:S(2)}) copy-start(bf16[512,1536]{1,0:T(8,128)(2,1)} %constant.29.clone.inverse) | copy-start | bytes 4718596
  92.9 3.8 %collective-permute-start.11 = (bf16[2,2,768,128]{3,2,1,0:T(8,128)(2,1)S(1)}, bf16[2,2,768,128]{3,2,1,0:T(8,128)(2,1)S(1)}, u32[]{:S(2)}, u32[]{:S(2)}) collective-permute-start(bf16[2,2,768,128]{3,2,1,0:T(8,128)(2,1)S(1)} %choose.3), channel_id=1, source_target_pairs={{0,4},{4,0},{8,12},{12,8},{16,20},{20,16},{24,28},{28,24},{32,36},... | collective-permute-start | bytes 2359304 | tf_op jit(solution)/shard_map/ppermute | solution.py:551
  93.0 12.7 %collective-permute-start.12 = (bf16[192,512]{1,0:T(8,128)(2,1)S(1)}, bf16[192,512]{1,0:T(8,128)(2,1)S(1)}, u32[]{:S(2)}, u32[]{:S(2)}) collective-permute-start(bf16[192,512]{1,0:T(8,128)(2,1)S(1)} %get-tuple-element.51), channel_id=1, source_target_pairs={{0,1},{1,2},{2,3},{3,0},{4,5},{5,6},{6,7},{7,4},{8,9},{9,10},{10,1... | collective-permute-start | bytes 589832 | tf_op jit(solution)/shard_map/ppermute | solution.py:531
  93.6 12.1 %collective-permute-start.13 = (bf16[192,512]{1,0:T(8,128)(2,1)S(1)}, bf16[192,512]{1,0:T(8,128)(2,1)S(1)}, u32[]{:S(2)}, u32[]{:S(2)}) collective-permute-start(bf16[192,512]{1,0:T(8,128)(2,1)S(1)} %get-tuple-element.52), channel_id=1, source_target_pairs={{0,2},{1,3},{2,0},{3,1},{4,6},{5,7},{6,4},{7,5},{8,10},{9,11},{10,... | collective-permute-start | bytes 589832 | tf_op jit(solution)/shard_map/ppermute | solution.py:531
  96.1 10.2 %collective-permute-start.14 = (bf16[192,512]{1,0:T(8,128)(2,1)S(1)}, bf16[192,512]{1,0:T(8,128)(2,1)S(1)}, u32[]{:S(2)}, u32[]{:S(2)}) collective-permute-start(bf16[192,512]{1,0:T(8,128)(2,1)S(1)} %get-tuple-element.53), channel_id=1, source_target_pairs={{0,3},{1,0},{2,1},{3,2},{4,7},{5,4},{6,5},{7,6},{8,11},{9,8},{10,9... | collective-permute-start | bytes 589832 | tf_op jit(solution)/shard_map/ppermute | solution.py:531
  107.4 14.8 %collective-permute-start.16 = (bf16[768,512]{1,0:T(8,128)(2,1)S(1)}, bf16[768,512]{1,0:T(8,128)(2,1)S(1)}, u32[]{:S(2)}, u32[]{:S(2)}) collective-permute-start(bf16[768,512]{1,0:T(8,128)(2,1)S(1)} %merge.1), channel_id=1, source_target_pairs={{0,4},{4,8},{8,12},{12,16},{16,20},{20,24},{24,28},{28,32},{32,36}... | collective-permute-start | bytes 2359304 | tf_op jit(solution)/shard_map/ppermute | solution.py:531
  108.1 7.4 %collective-permute-start.18 = (bf16[192,512]{1,0:T(8,128)(2,1)S(1)}, bf16[192,512]{1,0:T(8,128)(2,1)S(1)}, u32[]{:S(2)}, u32[]{:S(2)}) collective-permute-start(bf16[192,512]{1,0:T(8,128)(2,1)S(1)} %stack.8), channel_id=1, source_target_pairs={{0,1},{1,2},{2,3},{3,0},{4,5},{5,6},{6,7},{7,4},{8,9},{9,10},{10,1... | collective-permute-start | bytes 589832 | tf_op jit(solution)/shard_map/ppermute | solution.py:531
  109.2 10.6 %collective-permute-start.21 = (bf16[192,512]{1,0:T(8,128)(2,1)S(1)}, bf16[192,512]{1,0:T(8,128)(2,1)S(1)}, u32[]{:S(2)}, u32[]{:S(2)}) collective-permute-start(bf16[192,512]{1,0:T(8,128)(2,1)S(1)} %stack.9), channel_id=1, source_target_pairs={{0,3},{1,0},{2,1},{3,2},{4,7},{5,4},{6,5},{7,6},{8,11},{9,8},{10,9... | collective-permute-start | bytes 589832 | tf_op jit(solution)/shard_map/ppermute | solution.py:531
  112.9 9.3 %copy-start.10 = (s32[96]{0:T(128)S(1)}, s32[96]{0:T(128)}, u32[]{:S(2)}) copy-start(s32[96]{0:T(128)} %owners.3) | copy-start | bytes 1156
  112.9 8.1 %collective-permute-start.15 = (bf16[192,512]{1,0:T(8,128)(2,1)S(1)}, bf16[192,512]{1,0:T(8,128)(2,1)S(1)}, u32[]{:S(2)}, u32[]{:S(2)}) collective-permute-start(bf16[192,512]{1,0:T(8,128)(2,1)S(1)} %stack.6), channel_id=1, source_target_pairs={{0,2},{1,3},{2,0},{3,1},{4,6},{5,7},{6,4},{7,5},{8,10},{9,11},{10,... | collective-permute-start | bytes 589832 | tf_op jit(solution)/shard_map/ppermute | solution.py:531
  114.3 12.1 %collective-permute-start.17 = (bf16[192,512]{1,0:T(8,128)(2,1)S(1)}, bf16[192,512]{1,0:T(8,128)(2,1)S(1)}, u32[]{:S(2)}, u32[]{:S(2)}) collective-permute-start(bf16[192,512]{1,0:T(8,128)(2,1)S(1)} %stack.7.refs_4_), channel_id=1, source_target_pairs={{0,4},{4,8},{8,12},{12,16},{16,20},{20,24},{24,28},{28,32},{32,36}... | collective-permute-start | bytes 589832 | tf_op jit(solution)/shard_map/ppermute | solution.py:531
  115.5 10.9 %collective-permute-start.19 = (bf16[192,512]{1,0:T(8,128)(2,1)S(1)}, bf16[192,512]{1,0:T(8,128)(2,1)S(1)}, u32[]{:S(2)}, u32[]{:S(2)}) collective-permute-start(bf16[192,512]{1,0:T(8,128)(2,1)S(1)} %collective-permute-done.18.refs_5_), channel_id=1, source_target_pairs={{0,4},{4,8},{8,12},{12,16},{16,20},{20,24},{24,28},{28,32},{32,36}... | collective-permute-start | bytes 589832 | tf_op jit(solution)/shard_map/ppermute | solution.py:531
  119.8 8.7 %collective-permute-start.22 = (bf16[192,512]{1,0:T(8,128)(2,1)S(1)}, bf16[192,512]{1,0:T(8,128)(2,1)S(1)}, u32[]{:S(2)}, u32[]{:S(2)}) collective-permute-start(bf16[192,512]{1,0:T(8,128)(2,1)S(1)} %collective-permute-done.21.refs_7_), channel_id=1, source_target_pairs={{0,4},{4,8},{8,12},{12,16},{16,20},{20,24},{24,28},{28,32},{32,36}... | collective-permute-start | bytes 589832 | tf_op jit(solution)/shard_map/ppermute | solution.py:531
  122.2 8.4 %collective-permute-start.20 = (bf16[192,512]{1,0:T(8,128)(2,1)S(1)}, bf16[192,512]{1,0:T(8,128)(2,1)S(1)}, u32[]{:S(2)}, u32[]{:S(2)}) collective-permute-start(bf16[192,512]{1,0:T(8,128)(2,1)S(1)} %collective-permute-done.15.refs_6_), channel_id=1, source_target_pairs={{0,4},{4,8},{8,12},{12,16},{16,20},{20,24},{24,28},{28,32},{32,36}... | collective-permute-start | bytes 589832 | tf_op jit(solution)/shard_map/ppermute | solution.py:531

commit v6 on v5

--- a/solution.py
+++ b/solution.py
@@ -69,14 +69,15 @@
 
 
 def source_lanes():
-    pick = np.zeros((TM, 2, BLOCK, LANES))
-    for i in range(TM):
+    pick = np.zeros((PARTS, 2, LANES, LANES))
+    for pair in range(PARTS):
         for half in range(2):
-            for s in range(SEG_DEV):
-                for v in range(SRC_PART):
-                    part, at = divmod(v * (BLOCK // SOURCES), HALF_PART)
-                    lane = half * SRC_PART * SEGS + v * SEGS + i * SEG_DEV + s
-                    pick[i, half, (part * SEG_DEV + s) * HALF_PART + at, lane] = 1.0
+            for u in range(PAIR):
+                for s in range(SEG_DEV):
+                    for v in range(SRC_PART):
+                        lane = half * SRC_PART * SEGS + v * SEGS + (pair * PAIR + u) * SEG_DEV + s
+                        row = (u * SEG_DEV + s) * HALF_PART + v * (HALF_PART // SRC_PART)
+                        pick[pair, half, row, lane] = 1.0
     return pick.astype(ml_dtypes.bfloat16)
 
 
@@ -105,35 +106,30 @@
 PACK_STEPS = NB // PACK_BLOCKS
 
 
-def pack_kernel(own, records, quality, out, held, marks, order, rows, sem, mark_sem):
+def bits(value, shift, count):
+    return jnp.bitwise_and(jnp.right_shift(value, shift), count - 1)
+
+
+def pack_kernel(own, time, records, marks, out, order, rows):
     lanes = PACK_BLOCKS * BLOCK
-
-    def copy(step):
-        part = records.at[:, :, pl.ds(step * lanes, lanes)]
-        return pltpu.make_async_copy(part, held.at[step], sem.at[step])
-
-    pltpu.make_async_copy(quality, marks, mark_sem).start()
-    for step in range(PACK_STEPS):
-        copy(step).start()
     row = lax.broadcasted_iota(jnp.int32, order.shape, 0)
     lane = lax.broadcasted_iota(jnp.int32, order.shape, 1)
-    s, j = row // BLOCK, row // PART % TM
-    part, at = row // HALF_PART % 2, row % HALF_PART
+    s, j, part = bits(row, 7, SEG_DEV), bits(row, 5, TM), bits(row, 2, 2)
+    at = bits(row, 3, SRC_PART) * SRC_PART + bits(row, 0, SRC_PART)
+    part = jnp.bitwise_xor(part, bits(time[0], 0, 2))
     target = j * BLOCK + (part * SEG_DEV + s) * HALF_PART + at
     order[...] = jnp.where(lane == target, 1.0, 0.0).astype(BF16)
     row = lax.broadcasted_iota(jnp.int32, rows.shape, 0)
     lane = lax.broadcasted_iota(jnp.int32, rows.shape, 1)
-    s, n = row // ROWS, row % ROWS
+    s, n = bits(row, 6, SEG_DEV), bits(row, 0, ROWS)
     keep = (lane == n * SEG_DEV + s) & (n < SLAB)
     rows[...] = jnp.where(keep, 1.0, 0.0).astype(BF16)
-    pltpu.make_async_copy(quality, marks, mark_sem).wait()
     mark = jnp.concatenate([marks[s : s + 1, :] for s in range(SEG_DEV)], axis=1)
     mark = jnp.broadcast_to(mark.astype(F32), (16, SEG_DEV * BLOCK)).astype(BF16)
     mark = jnp.dot(mark, order[...], preferred_element_type=F32)[:1]
     row = lax.broadcasted_iota(jnp.int32, (ROWS, SEG_DEV * BLOCK), 0)
     for step in range(PACK_STEPS):
-        copy(step).wait()
-        flat = held[step].reshape(SLAB * SEG_DEV, lanes)
+        flat = records[:, :, step * lanes : (step + 1) * lanes].reshape(SLAB * SEG_DEV, lanes)
         flat = jnp.dot(rows[...], flat, preferred_element_type=F32).astype(BF16)
         x = jnp.concatenate(
             [
@@ -157,69 +153,69 @@
                 out[index * TM + j] = block[:, j * BLOCK : (j + 1) * BLOCK]
 
 
-def pack(own, records, quality):
+def pack(own, time, records, quality):
     return pl.pallas_call(
         pack_kernel,
         out_shape=jax.ShapeDtypeStruct((NB * TM, ROWS, BLOCK), BF16),
-        in_specs=[pl.BlockSpec(memory_space=pltpu.SMEM)]
-        + [pl.BlockSpec(memory_space=pltpu.HBM)] * 2,
+        in_specs=[pl.BlockSpec(memory_space=pltpu.SMEM)] * 2
+        + [pl.BlockSpec(memory_space=pltpu.VMEM)] * 2,
         out_specs=pl.BlockSpec(memory_space=pltpu.VMEM),
         scratch_shapes=[
-            pltpu.VMEM((PACK_STEPS, SLAB, SEG_DEV, PACK_BLOCKS * BLOCK), BF16),
-            pltpu.VMEM((SEG_DEV, BLOCK), jnp.int32),
             pltpu.VMEM((SEG_DEV * BLOCK, SEG_DEV * BLOCK), BF16),
             pltpu.VMEM((SEG_DEV * ROWS, SLAB * SEG_DEV), BF16),
-            pltpu.SemaphoreType.DMA((PACK_STEPS,)),
-            pltpu.SemaphoreType.DMA,
         ],
         compiler_params=pltpu.CompilerParams(vmem_limit_bytes=20 * MIB),
         name="pack",
-    )(own, records.transpose(1, 0, 2), quality)
-
-
-def whiten_kernel(own, slabs, table, inside, inverse_count, pick, low, high, sources):
-    first = lax.broadcasted_iota(jnp.int32, (F, LANES), 1) < LANES // 2
+    )(own, time, records.transpose(1, 0, 2), quality)
+
+
+def whiten_kernel(part, own, slabs, table, inside, inverse_count, *refs):
+    lane = lax.broadcasted_iota(jnp.int32, (1, LANES), 1)
+    sides = [(lane < LANES // 2).astype(F32), (lane >= LANES // 2).astype(F32)]
+    x = []
+    for pair in range(PARTS):
+        halves = []
+        for u in range(PAIR):
+            i = pair * PAIR + (u ^ part)
+            marks = slabs[pl.ds(own[0], 1), i, pl.ds(48, 16), :][0, SLAB - 48 : SLAB - 47, :]
+            keep = (marks.astype(F32) * sides[u]).astype(BF16)
+            halves.append(slabs[:, i].reshape(NB * ROWS, BLOCK) * keep)
+        x.append(halves[0] + halves[1])
+    spectrum = jnp.dot(table[...], jnp.concatenate(x, axis=1), preferred_element_type=F32)
+    re = spectrum[:F]
+    im = spectrum[F:]
+    magnitude = jnp.sqrt(re * re + im * im).astype(BF16)
+    level = jnp.dot(inside[...], magnitude, preferred_element_type=F32) * inverse_count[...]
+    inverse_level = 1.0 / (level + 1e-6)
+    white = refs[-1] if part else refs[1]
     total = jnp.zeros((F, LANES), F32)
-    spectra = []
-    for step in range(PARTS):
-        lanes = []
-        for i in range(PAIR):
-            at = step * PAIR + i
-            marks = slabs[pl.ds(own[0], 1), at, pl.ds(48, 16), :][0, SLAB - 48 : SLAB - 47, :]
-            lanes.append(slabs[:, at].reshape(NB * ROWS, BLOCK) * marks)
-        x = jnp.concatenate(lanes, axis=1)
-        spectra.append(jnp.dot(table[...], x, preferred_element_type=F32))
-    for step, spectrum in enumerate(spectra):
-        re = spectrum[:F]
-        im = spectrum[F:]
-        magnitude = jnp.sqrt(re * re + im * im).astype(BF16)
-        level = jnp.dot(inside[...], magnitude, preferred_element_type=F32) * inverse_count[...]
-        inverse_level = 1.0 / (level + 1e-6)
-        for half, part in ((0, re), (1, im)):
-            value = part * inverse_level
-            pair = [value[:, i * BLOCK : (i + 1) * BLOCK] for i in range(PAIR)]
-            turned = [pltpu.roll(one, LANES // 2, 1) for one in pair]
-            low[step, half] = jnp.where(first, pair[0], turned[1]).astype(BF16)
-            high[step, half] = jnp.where(first, turned[0], pair[1]).astype(BF16)
-            for i in range(PAIR):
-                total += jnp.dot(
-                    pair[i].astype(BF16), pick[step * PAIR + i, half], preferred_element_type=F32
-                )
-    sources[...] = total.astype(BF16)
-
-
-def whiten(own, slabs):
-    inside, inverse_count = smoothing()
-    shape = jax.ShapeDtypeStruct((PARTS, 2, F, LANES), BF16)
-    return pl.pallas_call(
-        whiten_kernel,
-        out_shape=(shape, shape, jax.ShapeDtypeStruct((F, LANES), BF16)),
+    for half, value in ((0, re), (1, im)):
+        value = (value * inverse_level).astype(BF16)
+        for pair in range(PARTS):
+            mine = value[:, pair * LANES : (pair + 1) * LANES]
+            white[pair, half] = mine
+            if not part:
+                total += jnp.dot(mine, refs[0][pair, half], preferred_element_type=F32)
+    if not part:
+        refs[2][...] = total.astype(BF16)
+
+
+def whiten(part, own, slabs, constants):
+    shapes = [jax.ShapeDtypeStruct((PARTS, 2, F, LANES), BF16)]
+    picks = []
+    if not part:
+        shapes.append(jax.ShapeDtypeStruct((F, LANES), BF16))
+        picks.append(source_lanes())
+    return pl.pallas_call(
+        functools.partial(whiten_kernel, part),
+        out_shape=shapes,
         in_specs=[pl.BlockSpec(memory_space=pltpu.SMEM)]
-        + [pl.BlockSpec(memory_space=pltpu.VMEM)] * 5,
-        out_specs=[pl.BlockSpec(memory_space=pltpu.VMEM)] * 3,
-        compiler_params=pltpu.CompilerParams(vmem_limit_bytes=24 * MIB),
+        + [pl.BlockSpec(memory_space=pltpu.VMEM)] * (4 + len(picks)),
+        out_specs=[pl.BlockSpec(memory_space=pltpu.VMEM)] * len(shapes),
+        compiler_params=pltpu.CompilerParams(vmem_limit_bytes=20 * MIB),
+        cost_estimate=pl.CostEstimate(flops=1, bytes_accessed=1, transcendentals=0),
         name="whiten",
-    )(own, slabs.reshape(NB, TM, ROWS, BLOCK), forward_table(), inside, inverse_count, source_lanes())
+    )(own, slabs, *constants, *picks)
 
 
 def choose_kernel(chan, below, above, *refs):
@@ -291,7 +287,7 @@
     return jnp.where(offset == 0, 1, jnp.where(offset == 2 * REACH, 2, near))
 
 
-def cross_kernel(chan, tiles, diag, order, *refs):
+def cross_kernel(part, chan, tiles, diag, order, *refs):
     receivers, (out, held, wide, sem) = refs[:-4], refs[-4:]
     step = pl.program_id(0)
     steps = F // STEP
@@ -335,7 +331,7 @@
             im = y[at + STEP : at + 2 * STEP, lanes]
             re_turned = pltpu.roll(re, LANES // 2, 1)
             im_turned = pltpu.roll(im, LANES // 2, 1)
-            index = i * count + s
+            index = i * count + (s ^ (part * SEG_DEV))
             wide[index] = jnp.where(left, re, im_turned)
             wide[index + 1] = jnp.where(left, re_turned, im)
             wide[SEGS + index] = jnp.where(left, im, -re_turned)
@@ -365,9 +361,9 @@
 UNROLL = 8
 
 
-def cross(chan, tiles, diag, receivers):
-    return pl.pallas_call(
-        cross_kernel,
+def cross(part, chan, tiles, diag, receivers):
+    return pl.pallas_call(
+        functools.partial(cross_kernel, part),
         out_shape=jax.ShapeDtypeStruct((SOURCES // 2, 2, F, LANES), BF16),
         grid_spec=pltpu.PrefetchScalarGridSpec(
             num_scalar_prefetch=2,
@@ -445,15 +441,14 @@
 
 def arrange(time, pieces, t):
     rows = SRC_PART * HALF_PART
-    parts = []
-    for ref in pieces:
-        count = ref.shape[0] // (TPS * rows)
-        parts += [(ref, part * TPS * rows) for part in range(count)]
-    for index, (ref, first) in enumerate(parts):
-        half, rel = divmod(index, TM)
-        value = ref[first + t * rows : first + (t + 1) * rows, :].astype(F32)
-        at = lax.rem(time + TM - rel, TM) * PART + half * HALF_PART
-        yield pl.multiple_of(at, HALF_PART), value.reshape(SRC_PART, HALF_PART, LAG_COUNT)
+    low, pieces = pieces[0], pieces[1:]
+    for rel in range(TM):
+        halves = []
+        for ref, first in ((low, rel * TPS * rows), (pieces[rel], 0)):
+            value = ref[first + t * rows : first + (t + 1) * rows, :].astype(F32)
+            halves.append(value.reshape(SRC_PART * HALF_PART // 4, 4, LAG_COUNT))
+        value = jnp.concatenate(halves, axis=1).reshape(SRC_PART, PART, LAG_COUNT)
+        yield pl.multiple_of(lax.rem(time + TM - rel, TM) * PART, PART), value
 
 
 def home_kernel(owners, chan, time, *refs):
@@ -465,7 +460,7 @@
         @pl.when(owners[chan[0] * TPS + t] == chan[0] * TCAP + slot)
         def _():
             for at, value in arrange(time[0], pieces, t):
-                out[0, :, pl.ds(at, HALF_PART), :] = value
+                out[0, :, pl.ds(at, PART), :] = value
 
 
 def home(owners, chan, time, pieces):
@@ -497,7 +492,7 @@
         @pl.when(mine)
         def _():
             for at, value in arrange(time[0], pieces, t):
-                held[t, :, pl.ds(at, HALF_PART), :] = value
+                held[t, :, pl.ds(at, PART), :] = value
             copy.start()
 
     for mine, copy in copies:
@@ -537,9 +532,11 @@
     tiles = tile_list.T
     swap = [(i, i ^ 1) for i in range(NB)]
 
-    slabs = pack(chan, records, quality)
+    slabs = pack(chan, time, records, quality)
     slabs = lax.all_to_all(slabs, ("chan", "tm"), split_axis=0, concat_axis=0, tiled=True)
-    low, high, sources = whiten(chan, slabs)
+    slabs = slabs.reshape(NB, TM, ROWS, BLOCK)
+    constants = (forward_table(), *smoothing())
+    low, sources = whiten(0, chan, slabs, constants)
     sources = [sources] + [shifted(sources, "tm", -rel) for rel in range(1, TM)]
 
     def halo(white):
@@ -553,18 +550,20 @@
     inverse = inverse_table()
     order = (2, 0, 1, 3)
     low = halo(low)
-    high, low[3] = lax.optimization_barrier((high, low[3]))
+    slabs, low[3] = lax.optimization_barrier((slabs, low[3]))
+    (high,) = whiten(1, chan, slabs, constants)
+    high, sources = lax.optimization_barrier((high, sources))
     high = halo(high)
-    low, sources = lax.optimization_barrier((low, sources))
     diag = diagonal(sources)
-    spectra = cross(chan, tiles, diag, complete(low, 2))
+    spectra = cross(0, chan, tiles, diag, complete(low, 2))
     parts = stack(spectra, tuple(range(TM)), inverse)
     stay_low = [shifted(part, "tm", rel) if rel else part for rel, part in enumerate(parts)]
     high, _ = lax.optimization_barrier((high, parts))
     high = complete(high, 1)
-    spectra = cross(chan, tiles, diag, high)
+    spectra = cross(1, chan, tiles, diag, high)
     spectra, stay_low = lax.optimization_barrier((spectra, stay_low))
-    move_low = shifted(merge(stay_low), "chan", 1)
+    merged = merge(stay_low)
+    move_low = shifted(merged, "chan", 1)
     stay_high, move_high = [None] * TM, [None] * TM
     for rel in order:
         (part,) = stack(spectra, (rel,), inverse)
@@ -572,7 +571,7 @@
         if rel == 2:
             stay_high[rel], move_low = lax.optimization_barrier((stay_high[rel], move_low))
         move_high[rel] = shifted(stay_high[rel], "chan", 1)
-    result = home(tile_slot_owner, chan, time, stay_low + stay_high)
+    result = home(tile_slot_owner, chan, time, [merged] + stay_high)
     return moved(tile_slot_owner, chan, time, [move_low] + move_high, result)
 
 

time: 132 us -> 132 us (level)
  waiting for transfers between devices: 29.9 us -> 25.6 us
  starting transfers between devices: 19.4 us -> 22.7 us
    ppermute x18, waiting for transfers between devices: 29.9 us -> 25.3 us  [shifted(): lax.ppermute(value, axis, [(i, (i + distance) % count) for i in range(cou...]
    ppermute x18, starting transfers between devices: 18.4 us -> 21.4 us  [shifted(): lax.ppermute(value, axis, [(i, (i + distance) % count) for i in range(cou...]
    pallas_call x1, Pallas kernels: 0.61 us -> 2.39 us  [moved(): pl.pallas_call(moved_kernel, out_shape=jax.ShapeDtypeStruct(result.shape,...]
    pallas_call x3 -> x4, Pallas kernels: 22.4 us -> 22.6 us  [the longest x2 16.3 us: cross(): pl.pallas_call(functools.partial(cross_kernel, part), out_shape=jax.Shape...]
  transfers between devices with their start and end apart: 23 -> 23, of which waited for: 13 -> 13; matrix products, arithmetic and copies ran while one was open for 0% -> 0% of each run, Pallas kernels for 21% -> 23%
where the time goes in v6:
time: 132 us; the launch traced here: 131 us
  blocking collectives  41.1 us (31%)
  Pallas kernels  39.4 us (30%)
  waiting for transfers between devices  25.6 us (19%)
  starting transfers between devices  22.7 us (17%)
  local copies, waits for them, and re-layouts  2.26 us (2%)
    all_to_all x1, blocking collectives, per_device(): lax.all_to_all(slabs, ('chan', 'tm'), split_axis=0, concat_axis=0, tiled=...  41.1 us
    ppermute x18, waiting for transfers between devices, shifted(): lax.ppermute(value, axis, [(i, (i + distance) % count) for i in range(cou...  25.3 us
    ppermute x18, starting transfers between devices, shifted(): lax.ppermute(value, axis, [(i, (i + distance) % count) for i in range(cou...  21.4 us
    pallas_call x2, Pallas kernels, cross(): pl.pallas_call(functools.partial(cross_kernel, part), out_shape=jax.Shape...  16.3 us
    pallas_call x2, Pallas kernels, whiten(): pl.pallas_call(functools.partial(whiten_kernel, part), out_shape=shapes,...  6.33 us
    pallas_call x5, Pallas kernels, stack(): pl.pallas_call(functools.partial(stack_kernel, rels), out_shape=[jax.Shap...  4.72 us
    pallas_call x1, Pallas kernels, home(): pl.pallas_call(home_kernel, out_shape=jax.ShapeDtypeStruct((TCAP, SRC_PAR...  4.22 us
  transfers between devices with their start and end apart: 23, of which 13 were waited for; matrix products, arithmetic and copies ran while one was open for 0% of the time, Pallas kernels for 23%

profile of v6, /device:TPU:0, one launch (start us, length us, event | category | flops | bytes accessed | tf_op | source)
XLA Modules:
  0.0 131.3 jit_solution(8094033274090629060)
XLA Ops:
  0.0 1.5 %copy-done.3 = bf16[4,60,4096]{2,0,1:T(4,128)(2,1)S(1)} copy-done((bf16[4,60,4096]{2,0,1:T(4,128)(2,1)S(1)}, bf16[4,60,4096]{2,0,1:T(4,128)(2,1)}, u32[]{:S(2)}) %copy-start.3) | copy-done | bytes 1966104
  1.5 0.7 copy-done.9
  2.2 2.1 %pack.1 = bf16[128,64,128]{2,1,0:T(8,128)(2,1)S(1)} custom-call(s32[1]{0:T(128)} %bitcast.own.chan, s32[1]{0:T(128)} %bitcast.1.time, bf16[60,4,4096]{2,1,0:T(4,128)(2,1)S(1)} %bitcast.7, s32[4,128]{1,0:T(4,128)S(1)} %copy-done.9), custom_call_target="tpu_custom_call" | custom-call | tf_op jit(solution)/shard_map/pack/pallas_call | solution.py:157
  4.4 41.1 %all_to_all.5 = bf16[128,64,128]{2,1,0:T(8,128)(2,1)S(1)} all-to-all(bf16[128,64,128]{2,1,0:T(8,128)(2,1)S(1)} %pack.1), channel_id=1, replica_groups=mesh['chan'=32,'tm'=4] {'chan','tm'}, dimensions={0} | all-to-all | bytes 4194304 | tf_op jit(solution)/shard_map/all_to_all | solution.py:536
  45.5 3.5 %whiten.2 = (bf16[2,2,768,128]{3,2,1,0:T(8,128)(2,1)S(1)}, bf16[768,128]{1,0:T(8,128)(2,1)S(1)}) custom-call(s32[1]{0:T(128)} %bitcast.own.chan, bf16[32,4,64,128]{3,2,1,0:T(8,128)(2,1)S(1)} %bitcast.5, bf16[1536,2048]{1,0:T(8,128)(2,1)S(1)} %copy-done.1, bf16[768,768]{1,0:T(8,128)(2,1)S(1)} %copy-done.2, f32[768,1]{1,0:T(8,128)S(1)} %copy-done.5, ...), custom_call_target="tpu_custom_call" | custom-call | flops 1 | bytes 1 | tf_op jit(solution)/shard_map/whiten/pallas_call | solution.py:209
  49.0 0.4 collective-permute-start
  49.3 0.6 collective-permute-start.7
  50.0 4.7 %collective-permute-start.8 = (bf16[2,2,768,128]{3,2,1,0:T(8,128)(2,1)S(1)}, bf16[2,2,768,128]{3,2,1,0:T(8,128)(2,1)S(1)}, u32[]{:S(2)}, u32[]{:S(2)}) collective-permute-start(bf16[2,2,768,128]{3,2,1,0:T(8,128)(2,1)S(1)} %get-tuple-element.31.refs_0_), channel_id=1, source_target_pairs={{0,120},{4,124},{8,0},{12,4},{16,8},{20,12},{24,16},{28,20},{32,24... | collective-permute-start | bytes 2359304 | tf_op jit(solution)/shard_map/ppermute | solution.py:526
  54.7 1.4 %collective-permute-start.1 = (bf16[768,128]{1,0:T(8,128)(2,1)S(1)}, bf16[768,128]{1,0:T(8,128)(2,1)S(1)}, u32[]{:S(2)}, u32[]{:S(2)}) collective-permute-start(bf16[768,128]{1,0:T(8,128)(2,1)S(1)} %get-tuple-element.34.s0), channel_id=1, source_target_pairs={{0,3},{1,0},{2,1},{3,2},{4,7},{5,4},{6,5},{7,6},{8,11},{9,8},{10,9... | collective-permute-start | bytes 589832 | tf_op jit(solution)/shard_map/ppermute | solution.py:526
  56.1 1.2 collective-permute-start.2
  57.3 2.9 %whiten.3.refs_0_ = bf16[2,2,768,128]{3,2,1,0:T(8,128)(2,1)S(1)} custom-call(s32[1]{0:T(128)} %bitcast.own.chan, bf16[32,4,64,128]{3,2,1,0:T(8,128)(2,1)S(1)} %bitcast.6, bf16[1536,2048]{1,0:T(8,128)(2,1)S(1)} %copy-done.1, bf16[768,768]{1,0:T(8,128)(2,1)S(1)} %copy-done.2, f32[768,1]{1,0:T(8,128)S(1)} %copy-done.5), custom_call_target="tpu_custom_call" | custom-call | flops 1 | bytes 1 | tf_op jit(solution)/shard_map/whiten/pallas_call | solution.py:209
  60.2 2.3 %collective-permute-done.1.s1 = bf16[768,128]{1,0:T(8,128)(2,1)S(1)} collective-permute-done((bf16[768,128]{1,0:T(8,128)(2,1)S(1)}, bf16[768,128]{1,0:T(8,128)(2,1)S(1)}, u32[]{:S(2)}, u32[]{:S(2)}) %collective-permute-start.1) | collective-permute-done | bytes 196640 | tf_op jit(solution)/shard_map/ppermute | solution.py:526
  62.5 3.0 %collective-permute-done.2.s2 = bf16[768,128]{1,0:T(8,128)(2,1)S(1)} collective-permute-done((bf16[768,128]{1,0:T(8,128)(2,1)S(1)}, bf16[768,128]{1,0:T(8,128)(2,1)S(1)}, u32[]{:S(2)}, u32[]{:S(2)}) %collective-permute-start.2) | collective-permute-done | bytes 196640 | tf_op jit(solution)/shard_map/ppermute | solution.py:526
  65.5 2.8 %collective-permute-done.3.s3 = bf16[768,128]{1,0:T(8,128)(2,1)S(1)} collective-permute-done((bf16[768,128]{1,0:T(8,128)(2,1)S(1)}, bf16[768,128]{1,0:T(8,128)(2,1)S(1)}, u32[]{:S(2)}, u32[]{:S(2)}) %collective-permute-start.3) | collective-permute-done | bytes 196640 | tf_op jit(solution)/shard_map/ppermute | solution.py:526
  68.2 5.3 %collective-permute-start.5 = (bf16[2,2,768,128]{3,2,1,0:T(8,128)(2,1)S(1)}, bf16[2,2,768,128]{3,2,1,0:T(8,128)(2,1)S(1)}, u32[]{:S(2)}, u32[]{:S(2)}) collective-permute-start(bf16[2,2,768,128]{3,2,1,0:T(8,128)(2,1)S(1)} %whiten.3.refs_0_), channel_id=1, source_target_pairs={{0,120},{4,124},{8,0},{12,4},{16,8},{20,12},{24,16},{28,20},{32,24... | collective-permute-start | bytes 2359304 | tf_op jit(solution)/shard_map/ppermute | solution.py:526
  73.6 0.4 choose.2
  74.0 0.6 collective-permute-start.10
  74.6 0.3 collective-permute-start.9
  74.9 1.8 %diagonal.1.diag = bf16[96,128,256]{2,1,0:T(8,128)(2,1)S(1)} custom-call(bf16[768,128]{1,0:T(8,128)(2,1)S(1)} %get-tuple-element.34.s0, bf16[768,128]{1,0:T(8,128)(2,1)S(1)} %collective-permute-done.1.s1, bf16[768,128]{1,0:T(8,128)(2,1)S(1)} %collective-permute-done.2.s2, bf16[768,128]{1,0:T(8,128)(2,1)S(1)} %collective-permute-done.3.s3, ...), custom_call_target="tpu_custom_call" | custom-call | flops 1 | bytes 1 | tf_op jit(solution)/shard_map/diagonal/pallas_call | solution.py:269
  76.7 0.3 collective-permute-done.9.refs_4_
  77.0 8.1 %cross.2.spectra = bf16[8,2,768,128]{3,2,1,0:T(8,128)(2,1)S(1)} custom-call(s32[1]{0:T(128)} %bitcast.own.chan, s32[2,96]{1,0:T(2,128)S(1)} %bitcast.8, bf16[96,128,256]{2,1,0:T(8,128)(2,1)S(1)} %diagonal.1.diag, bf16[384,512]{1,0:T(8,128)(2,1)S(1)} %copy-done.4, bf16[2,2,768,128]{3,2,1,0:T(8,128)(2,1)S(1)} %get-tuple-element.31.refs_0_, ...), custom_call_target="tpu_custom_call" | custom-call | flops 1 | bytes 1 | tf_op jit(solution)/shard_map/cross/pallas_call | solution.py:365
  85.1 2.0 %stack.5 = (bf16[192,512]{1,0:T(8,128)(2,1)S(1)}, bf16[192,512]{1,0:T(8,128)(2,1)S(1)}, bf16[192,512]{1,0:T(8,128)(2,1)S(1)}, bf16[192,512]{1,0:T(8,128)(2,1)S(1)}) custom-call(bf16[8,2,768,128]{3,2,1,0:T(8,128)(2,1)S(1)} %cross.2.spectra, bf16[512,1536]{1,0:T(8,128)(2,1)S(1)} %copy-done), custom_call_target="tpu_custom_call" | custom-call | flops 1 | bytes 1 | tf_op jit(solution)/shard_map/stack/pallas_call | solution.py:404
  87.1 3.8 %collective-permute-done.4.below.refs_1_ = bf16[2,2,768,128]{3,2,1,0:T(8,128)(2,1)S(1)} collective-permute-done((bf16[2,2,768,128]{3,2,1,0:T(8,128)(2,1)S(1)}, bf16[2,2,768,128]{3,2,1,0:T(8,128)(2,1)S(1)}, u32[]{:S(2)}, u32[]{:S(2)}) %collective-permute-start.4) | collective-permute-done | bytes 786464 | tf_op jit(solution)/shard_map/ppermute | solution.py:526
  91.1 0.1 collective-permute-start.11
  91.2 0.1 collective-permute-start.12
  91.2 1.3 collective-permute-start.13
  92.5 2.4 %collective-permute-start.14 = (bf16[192,512]{1,0:T(8,128)(2,1)S(1)}, bf16[192,512]{1,0:T(8,128)(2,1)S(1)}, u32[]{:S(2)}, u32[]{:S(2)}) collective-permute-start(bf16[192,512]{1,0:T(8,128)(2,1)S(1)} %get-tuple-element.45), channel_id=1, source_target_pairs={{0,3},{1,0},{2,1},{3,2},{4,7},{5,4},{6,5},{7,6},{8,11},{9,8},{10,9... | collective-permute-start | bytes 589832 | tf_op jit(solution)/shard_map/ppermute | solution.py:526
  94.9 8.2 %cross.3.spectra = bf16[8,2,768,128]{3,2,1,0:T(8,128)(2,1)S(1)} custom-call(s32[1]{0:T(128)} %bitcast.own.chan, s32[2,96]{1,0:T(2,128)S(1)} %bitcast.9, bf16[96,128,256]{2,1,0:T(8,128)(2,1)S(1)} %diagonal.1.diag, bf16[384,512]{1,0:T(8,128)(2,1)S(1)} %copy-done.4, bf16[2,2,768,128]{3,2,1,0:T(8,128)(2,1)S(1)} %whiten.3.refs_0_, ...), custom_call_target="tpu_custom_call" | custom-call | flops 1 | bytes 1 | tf_op jit(solution)/shard_map/cross/pallas_call | solution.py:365
  103.1 0.8 collective-permute-done.12.refs_1_
  103.9 0.6 collective-permute-done.14.refs_3_
  104.5 1.0 merge.1.refs_0_
  105.6 0.1 collective-permute-start.16
  105.6 0.7 stack.8
  106.3 0.4 collective-permute-start.18
  106.8 0.7 stack.9
  107.5 2.9 %collective-permute-start.21 = (bf16[192,512]{1,0:T(8,128)(2,1)S(1)}, bf16[192,512]{1,0:T(8,128)(2,1)S(1)}, u32[]{:S(2)}, u32[]{:S(2)}) collective-permute-start(bf16[192,512]{1,0:T(8,128)(2,1)S(1)} %stack.9), channel_id=1, source_target_pairs={{0,3},{1,0},{2,1},{3,2},{4,7},{5,4},{6,5},{7,6},{8,11},{9,8},{10,9... | collective-permute-start | bytes 589832 | tf_op jit(solution)/shard_map/ppermute | solution.py:526
  110.4 0.7 stack.6
  111.1 0.8 collective-permute-start.15
  111.9 0.7 stack.7.refs_1_
  112.6 0.1 collective-permute-start.17
  112.6 1.2 collective-permute-done.18.refs_2_
  113.8 4.3 %collective-permute-done.21.refs_4_ = bf16[192,512]{1,0:T(8,128)(2,1)S(1)} collective-permute-done((bf16[192,512]{1,0:T(8,128)(2,1)S(1)}, bf16[192,512]{1,0:T(8,128)(2,1)S(1)}, u32[]{:S(2)}, u32[]{:S(2)}) %collective-permute-start.21) | collective-permute-done | bytes 196640 | tf_op jit(solution)/shard_map/ppermute | solution.py:526
  118.1 1.1 collective-permute-done.15.refs_3_
  119.2 1.2 collective-permute-done.16.refs_0_
  120.4 4.2 %home.1.refs_5_ = f32[6,4,128,512]{3,2,1,0:T(8,128)} custom-call(s32[96]{0:T(128)S(1)} %copy-done.10, s32[1]{0:T(128)} %bitcast.own.chan, s32[1]{0:T(128)} %bitcast.1.time, bf16[768,512]{1,0:T(8,128)(2,1)S(1)} %merge.1.refs_0_, bf16[192,512]{1,0:T(8,128)(2,1)S(1)} %stack.7.refs_1_, bf16[192,512]{1,0:T(8,128)(2,1)S(1)} %collective-permute-done.18.refs_2_, ...), custom_call_target="tpu_custom_call" | custom-call | flops 1 | bytes 1 | tf_op jit(solution)/shard_map/home/pallas_call | solution.py:467
  124.6 2.1 %collective-permute-done.22.refs_4_ = bf16[192,512]{1,0:T(8,128)(2,1)S(1)} collective-permute-done((bf16[192,512]{1,0:T(8,128)(2,1)S(1)}, bf16[192,512]{1,0:T(8,128)(2,1)S(1)}, u32[]{:S(2)}, u32[]{:S(2)}) %collective-permute-start.22) | collective-permute-done | bytes 196640 | tf_op jit(solution)/shard_map/ppermute | solution.py:526
  126.7 2.1 %collective-permute-done.20.refs_3_ = bf16[192,512]{1,0:T(8,128)(2,1)S(1)} collective-permute-done((bf16[192,512]{1,0:T(8,128)(2,1)S(1)}, bf16[192,512]{1,0:T(8,128)(2,1)S(1)}, u32[]{:S(2)}, u32[]{:S(2)}) %collective-permute-start.20) | collective-permute-done | bytes 196640 | tf_op jit(solution)/shard_map/ppermute | solution.py:526
  128.8 2.4 %moved.1 = f32[6,4,128,512]{3,2,1,0:T(8,128)} custom-call(s32[96]{0:T(128)S(1)} %copy-done.10, s32[1]{0:T(128)} %bitcast.own.chan, s32[1]{0:T(128)} %bitcast.1.time, bf16[768,512]{1,0:T(8,128)(2,1)S(1)} %collective-permute-done.16.refs_0_, bf16[192,512]{1,0:T(8,128)(2,1)S(1)} %collective-permute-done.17.refs_1_, ...), custom_call_target="tpu_custom_call", output_to_operand_aliasing={{}: (8, {})} | custom-call | flops 1 | bytes 1 | tf_op jit(solution)/shard_map/moved/pallas_call | solution.py:506
  (37 shorter events, 0.1 us)
Async XLA Ops:
  0.0 1.5 %copy-start.3 = (bf16[4,60,4096]{2,0,1:T(4,128)(2,1)S(1)}, bf16[4,60,4096]{2,0,1:T(4,128)(2,1)}, u32[]{:S(2)}) copy-start(bf16[4,60,4096]{2,0,1:T(4,128)(2,1)} %param.12) | copy-start | bytes 5898244
  1.5 0.7 copy-start.9
  2.2 43.2 %copy-start.1 = (bf16[1536,2048]{1,0:T(8,128)(2,1)S(1)}, bf16[1536,2048]{1,0:T(8,128)(2,1)}, u32[]{:S(2)}) copy-start(bf16[1536,2048]{1,0:T(8,128)(2,1)} %constant.23.clone.table) | copy-start | bytes 18874372
  2.2 43.2 %copy-start.2 = (bf16[768,768]{1,0:T(8,128)(2,1)S(1)}, bf16[768,768]{1,0:T(8,128)(2,1)}, u32[]{:S(2)}) copy-start(bf16[768,768]{1,0:T(8,128)(2,1)} %constant.24.clone.inside) | copy-start | bytes 3538948
  2.2 43.2 %copy-start.5 = (f32[768,1]{1,0:T(8,128)S(1)}, f32[768,1]{1,0:T(8,128)}, u32[]{:S(2)}) copy-start(f32[768,1]{1,0:T(8,128)} %constant.25.clone.inverse_count) | copy-start | bytes 9220
  2.2 43.2 %copy-start.7 = (bf16[2,2,128,128]{3,2,1,0:T(8,128)(2,1)S(1)}, bf16[2,2,128,128]{3,2,1,0:T(8,128)(2,1)}, u32[]{:S(2)}) copy-start(bf16[2,2,128,128]{3,2,1,0:T(8,128)(2,1)} %constant.26.clone.refs_0_) | copy-start | bytes 393220
  49.0 8.4 %collective-permute-start = (bf16[2,2,768,128]{3,2,1,0:T(8,128)(2,1)S(1)}, bf16[2,2,768,128]{3,2,1,0:T(8,128)(2,1)S(1)}, u32[]{:S(2)}, u32[]{:S(2)}) collective-permute-start(bf16[2,2,768,128]{3,2,1,0:T(8,128)(2,1)S(1)} %get-tuple-element.31.refs_0_), channel_id=1, source_target_pairs={{0,4},{4,0},{8,12},{12,8},{16,20},{20,16},{24,28},{28,24},{32,36},... | collective-permute-start | bytes 2359304 | tf_op jit(solution)/shard_map/ppermute | solution.py:543
  49.3 24.2 %collective-permute-start.7 = (bf16[2,2,768,128]{3,2,1,0:T(8,128)(2,1)S(1)}, bf16[2,2,768,128]{3,2,1,0:T(8,128)(2,1)S(1)}, u32[]{:S(2)}, u32[]{:S(2)}) collective-permute-start(bf16[2,2,768,128]{3,2,1,0:T(8,128)(2,1)S(1)} %get-tuple-element.31.refs_0_), channel_id=1, source_target_pairs={{0,8},{4,12},{8,16},{12,20},{16,24},{20,28},{24,32},{28,36},{32,40... | collective-permute-start | bytes 2359304 | tf_op jit(solution)/shard_map/ppermute | solution.py:526
  50.0 23.6 %collective-permute-start.8 = (bf16[2,2,768,128]{3,2,1,0:T(8,128)(2,1)S(1)}, bf16[2,2,768,128]{3,2,1,0:T(8,128)(2,1)S(1)}, u32[]{:S(2)}, u32[]{:S(2)}) collective-permute-start(bf16[2,2,768,128]{3,2,1,0:T(8,128)(2,1)S(1)} %get-tuple-element.31.refs_0_), channel_id=1, source_target_pairs={{0,120},{4,124},{8,0},{12,4},{16,8},{20,12},{24,16},{28,20},{32,24... | collective-permute-start | bytes 2359304 | tf_op jit(solution)/shard_map/ppermute | solution.py:526
  54.7 20.2 %copy-start.6 = (bf16[4,128,256]{2,1,0:T(8,128)(2,1)S(1)}, bf16[4,128,256]{2,1,0:T(8,128)(2,1)}, u32[]{:S(2)}) copy-start(bf16[4,128,256]{2,1,0:T(8,128)(2,1)} %constant.27.clone.spread) | copy-start | bytes 786436
  54.7 7.8 %collective-permute-start.1 = (bf16[768,128]{1,0:T(8,128)(2,1)S(1)}, bf16[768,128]{1,0:T(8,128)(2,1)S(1)}, u32[]{:S(2)}, u32[]{:S(2)}) collective-permute-start(bf16[768,128]{1,0:T(8,128)(2,1)S(1)} %get-tuple-element.34.s0), channel_id=1, source_target_pairs={{0,3},{1,0},{2,1},{3,2},{4,7},{5,4},{6,5},{7,6},{8,11},{9,8},{10,9... | collective-permute-start | bytes 589832 | tf_op jit(solution)/shard_map/ppermute | solution.py:526
  56.1 9.4 %collective-permute-start.2 = (bf16[768,128]{1,0:T(8,128)(2,1)S(1)}, bf16[768,128]{1,0:T(8,128)(2,1)S(1)}, u32[]{:S(2)}, u32[]{:S(2)}) collective-permute-start(bf16[768,128]{1,0:T(8,128)(2,1)S(1)} %get-tuple-element.34.s0), channel_id=1, source_target_pairs={{0,2},{1,3},{2,0},{3,1},{4,6},{5,7},{6,4},{7,5},{8,10},{9,11},{10,... | collective-permute-start | bytes 589832 | tf_op jit(solution)/shard_map/ppermute | solution.py:526
  57.3 10.9 %collective-permute-start.3 = (bf16[768,128]{1,0:T(8,128)(2,1)S(1)}, bf16[768,128]{1,0:T(8,128)(2,1)S(1)}, u32[]{:S(2)}, u32[]{:S(2)}) collective-permute-start(bf16[768,128]{1,0:T(8,128)(2,1)S(1)} %get-tuple-element.34.s0), channel_id=1, source_target_pairs={{0,1},{1,2},{2,3},{3,0},{4,5},{5,6},{6,7},{7,4},{8,9},{9,10},{10,1... | collective-permute-start | bytes 589832 | tf_op jit(solution)/shard_map/ppermute | solution.py:526
  68.2 22.8 %collective-permute-start.4 = (bf16[2,2,768,128]{3,2,1,0:T(8,128)(2,1)S(1)}, bf16[2,2,768,128]{3,2,1,0:T(8,128)(2,1)S(1)}, u32[]{:S(2)}, u32[]{:S(2)}) collective-permute-start(bf16[2,2,768,128]{3,2,1,0:T(8,128)(2,1)S(1)} %whiten.3.refs_0_), channel_id=1, source_target_pairs={{0,8},{4,12},{8,16},{12,20},{16,24},{20,28},{24,32},{28,36},{32,40... | collective-permute-start | bytes 2359304 | tf_op jit(solution)/shard_map/ppermute | solution.py:526
  68.2 22.8 %collective-permute-start.5 = (bf16[2,2,768,128]{3,2,1,0:T(8,128)(2,1)S(1)}, bf16[2,2,768,128]{3,2,1,0:T(8,128)(2,1)S(1)}, u32[]{:S(2)}, u32[]{:S(2)}) collective-permute-start(bf16[2,2,768,128]{3,2,1,0:T(8,128)(2,1)S(1)} %whiten.3.refs_0_), channel_id=1, source_target_pairs={{0,120},{4,124},{8,0},{12,4},{16,8},{20,12},{24,16},{28,20},{32,24... | collective-permute-start | bytes 2359304 | tf_op jit(solution)/shard_map/ppermute | solution.py:526
  73.6 17.4 %collective-permute-start.6 = (bf16[2,2,768,128]{3,2,1,0:T(8,128)(2,1)S(1)}, bf16[2,2,768,128]{3,2,1,0:T(8,128)(2,1)S(1)}, u32[]{:S(2)}, u32[]{:S(2)}) collective-permute-start(bf16[2,2,768,128]{3,2,1,0:T(8,128)(2,1)S(1)} %whiten.3.refs_0_), channel_id=1, source_target_pairs={{0,4},{4,0},{8,12},{12,8},{16,20},{20,16},{24,28},{28,24},{32,36},... | collective-permute-start | bytes 2359304 | tf_op jit(solution)/shard_map/ppermute | solution.py:543
  74.0 2.7 %collective-permute-start.10 = (bf16[1,2,768,128]{3,2,1,0:T(8,128)(2,1)S(1)}, bf16[1,2,768,128]{3,2,1,0:T(8,128)(2,1)S(1)}, u32[]{:S(2)}, u32[]{:S(2)}) collective-permute-start(bf16[1,2,768,128]{3,2,1,0:T(8,128)(2,1)S(1)} %get-tuple-element.41), channel_id=1, source_target_pairs={{0,4},{4,0},{8,12},{12,8},{16,20},{20,16},{24,28},{28,24},{32,36},... | collective-permute-start | bytes 1179656 | tf_op jit(solution)/shard_map/ppermute | solution.py:548
  74.6 2.4 %copy-start.4 = (bf16[384,512]{1,0:T(8,128)(2,1)S(1)}, bf16[384,512]{1,0:T(8,128)(2,1)}, u32[]{:S(2)}) copy-start(bf16[384,512]{1,0:T(8,128)(2,1)} %constant.28.clone.order) | copy-start | bytes 1179652
  74.6 2.4 %copy-start.8 = (s32[96,2]{0,1:T(2,128)S(1)}, s32[96,2]{0,1:T(2,128)}, u32[]{:S(2)}) copy-start(s32[96,2]{0,1:T(2,128)} %param.14) | copy-start | bytes 2308
  74.6 2.4 %collective-permute-start.9 = (bf16[1,2,768,128]{3,2,1,0:T(8,128)(2,1)S(1)}, bf16[1,2,768,128]{3,2,1,0:T(8,128)(2,1)S(1)}, u32[]{:S(2)}, u32[]{:S(2)}) collective-permute-start(bf16[1,2,768,128]{3,2,1,0:T(8,128)(2,1)S(1)} %get-tuple-element.40), channel_id=1, source_target_pairs={{0,4},{4,0},{8,12},{12,8},{16,20},{20,16},{24,28},{28,24},{32,36},... | collective-permute-start | bytes 1179656 | tf_op jit(solution)/shard_map/ppermute | solution.py:548
  77.0 8.1 %copy-start = (bf16[512,1536]{1,0:T(8,128)(2,1)S(1)}, bf16[512,1536]{1,0:T(8,128)(2,1)}, u32[]{:S(2)}) copy-start(bf16[512,1536]{1,0:T(8,128)(2,1)} %constant.29.clone.inverse) | copy-start | bytes 4718596
  91.1 3.8 %collective-permute-start.11 = (bf16[2,2,768,128]{3,2,1,0:T(8,128)(2,1)S(1)}, bf16[2,2,768,128]{3,2,1,0:T(8,128)(2,1)S(1)}, u32[]{:S(2)}, u32[]{:S(2)}) collective-permute-start(bf16[2,2,768,128]{3,2,1,0:T(8,128)(2,1)S(1)} %choose.3), channel_id=1, source_target_pairs={{0,4},{4,0},{8,12},{12,8},{16,20},{20,16},{24,28},{28,24},{32,36},... | collective-permute-start | bytes 2359304 | tf_op jit(solution)/shard_map/ppermute | solution.py:548
  91.2 12.7 %collective-permute-start.12 = (bf16[192,512]{1,0:T(8,128)(2,1)S(1)}, bf16[192,512]{1,0:T(8,128)(2,1)S(1)}, u32[]{:S(2)}, u32[]{:S(2)}) collective-permute-start(bf16[192,512]{1,0:T(8,128)(2,1)S(1)} %get-tuple-element.43), channel_id=1, source_target_pairs={{0,1},{1,2},{2,3},{3,0},{4,5},{5,6},{6,7},{7,4},{8,9},{9,10},{10,1... | collective-permute-start | bytes 589832 | tf_op jit(solution)/shard_map/ppermute | solution.py:526
  91.2 12.7 %collective-permute-start.13 = (bf16[192,512]{1,0:T(8,128)(2,1)S(1)}, bf16[192,512]{1,0:T(8,128)(2,1)S(1)}, u32[]{:S(2)}, u32[]{:S(2)}) collective-permute-start(bf16[192,512]{1,0:T(8,128)(2,1)S(1)} %get-tuple-element.44), channel_id=1, source_target_pairs={{0,2},{1,3},{2,0},{3,1},{4,6},{5,7},{6,4},{7,5},{8,10},{9,11},{10,... | collective-permute-start | bytes 589832 | tf_op jit(solution)/shard_map/ppermute | solution.py:526
  92.5 12.0 %collective-permute-start.14 = (bf16[192,512]{1,0:T(8,128)(2,1)S(1)}, bf16[192,512]{1,0:T(8,128)(2,1)S(1)}, u32[]{:S(2)}, u32[]{:S(2)}) collective-permute-start(bf16[192,512]{1,0:T(8,128)(2,1)S(1)} %get-tuple-element.45), channel_id=1, source_target_pairs={{0,3},{1,0},{2,1},{3,2},{4,7},{5,4},{6,5},{7,6},{8,11},{9,8},{10,9... | collective-permute-start | bytes 589832 | tf_op jit(solution)/shard_map/ppermute | solution.py:526
  105.6 14.8 %collective-permute-start.16 = (bf16[768,512]{1,0:T(8,128)(2,1)S(1)}, bf16[768,512]{1,0:T(8,128)(2,1)S(1)}, u32[]{:S(2)}, u32[]{:S(2)}) collective-permute-start(bf16[768,512]{1,0:T(8,128)(2,1)S(1)} %merge.1.refs_0_), channel_id=1, source_target_pairs={{0,4},{4,8},{8,12},{12,16},{16,20},{20,24},{24,28},{28,32},{32,36}... | collective-permute-start | bytes 2359304 | tf_op jit(solution)/shard_map/ppermute | solution.py:526
  106.3 7.5 %collective-permute-start.18 = (bf16[192,512]{1,0:T(8,128)(2,1)S(1)}, bf16[192,512]{1,0:T(8,128)(2,1)S(1)}, u32[]{:S(2)}, u32[]{:S(2)}) collective-permute-start(bf16[192,512]{1,0:T(8,128)(2,1)S(1)} %stack.8), channel_id=1, source_target_pairs={{0,1},{1,2},{2,3},{3,0},{4,5},{5,6},{6,7},{7,4},{8,9},{9,10},{10,1... | collective-permute-start | bytes 589832 | tf_op jit(solution)/shard_map/ppermute | solution.py:526
  107.5 10.6 %collective-permute-start.21 = (bf16[192,512]{1,0:T(8,128)(2,1)S(1)}, bf16[192,512]{1,0:T(8,128)(2,1)S(1)}, u32[]{:S(2)}, u32[]{:S(2)}) collective-permute-start(bf16[192,512]{1,0:T(8,128)(2,1)S(1)} %stack.9), channel_id=1, source_target_pairs={{0,3},{1,0},{2,1},{3,2},{4,7},{5,4},{6,5},{7,6},{8,11},{9,8},{10,9... | collective-permute-start | bytes 589832 | tf_op jit(solution)/shard_map/ppermute | solution.py:526
  111.1 9.3 %copy-start.10 = (s32[96]{0:T(128)S(1)}, s32[96]{0:T(128)}, u32[]{:S(2)}) copy-start(s32[96]{0:T(128)} %owners.3) | copy-start | bytes 1156
  111.1 8.1 %collective-permute-start.15 = (bf16[192,512]{1,0:T(8,128)(2,1)S(1)}, bf16[192,512]{1,0:T(8,128)(2,1)S(1)}, u32[]{:S(2)}, u32[]{:S(2)}) collective-permute-start(bf16[192,512]{1,0:T(8,128)(2,1)S(1)} %stack.6), channel_id=1, source_target_pairs={{0,2},{1,3},{2,0},{3,1},{4,6},{5,7},{6,4},{7,5},{8,10},{9,11},{10,... | collective-permute-start | bytes 589832 | tf_op jit(solution)/shard_map/ppermute | solution.py:526
  112.6 12.0 %collective-permute-start.17 = (bf16[192,512]{1,0:T(8,128)(2,1)S(1)}, bf16[192,512]{1,0:T(8,128)(2,1)S(1)}, u32[]{:S(2)}, u32[]{:S(2)}) collective-permute-start(bf16[192,512]{1,0:T(8,128)(2,1)S(1)} %stack.7.refs_1_), channel_id=1, source_target_pairs={{0,4},{4,8},{8,12},{12,16},{16,20},{20,24},{24,28},{28,32},{32,36}... | collective-permute-start | bytes 589832 | tf_op jit(solution)/shard_map/ppermute | solution.py:526
  113.8 10.8 %collective-permute-start.19 = (bf16[192,512]{1,0:T(8,128)(2,1)S(1)}, bf16[192,512]{1,0:T(8,128)(2,1)S(1)}, u32[]{:S(2)}, u32[]{:S(2)}) collective-permute-start(bf16[192,512]{1,0:T(8,128)(2,1)S(1)} %collective-permute-done.18.refs_2_), channel_id=1, source_target_pairs={{0,4},{4,8},{8,12},{12,16},{16,20},{20,24},{24,28},{28,32},{32,36}... | collective-permute-start | bytes 589832 | tf_op jit(solution)/shard_map/ppermute | solution.py:526
  118.1 8.6 %collective-permute-start.22 = (bf16[192,512]{1,0:T(8,128)(2,1)S(1)}, bf16[192,512]{1,0:T(8,128)(2,1)S(1)}, u32[]{:S(2)}, u32[]{:S(2)}) collective-permute-start(bf16[192,512]{1,0:T(8,128)(2,1)S(1)} %collective-permute-done.21.refs_4_), channel_id=1, source_target_pairs={{0,4},{4,8},{8,12},{12,16},{16,20},{20,24},{24,28},{28,32},{32,36}... | collective-permute-start | bytes 589832 | tf_op jit(solution)/shard_map/ppermute | solution.py:526
  120.4 8.4 %collective-permute-start.20 = (bf16[192,512]{1,0:T(8,128)(2,1)S(1)}, bf16[192,512]{1,0:T(8,128)(2,1)S(1)}, u32[]{:S(2)}, u32[]{:S(2)}) collective-permute-start(bf16[192,512]{1,0:T(8,128)(2,1)S(1)} %collective-permute-done.15.refs_3_), channel_id=1, source_target_pairs={{0,4},{4,8},{8,12},{12,16},{16,20},{20,24},{24,28},{28,32},{32,36}... | collective-permute-start | bytes 589832 | tf_op jit(solution)/shard_map/ppermute | solution.py:526

commit v7 on v6

--- a/solution.py
+++ b/solution.py
@@ -439,12 +439,11 @@
     )(*pieces)
 
 
-def arrange(time, pieces, t):
+def arrange(time, low, pieces, rels, t):
     rows = SRC_PART * HALF_PART
-    low, pieces = pieces[0], pieces[1:]
-    for rel in range(TM):
+    for rel, piece in zip(rels, pieces):
         halves = []
-        for ref, first in ((low, rel * TPS * rows), (pieces[rel], 0)):
+        for ref, first in ((low, rel * TPS * rows), (piece, 0)):
             value = ref[first + t * rows : first + (t + 1) * rows, :].astype(F32)
             halves.append(value.reshape(SRC_PART * HALF_PART // 4, 4, LAG_COUNT))
         value = jnp.concatenate(halves, axis=1).reshape(SRC_PART, PART, LAG_COUNT)
@@ -459,7 +458,7 @@
 
         @pl.when(owners[chan[0] * TPS + t] == chan[0] * TCAP + slot)
         def _():
-            for at, value in arrange(time[0], pieces, t):
+            for at, value in arrange(time[0], pieces[0], pieces[1:], range(TM), t):
                 out[0, :, pl.ds(at, PART), :] = value
 
 
@@ -479,40 +478,44 @@
     )(owners, chan, time, *pieces)
 
 
-def moved_kernel(owners, chan, time, *refs):
-    pieces, (_, out, held, sem) = refs[:-4], refs[-4:]
+def moved_kernel(rels, owners, chan, time, *refs):
+    (low, *pieces), (_, out, held, sem) = refs[:-4], refs[-4:]
     source = lax.rem(chan[0] + NB - 1, NB)
     copies = []
     for t in range(TPS):
         slot = owners[source * TPS + t] - chan[0] * TCAP
         mine = (slot >= 0) & (slot < TCAP)
-        copy = pltpu.make_async_copy(held.at[t], out.at[jnp.clip(slot, 0, TCAP - 1)], sem.at[t])
-        copies.append((mine, copy))
+        place = out.at[jnp.clip(slot, 0, TCAP - 1)]
 
         @pl.when(mine)
         def _():
-            for at, value in arrange(time[0], pieces, t):
-                held[t, :, pl.ds(at, PART), :] = value
-            copy.start()
-
-    for mine, copy in copies:
+            for index, (at, value) in enumerate(arrange(time[0], low, pieces, rels, t)):
+                held[t, index] = value
+                part = place.at[:, pl.ds(at, PART), :]
+                pltpu.make_async_copy(held.at[t, index], part, sem.at[t, index]).start()
+
+        copies.append((mine, place, t))
+
+    for mine, place, t in copies:
 
         @pl.when(mine)
         def _():
-            copy.wait()
-
-
-def moved(owners, chan, time, pieces, result):
-    return pl.pallas_call(
-        moved_kernel,
+            for index in range(len(rels)):
+                part = place.at[:, pl.ds(0, PART), :]
+                pltpu.make_async_copy(held.at[t, index], part, sem.at[t, index]).wait()
+
+
+def moved(rels, owners, chan, time, pieces, result):
+    return pl.pallas_call(
+        functools.partial(moved_kernel, rels),
         out_shape=jax.ShapeDtypeStruct(result.shape, result.dtype),
         in_specs=[pl.BlockSpec(memory_space=pltpu.SMEM)] * 3
         + [pl.BlockSpec(memory_space=pltpu.VMEM) for _ in pieces]
         + [pl.BlockSpec(memory_space=pl.ANY)],
         out_specs=pl.BlockSpec(memory_space=pl.ANY),
         scratch_shapes=[
-            pltpu.VMEM((TPS, SRC_PART, BLOCK, LAG_COUNT), F32),
-            pltpu.SemaphoreType.DMA((TPS,)),
+            pltpu.VMEM((TPS, len(rels), SRC_PART, PART, LAG_COUNT), F32),
+            pltpu.SemaphoreType.DMA((TPS, len(rels))),
         ],
         input_output_aliases={3 + len(pieces): 0},
         compiler_params=pltpu.CompilerParams(vmem_limit_bytes=12 * MIB),
@@ -568,11 +571,13 @@
     for rel in order:
         (part,) = stack(spectra, (rel,), inverse)
         stay_high[rel] = shifted(part, "tm", rel) if rel else part
-        if rel == 2:
-            stay_high[rel], move_low = lax.optimization_barrier((stay_high[rel], move_low))
         move_high[rel] = shifted(stay_high[rel], "chan", 1)
+    stay_high, move_low = lax.optimization_barrier((stay_high, move_low))
     result = home(tile_slot_owner, chan, time, [merged] + stay_high)
-    return moved(tile_slot_owner, chan, time, [move_low] + move_high, result)
+    for rels in ((0, 2, 1), (3,)):
+        pieces = [move_low] + [move_high[rel] for rel in rels]
+        result = moved(rels, tile_slot_owner, chan, time, pieces, result)
+    return result
 
 
 def solution(mesh):

time: 132 us -> 131 us (level)
  waiting for transfers between devices: 25.6 us -> 23.9 us
    ppermute x18, waiting for transfers between devices: 25.3 us -> 23.6 us  [shifted(): lax.ppermute(value, axis, [(i, (i + distance) % count) for i in range(cou...]
    pallas_call x1 -> x2, Pallas kernels: 2.39 us -> 3.22 us  [moved(): pl.pallas_call(functools.partial(moved_kernel, rels), out_shape=jax.Shape...]
  transfers between devices with their start and end apart: 23 -> 23, of which waited for: 13 -> 14; matrix products, arithmetic and copies ran while one was open for 0% -> 0% of each run, Pallas kernels for 23% -> 25%
where the time goes in v7:
time: 131 us
  blocking collectives  41.1 us (31%)
  Pallas kernels  40.3 us (31%)
  waiting for transfers between devices  23.9 us (18%)
  starting transfers between devices  23.1 us (18%)
  local copies, waits for them, and re-layouts  2.26 us (2%)
    all_to_all x1, blocking collectives, per_device(): lax.all_to_all(slabs, ('chan', 'tm'), split_axis=0, concat_axis=0, tiled=...  41.1 us
    ppermute x18, waiting for transfers between devices, shifted(): lax.ppermute(value, axis, [(i, (i + distance) % count) for i in range(cou...  23.6 us
    ppermute x18, starting transfers between devices, shifted(): lax.ppermute(value, axis, [(i, (i + distance) % count) for i in range(cou...  21.8 us
    pallas_call x2, Pallas kernels, cross(): pl.pallas_call(functools.partial(cross_kernel, part), out_shape=jax.Shape...  16.5 us
    pallas_call x2, Pallas kernels, whiten(): pl.pallas_call(functools.partial(whiten_kernel, part), out_shape=shapes,...  6.33 us
    pallas_call x5, Pallas kernels, stack(): pl.pallas_call(functools.partial(stack_kernel, rels), out_shape=[jax.Shap...  4.73 us
    pallas_call x1, Pallas kernels, home(): pl.pallas_call(home_kernel, out_shape=jax.ShapeDtypeStruct((TCAP, SRC_PAR...  4.09 us
    pallas_call x2, Pallas kernels, moved(): pl.pallas_call(functools.partial(moved_kernel, rels), out_shape=jax.Shape...  3.22 us
  transfers between devices with their start and end apart: 23, of which 14 were waited for; matrix products, arithmetic and copies ran while one was open for 0% of the time, Pallas kernels for 25%

profile of v7, /device:TPU:0, one launch (start us, length us, event | category | flops | bytes accessed | tf_op | source)
XLA Modules:
  0.0 131.0 jit_solution(3027002717106930372)
XLA Ops:
  0.0 1.5 %copy-done.3 = bf16[4,60,4096]{2,0,1:T(4,128)(2,1)S(1)} copy-done((bf16[4,60,4096]{2,0,1:T(4,128)(2,1)S(1)}, bf16[4,60,4096]{2,0,1:T(4,128)(2,1)}, u32[]{:S(2)}) %copy-start.3) | copy-done | bytes 1966104
  1.5 0.7 copy-done.10
  2.2 2.1 %pack.1 = bf16[128,64,128]{2,1,0:T(8,128)(2,1)S(1)} custom-call(s32[1]{0:T(128)} %bitcast.own.chan, s32[1]{0:T(128)} %bitcast.1.time, bf16[60,4,4096]{2,1,0:T(4,128)(2,1)S(1)} %bitcast.7, s32[4,128]{1,0:T(4,128)S(1)} %copy-done.10), custom_call_target="tpu_custom_call" | custom-call | tf_op jit(solution)/shard_map/pack/pallas_call | solution.py:157
  4.4 41.1 %all_to_all.5 = bf16[128,64,128]{2,1,0:T(8,128)(2,1)S(1)} all-to-all(bf16[128,64,128]{2,1,0:T(8,128)(2,1)S(1)} %pack.1), channel_id=1, replica_groups=mesh['chan'=32,'tm'=4] {'chan','tm'}, dimensions={0} | all-to-all | bytes 4194304 | tf_op jit(solution)/shard_map/all_to_all | solution.py:539
  45.5 3.5 %whiten.2 = (bf16[2,2,768,128]{3,2,1,0:T(8,128)(2,1)S(1)}, bf16[768,128]{1,0:T(8,128)(2,1)S(1)}) custom-call(s32[1]{0:T(128)} %bitcast.own.chan, bf16[32,4,64,128]{3,2,1,0:T(8,128)(2,1)S(1)} %bitcast.5, bf16[1536,2048]{1,0:T(8,128)(2,1)S(1)} %copy-done.1, bf16[768,768]{1,0:T(8,128)(2,1)S(1)} %copy-done.2, f32[768,1]{1,0:T(8,128)S(1)} %copy-done.5, ...), custom_call_target="tpu_custom_call" | custom-call | flops 1 | bytes 1 | tf_op jit(solution)/shard_map/whiten/pallas_call | solution.py:209
  49.0 0.4 collective-permute-start
  49.3 0.6 collective-permute-start.7
  50.0 4.7 %collective-permute-start.8 = (bf16[2,2,768,128]{3,2,1,0:T(8,128)(2,1)S(1)}, bf16[2,2,768,128]{3,2,1,0:T(8,128)(2,1)S(1)}, u32[]{:S(2)}, u32[]{:S(2)}) collective-permute-start(bf16[2,2,768,128]{3,2,1,0:T(8,128)(2,1)S(1)} %get-tuple-element.34.refs_0_), channel_id=1, source_target_pairs={{0,120},{4,124},{8,0},{12,4},{16,8},{20,12},{24,16},{28,20},{32,24... | collective-permute-start | bytes 2359304 | tf_op jit(solution)/shard_map/ppermute | solution.py:529
  54.7 1.4 %collective-permute-start.1 = (bf16[768,128]{1,0:T(8,128)(2,1)S(1)}, bf16[768,128]{1,0:T(8,128)(2,1)S(1)}, u32[]{:S(2)}, u32[]{:S(2)}) collective-permute-start(bf16[768,128]{1,0:T(8,128)(2,1)S(1)} %get-tuple-element.37.s0), channel_id=1, source_target_pairs={{0,3},{1,0},{2,1},{3,2},{4,7},{5,4},{6,5},{7,6},{8,11},{9,8},{10,9... | collective-permute-start | bytes 589832 | tf_op jit(solution)/shard_map/ppermute | solution.py:529
  56.1 1.2 collective-permute-start.2
  57.3 2.9 %whiten.3.refs_0_ = bf16[2,2,768,128]{3,2,1,0:T(8,128)(2,1)S(1)} custom-call(s32[1]{0:T(128)} %bitcast.own.chan, bf16[32,4,64,128]{3,2,1,0:T(8,128)(2,1)S(1)} %bitcast.6, bf16[1536,2048]{1,0:T(8,128)(2,1)S(1)} %copy-done.1, bf16[768,768]{1,0:T(8,128)(2,1)S(1)} %copy-done.2, f32[768,1]{1,0:T(8,128)S(1)} %copy-done.5), custom_call_target="tpu_custom_call" | custom-call | flops 1 | bytes 1 | tf_op jit(solution)/shard_map/whiten/pallas_call | solution.py:209
  60.2 2.3 %collective-permute-done.1.s1 = bf16[768,128]{1,0:T(8,128)(2,1)S(1)} collective-permute-done((bf16[768,128]{1,0:T(8,128)(2,1)S(1)}, bf16[768,128]{1,0:T(8,128)(2,1)S(1)}, u32[]{:S(2)}, u32[]{:S(2)}) %collective-permute-start.1) | collective-permute-done | bytes 196640 | tf_op jit(solution)/shard_map/ppermute | solution.py:529
  62.5 3.0 %collective-permute-done.2.s2 = bf16[768,128]{1,0:T(8,128)(2,1)S(1)} collective-permute-done((bf16[768,128]{1,0:T(8,128)(2,1)S(1)}, bf16[768,128]{1,0:T(8,128)(2,1)S(1)}, u32[]{:S(2)}, u32[]{:S(2)}) %collective-permute-start.2) | collective-permute-done | bytes 196640 | tf_op jit(solution)/shard_map/ppermute | solution.py:529
  65.5 2.8 %collective-permute-done.3.s3 = bf16[768,128]{1,0:T(8,128)(2,1)S(1)} collective-permute-done((bf16[768,128]{1,0:T(8,128)(2,1)S(1)}, bf16[768,128]{1,0:T(8,128)(2,1)S(1)}, u32[]{:S(2)}, u32[]{:S(2)}) %collective-permute-start.3) | collective-permute-done | bytes 196640 | tf_op jit(solution)/shard_map/ppermute | solution.py:529
  68.2 5.3 %collective-permute-start.5 = (bf16[2,2,768,128]{3,2,1,0:T(8,128)(2,1)S(1)}, bf16[2,2,768,128]{3,2,1,0:T(8,128)(2,1)S(1)}, u32[]{:S(2)}, u32[]{:S(2)}) collective-permute-start(bf16[2,2,768,128]{3,2,1,0:T(8,128)(2,1)S(1)} %whiten.3.refs_0_), channel_id=1, source_target_pairs={{0,120},{4,124},{8,0},{12,4},{16,8},{20,12},{24,16},{28,20},{32,24... | collective-permute-start | bytes 2359304 | tf_op jit(solution)/shard_map/ppermute | solution.py:529
  73.6 0.4 choose.2
  74.0 0.6 collective-permute-start.10
  74.6 0.3 collective-permute-start.9
  74.9 1.8 %diagonal.1.diag = bf16[96,128,256]{2,1,0:T(8,128)(2,1)S(1)} custom-call(bf16[768,128]{1,0:T(8,128)(2,1)S(1)} %get-tuple-element.37.s0, bf16[768,128]{1,0:T(8,128)(2,1)S(1)} %collective-permute-done.1.s1, bf16[768,128]{1,0:T(8,128)(2,1)S(1)} %collective-permute-done.2.s2, bf16[768,128]{1,0:T(8,128)(2,1)S(1)} %collective-permute-done.3.s3, ...), custom_call_target="tpu_custom_call" | custom-call | flops 1 | bytes 1 | tf_op jit(solution)/shard_map/diagonal/pallas_call | solution.py:269
  76.7 0.3 collective-permute-done.9.refs_4_
  77.0 8.4 %cross.2.spectra = bf16[8,2,768,128]{3,2,1,0:T(8,128)(2,1)S(1)} custom-call(s32[1]{0:T(128)} %bitcast.own.chan, s32[2,96]{1,0:T(2,128)S(1)} %bitcast.8, bf16[96,128,256]{2,1,0:T(8,128)(2,1)S(1)} %diagonal.1.diag, bf16[384,512]{1,0:T(8,128)(2,1)S(1)} %copy-done.4, bf16[2,2,768,128]{3,2,1,0:T(8,128)(2,1)S(1)} %get-tuple-element.34.refs_0_, ...), custom_call_target="tpu_custom_call" | custom-call | flops 1 | bytes 1 | tf_op jit(solution)/shard_map/cross/pallas_call | solution.py:365
  85.4 2.0 %stack.5 = (bf16[192,512]{1,0:T(8,128)(2,1)S(1)}, bf16[192,512]{1,0:T(8,128)(2,1)S(1)}, bf16[192,512]{1,0:T(8,128)(2,1)S(1)}, bf16[192,512]{1,0:T(8,128)(2,1)S(1)}) custom-call(bf16[8,2,768,128]{3,2,1,0:T(8,128)(2,1)S(1)} %cross.2.spectra, bf16[512,1536]{1,0:T(8,128)(2,1)S(1)} %copy-done), custom_call_target="tpu_custom_call" | custom-call | flops 1 | bytes 1 | tf_op jit(solution)/shard_map/stack/pallas_call | solution.py:404
  87.4 3.6 %collective-permute-done.4.below.refs_1_ = bf16[2,2,768,128]{3,2,1,0:T(8,128)(2,1)S(1)} collective-permute-done((bf16[2,2,768,128]{3,2,1,0:T(8,128)(2,1)S(1)}, bf16[2,2,768,128]{3,2,1,0:T(8,128)(2,1)S(1)}, u32[]{:S(2)}, u32[]{:S(2)}) %collective-permute-start.4) | collective-permute-done | bytes 786464 | tf_op jit(solution)/shard_map/ppermute | solution.py:529
  91.1 0.1 collective-permute-start.11
  91.2 0.1 collective-permute-start.12
  91.2 1.3 collective-permute-start.13
  92.5 2.4 %collective-permute-start.14 = (bf16[192,512]{1,0:T(8,128)(2,1)S(1)}, bf16[192,512]{1,0:T(8,128)(2,1)S(1)}, u32[]{:S(2)}, u32[]{:S(2)}) collective-permute-start(bf16[192,512]{1,0:T(8,128)(2,1)S(1)} %get-tuple-element.48), channel_id=1, source_target_pairs={{0,3},{1,0},{2,1},{3,2},{4,7},{5,4},{6,5},{7,6},{8,11},{9,8},{10,9... | collective-permute-start | bytes 589832 | tf_op jit(solution)/shard_map/ppermute | solution.py:529
  94.9 8.2 %cross.3.spectra = bf16[8,2,768,128]{3,2,1,0:T(8,128)(2,1)S(1)} custom-call(s32[1]{0:T(128)} %bitcast.own.chan, s32[2,96]{1,0:T(2,128)S(1)} %bitcast.9, bf16[96,128,256]{2,1,0:T(8,128)(2,1)S(1)} %diagonal.1.diag, bf16[384,512]{1,0:T(8,128)(2,1)S(1)} %copy-done.4, bf16[2,2,768,128]{3,2,1,0:T(8,128)(2,1)S(1)} %whiten.3.refs_0_, ...), custom_call_target="tpu_custom_call" | custom-call | flops 1 | bytes 1 | tf_op jit(solution)/shard_map/cross/pallas_call | solution.py:365
  103.1 0.8 collective-permute-done.12.refs_1_
  103.9 0.6 collective-permute-done.14.refs_3_
  104.5 1.0 merge.1.refs_0_
  105.6 0.7 stack.8
  106.3 1.2 collective-permute-start.16
  107.5 0.7 stack.7
  108.2 2.3 %collective-permute-start.15 = (bf16[192,512]{1,0:T(8,128)(2,1)S(1)}, bf16[192,512]{1,0:T(8,128)(2,1)S(1)}, u32[]{:S(2)}, u32[]{:S(2)}) collective-permute-start(bf16[192,512]{1,0:T(8,128)(2,1)S(1)} %stack.7), channel_id=1, source_target_pairs={{0,1},{1,2},{2,3},{3,0},{4,5},{5,6},{6,7},{7,4},{8,9},{9,10},{10,1... | collective-permute-start | bytes 589832 | tf_op jit(solution)/shard_map/ppermute | solution.py:529
  110.5 0.7 stack.9
  111.2 1.1 collective-permute-start.17
  112.3 0.7 stack.6.refs_1_
  113.0 2.7 %collective-permute-done.16.refs_3_ = bf16[192,512]{1,0:T(8,128)(2,1)S(1)} collective-permute-done((bf16[192,512]{1,0:T(8,128)(2,1)S(1)}, bf16[192,512]{1,0:T(8,128)(2,1)S(1)}, u32[]{:S(2)}, u32[]{:S(2)}) %collective-permute-start.16) | collective-permute-done | bytes 196640 | tf_op jit(solution)/shard_map/ppermute | solution.py:529
  115.8 2.5 %collective-permute-done.15.refs_2_ = bf16[192,512]{1,0:T(8,128)(2,1)S(1)} collective-permute-done((bf16[192,512]{1,0:T(8,128)(2,1)S(1)}, bf16[192,512]{1,0:T(8,128)(2,1)S(1)}, u32[]{:S(2)}, u32[]{:S(2)}) %collective-permute-start.15) | collective-permute-done | bytes 196640 | tf_op jit(solution)/shard_map/ppermute | solution.py:529
  118.3 0.3 collective-permute-done.17.refs_4_
  118.6 1.8 %collective-permute-done.18.refs_0_ = bf16[768,512]{1,0:T(8,128)(2,1)S(1)} collective-permute-done((bf16[768,512]{1,0:T(8,128)(2,1)S(1)}, bf16[768,512]{1,0:T(8,128)(2,1)S(1)}, u32[]{:S(2)}, u32[]{:S(2)}) %collective-permute-start.18) | collective-permute-done | bytes 786464 | tf_op jit(solution)/shard_map/ppermute | solution.py:529
  120.4 4.1 %home.1.refs_4_ = f32[6,4,128,512]{3,2,1,0:T(8,128)} custom-call(s32[96]{0:T(128)S(1)} %copy-done.8, s32[1]{0:T(128)} %bitcast.own.chan, s32[1]{0:T(128)} %bitcast.1.time, bf16[768,512]{1,0:T(8,128)(2,1)S(1)} %merge.1.refs_0_, bf16[192,512]{1,0:T(8,128)(2,1)S(1)} %stack.6.refs_1_, bf16[192,512]{1,0:T(8,128)(2,1)S(1)} %collective-permute-done.15.refs_2_, ...), custom_call_target="tpu_custom_call" | custom-call | flops 1 | bytes 1 | tf_op jit(solution)/shard_map/home/pallas_call | solution.py:466
  124.5 0.1 collective-permute-done.21.refs_2_
  124.6 2.8 %collective-permute-done.22.refs_3_ = bf16[192,512]{1,0:T(8,128)(2,1)S(1)} collective-permute-done((bf16[192,512]{1,0:T(8,128)(2,1)S(1)}, bf16[192,512]{1,0:T(8,128)(2,1)S(1)}, u32[]{:S(2)}, u32[]{:S(2)}) %collective-permute-start.22) | collective-permute-done | bytes 196640 | tf_op jit(solution)/shard_map/ppermute | solution.py:529
  127.4 1.8 %moved.2.refs_2_ = f32[6,4,128,512]{3,2,1,0:T(8,128)} custom-call(s32[96]{0:T(128)S(1)} %copy-done.8, s32[1]{0:T(128)} %bitcast.own.chan, s32[1]{0:T(128)} %bitcast.1.time, bf16[768,512]{1,0:T(8,128)(2,1)S(1)} %collective-permute-done.18.refs_0_, bf16[192,512]{1,0:T(8,128)(2,1)S(1)} %collective-permute-done.20.refs_1_, ...), custom_call_target="tpu_custom_call", output_to_operand_aliasing={{}: (7, {})} | custom-call | flops 1 | bytes 1 | tf_op jit(solution)/shard_map/moved/pallas_call | solution.py:509
  129.2 0.3 collective-permute-done.19.refs_1_
  129.5 1.4 %moved.3 = f32[6,4,128,512]{3,2,1,0:T(8,128)} custom-call(s32[96]{0:T(128)S(1)} %copy-done.8, s32[1]{0:T(128)} %bitcast.own.chan, s32[1]{0:T(128)} %bitcast.1.time, bf16[768,512]{1,0:T(8,128)(2,1)S(1)} %collective-permute-done.18.refs_0_, bf16[192,512]{1,0:T(8,128)(2,1)S(1)} %collective-permute-done.19.refs_1_, ...), custom_call_target="tpu_custom_call", output_to_operand_aliasing={{}: (5, {})} | custom-call | flops 1 | bytes 1 | tf_op jit(solution)/shard_map/moved/pallas_call | solution.py:509
  (38 shorter events, 0.3 us)
Async XLA Ops:
  0.0 1.5 %copy-start.3 = (bf16[4,60,4096]{2,0,1:T(4,128)(2,1)S(1)}, bf16[4,60,4096]{2,0,1:T(4,128)(2,1)}, u32[]{:S(2)}) copy-start(bf16[4,60,4096]{2,0,1:T(4,128)(2,1)} %param.12) | copy-start | bytes 5898244
  1.5 0.7 copy-start.10
  2.2 43.2 %copy-start.1 = (bf16[1536,2048]{1,0:T(8,128)(2,1)S(1)}, bf16[1536,2048]{1,0:T(8,128)(2,1)}, u32[]{:S(2)}) copy-start(bf16[1536,2048]{1,0:T(8,128)(2,1)} %constant.23.clone.table) | copy-start | bytes 18874372
  2.2 43.2 %copy-start.2 = (bf16[768,768]{1,0:T(8,128)(2,1)S(1)}, bf16[768,768]{1,0:T(8,128)(2,1)}, u32[]{:S(2)}) copy-start(bf16[768,768]{1,0:T(8,128)(2,1)} %constant.24.clone.inside) | copy-start | bytes 3538948
  2.2 43.2 %copy-start.5 = (f32[768,1]{1,0:T(8,128)S(1)}, f32[768,1]{1,0:T(8,128)}, u32[]{:S(2)}) copy-start(f32[768,1]{1,0:T(8,128)} %constant.25.clone.inverse_count) | copy-start | bytes 9220
  2.2 43.2 %copy-start.7 = (bf16[2,2,128,128]{3,2,1,0:T(8,128)(2,1)S(1)}, bf16[2,2,128,128]{3,2,1,0:T(8,128)(2,1)}, u32[]{:S(2)}) copy-start(bf16[2,2,128,128]{3,2,1,0:T(8,128)(2,1)} %constant.26.clone.refs_0_) | copy-start | bytes 393220
  49.0 8.4 %collective-permute-start = (bf16[2,2,768,128]{3,2,1,0:T(8,128)(2,1)S(1)}, bf16[2,2,768,128]{3,2,1,0:T(8,128)(2,1)S(1)}, u32[]{:S(2)}, u32[]{:S(2)}) collective-permute-start(bf16[2,2,768,128]{3,2,1,0:T(8,128)(2,1)S(1)} %get-tuple-element.34.refs_0_), channel_id=1, source_target_pairs={{0,4},{4,0},{8,12},{12,8},{16,20},{20,16},{24,28},{28,24},{32,36},... | collective-permute-start | bytes 2359304 | tf_op jit(solution)/shard_map/ppermute | solution.py:546
  49.3 24.2 %collective-permute-start.7 = (bf16[2,2,768,128]{3,2,1,0:T(8,128)(2,1)S(1)}, bf16[2,2,768,128]{3,2,1,0:T(8,128)(2,1)S(1)}, u32[]{:S(2)}, u32[]{:S(2)}) collective-permute-start(bf16[2,2,768,128]{3,2,1,0:T(8,128)(2,1)S(1)} %get-tuple-element.34.refs_0_), channel_id=1, source_target_pairs={{0,8},{4,12},{8,16},{12,20},{16,24},{20,28},{24,32},{28,36},{32,40... | collective-permute-start | bytes 2359304 | tf_op jit(solution)/shard_map/ppermute | solution.py:529
  50.0 23.6 %collective-permute-start.8 = (bf16[2,2,768,128]{3,2,1,0:T(8,128)(2,1)S(1)}, bf16[2,2,768,128]{3,2,1,0:T(8,128)(2,1)S(1)}, u32[]{:S(2)}, u32[]{:S(2)}) collective-permute-start(bf16[2,2,768,128]{3,2,1,0:T(8,128)(2,1)S(1)} %get-tuple-element.34.refs_0_), channel_id=1, source_target_pairs={{0,120},{4,124},{8,0},{12,4},{16,8},{20,12},{24,16},{28,20},{32,24... | collective-permute-start | bytes 2359304 | tf_op jit(solution)/shard_map/ppermute | solution.py:529
  54.7 20.2 %copy-start.6 = (bf16[4,128,256]{2,1,0:T(8,128)(2,1)S(1)}, bf16[4,128,256]{2,1,0:T(8,128)(2,1)}, u32[]{:S(2)}) copy-start(bf16[4,128,256]{2,1,0:T(8,128)(2,1)} %constant.27.clone.spread) | copy-start | bytes 786436
  54.7 7.8 %collective-permute-start.1 = (bf16[768,128]{1,0:T(8,128)(2,1)S(1)}, bf16[768,128]{1,0:T(8,128)(2,1)S(1)}, u32[]{:S(2)}, u32[]{:S(2)}) collective-permute-start(bf16[768,128]{1,0:T(8,128)(2,1)S(1)} %get-tuple-element.37.s0), channel_id=1, source_target_pairs={{0,3},{1,0},{2,1},{3,2},{4,7},{5,4},{6,5},{7,6},{8,11},{9,8},{10,9... | collective-permute-start | bytes 589832 | tf_op jit(solution)/shard_map/ppermute | solution.py:529
  56.1 9.4 %collective-permute-start.2 = (bf16[768,128]{1,0:T(8,128)(2,1)S(1)}, bf16[768,128]{1,0:T(8,128)(2,1)S(1)}, u32[]{:S(2)}, u32[]{:S(2)}) collective-permute-start(bf16[768,128]{1,0:T(8,128)(2,1)S(1)} %get-tuple-element.37.s0), channel_id=1, source_target_pairs={{0,2},{1,3},{2,0},{3,1},{4,6},{5,7},{6,4},{7,5},{8,10},{9,11},{10,... | collective-permute-start | bytes 589832 | tf_op jit(solution)/shard_map/ppermute | solution.py:529
  57.3 10.9 %collective-permute-start.3 = (bf16[768,128]{1,0:T(8,128)(2,1)S(1)}, bf16[768,128]{1,0:T(8,128)(2,1)S(1)}, u32[]{:S(2)}, u32[]{:S(2)}) collective-permute-start(bf16[768,128]{1,0:T(8,128)(2,1)S(1)} %get-tuple-element.37.s0), channel_id=1, source_target_pairs={{0,1},{1,2},{2,3},{3,0},{4,5},{5,6},{6,7},{7,4},{8,9},{9,10},{10,1... | collective-permute-start | bytes 589832 | tf_op jit(solution)/shard_map/ppermute | solution.py:529
  68.2 22.8 %collective-permute-start.4 = (bf16[2,2,768,128]{3,2,1,0:T(8,128)(2,1)S(1)}, bf16[2,2,768,128]{3,2,1,0:T(8,128)(2,1)S(1)}, u32[]{:S(2)}, u32[]{:S(2)}) collective-permute-start(bf16[2,2,768,128]{3,2,1,0:T(8,128)(2,1)S(1)} %whiten.3.refs_0_), channel_id=1, source_target_pairs={{0,8},{4,12},{8,16},{12,20},{16,24},{20,28},{24,32},{28,36},{32,40... | collective-permute-start | bytes 2359304 | tf_op jit(solution)/shard_map/ppermute | solution.py:529
  68.2 22.8 %collective-permute-start.5 = (bf16[2,2,768,128]{3,2,1,0:T(8,128)(2,1)S(1)}, bf16[2,2,768,128]{3,2,1,0:T(8,128)(2,1)S(1)}, u32[]{:S(2)}, u32[]{:S(2)}) collective-permute-start(bf16[2,2,768,128]{3,2,1,0:T(8,128)(2,1)S(1)} %whiten.3.refs_0_), channel_id=1, source_target_pairs={{0,120},{4,124},{8,0},{12,4},{16,8},{20,12},{24,16},{28,20},{32,24... | collective-permute-start | bytes 2359304 | tf_op jit(solution)/shard_map/ppermute | solution.py:529
  73.6 17.4 %collective-permute-start.6 = (bf16[2,2,768,128]{3,2,1,0:T(8,128)(2,1)S(1)}, bf16[2,2,768,128]{3,2,1,0:T(8,128)(2,1)S(1)}, u32[]{:S(2)}, u32[]{:S(2)}) collective-permute-start(bf16[2,2,768,128]{3,2,1,0:T(8,128)(2,1)S(1)} %whiten.3.refs_0_), channel_id=1, source_target_pairs={{0,4},{4,0},{8,12},{12,8},{16,20},{20,16},{24,28},{28,24},{32,36},... | collective-permute-start | bytes 2359304 | tf_op jit(solution)/shard_map/ppermute | solution.py:546
  74.0 2.7 %collective-permute-start.10 = (bf16[1,2,768,128]{3,2,1,0:T(8,128)(2,1)S(1)}, bf16[1,2,768,128]{3,2,1,0:T(8,128)(2,1)S(1)}, u32[]{:S(2)}, u32[]{:S(2)}) collective-permute-start(bf16[1,2,768,128]{3,2,1,0:T(8,128)(2,1)S(1)} %get-tuple-element.44), channel_id=1, source_target_pairs={{0,4},{4,0},{8,12},{12,8},{16,20},{20,16},{24,28},{28,24},{32,36},... | collective-permute-start | bytes 1179656 | tf_op jit(solution)/shard_map/ppermute | solution.py:551
  74.6 2.4 %copy-start.4 = (bf16[384,512]{1,0:T(8,128)(2,1)S(1)}, bf16[384,512]{1,0:T(8,128)(2,1)}, u32[]{:S(2)}) copy-start(bf16[384,512]{1,0:T(8,128)(2,1)} %constant.28.clone.order) | copy-start | bytes 1179652
  74.6 2.4 %copy-start.9 = (s32[96,2]{0,1:T(2,128)S(1)}, s32[96,2]{0,1:T(2,128)}, u32[]{:S(2)}) copy-start(s32[96,2]{0,1:T(2,128)} %param.14) | copy-start | bytes 2308
  74.6 2.4 %collective-permute-start.9 = (bf16[1,2,768,128]{3,2,1,0:T(8,128)(2,1)S(1)}, bf16[1,2,768,128]{3,2,1,0:T(8,128)(2,1)S(1)}, u32[]{:S(2)}, u32[]{:S(2)}) collective-permute-start(bf16[1,2,768,128]{3,2,1,0:T(8,128)(2,1)S(1)} %get-tuple-element.43), channel_id=1, source_target_pairs={{0,4},{4,0},{8,12},{12,8},{16,20},{20,16},{24,28},{28,24},{32,36},... | collective-permute-start | bytes 1179656 | tf_op jit(solution)/shard_map/ppermute | solution.py:551
  77.0 8.4 %copy-start = (bf16[512,1536]{1,0:T(8,128)(2,1)S(1)}, bf16[512,1536]{1,0:T(8,128)(2,1)}, u32[]{:S(2)}) copy-start(bf16[512,1536]{1,0:T(8,128)(2,1)} %constant.29.clone.inverse) | copy-start | bytes 4718596
  91.1 3.8 %collective-permute-start.11 = (bf16[2,2,768,128]{3,2,1,0:T(8,128)(2,1)S(1)}, bf16[2,2,768,128]{3,2,1,0:T(8,128)(2,1)S(1)}, u32[]{:S(2)}, u32[]{:S(2)}) collective-permute-start(bf16[2,2,768,128]{3,2,1,0:T(8,128)(2,1)S(1)} %choose.3), channel_id=1, source_target_pairs={{0,4},{4,0},{8,12},{12,8},{16,20},{20,16},{24,28},{28,24},{32,36},... | collective-permute-start | bytes 2359304 | tf_op jit(solution)/shard_map/ppermute | solution.py:551
  91.2 12.7 %collective-permute-start.12 = (bf16[192,512]{1,0:T(8,128)(2,1)S(1)}, bf16[192,512]{1,0:T(8,128)(2,1)S(1)}, u32[]{:S(2)}, u32[]{:S(2)}) collective-permute-start(bf16[192,512]{1,0:T(8,128)(2,1)S(1)} %get-tuple-element.46), channel_id=1, source_target_pairs={{0,1},{1,2},{2,3},{3,0},{4,5},{5,6},{6,7},{7,4},{8,9},{9,10},{10,1... | collective-permute-start | bytes 589832 | tf_op jit(solution)/shard_map/ppermute | solution.py:529
  91.2 12.7 %collective-permute-start.13 = (bf16[192,512]{1,0:T(8,128)(2,1)S(1)}, bf16[192,512]{1,0:T(8,128)(2,1)S(1)}, u32[]{:S(2)}, u32[]{:S(2)}) collective-permute-start(bf16[192,512]{1,0:T(8,128)(2,1)S(1)} %get-tuple-element.47), channel_id=1, source_target_pairs={{0,2},{1,3},{2,0},{3,1},{4,6},{5,7},{6,4},{7,5},{8,10},{9,11},{10,... | collective-permute-start | bytes 589832 | tf_op jit(solution)/shard_map/ppermute | solution.py:529
  92.5 12.0 %collective-permute-start.14 = (bf16[192,512]{1,0:T(8,128)(2,1)S(1)}, bf16[192,512]{1,0:T(8,128)(2,1)S(1)}, u32[]{:S(2)}, u32[]{:S(2)}) collective-permute-start(bf16[192,512]{1,0:T(8,128)(2,1)S(1)} %get-tuple-element.48), channel_id=1, source_target_pairs={{0,3},{1,0},{2,1},{3,2},{4,7},{5,4},{6,5},{7,6},{8,11},{9,8},{10,9... | collective-permute-start | bytes 589832 | tf_op jit(solution)/shard_map/ppermute | solution.py:529
  105.6 14.8 %collective-permute-start.18 = (bf16[768,512]{1,0:T(8,128)(2,1)S(1)}, bf16[768,512]{1,0:T(8,128)(2,1)S(1)}, u32[]{:S(2)}, u32[]{:S(2)}) collective-permute-start(bf16[768,512]{1,0:T(8,128)(2,1)S(1)} %merge.1.refs_0_), channel_id=1, source_target_pairs={{0,4},{4,8},{8,12},{12,16},{16,20},{20,24},{24,28},{28,32},{32,36}... | collective-permute-start | bytes 2359304 | tf_op jit(solution)/shard_map/ppermute | solution.py:529
  106.3 9.4 %collective-permute-start.16 = (bf16[192,512]{1,0:T(8,128)(2,1)S(1)}, bf16[192,512]{1,0:T(8,128)(2,1)S(1)}, u32[]{:S(2)}, u32[]{:S(2)}) collective-permute-start(bf16[192,512]{1,0:T(8,128)(2,1)S(1)} %stack.8), channel_id=1, source_target_pairs={{0,2},{1,3},{2,0},{3,1},{4,6},{5,7},{6,4},{7,5},{8,10},{9,11},{10,... | collective-permute-start | bytes 589832 | tf_op jit(solution)/shard_map/ppermute | solution.py:529
  108.2 10.1 %collective-permute-start.15 = (bf16[192,512]{1,0:T(8,128)(2,1)S(1)}, bf16[192,512]{1,0:T(8,128)(2,1)S(1)}, u32[]{:S(2)}, u32[]{:S(2)}) collective-permute-start(bf16[192,512]{1,0:T(8,128)(2,1)S(1)} %stack.7), channel_id=1, source_target_pairs={{0,1},{1,2},{2,3},{3,0},{4,5},{5,6},{6,7},{7,4},{8,9},{9,10},{10,1... | collective-permute-start | bytes 589832 | tf_op jit(solution)/shard_map/ppermute | solution.py:529
  111.2 9.2 %copy-start.8 = (s32[96]{0:T(128)S(1)}, s32[96]{0:T(128)}, u32[]{:S(2)}) copy-start(s32[96]{0:T(128)} %owners.5) | copy-start | bytes 1156
  111.2 7.4 %collective-permute-start.17 = (bf16[192,512]{1,0:T(8,128)(2,1)S(1)}, bf16[192,512]{1,0:T(8,128)(2,1)S(1)}, u32[]{:S(2)}, u32[]{:S(2)}) collective-permute-start(bf16[192,512]{1,0:T(8,128)(2,1)S(1)} %stack.9), channel_id=1, source_target_pairs={{0,3},{1,0},{2,1},{3,2},{4,7},{5,4},{6,5},{7,6},{8,11},{9,8},{10,9... | collective-permute-start | bytes 589832 | tf_op jit(solution)/shard_map/ppermute | solution.py:529
  113.0 11.5 %collective-permute-start.20 = (bf16[192,512]{1,0:T(8,128)(2,1)S(1)}, bf16[192,512]{1,0:T(8,128)(2,1)S(1)}, u32[]{:S(2)}, u32[]{:S(2)}) collective-permute-start(bf16[192,512]{1,0:T(8,128)(2,1)S(1)} %stack.6.refs_1_), channel_id=1, source_target_pairs={{0,4},{4,8},{8,12},{12,16},{16,20},{20,24},{24,28},{28,32},{32,36}... | collective-permute-start | bytes 589832 | tf_op jit(solution)/shard_map/ppermute | solution.py:529
  115.8 8.8 %collective-permute-start.21 = (bf16[192,512]{1,0:T(8,128)(2,1)S(1)}, bf16[192,512]{1,0:T(8,128)(2,1)S(1)}, u32[]{:S(2)}, u32[]{:S(2)}) collective-permute-start(bf16[192,512]{1,0:T(8,128)(2,1)S(1)} %collective-permute-done.16.refs_3_), channel_id=1, source_target_pairs={{0,4},{4,8},{8,12},{12,16},{16,20},{20,24},{24,28},{28,32},{32,36}... | collective-permute-start | bytes 589832 | tf_op jit(solution)/shard_map/ppermute | solution.py:529
  118.3 9.1 %collective-permute-start.22 = (bf16[192,512]{1,0:T(8,128)(2,1)S(1)}, bf16[192,512]{1,0:T(8,128)(2,1)S(1)}, u32[]{:S(2)}, u32[]{:S(2)}) collective-permute-start(bf16[192,512]{1,0:T(8,128)(2,1)S(1)} %collective-permute-done.15.refs_2_), channel_id=1, source_target_pairs={{0,4},{4,8},{8,12},{12,16},{16,20},{20,24},{24,28},{28,32},{32,36}... | collective-permute-start | bytes 589832 | tf_op jit(solution)/shard_map/ppermute | solution.py:529
  118.6 10.9 %collective-permute-start.19 = (bf16[192,512]{1,0:T(8,128)(2,1)S(1)}, bf16[192,512]{1,0:T(8,128)(2,1)S(1)}, u32[]{:S(2)}, u32[]{:S(2)}) collective-permute-start(bf16[192,512]{1,0:T(8,128)(2,1)S(1)} %collective-permute-done.17.refs_4_), channel_id=1, source_target_pairs={{0,4},{4,8},{8,12},{12,16},{16,20},{20,24},{24,28},{28,32},{32,36}... | collective-permute-start | bytes 589832 | tf_op jit(solution)/shard_map/ppermute | solution.py:529

commit v8 on v7

--- a/solution.py
+++ b/solution.py
@@ -568,8 +568,10 @@
     merged = merge(stay_low)
     move_low = shifted(merged, "chan", 1)
     stay_high, move_high = [None] * TM, [None] * TM
+    parts = dict(zip((2, 1, 3), stack(spectra, (2, 1, 3), inverse)))
+    (parts[0],) = stack(spectra, (0,), inverse)
     for rel in order:
-        (part,) = stack(spectra, (rel,), inverse)
+        part = parts[rel]
         stay_high[rel] = shifted(part, "tm", rel) if rel else part
         move_high[rel] = shifted(stay_high[rel], "chan", 1)
     stay_high, move_low = lax.optimization_barrier((stay_high, move_low))

time: 131 us -> 132 us (level)
  waiting for transfers between devices: 23.9 us -> 25.4 us
    ppermute x18, waiting for transfers between devices: 23.6 us -> 25.1 us  [shifted(): lax.ppermute(value, axis, [(i, (i + distance) % count) for i in range(cou...]
    pallas_call x5 -> x3, Pallas kernels: 4.73 us -> 4.28 us  [stack(): pl.pallas_call(functools.partial(stack_kernel, rels), out_shape=[jax.Shap...]
  transfers between devices with their start and end apart: 23 -> 23, of which waited for: 14 -> 14; matrix products, arithmetic and copies ran while one was open for 0% -> 0% of each run, Pallas kernels for 25% -> 24%
where the time goes in v8:
time: 132 us
  blocking collectives  41.1 us (31%)
  Pallas kernels  39.8 us (30%)
  waiting for transfers between devices  25.4 us (19%)
  starting transfers between devices  23 us (17%)
  local copies, waits for them, and re-layouts  2.26 us (2%)
    all_to_all x1, blocking collectives, per_device(): lax.all_to_all(slabs, ('chan', 'tm'), split_axis=0, concat_axis=0, tiled=...  41.1 us
    ppermute x18, waiting for transfers between devices, shifted(): lax.ppermute(value, axis, [(i, (i + distance) % count) for i in range(cou...  25.1 us
    ppermute x18, starting transfers between devices, shifted(): lax.ppermute(value, axis, [(i, (i + distance) % count) for i in range(cou...  21.7 us
    pallas_call x2, Pallas kernels, cross(): pl.pallas_call(functools.partial(cross_kernel, part), out_shape=jax.Shape...  16.5 us
    pallas_call x2, Pallas kernels, whiten(): pl.pallas_call(functools.partial(whiten_kernel, part), out_shape=shapes,...  6.33 us
    pallas_call x1, Pallas kernels, home(): pl.pallas_call(home_kernel, out_shape=jax.ShapeDtypeStruct((TCAP, SRC_PAR...  4.35 us
    pallas_call x3, Pallas kernels, stack(): pl.pallas_call(functools.partial(stack_kernel, rels), out_shape=[jax.Shap...  4.28 us
    pallas_call x2, Pallas kernels, moved(): pl.pallas_call(functools.partial(moved_kernel, rels), out_shape=jax.Shape...  2.9 us
  transfers between devices with their start and end apart: 23, of which 14 were waited for; matrix products, arithmetic and copies ran while one was open for 0% of the time, Pallas kernels for 24%

profile of v8, /device:TPU:0, one launch (start us, length us, event | category | flops | bytes accessed | tf_op | source)
XLA Modules:
  0.0 131.9 jit_solution(10234693346723066919)
XLA Ops:
  0.0 1.5 %copy-done.3 = bf16[4,60,4096]{2,0,1:T(4,128)(2,1)S(1)} copy-done((bf16[4,60,4096]{2,0,1:T(4,128)(2,1)S(1)}, bf16[4,60,4096]{2,0,1:T(4,128)(2,1)}, u32[]{:S(2)}) %copy-start.3) | copy-done | bytes 1966104
  1.5 0.7 copy-done.10
  2.2 2.1 %pack.1 = bf16[128,64,128]{2,1,0:T(8,128)(2,1)S(1)} custom-call(s32[1]{0:T(128)} %bitcast.own.chan, s32[1]{0:T(128)} %bitcast.1.time, bf16[60,4,4096]{2,1,0:T(4,128)(2,1)S(1)} %bitcast.7, s32[4,128]{1,0:T(4,128)S(1)} %copy-done.10), custom_call_target="tpu_custom_call" | custom-call | tf_op jit(solution)/shard_map/pack/pallas_call | solution.py:157
  4.4 41.1 %all_to_all.5 = bf16[128,64,128]{2,1,0:T(8,128)(2,1)S(1)} all-to-all(bf16[128,64,128]{2,1,0:T(8,128)(2,1)S(1)} %pack.1), channel_id=1, replica_groups=mesh['chan'=32,'tm'=4] {'chan','tm'}, dimensions={0} | all-to-all | bytes 4194304 | tf_op jit(solution)/shard_map/all_to_all | solution.py:539
  45.5 3.5 %whiten.2 = (bf16[2,2,768,128]{3,2,1,0:T(8,128)(2,1)S(1)}, bf16[768,128]{1,0:T(8,128)(2,1)S(1)}) custom-call(s32[1]{0:T(128)} %bitcast.own.chan, bf16[32,4,64,128]{3,2,1,0:T(8,128)(2,1)S(1)} %bitcast.5, bf16[1536,2048]{1,0:T(8,128)(2,1)S(1)} %copy-done, bf16[768,768]{1,0:T(8,128)(2,1)S(1)} %copy-done.2, f32[768,1]{1,0:T(8,128)S(1)} %copy-done.5, ...), custom_call_target="tpu_custom_call" | custom-call | flops 1 | bytes 1 | tf_op jit(solution)/shard_map/whiten/pallas_call | solution.py:209
  49.0 0.4 collective-permute-start
  49.3 0.6 collective-permute-start.7
  50.0 4.7 %collective-permute-start.8 = (bf16[2,2,768,128]{3,2,1,0:T(8,128)(2,1)S(1)}, bf16[2,2,768,128]{3,2,1,0:T(8,128)(2,1)S(1)}, u32[]{:S(2)}, u32[]{:S(2)}) collective-permute-start(bf16[2,2,768,128]{3,2,1,0:T(8,128)(2,1)S(1)} %get-tuple-element.37.refs_0_), channel_id=1, source_target_pairs={{0,120},{4,124},{8,0},{12,4},{16,8},{20,12},{24,16},{28,20},{32,24... | collective-permute-start | bytes 2359304 | tf_op jit(solution)/shard_map/ppermute | solution.py:529
  54.7 1.4 %collective-permute-start.1 = (bf16[768,128]{1,0:T(8,128)(2,1)S(1)}, bf16[768,128]{1,0:T(8,128)(2,1)S(1)}, u32[]{:S(2)}, u32[]{:S(2)}) collective-permute-start(bf16[768,128]{1,0:T(8,128)(2,1)S(1)} %get-tuple-element.40.s0), channel_id=1, source_target_pairs={{0,3},{1,0},{2,1},{3,2},{4,7},{5,4},{6,5},{7,6},{8,11},{9,8},{10,9... | collective-permute-start | bytes 589832 | tf_op jit(solution)/shard_map/ppermute | solution.py:529
  56.1 1.2 collective-permute-start.2
  57.3 2.9 %whiten.3.refs_0_ = bf16[2,2,768,128]{3,2,1,0:T(8,128)(2,1)S(1)} custom-call(s32[1]{0:T(128)} %bitcast.own.chan, bf16[32,4,64,128]{3,2,1,0:T(8,128)(2,1)S(1)} %bitcast.6, bf16[1536,2048]{1,0:T(8,128)(2,1)S(1)} %copy-done, bf16[768,768]{1,0:T(8,128)(2,1)S(1)} %copy-done.2, f32[768,1]{1,0:T(8,128)S(1)} %copy-done.5), custom_call_target="tpu_custom_call" | custom-call | flops 1 | bytes 1 | tf_op jit(solution)/shard_map/whiten/pallas_call | solution.py:209
  60.2 2.3 %collective-permute-done.1.s1 = bf16[768,128]{1,0:T(8,128)(2,1)S(1)} collective-permute-done((bf16[768,128]{1,0:T(8,128)(2,1)S(1)}, bf16[768,128]{1,0:T(8,128)(2,1)S(1)}, u32[]{:S(2)}, u32[]{:S(2)}) %collective-permute-start.1) | collective-permute-done | bytes 196640 | tf_op jit(solution)/shard_map/ppermute | solution.py:529
  62.5 3.0 %collective-permute-done.2.s2 = bf16[768,128]{1,0:T(8,128)(2,1)S(1)} collective-permute-done((bf16[768,128]{1,0:T(8,128)(2,1)S(1)}, bf16[768,128]{1,0:T(8,128)(2,1)S(1)}, u32[]{:S(2)}, u32[]{:S(2)}) %collective-permute-start.2) | collective-permute-done | bytes 196640 | tf_op jit(solution)/shard_map/ppermute | solution.py:529
  65.5 2.8 %collective-permute-done.3.s3 = bf16[768,128]{1,0:T(8,128)(2,1)S(1)} collective-permute-done((bf16[768,128]{1,0:T(8,128)(2,1)S(1)}, bf16[768,128]{1,0:T(8,128)(2,1)S(1)}, u32[]{:S(2)}, u32[]{:S(2)}) %collective-permute-start.3) | collective-permute-done | bytes 196640 | tf_op jit(solution)/shard_map/ppermute | solution.py:529
  68.2 5.3 %collective-permute-start.5 = (bf16[2,2,768,128]{3,2,1,0:T(8,128)(2,1)S(1)}, bf16[2,2,768,128]{3,2,1,0:T(8,128)(2,1)S(1)}, u32[]{:S(2)}, u32[]{:S(2)}) collective-permute-start(bf16[2,2,768,128]{3,2,1,0:T(8,128)(2,1)S(1)} %whiten.3.refs_0_), channel_id=1, source_target_pairs={{0,120},{4,124},{8,0},{12,4},{16,8},{20,12},{24,16},{28,20},{32,24... | collective-permute-start | bytes 2359304 | tf_op jit(solution)/shard_map/ppermute | solution.py:529
  73.6 0.4 choose.2
  74.0 0.6 collective-permute-start.10
  74.6 0.3 collective-permute-start.9
  74.9 1.8 %diagonal.1.diag = bf16[96,128,256]{2,1,0:T(8,128)(2,1)S(1)} custom-call(bf16[768,128]{1,0:T(8,128)(2,1)S(1)} %get-tuple-element.40.s0, bf16[768,128]{1,0:T(8,128)(2,1)S(1)} %collective-permute-done.1.s1, bf16[768,128]{1,0:T(8,128)(2,1)S(1)} %collective-permute-done.2.s2, bf16[768,128]{1,0:T(8,128)(2,1)S(1)} %collective-permute-done.3.s3, ...), custom_call_target="tpu_custom_call" | custom-call | flops 1 | bytes 1 | tf_op jit(solution)/shard_map/diagonal/pallas_call | solution.py:269
  76.7 0.3 collective-permute-done.9.refs_4_
  77.0 8.4 %cross.2.spectra = bf16[8,2,768,128]{3,2,1,0:T(8,128)(2,1)S(1)} custom-call(s32[1]{0:T(128)} %bitcast.own.chan, s32[2,96]{1,0:T(2,128)S(1)} %bitcast.8, bf16[96,128,256]{2,1,0:T(8,128)(2,1)S(1)} %diagonal.1.diag, bf16[384,512]{1,0:T(8,128)(2,1)S(1)} %copy-done.4, bf16[2,2,768,128]{3,2,1,0:T(8,128)(2,1)S(1)} %get-tuple-element.37.refs_0_, ...), custom_call_target="tpu_custom_call" | custom-call | flops 1 | bytes 1 | tf_op jit(solution)/shard_map/cross/pallas_call | solution.py:365
  85.4 2.0 %stack.3 = (bf16[192,512]{1,0:T(8,128)(2,1)S(1)}, bf16[192,512]{1,0:T(8,128)(2,1)S(1)}, bf16[192,512]{1,0:T(8,128)(2,1)S(1)}, bf16[192,512]{1,0:T(8,128)(2,1)S(1)}) custom-call(bf16[8,2,768,128]{3,2,1,0:T(8,128)(2,1)S(1)} %cross.2.spectra, bf16[512,1536]{1,0:T(8,128)(2,1)S(1)} %copy-done.1), custom_call_target="tpu_custom_call" | custom-call | flops 1 | bytes 1 | tf_op jit(solution)/shard_map/stack/pallas_call | solution.py:404
  87.4 3.6 %collective-permute-done.4.below.refs_1_ = bf16[2,2,768,128]{3,2,1,0:T(8,128)(2,1)S(1)} collective-permute-done((bf16[2,2,768,128]{3,2,1,0:T(8,128)(2,1)S(1)}, bf16[2,2,768,128]{3,2,1,0:T(8,128)(2,1)S(1)}, u32[]{:S(2)}, u32[]{:S(2)}) %collective-permute-start.4) | collective-permute-done | bytes 786464 | tf_op jit(solution)/shard_map/ppermute | solution.py:529
  91.1 0.1 collective-permute-start.11
  91.2 0.1 collective-permute-start.12
  91.2 1.3 collective-permute-start.13
  92.5 2.4 %collective-permute-start.14 = (bf16[192,512]{1,0:T(8,128)(2,1)S(1)}, bf16[192,512]{1,0:T(8,128)(2,1)S(1)}, u32[]{:S(2)}, u32[]{:S(2)}) collective-permute-start(bf16[192,512]{1,0:T(8,128)(2,1)S(1)} %get-tuple-element.51), channel_id=1, source_target_pairs={{0,3},{1,0},{2,1},{3,2},{4,7},{5,4},{6,5},{7,6},{8,11},{9,8},{10,9... | collective-permute-start | bytes 589832 | tf_op jit(solution)/shard_map/ppermute | solution.py:529
  94.9 8.2 %cross.3.spectra = bf16[8,2,768,128]{3,2,1,0:T(8,128)(2,1)S(1)} custom-call(s32[1]{0:T(128)} %bitcast.own.chan, s32[2,96]{1,0:T(2,128)S(1)} %bitcast.9, bf16[96,128,256]{2,1,0:T(8,128)(2,1)S(1)} %diagonal.1.diag, bf16[384,512]{1,0:T(8,128)(2,1)S(1)} %copy-done.4, bf16[2,2,768,128]{3,2,1,0:T(8,128)(2,1)S(1)} %whiten.3.refs_0_, ...), custom_call_target="tpu_custom_call" | custom-call | flops 1 | bytes 1 | tf_op jit(solution)/shard_map/cross/pallas_call | solution.py:365
  103.1 0.8 collective-permute-done.12.refs_1_
  103.9 0.6 collective-permute-done.14.refs_3_
  104.5 1.0 merge.1.refs_0_
  105.6 0.1 collective-permute-start.18
  105.6 1.6 %stack.5 = (bf16[192,512]{1,0:T(8,128)(2,1)S(1)}, bf16[192,512]{1,0:T(8,128)(2,1)S(1)}, bf16[192,512]{1,0:T(8,128)(2,1)S(1)}) custom-call(bf16[8,2,768,128]{3,2,1,0:T(8,128)(2,1)S(1)} %cross.3.spectra, bf16[512,1536]{1,0:T(8,128)(2,1)S(1)} %copy-done.1), custom_call_target="tpu_custom_call" | custom-call | flops 1 | bytes 1 | tf_op jit(solution)/shard_map/stack/pallas_call | solution.py:404
  107.3 1.2 collective-permute-start.16
  108.4 2.2 %collective-permute-start.15 = (bf16[192,512]{1,0:T(8,128)(2,1)S(1)}, bf16[192,512]{1,0:T(8,128)(2,1)S(1)}, u32[]{:S(2)}, u32[]{:S(2)}) collective-permute-start(bf16[192,512]{1,0:T(8,128)(2,1)S(1)} %get-tuple-element.57), channel_id=1, source_target_pairs={{0,1},{1,2},{2,3},{3,0},{4,5},{5,6},{6,7},{7,4},{8,9},{9,10},{10,1... | collective-permute-start | bytes 589832 | tf_op jit(solution)/shard_map/ppermute | solution.py:529
  110.7 1.0 collective-permute-start.17
  111.7 0.7 stack.4.refs_1_
  112.4 0.1 collective-permute-start.20
  112.4 4.3 %collective-permute-done.16.refs_3_ = bf16[192,512]{1,0:T(8,128)(2,1)S(1)} collective-permute-done((bf16[192,512]{1,0:T(8,128)(2,1)S(1)}, bf16[192,512]{1,0:T(8,128)(2,1)S(1)}, u32[]{:S(2)}, u32[]{:S(2)}) %collective-permute-start.16) | collective-permute-done | bytes 196640 | tf_op jit(solution)/shard_map/ppermute | solution.py:529
  116.7 2.5 %collective-permute-done.15.refs_2_ = bf16[192,512]{1,0:T(8,128)(2,1)S(1)} collective-permute-done((bf16[192,512]{1,0:T(8,128)(2,1)S(1)}, bf16[192,512]{1,0:T(8,128)(2,1)S(1)}, u32[]{:S(2)}, u32[]{:S(2)}) %collective-permute-start.15) | collective-permute-done | bytes 196640 | tf_op jit(solution)/shard_map/ppermute | solution.py:529
  119.2 0.4 collective-permute-done.17.refs_4_
  119.6 0.8 collective-permute-done.18.refs_0_
  120.4 4.4 %home.1.refs_4_ = f32[6,4,128,512]{3,2,1,0:T(8,128)} custom-call(s32[96]{0:T(128)S(1)} %copy-done.8, s32[1]{0:T(128)} %bitcast.own.chan, s32[1]{0:T(128)} %bitcast.1.time, bf16[768,512]{1,0:T(8,128)(2,1)S(1)} %merge.1.refs_0_, bf16[192,512]{1,0:T(8,128)(2,1)S(1)} %stack.4.refs_1_, bf16[192,512]{1,0:T(8,128)(2,1)S(1)} %collective-permute-done.15.refs_2_, ...), custom_call_target="tpu_custom_call" | custom-call | flops 1 | bytes 1 | tf_op jit(solution)/shard_map/home/pallas_call | solution.py:466
  124.7 0.4 collective-permute-done.21.refs_2_
  125.1 3.2 %collective-permute-done.22.refs_3_ = bf16[192,512]{1,0:T(8,128)(2,1)S(1)} collective-permute-done((bf16[192,512]{1,0:T(8,128)(2,1)S(1)}, bf16[192,512]{1,0:T(8,128)(2,1)S(1)}, u32[]{:S(2)}, u32[]{:S(2)}) %collective-permute-start.22) | collective-permute-done | bytes 196640 | tf_op jit(solution)/shard_map/ppermute | solution.py:529
  128.3 1.6 %moved.2.refs_2_ = f32[6,4,128,512]{3,2,1,0:T(8,128)} custom-call(s32[96]{0:T(128)S(1)} %copy-done.8, s32[1]{0:T(128)} %bitcast.own.chan, s32[1]{0:T(128)} %bitcast.1.time, bf16[768,512]{1,0:T(8,128)(2,1)S(1)} %collective-permute-done.18.refs_0_, bf16[192,512]{1,0:T(8,128)(2,1)S(1)} %collective-permute-done.20.refs_1_, ...), custom_call_target="tpu_custom_call", output_to_operand_aliasing={{}: (7, {})} | custom-call | flops 1 | bytes 1 | tf_op jit(solution)/shard_map/moved/pallas_call | solution.py:509
  129.9 0.5 collective-permute-done.19.refs_1_
  130.4 1.3 %moved.3 = f32[6,4,128,512]{3,2,1,0:T(8,128)} custom-call(s32[96]{0:T(128)S(1)} %copy-done.8, s32[1]{0:T(128)} %bitcast.own.chan, s32[1]{0:T(128)} %bitcast.1.time, bf16[768,512]{1,0:T(8,128)(2,1)S(1)} %collective-permute-done.18.refs_0_, bf16[192,512]{1,0:T(8,128)(2,1)S(1)} %collective-permute-done.19.refs_1_, ...), custom_call_target="tpu_custom_call", output_to_operand_aliasing={{}: (5, {})} | custom-call | flops 1 | bytes 1 | tf_op jit(solution)/shard_map/moved/pallas_call | solution.py:509
  (36 shorter events, 0.2 us)
Async XLA Ops:
  0.0 1.5 %copy-start.3 = (bf16[4,60,4096]{2,0,1:T(4,128)(2,1)S(1)}, bf16[4,60,4096]{2,0,1:T(4,128)(2,1)}, u32[]{:S(2)}) copy-start(bf16[4,60,4096]{2,0,1:T(4,128)(2,1)} %param.12) | copy-start | bytes 5898244
  1.5 0.7 copy-start.10
  2.2 43.2 %copy-start = (bf16[1536,2048]{1,0:T(8,128)(2,1)S(1)}, bf16[1536,2048]{1,0:T(8,128)(2,1)}, u32[]{:S(2)}) copy-start(bf16[1536,2048]{1,0:T(8,128)(2,1)} %constant.23.clone.table) | copy-start | bytes 18874372
  2.2 43.2 %copy-start.2 = (bf16[768,768]{1,0:T(8,128)(2,1)S(1)}, bf16[768,768]{1,0:T(8,128)(2,1)}, u32[]{:S(2)}) copy-start(bf16[768,768]{1,0:T(8,128)(2,1)} %constant.24.clone.inside) | copy-start | bytes 3538948
  2.2 43.2 %copy-start.5 = (f32[768,1]{1,0:T(8,128)S(1)}, f32[768,1]{1,0:T(8,128)}, u32[]{:S(2)}) copy-start(f32[768,1]{1,0:T(8,128)} %constant.25.clone.inverse_count) | copy-start | bytes 9220
  2.2 43.2 %copy-start.7 = (bf16[2,2,128,128]{3,2,1,0:T(8,128)(2,1)S(1)}, bf16[2,2,128,128]{3,2,1,0:T(8,128)(2,1)}, u32[]{:S(2)}) copy-start(bf16[2,2,128,128]{3,2,1,0:T(8,128)(2,1)} %constant.26.clone.refs_0_) | copy-start | bytes 393220
  49.0 8.4 %collective-permute-start = (bf16[2,2,768,128]{3,2,1,0:T(8,128)(2,1)S(1)}, bf16[2,2,768,128]{3,2,1,0:T(8,128)(2,1)S(1)}, u32[]{:S(2)}, u32[]{:S(2)}) collective-permute-start(bf16[2,2,768,128]{3,2,1,0:T(8,128)(2,1)S(1)} %get-tuple-element.37.refs_0_), channel_id=1, source_target_pairs={{0,4},{4,0},{8,12},{12,8},{16,20},{20,16},{24,28},{28,24},{32,36},... | collective-permute-start | bytes 2359304 | tf_op jit(solution)/shard_map/ppermute | solution.py:546
  49.3 24.2 %collective-permute-start.7 = (bf16[2,2,768,128]{3,2,1,0:T(8,128)(2,1)S(1)}, bf16[2,2,768,128]{3,2,1,0:T(8,128)(2,1)S(1)}, u32[]{:S(2)}, u32[]{:S(2)}) collective-permute-start(bf16[2,2,768,128]{3,2,1,0:T(8,128)(2,1)S(1)} %get-tuple-element.37.refs_0_), channel_id=1, source_target_pairs={{0,8},{4,12},{8,16},{12,20},{16,24},{20,28},{24,32},{28,36},{32,40... | collective-permute-start | bytes 2359304 | tf_op jit(solution)/shard_map/ppermute | solution.py:529
  50.0 23.6 %collective-permute-start.8 = (bf16[2,2,768,128]{3,2,1,0:T(8,128)(2,1)S(1)}, bf16[2,2,768,128]{3,2,1,0:T(8,128)(2,1)S(1)}, u32[]{:S(2)}, u32[]{:S(2)}) collective-permute-start(bf16[2,2,768,128]{3,2,1,0:T(8,128)(2,1)S(1)} %get-tuple-element.37.refs_0_), channel_id=1, source_target_pairs={{0,120},{4,124},{8,0},{12,4},{16,8},{20,12},{24,16},{28,20},{32,24... | collective-permute-start | bytes 2359304 | tf_op jit(solution)/shard_map/ppermute | solution.py:529
  54.7 20.2 %copy-start.6 = (bf16[4,128,256]{2,1,0:T(8,128)(2,1)S(1)}, bf16[4,128,256]{2,1,0:T(8,128)(2,1)}, u32[]{:S(2)}) copy-start(bf16[4,128,256]{2,1,0:T(8,128)(2,1)} %constant.27.clone.spread) | copy-start | bytes 786436
  54.7 7.8 %collective-permute-start.1 = (bf16[768,128]{1,0:T(8,128)(2,1)S(1)}, bf16[768,128]{1,0:T(8,128)(2,1)S(1)}, u32[]{:S(2)}, u32[]{:S(2)}) collective-permute-start(bf16[768,128]{1,0:T(8,128)(2,1)S(1)} %get-tuple-element.40.s0), channel_id=1, source_target_pairs={{0,3},{1,0},{2,1},{3,2},{4,7},{5,4},{6,5},{7,6},{8,11},{9,8},{10,9... | collective-permute-start | bytes 589832 | tf_op jit(solution)/shard_map/ppermute | solution.py:529
  56.1 9.4 %collective-permute-start.2 = (bf16[768,128]{1,0:T(8,128)(2,1)S(1)}, bf16[768,128]{1,0:T(8,128)(2,1)S(1)}, u32[]{:S(2)}, u32[]{:S(2)}) collective-permute-start(bf16[768,128]{1,0:T(8,128)(2,1)S(1)} %get-tuple-element.40.s0), channel_id=1, source_target_pairs={{0,2},{1,3},{2,0},{3,1},{4,6},{5,7},{6,4},{7,5},{8,10},{9,11},{10,... | collective-permute-start | bytes 589832 | tf_op jit(solution)/shard_map/ppermute | solution.py:529
  57.3 10.9 %collective-permute-start.3 = (bf16[768,128]{1,0:T(8,128)(2,1)S(1)}, bf16[768,128]{1,0:T(8,128)(2,1)S(1)}, u32[]{:S(2)}, u32[]{:S(2)}) collective-permute-start(bf16[768,128]{1,0:T(8,128)(2,1)S(1)} %get-tuple-element.40.s0), channel_id=1, source_target_pairs={{0,1},{1,2},{2,3},{3,0},{4,5},{5,6},{6,7},{7,4},{8,9},{9,10},{10,1... | collective-permute-start | bytes 589832 | tf_op jit(solution)/shard_map/ppermute | solution.py:529
  68.2 22.8 %collective-permute-start.4 = (bf16[2,2,768,128]{3,2,1,0:T(8,128)(2,1)S(1)}, bf16[2,2,768,128]{3,2,1,0:T(8,128)(2,1)S(1)}, u32[]{:S(2)}, u32[]{:S(2)}) collective-permute-start(bf16[2,2,768,128]{3,2,1,0:T(8,128)(2,1)S(1)} %whiten.3.refs_0_), channel_id=1, source_target_pairs={{0,8},{4,12},{8,16},{12,20},{16,24},{20,28},{24,32},{28,36},{32,40... | collective-permute-start | bytes 2359304 | tf_op jit(solution)/shard_map/ppermute | solution.py:529
  68.2 22.8 %collective-permute-start.5 = (bf16[2,2,768,128]{3,2,1,0:T(8,128)(2,1)S(1)}, bf16[2,2,768,128]{3,2,1,0:T(8,128)(2,1)S(1)}, u32[]{:S(2)}, u32[]{:S(2)}) collective-permute-start(bf16[2,2,768,128]{3,2,1,0:T(8,128)(2,1)S(1)} %whiten.3.refs_0_), channel_id=1, source_target_pairs={{0,120},{4,124},{8,0},{12,4},{16,8},{20,12},{24,16},{28,20},{32,24... | collective-permute-start | bytes 2359304 | tf_op jit(solution)/shard_map/ppermute | solution.py:529
  73.6 17.4 %collective-permute-start.6 = (bf16[2,2,768,128]{3,2,1,0:T(8,128)(2,1)S(1)}, bf16[2,2,768,128]{3,2,1,0:T(8,128)(2,1)S(1)}, u32[]{:S(2)}, u32[]{:S(2)}) collective-permute-start(bf16[2,2,768,128]{3,2,1,0:T(8,128)(2,1)S(1)} %whiten.3.refs_0_), channel_id=1, source_target_pairs={{0,4},{4,0},{8,12},{12,8},{16,20},{20,16},{24,28},{28,24},{32,36},... | collective-permute-start | bytes 2359304 | tf_op jit(solution)/shard_map/ppermute | solution.py:546
  74.0 2.7 %collective-permute-start.10 = (bf16[1,2,768,128]{3,2,1,0:T(8,128)(2,1)S(1)}, bf16[1,2,768,128]{3,2,1,0:T(8,128)(2,1)S(1)}, u32[]{:S(2)}, u32[]{:S(2)}) collective-permute-start(bf16[1,2,768,128]{3,2,1,0:T(8,128)(2,1)S(1)} %get-tuple-element.47), channel_id=1, source_target_pairs={{0,4},{4,0},{8,12},{12,8},{16,20},{20,16},{24,28},{28,24},{32,36},... | collective-permute-start | bytes 1179656 | tf_op jit(solution)/shard_map/ppermute | solution.py:551
  74.6 2.4 %copy-start.4 = (bf16[384,512]{1,0:T(8,128)(2,1)S(1)}, bf16[384,512]{1,0:T(8,128)(2,1)}, u32[]{:S(2)}) copy-start(bf16[384,512]{1,0:T(8,128)(2,1)} %constant.28.clone.order) | copy-start | bytes 1179652
  74.6 2.4 %copy-start.9 = (s32[96,2]{0,1:T(2,128)S(1)}, s32[96,2]{0,1:T(2,128)}, u32[]{:S(2)}) copy-start(s32[96,2]{0,1:T(2,128)} %param.14) | copy-start | bytes 2308
  74.6 2.4 %collective-permute-start.9 = (bf16[1,2,768,128]{3,2,1,0:T(8,128)(2,1)S(1)}, bf16[1,2,768,128]{3,2,1,0:T(8,128)(2,1)S(1)}, u32[]{:S(2)}, u32[]{:S(2)}) collective-permute-start(bf16[1,2,768,128]{3,2,1,0:T(8,128)(2,1)S(1)} %get-tuple-element.46), channel_id=1, source_target_pairs={{0,4},{4,0},{8,12},{12,8},{16,20},{20,16},{24,28},{28,24},{32,36},... | collective-permute-start | bytes 1179656 | tf_op jit(solution)/shard_map/ppermute | solution.py:551
  77.0 8.4 %copy-start.1 = (bf16[512,1536]{1,0:T(8,128)(2,1)S(1)}, bf16[512,1536]{1,0:T(8,128)(2,1)}, u32[]{:S(2)}) copy-start(bf16[512,1536]{1,0:T(8,128)(2,1)} %constant.29.clone.inverse) | copy-start | bytes 4718596
  91.1 3.8 %collective-permute-start.11 = (bf16[2,2,768,128]{3,2,1,0:T(8,128)(2,1)S(1)}, bf16[2,2,768,128]{3,2,1,0:T(8,128)(2,1)S(1)}, u32[]{:S(2)}, u32[]{:S(2)}) collective-permute-start(bf16[2,2,768,128]{3,2,1,0:T(8,128)(2,1)S(1)} %choose.3), channel_id=1, source_target_pairs={{0,4},{4,0},{8,12},{12,8},{16,20},{20,16},{24,28},{28,24},{32,36},... | collective-permute-start | bytes 2359304 | tf_op jit(solution)/shard_map/ppermute | solution.py:551
  91.2 12.7 %collective-permute-start.12 = (bf16[192,512]{1,0:T(8,128)(2,1)S(1)}, bf16[192,512]{1,0:T(8,128)(2,1)S(1)}, u32[]{:S(2)}, u32[]{:S(2)}) collective-permute-start(bf16[192,512]{1,0:T(8,128)(2,1)S(1)} %get-tuple-element.49), channel_id=1, source_target_pairs={{0,1},{1,2},{2,3},{3,0},{4,5},{5,6},{6,7},{7,4},{8,9},{9,10},{10,1... | collective-permute-start | bytes 589832 | tf_op jit(solution)/shard_map/ppermute | solution.py:529
  91.2 12.7 %collective-permute-start.13 = (bf16[192,512]{1,0:T(8,128)(2,1)S(1)}, bf16[192,512]{1,0:T(8,128)(2,1)S(1)}, u32[]{:S(2)}, u32[]{:S(2)}) collective-permute-start(bf16[192,512]{1,0:T(8,128)(2,1)S(1)} %get-tuple-element.50), channel_id=1, source_target_pairs={{0,2},{1,3},{2,0},{3,1},{4,6},{5,7},{6,4},{7,5},{8,10},{9,11},{10,... | collective-permute-start | bytes 589832 | tf_op jit(solution)/shard_map/ppermute | solution.py:529
  92.5 12.0 %collective-permute-start.14 = (bf16[192,512]{1,0:T(8,128)(2,1)S(1)}, bf16[192,512]{1,0:T(8,128)(2,1)S(1)}, u32[]{:S(2)}, u32[]{:S(2)}) collective-permute-start(bf16[192,512]{1,0:T(8,128)(2,1)S(1)} %get-tuple-element.51), channel_id=1, source_target_pairs={{0,3},{1,0},{2,1},{3,2},{4,7},{5,4},{6,5},{7,6},{8,11},{9,8},{10,9... | collective-permute-start | bytes 589832 | tf_op jit(solution)/shard_map/ppermute | solution.py:529
  105.6 14.8 %collective-permute-start.18 = (bf16[768,512]{1,0:T(8,128)(2,1)S(1)}, bf16[768,512]{1,0:T(8,128)(2,1)S(1)}, u32[]{:S(2)}, u32[]{:S(2)}) collective-permute-start(bf16[768,512]{1,0:T(8,128)(2,1)S(1)} %merge.1.refs_0_), channel_id=1, source_target_pairs={{0,4},{4,8},{8,12},{12,16},{16,20},{20,24},{24,28},{28,32},{32,36}... | collective-permute-start | bytes 2359304 | tf_op jit(solution)/shard_map/ppermute | solution.py:529
  107.2 13.1 %copy-start.8 = (s32[96]{0:T(128)S(1)}, s32[96]{0:T(128)}, u32[]{:S(2)}) copy-start(s32[96]{0:T(128)} %owners.5) | copy-start | bytes 1156
  107.3 9.4 %collective-permute-start.16 = (bf16[192,512]{1,0:T(8,128)(2,1)S(1)}, bf16[192,512]{1,0:T(8,128)(2,1)S(1)}, u32[]{:S(2)}, u32[]{:S(2)}) collective-permute-start(bf16[192,512]{1,0:T(8,128)(2,1)S(1)} %get-tuple-element.58), channel_id=1, source_target_pairs={{0,2},{1,3},{2,0},{3,1},{4,6},{5,7},{6,4},{7,5},{8,10},{9,11},{10,... | collective-permute-start | bytes 589832 | tf_op jit(solution)/shard_map/ppermute | solution.py:529
  108.4 10.8 %collective-permute-start.15 = (bf16[192,512]{1,0:T(8,128)(2,1)S(1)}, bf16[192,512]{1,0:T(8,128)(2,1)S(1)}, u32[]{:S(2)}, u32[]{:S(2)}) collective-permute-start(bf16[192,512]{1,0:T(8,128)(2,1)S(1)} %get-tuple-element.57), channel_id=1, source_target_pairs={{0,1},{1,2},{2,3},{3,0},{4,5},{5,6},{6,7},{7,4},{8,9},{9,10},{10,1... | collective-permute-start | bytes 589832 | tf_op jit(solution)/shard_map/ppermute | solution.py:529
  110.7 8.9 %collective-permute-start.17 = (bf16[192,512]{1,0:T(8,128)(2,1)S(1)}, bf16[192,512]{1,0:T(8,128)(2,1)S(1)}, u32[]{:S(2)}, u32[]{:S(2)}) collective-permute-start(bf16[192,512]{1,0:T(8,128)(2,1)S(1)} %get-tuple-element.59), channel_id=1, source_target_pairs={{0,3},{1,0},{2,1},{3,2},{4,7},{5,4},{6,5},{7,6},{8,11},{9,8},{10,9... | collective-permute-start | bytes 589832 | tf_op jit(solution)/shard_map/ppermute | solution.py:529
  112.4 12.4 %collective-permute-start.20 = (bf16[192,512]{1,0:T(8,128)(2,1)S(1)}, bf16[192,512]{1,0:T(8,128)(2,1)S(1)}, u32[]{:S(2)}, u32[]{:S(2)}) collective-permute-start(bf16[192,512]{1,0:T(8,128)(2,1)S(1)} %stack.4.refs_1_), channel_id=1, source_target_pairs={{0,4},{4,8},{8,12},{12,16},{16,20},{20,24},{24,28},{28,32},{32,36}... | collective-permute-start | bytes 589832 | tf_op jit(solution)/shard_map/ppermute | solution.py:529
  116.7 8.4 %collective-permute-start.21 = (bf16[192,512]{1,0:T(8,128)(2,1)S(1)}, bf16[192,512]{1,0:T(8,128)(2,1)S(1)}, u32[]{:S(2)}, u32[]{:S(2)}) collective-permute-start(bf16[192,512]{1,0:T(8,128)(2,1)S(1)} %collective-permute-done.16.refs_3_), channel_id=1, source_target_pairs={{0,4},{4,8},{8,12},{12,16},{16,20},{20,24},{24,28},{28,32},{32,36}... | collective-permute-start | bytes 589832 | tf_op jit(solution)/shard_map/ppermute | solution.py:529
  119.2 9.1 %collective-permute-start.22 = (bf16[192,512]{1,0:T(8,128)(2,1)S(1)}, bf16[192,512]{1,0:T(8,128)(2,1)S(1)}, u32[]{:S(2)}, u32[]{:S(2)}) collective-permute-start(bf16[192,512]{1,0:T(8,128)(2,1)S(1)} %collective-permute-done.15.refs_2_), channel_id=1, source_target_pairs={{0,4},{4,8},{8,12},{12,16},{16,20},{20,24},{24,28},{28,32},{32,36}... | collective-permute-start | bytes 589832 | tf_op jit(solution)/shard_map/ppermute | solution.py:529
  119.6 10.8 %collective-permute-start.19 = (bf16[192,512]{1,0:T(8,128)(2,1)S(1)}, bf16[192,512]{1,0:T(8,128)(2,1)S(1)}, u32[]{:S(2)}, u32[]{:S(2)}) collective-permute-start(bf16[192,512]{1,0:T(8,128)(2,1)S(1)} %collective-permute-done.17.refs_4_), channel_id=1, source_target_pairs={{0,4},{4,8},{8,12},{12,16},{16,20},{20,24},{24,28},{28,32},{32,36}... | collective-permute-start | bytes 589832 | tf_op jit(solution)/shard_map/ppermute | solution.py:529
